TPU v7x, 256 devices: a whole 4x4x8 slice. The times are simulated.
256 devices in a mesh: replica: 8 (over z_lo, core), fsdp: 32 (over z_hi, y, x).
Axes of the slice: x: 4, y: 4, z: 8 (z_hi: 2, z_lo: 4; z = z_hi * 4 + z_lo), core: 2. Of those that a mesh axis runs over, the one named last changes fastest.
Arguments:
- layer_index: int32 [8], P('replica'), may hold values from 0 to 3
- inputs: bfloat16 [65536, 4608], P(('replica', 'fsdp')), may hold values from -24 to 24
- norm_gain: float32 [4608], replicated, may hold values from 0.1 to 1.9
- cotangent: bfloat16 [65536, 1024], P(('replica', 'fsdp')), may hold values from -6 to 6
- local_fragment: bfloat16 [8, 4, 4608, 1024], P('replica', None, 'fsdp'), may hold values from -6 to 6
- global_fragment: float32 [4, 4608, 1024], P(None, 'fsdp'), may hold values from -6 to 6
- momentum: float32 [4, 4608, 1024], P(None, 'fsdp'), may hold values from -4 to 4
Outputs:
- keys_block: bfloat16 [65536, 1024], P(('replica', 'fsdp'))
- weight_grad: float32 [8, 4608, 1024], P('replica', 'fsdp')
- new_global: float32 [4, 4608, 1024], P(None, 'fsdp')
- new_momentum: float32 [4, 4608, 1024], P(None, 'fsdp')
Inputs may be any that keep to these rules, and one draw needn't show every extreme that they name: `layer_index`: a layer of the fragment for each replica.
All inputs are finite; a program needn't handle non-finite values.
Results may differ from a plain program's by a relative error of at most 0.0049.
Values may be sent and summed in bfloat16 or wider, within the bound.
No kernel may reach another device: no remote copies, remote signals or barrier semaphores. Data moves between devices by JAX's collectives and lax.ppermute only.
A program may use at most 128 MiB of HBM per device.

v0:
```python
import jax
import jax.numpy as jnp
from jax import lax
from jax.sharding import PartitionSpec as P


def body(layer_index, inputs, norm_gain, cotangent, local_fragment, global_fragment, momentum):
    width = inputs.shape[1]
    scale_factor = float(width) ** (-0.5)
    values = inputs.astype(jnp.float32)
    stats = jnp.mean(values * values, axis=1, keepdims=True)
    normed = (values * lax.rsqrt(stats + 1e-06) * norm_gain[None, :]).astype(jnp.bfloat16)
    own_fragment = local_fragment[0]
    layer = lax.dynamic_index_in_dim(own_fragment, layer_index[0], 0, keepdims=False)
    columns = normed
    key_sum = jnp.dot(
        columns,
        lax.all_gather(layer, "fsdp", axis=0, tiled=True),
        preferred_element_type=jnp.float32,
    )
    keys_block = (key_sum * scale_factor).astype(jnp.bfloat16)
    columns = normed
    product = lax.dot_general(
        columns, cotangent, (((0,), (0,)), ((), ())), preferred_element_type=jnp.float32
    )
    grad_shard = lax.psum_scatter(product * scale_factor, "fsdp", scatter_dimension=0, tiled=True)
    weight_grad = grad_shard[None]
    delta = global_fragment - own_fragment.astype(jnp.float32)
    replicas = lax.axis_size("replica")
    average = lax.psum(delta, "replica") / replicas
    new_momentum = 0.9 * momentum + average
    new_global = global_fragment - 0.7 * (average + 0.9 * new_momentum)
    return (keys_block, weight_grad, new_global, new_momentum)


def solution(mesh):
    placed = (
        P("replica"),
        P(("replica", "fsdp"), None),
        P(),
        P(("replica", "fsdp"), None),
        P("replica", None, "fsdp", None),
        P(None, "fsdp", None),
        P(None, "fsdp", None),
    )
    return jax.shard_map(
        body,
        mesh=mesh,
        in_specs=placed,
        out_specs=(
            P(("replica", "fsdp"), None),
            P("replica", "fsdp", None),
            P(None, "fsdp", None),
            P(None, "fsdp", None),
        ),
        check_vma=False,
    )
```

profile of v0, /device:TPU:1, one launch (start us, length us, event | category | flops | bytes accessed | tf_op | source)
XLA Modules:
  0.0 553.4 jit_solution(4965488777257141292)
XLA Ops:
  8.0 0.0 copy-start
  8.0 0.0 all-reduce.2.cloned.1.call-start
  8.1 4.0 convert_subtract_fusion
  12.0 0.0 copy-start.1
  12.0 0.0 copy-start.2
  12.0 0.0 all-reduce.2.cloned.1.call-update
  12.1 0.0 all-gather.3.cloned.1.call-start
  12.9 1.7 constant_dynamic-slice_fusion
  14.6 0.0 all-gather.3.cloned.1.call-update
  14.7 0.0 reduce-scatter.2.cloned.1.call-start
  14.7 0.0 copy-done.1
  14.7 0.5 fusion.2
  15.3 0.0 copy-done
  15.3 0.0 copy-done.2
  15.3 8.0 %convolution_multiply_fusion = f32[4608,1024]{1,0:T(8,128)} fusion(bf16[256,1024]{1,0:T(8,128)(2,1)S(1)} %copy-done, bf16[256,4608]{1,0:T(8,128)(2,1)S(1)} %copy-done.1, f32[4608]{0:T(1024)S(1)} %copy-done.2, f32[256]{0:T(256)S(1)} %add_rsqrt_fusion), kind=kOutput, calls=%fused_computation | convolution fusion | flops 2425356288 | bytes 21777408 | tf_op jit(solution)/shard_map/dot_general | solution.py:23
  23.3 0.0 reduce-scatter.2.cloned.1.call-update
  23.3 149.0 %all-reduce.2.cloned.1.call-done = f32[4,144,1024]{2,1,0:T(8,128)} async-done(((f32[4,144,1024]{2,1,0:T(8,128)}), f32[4,144,1024]{2,1,0:T(8,128)}) %all-reduce.2.cloned.1.call-update) | async-done | bytes 2359312 | tf_op jit(solution)/shard_map/psum | solution.py:30
  172.3 6.7 %multiply_subtract_fusion = (f32[4,144,1024]{2,1,0:T(8,128)}, f32[4,144,1024]{2,1,0:T(8,128)}) fusion(f32[4,144,1024]{2,1,0:T(8,128)} %param.12, f32[4,144,1024]{2,1,0:T(8,128)} %all-reduce.2.cloned.1.call-done, f32[4,144,1024]{2,1,0:T(8,128)} %param.13), kind=kLoop, calls=%fused_computation.9 | loop fusion | flops 4128768 | bytes 11796480 | tf_op jit(solution)/shard_map/sub | solution.py:32
  179.0 0.0 all-gather.3.cloned.1.call-done
  179.0 7.2 %fusion.8 = bf16[256,1024]{1,0:T(8,128)(2,1)} fusion(bf16[1,1,4608,1024]{3,2,1,0:T(8,128)(2,1)} %all-gather.3.cloned.1.call-done, bf16[256,4608]{1,0:T(8,128)(2,1)S(1)} %copy-done.1, f32[4608]{0:T(1024)S(1)} %copy-done.2, f32[256]{0:T(256)S(1)} %add_rsqrt_fusion), kind=kOutput, calls=%fused_computation.12 | convolution fusion | flops 2421161984 | bytes 12340224 | tf_op jit(solution)/shard_map/dot_general | solution.py:16
  186.2 359.8 %reduce-scatter.2.cloned.1.call-done = f32[144,1024]{1,0:T(8,128)} async-done(((f32[4608,1024]{1,0:T(8,128)}), f32[144,1024]{1,0:T(8,128)}) %reduce-scatter.2.cloned.1.call-update) | async-done | bytes 589840 | tf_op jit(solution)/shard_map/reduce_scatter | solution.py:26
  (1 shorter events, 0.0 us)
Async XLA Ops:
  8.0 7.3 %copy-start = (bf16[256,1024]{1,0:T(8,128)(2,1)S(1)}, bf16[256,1024]{1,0:T(8,128)(2,1)}, u32[]{:S(2)}) copy-start(bf16[256,1024]{1,0:T(8,128)(2,1)} %param.10) | copy-start | bytes 1572868
  8.0 164.3 %all-reduce.2.cloned.1.call-start = ((), (), s32[]{:S(2)}) async-start(), calls=%async_computation.2 | async-start | bytes 4718592 | tf_op jit(solution)/shard_map/psum | solution.py:30
  12.0 2.7 copy-start.1
  12.0 3.2 copy-start.2
  12.1 166.9 %all-gather.3.cloned.1.call-start = ((), (), s32[]{:S(2)}) async-start(), calls=%async_computation.3 | async-start | bytes 9732096 | tf_op jit(solution)/shard_map/all_gather | solution.py:18
  14.7 531.3 %reduce-scatter.2.cloned.1.call-start = ((), (), s32[]{:S(2)}) async-start(), calls=%async_computation.1 | async-start | bytes 19464192 | tf_op jit(solution)/shard_map/reduce_scatter | solution.py:26
Sparse Core Ops, SparseCore 0:
  12.2 160.0 all-reduce.1
Sparse Core Ops, SparseCore 1:
  16.5 144.9 all-gather.2
  168.1 377.8 reduce-scatter.1
where the time goes:
time: 555 us; the launch traced here: 553 us
  waiting for transfers between devices  509 us (92%)
  between operations  16.3 us (3%)
  matrix products  15.2 us (3%)
  other arithmetic  11.2 us (2%)
    reduce_scatter x1, waiting for transfers between devices, body(): lax.psum_scatter(product * scale_factor, 'fsdp', scatter_dimension=0, til...  360 us
    psum x1, waiting for transfers between devices, body(): average = lax.psum(delta, 'replica') / replicas  149 us
  transfers between devices with their start and end apart: 3, of which 2 were waited for; matrix products, arithmetic and copies ran while one was open for 4% of the time, Pallas kernels for 0%

commit v1 on v0

v1 whole, which is shorter than its diff:
```python
import jax
import jax.numpy as jnp
from jax import lax
from jax.experimental import pallas as pl
from jax.experimental.pallas import tpu as pltpu
from jax.sharding import PartitionSpec as P

D = 4608
KV = 1024
ROWS = 144
WIDE = 576
TOK = 256
SCALE = float(D) ** -0.5
BF = jnp.bfloat16
F32 = jnp.float32
LIMIT = 48 * 1024 * 1024


def _place():
    f = lax.axis_index("fsdp")
    r = lax.axis_index("replica")
    return r // 2, r % 2, f // 16, (f // 4) % 4, f % 4


def _shift_y(v, k):
    perm = [(i, (i // 16) * 16 + ((i // 4 + k) % 4) * 4 + i % 4) for i in range(32)]
    return lax.ppermute(v, "fsdp", perm)


def _shift_x(v, k):
    return lax.ppermute(v, "fsdp", [(i, (i // 4) * 4 + (i + k) % 4) for i in range(32)])


def _swap_zh(v):
    return lax.ppermute(v, "fsdp", [(i, (i + 16) % 32) for i in range(32)])


def _shift_zl(v, k):
    return lax.ppermute(v, "replica", [(i, (i + 2 * k) % 8) for i in range(8)])


def _swap_core(v):
    return lax.ppermute(v, "replica", [(i, i ^ 1) for i in range(8)])


def _call(kernel, name, outs, scratch=(), flops=0, traffic=0, **kw):
    return pl.pallas_call(
        kernel,
        name=name,
        out_shape=[jax.ShapeDtypeStruct(s, d) for s, d in outs],
        scratch_shapes=list(scratch),
        compiler_params=pltpu.CompilerParams(vmem_limit_bytes=LIMIT),
        cost_estimate=pl.CostEstimate(flops=flops, bytes_accessed=traffic, transcendentals=0),
        **kw,
    )


def _vmem(n):
    return [pl.BlockSpec(memory_space=pltpu.VMEM)] * n


def _pick_kernel(index_ref, frag_ref, used_ref, s1_ref, s2_ref, s3_ref, own_ref, sems):
    zl = _place()[0]
    copies = [pltpu.make_async_copy(frag_ref.at[0, index_ref[0]], used_ref, sems.at[0])]
    for k, out in ((1, s1_ref), (2, s2_ref), (3, s3_ref), (0, own_ref)):
        copies.append(pltpu.make_async_copy(frag_ref.at[0, (zl + k) % 4], out, sems.at[k + 1]))
    for c in copies:
        c.start()
    for c in copies:
        c.wait()


def _norm_kernel(x_ref, gain_ref, *rest):
    outs, held = rest[:8], rest[8]
    _, _, zh, y, _ = _place()
    values = x_ref[...].astype(F32)
    stats = jnp.mean(values * values, axis=1, keepdims=True)
    normed = (values * lax.rsqrt(stats + 1e-06) * gain_ref[...]).astype(BF)
    for q in range(8):
        held[q] = normed[:, q * WIDE : (q + 1) * WIDE]
    for h in range(2):
        half = (zh + 1 - h) % 2
        for k in range(4):
            outs[h * 4 + k][...] = held[half * 4 + (y + k) % 4]


def _grad_kernel(n0, n1, n2, n3, c0, c1, c2, c3, own_ref, o1_ref, o2_ref, o3_ref, total):
    x = _place()[4]
    normed = jnp.concatenate([n0[...], n1[...], n2[...], n3[...]], axis=0)
    cot = jnp.concatenate([c0[...], c1[...], c2[...], c3[...]], axis=0)
    total[...] = lax.dot_general(normed, cot, (((0,), (0,)), ((), ())), preferred_element_type=F32)
    for k, out in ((0, own_ref), (1, o1_ref), (2, o2_ref), (3, o3_ref)):
        first = pl.multiple_of(((x + k) % 4) * ROWS, 16)
        out[...] = (total[pl.ds(first, ROWS), :] * SCALE).astype(out.dtype)


def _keys_kernel(*refs):
    other, own = refs[0:4], refs[4:8]
    pairs = refs[8:12]
    outs = refs[12:16]
    layer = refs[16]
    x = _place()[4]
    for k in range(4):
        first = pl.multiple_of(((x + 4 - k) % 4) * ROWS, 16)
        for h in range(2):
            layer[h, pl.ds(first, ROWS), :] = pairs[k][h]
    for k in range(4):
        part = jnp.dot(other[k][...], layer[0], preferred_element_type=F32)
        part += jnp.dot(own[k][...], layer[1], preferred_element_type=F32)
        outs[k][...] = (part * SCALE).astype(outs[k].dtype)


def _outer_kernel(place_ref, own_ref, near_ref, far_ref, global_ref, momentum_ref, new_global_ref, new_momentum_ref, average):
    k = pl.program_id(0)
    core = place_ref[1]

    @pl.when(k == 0)
    def _():
        average[...] = own_ref[...].reshape(2, ROWS // 2, KV)

    @pl.when(k > 0)
    def _():
        average[core] = near_ref[k - 1]
        average[1 - core] = far_ref[k - 1]

    mean = average[...].reshape(ROWS, KV)
    shared = global_ref[0]
    momentum = 0.9 * momentum_ref[0] + mean
    new_momentum_ref[0] = momentum
    new_global_ref[0] = shared - 0.7 * (mean + 0.9 * momentum)


def body(layer_index, inputs, norm_gain, cotangent, local_fragment, global_fragment, momentum):
    zl, core, zh, y, x = _place()
    any_spec = pl.BlockSpec(memory_space=pl.ANY)

    used, s1, s2, s3, s0 = _call(
        _pick_kernel,
        "pick",
        [((ROWS, KV), BF)] * 5,
        [pltpu.SemaphoreType.DMA((5,))],
        traffic=3_000_000,
        in_specs=[pl.BlockSpec(memory_space=pltpu.SMEM), any_spec],
        out_specs=[any_spec] * 5,
    )(layer_index, local_fragment)
    used_other = _swap_zh(used)
    cot = [cotangent] + [_shift_y(cotangent, k) for k in (1, 2, 3)]

    rows = 64
    pieces = _call(
        _norm_kernel,
        "normed",
        [((TOK, WIDE), BF)] * 8,
        [pltpu.VMEM((8, rows, WIDE), BF)],
        traffic=5_000_000,
        flops=20_000_000,
        grid=(TOK // rows,),
        in_specs=[pl.BlockSpec((rows, D), lambda i: (i, 0)), pl.BlockSpec((1, D), lambda i: (0, 0))],
        out_specs=[pl.BlockSpec((rows, WIDE), lambda i: (i, 0))] * 8,
    )(inputs, norm_gain[None, :])
    other = [pieces[0]] + [_shift_y(pieces[k], k) for k in (1, 2, 3)]
    own = [pieces[4]] + [_shift_y(pieces[4 + k], k) for k in (1, 2, 3)]

    pair = jnp.stack([used_other, used])
    pairs = [pair] + [_shift_x(pair, k) for k in (1, 2, 3)]

    locals_ = [s0] + [_shift_zl(s, k) for s, k in ((s1, 1), (s2, 2), (s3, 3))]
    shared = lax.dynamic_index_in_dim(global_fragment, zl, 0, keepdims=False)
    delta = sum(shared - v.astype(F32) for v in locals_)
    average = (delta + _swap_core(delta)) / 8.0
    half = lax.dynamic_slice_in_dim(average, core * (ROWS // 2), ROWS // 2, 0)
    near = jnp.stack([_shift_zl(half, k) for k in (1, 2, 3)])
    far = _swap_core(near)

    def by_layer(k, place):
        return ((place[0] + 4 - k) % 4, 0, 0)

    block = pl.BlockSpec((1, ROWS, KV), by_layer)
    whole = lambda *shape: pl.BlockSpec(shape, lambda k, place: (0,) * len(shape))
    new_global, new_momentum = pl.pallas_call(
        _outer_kernel,
        name="outer_step",
        out_shape=[jax.ShapeDtypeStruct((4, ROWS, KV), F32)] * 2,
        grid_spec=pltpu.PrefetchScalarGridSpec(
            num_scalar_prefetch=1,
            grid=(4,),
            in_specs=[whole(ROWS, KV), whole(3, ROWS // 2, KV), whole(3, ROWS // 2, KV), block, block],
            out_specs=[block, block],
            scratch_shapes=[pltpu.VMEM((2, ROWS // 2, KV), F32)],
        ),
        compiler_params=pltpu.CompilerParams(vmem_limit_bytes=LIMIT),
        cost_estimate=pl.CostEstimate(flops=4_000_000, bytes_accessed=12_000_000, transcendentals=0),
    )(jnp.stack([zl, core]).astype(jnp.int32), average, near, far, global_fragment, momentum)

    def grad(parts):
        return _call(
            _grad_kernel,
            "grad",
            [((ROWS, KV), F32)] + [((ROWS, KV), BF)] * 3,
            [pltpu.VMEM((WIDE, KV), F32)],
            flops=2 * WIDE * KV * 4 * TOK,
            traffic=5_000_000,
            in_specs=_vmem(8),
            out_specs=_vmem(4),
        )(*parts, *cot)

    g0, g1, g2, g3 = grad(other)
    far_sum = g0 + sum(_shift_x(g, k).astype(F32) for g, k in ((g1, 1), (g2, 2), (g3, 3)))
    from_zh = _swap_zh(far_sum.astype(BF))
    g0, g1, g2, g3 = grad(own)
    near_sum = g0 + sum(_shift_x(g, k).astype(F32) for g, k in ((g1, 1), (g2, 2), (g3, 3)))
    weight_grad = (near_sum + from_zh.astype(F32))[None]

    k0, k1, k2, k3 = _call(
        _keys_kernel,
        "keys",
        [((TOK, KV), F32)] + [((TOK, KV), BF)] * 3,
        [pltpu.VMEM((2, WIDE, KV), BF)],
        flops=2 * 4 * TOK * 2 * WIDE * KV,
        traffic=8_000_000,
        in_specs=_vmem(12),
        out_specs=_vmem(4),
    )(*other, *own, *pairs)
    keys = k0 + sum(_shift_y(v, -k).astype(F32) for v, k in ((k1, 1), (k2, 2), (k3, 3)))
    return keys.astype(BF), weight_grad, new_global, new_momentum


def solution(mesh):
    placed = (
        P("replica"),
        P(("replica", "fsdp"), None),
        P(),
        P(("replica", "fsdp"), None),
        P("replica", None, "fsdp", None),
        P(None, "fsdp", None),
        P(None, "fsdp", None),
    )
    return jax.shard_map(
        body,
        mesh=mesh,
        in_specs=placed,
        out_specs=(
            P(("replica", "fsdp"), None),
            P("replica", "fsdp", None),
            P(None, "fsdp", None),
            P(None, "fsdp", None),
        ),
        check_vma=False,
    )
```

time: 555 us -> 182 us (0.33)
  waiting for transfers between devices: 509 us -> 56.7 us
  starting transfers between devices: 0.13 us -> 84.8 us
  Pallas kernels: 0 us -> 20 us
  matrix products: 15.2 us -> 0 us
  between operations: 16.3 us -> 1.66 us
  local copies, waits for them, and re-layouts: 1.73 us -> 10.8 us
    reduce_scatter x1 -> x0, waiting for transfers between devices: 360 us -> none  [body(): lax.psum_scatter(product * scale_factor, 'fsdp', scatter_dimension=0, til...]
    psum x1 -> x0, waiting for transfers between devices: 149 us -> none  [body(): average = lax.psum(delta, 'replica') / replicas]
    ppermute x0 -> x31, starting transfers between devices: none -> 84.8 us  [the longest x2 30.4 us: _swap_core(): return lax.ppermute(v, 'replica', [(i, i ^ 1) for i in range(8)])]
    ppermute x0 -> x31, waiting for transfers between devices: none -> 56.7 us  [the longest x12 26.8 us: _shift_y(): return lax.ppermute(v, 'fsdp', perm)]
    pallas_call x0 -> x6, Pallas kernels: none -> 20 us  [the longest x2 5.95 us: grad(): _call(_grad_kernel, 'grad', [((ROWS, KV), F32)] + [((ROWS, KV), BF)] * 3,...]
    dot_general x2 -> x0, matrix products: 15.2 us -> none  [the longest x1 8.03 us: body(): lax.dot_general(columns, cotangent, (((0,), (0,)), ((), ())), preferred_e...]
    sub x2 -> x0, other arithmetic: 10.6 us -> none  [the longest x1 6.67 us: body(): new_global = global_fragment - 0.7 * (average + 0.9 * new_momentum)]
    unnamed x6 -> x64, local copies, waits for them, and re-layouts: 0.02 us -> 9.84 us
  transfers between devices with their start and end apart: 3 -> 31, of which waited for: 2 -> 9; matrix products, arithmetic and copies ran while one was open for 4% -> 4% of each run, Pallas kernels for 0% -> 7%
where the time goes in v1:
time: 182 us; the launch traced here: 181 us
  starting transfers between devices  84.8 us (47%)
  waiting for transfers between devices  56.7 us (31%)
  Pallas kernels  20 us (11%)
  local copies, waits for them, and re-layouts  10.8 us (6%)
  other arithmetic  7.09 us (4%)
    ppermute x2, starting transfers between devices, _swap_core(): return lax.ppermute(v, 'replica', [(i, i ^ 1) for i in range(8)])  30.4 us
    ppermute x12, waiting for transfers between devices, _shift_y(): return lax.ppermute(v, 'fsdp', perm)  26.8 us
    ppermute x2, starting transfers between devices, _swap_zh(): return lax.ppermute(v, 'fsdp', [(i, (i + 16) % 32) for i in range(32)])  22.2 us
    ppermute x6, waiting for transfers between devices, _shift_zl(): return lax.ppermute(v, 'replica', [(i, (i + 2 * k) % 8) for i in range(8)])  20.9 us
    ppermute x12, starting transfers between devices, _shift_y(): return lax.ppermute(v, 'fsdp', perm)  12.7 us
    ppermute x9, starting transfers between devices, _shift_x(): lax.ppermute(v, 'fsdp', [(i, i // 4 * 4 + (i + k) % 4) for i in range(32)])  11.2 us
    unnamed x64, local copies, waits for them, and re-layouts  9.84 us
    ppermute x6, starting transfers between devices, _shift_zl(): return lax.ppermute(v, 'replica', [(i, (i + 2 * k) % 8) for i in range(8)])  8.27 us
  transfers between devices with their start and end apart: 31, of which 9 were waited for; matrix products, arithmetic and copies ran while one was open for 4% of the time, Pallas kernels for 7%

profile of v1, /device:TPU:1, one launch (start us, length us, event | category | flops | bytes accessed | tf_op | source)
XLA Modules:
  0.0 181.0 jit_solution(5383674008636244661)
XLA Ops:
  3.2 2.7 %normed.1 = (bf16[256,576]{1,0:T(8,128)(2,1)S(1)}, bf16[256,576]{1,0:T(8,128)(2,1)S(1)}, bf16[256,576]{1,0:T(8,128)(2,1)}, bf16[256,576]{1,0:T(8,128)(2,1)}, bf1...) custom-call(bf16[256,4608]{1,0:T(8,128)(2,1)S(1)} %copy-done.1, ...), custom_call_target="tpu_custom_call" | custom-call | flops 20000000 | bytes 5000000 | tf_op jit(solution)/shard_map/normed/pallas_call | solution.py:150
  5.9 2.2 %collective-permute-start = (bf16[256,576]{1,0:T(8,128)(2,1)S(1)}, bf16[256,576]{1,0:T(8,128)(2,1)S(1)}, u32[]{:S(2)}, u32[]{:S(2)}) collective-permute-start(bf16[256,576]{1,0:T(8,128)(2,1)S(1)} %get-tuple-element.32), channel_id=1, source_target_pairs={{0,4},{1,5},{2,6},{3,7},{4,8},{5,9},{6,10},{7,11},{8,12},{9,13},{1... | collective-permute-start | bytes 884744 | tf_op jit(solution)/shard_map/ppermute | solution.py:27
  8.1 2.6 %collective-permute-start.1 = (bf16[256,576]{1,0:T(8,128)(2,1)}, bf16[256,576]{1,0:T(8,128)(2,1)S(1)}, u32[]{:S(2)}, u32[]{:S(2)}) collective-permute-start(bf16[256,576]{1,0:T(8,128)(2,1)} %get-tuple-element.33), channel_id=1, source_target_pairs={{0,8},{1,9},{2,10},{3,11},{4,12},{5,13},{6,14},{7,15},{8,0},{9,1},... | collective-permute-start | bytes 884744 | tf_op jit(solution)/shard_map/ppermute | solution.py:27
  13.7 4.4 %collective-permute-start.25 = (bf16[144,1024]{1,0:T(8,128)(2,1)}, bf16[144,1024]{1,0:T(8,128)(2,1)}, u32[]{:S(2)}, u32[]{:S(2)}) collective-permute-start(bf16[144,1024]{1,0:T(8,128)(2,1)} %get-tuple-element.55), channel_id=1, source_target_pairs={{0,192},{32,224},{64,0},{96,32},{128,64},{160,96},{192,128},{224,1... | collective-permute-start | bytes 884744 | tf_op jit(solution)/shard_map/ppermute | solution.py:39
  20.3 4.6 %collective-permute-done.1.refs_2_.n2 = bf16[256,576]{1,0:T(8,128)(2,1)S(1)} collective-permute-done((bf16[256,576]{1,0:T(8,128)(2,1)}, bf16[256,576]{1,0:T(8,128)(2,1)S(1)}, u32[]{:S(2)}, u32[]{:S(2)}) %collective-permute-start.1) | collective-permute-done | bytes 294944 | tf_op jit(solution)/shard_map/ppermute | solution.py:27
  25.2 16.9 %collective-permute-done.24 = bf16[144,1024]{1,0:T(8,128)(2,1)} collective-permute-done((bf16[144,1024]{1,0:T(8,128)(2,1)}, bf16[144,1024]{1,0:T(8,128)(2,1)}, u32[]{:S(2)}, u32[]{:S(2)}) %collective-permute-start.24) | collective-permute-done | bytes 294944 | tf_op jit(solution)/shard_map/ppermute | solution.py:39
  43.1 12.0 %collective-permute-start.6 = (bf16[144,1024]{1,0:T(8,128)(2,1)S(1)}, bf16[144,1024]{1,0:T(8,128)(2,1)S(1)}, u32[]{:S(2)}, u32[]{:S(2)}) collective-permute-start(bf16[144,1024]{1,0:T(8,128)(2,1)S(1)} %get-tuple-element.39), channel_id=1, source_target_pairs={{0,16},{1,17},{2,18},{3,19},{4,20},{5,21},{6,22},{7,23},{8,24},{9,... | collective-permute-start | bytes 884744 | tf_op jit(solution)/shard_map/ppermute | solution.py:35
  55.1 2.2 %fusion.2 = f32[144,1024]{1,0:T(8,128)} fusion(bf16[144,1024]{1,0:T(8,128)(2,1)} %collective-permute-done.25, bf16[144,1024]{1,0:T(8,128)(2,1)} %collective-permute-done.24, bf16[144,1024]{1,0:T(8,128)(2,1)} %collective-permute-done.23, bf16[144,1024]{1,0:T(8,128)(2,1)S(1)} %get-tuple-element.52, f32[4,144,1024]{2,1,0:T(8,128)S(1)} %copy-done, s32[]{:T(128)S(6)} %select_n.20), kind=kLoop, calls=%fused_computation.9 | loop fusion | flops 1622016 | bytes 2359300 | tf_op jit(solution)/shard_map/add | solution.py:169
  57.3 2.8 %collective-permute-start.26 = (f32[144,1024]{1,0:T(8,128)}, f32[144,1024]{1,0:T(8,128)}, u32[]{:S(2)}, u32[]{:S(2)}) collective-permute-start(f32[144,1024]{1,0:T(8,128)} %fusion.2), channel_id=1, source_target_pairs={{0,32},{32,0},{64,96},{96,64},{128,160},{160,128},{192,224},{224,1... | collective-permute-start | bytes 1769480 | tf_op jit(solution)/shard_map/ppermute | solution.py:43
  60.1 3.3 %collective-permute-done.6 = bf16[144,1024]{1,0:T(8,128)(2,1)S(1)} collective-permute-done((bf16[144,1024]{1,0:T(8,128)(2,1)S(1)}, bf16[144,1024]{1,0:T(8,128)(2,1)S(1)}, u32[]{:S(2)}, u32[]{:S(2)}) %collective-permute-start.6) | collective-permute-done | bytes 294944 | tf_op jit(solution)/shard_map/ppermute | solution.py:35
  69.5 3.3 %grad.3 = (f32[144,1024]{1,0:T(8,128)S(1)}, bf16[144,1024]{1,0:T(8,128)(2,1)S(1)}, bf16[144,1024]{1,0:T(8,128)(2,1)S(1)}, bf16[144,1024]{1,0:T(8,128)(2,1)}) custom-call(bf16[256,576]{1,0:T(8,128)(2,1)S(1)} %copy-done.12, bf16[256,576]{1,0:T(8,128)(2,1)S(1)} %copy-done.18, bf16[256,576]{1,0:T(8,128)(2,1)S(1)} %copy-done.21, ...), custom_call_target="tpu_custom_call" | custom-call | flops 1207959552 | bytes 5000000 | tf_op jit(solution)/shard_map/grad/pallas_call | solution.py:196
  75.7 2.5 %collective-permute-start.21 = (bf16[144,1024]{1,0:T(8,128)(2,1)}, bf16[144,1024]{1,0:T(8,128)(2,1)}, u32[]{:S(2)}, u32[]{:S(2)}) collective-permute-start(bf16[144,1024]{1,0:T(8,128)(2,1)} %get-tuple-element.51), channel_id=1, source_target_pairs={{0,3},{1,0},{2,1},{3,2},{4,7},{5,4},{6,5},{7,6},{8,11},{9,8},{10,9... | collective-permute-start | bytes 884744 | tf_op jit(solution)/shard_map/ppermute | solution.py:31
  80.7 1.9 %collective-permute-start.8 = (bf16[2,144,1024]{2,1,0:T(8,128)(2,1)S(1)}, bf16[2,144,1024]{2,1,0:T(8,128)(2,1)S(1)}, u32[]{:S(2)}, u32[]{:S(2)}) collective-permute-start(bf16[2,144,1024]{2,1,0:T(8,128)(2,1)S(1)} %pad_maximum_fusion.1.refs_8_), channel_id=1, source_target_pairs={{0,2},{1,3},{2,0},{3,1},{4,6},{5,7},{6,4},{7,5},{8,10},{9,11},{10,... | collective-permute-start | bytes 1769480 | tf_op jit(solution)/shard_map/ppermute | solution.py:31
  82.7 5.5 %collective-permute-done.21 = bf16[144,1024]{1,0:T(8,128)(2,1)} collective-permute-done((bf16[144,1024]{1,0:T(8,128)(2,1)}, bf16[144,1024]{1,0:T(8,128)(2,1)}, u32[]{:S(2)}, u32[]{:S(2)}) %collective-permute-start.21) | collective-permute-done | bytes 294944 | tf_op jit(solution)/shard_map/ppermute | solution.py:31
  88.2 3.9 %collective-permute-start.9 = (bf16[2,144,1024]{2,1,0:T(8,128)(2,1)S(1)}, bf16[2,144,1024]{2,1,0:T(8,128)(2,1)S(1)}, u32[]{:S(2)}, u32[]{:S(2)}) collective-permute-start(bf16[2,144,1024]{2,1,0:T(8,128)(2,1)S(1)} %pad_maximum_fusion.1.refs_8_), channel_id=1, source_target_pairs={{0,3},{1,0},{2,1},{3,2},{4,7},{5,4},{6,5},{7,6},{8,11},{9,8},{10,9... | collective-permute-start | bytes 1769480 | tf_op jit(solution)/shard_map/ppermute | solution.py:31
  92.4 3.3 %collective-permute-start.27 = (f32[72,1024]{1,0:T(8,128)S(1)}, f32[72,1024]{1,0:T(8,128)S(1)}, u32[]{:S(2)}, u32[]{:S(2)}) collective-permute-start(f32[72,1024]{1,0:T(8,128)S(1)} %constant_dynamic-slice_fusion), channel_id=1, source_target_pairs={{0,64},{32,96},{64,128},{96,160},{128,192},{160,224},{192,0},{224,... | collective-permute-start | bytes 884744 | tf_op jit(solution)/shard_map/ppermute | solution.py:39
  97.6 2.7 %grad.2 = (f32[144,1024]{1,0:T(8,128)S(1)}, bf16[144,1024]{1,0:T(8,128)(2,1)S(1)}, bf16[144,1024]{1,0:T(8,128)(2,1)S(1)}, bf16[144,1024]{1,0:T(8,128)(2,1)S(1)}) custom-call(bf16[256,576]{1,0:T(8,128)(2,1)S(1)} %copy-done.15, bf16[256,576]{1,0:T(8,128)(2,1)S(1)} %copy-done.24, bf16[256,576]{1,0:T(8,128)(2,1)} %collective-permute-done.4.refs_6_.n2, ...), custom_call_target="tpu_custom_call" | custom-call | flops 1207959552 | bytes 5000000 | tf_op jit(solution)/shard_map/grad/pallas_call | solution.py:196
  101.7 3.5 %collective-permute-done.28 = f32[72,1024]{1,0:T(8,128)S(1)} collective-permute-done((f32[72,1024]{1,0:T(8,128)S(1)}, f32[72,1024]{1,0:T(8,128)S(1)}, u32[]{:S(2)}, u32[]{:S(2)}) %collective-permute-start.28) | collective-permute-done | bytes 294944 | tf_op jit(solution)/shard_map/ppermute | solution.py:39
  106.2 10.2 %collective-permute-start.22 = (bf16[144,1024]{1,0:T(8,128)(2,1)S(1)}, bf16[144,1024]{1,0:T(8,128)(2,1)S(1)}, u32[]{:S(2)}, u32[]{:S(2)}) collective-permute-start(bf16[144,1024]{1,0:T(8,128)(2,1)S(1)} %add_convert_fusion.1), channel_id=1, source_target_pairs={{0,16},{1,17},{2,18},{3,19},{4,20},{5,21},{6,22},{7,23},{8,24},{9,... | collective-permute-start | bytes 884744 | tf_op jit(solution)/shard_map/ppermute | solution.py:35
  116.4 27.6 %collective-permute-start.30 = (f32[3,72,1024]{2,1,0:T(8,128)S(1)}, f32[3,72,1024]{2,1,0:T(8,128)S(1)}, u32[]{:S(2)}, u32[]{:S(2)}) collective-permute-start(f32[3,72,1024]{2,1,0:T(8,128)S(1)} %pad_maximum_fusion.near_ref), channel_id=1, source_target_pairs={{0,32},{32,0},{64,96},{96,64},{128,160},{160,128},{192,224},{224,1... | collective-permute-start | bytes 2654216 | tf_op jit(solution)/shard_map/ppermute | solution.py:43
  144.0 5.1 %keys.1 = (f32[256,1024]{1,0:T(8,128)}, bf16[256,1024]{1,0:T(8,128)(2,1)S(1)}, bf16[256,1024]{1,0:T(8,128)(2,1)S(1)}, bf16[256,1024]{1,0:T(8,128)(2,1)S(1)}) custom-call(bf16[256,576]{1,0:T(8,128)(2,1)S(1)} %copy-done.13, bf16[256,576]{1,0:T(8,128)(2,1)S(1)} %copy-done.19, bf16[256,576]{1,0:T(8,128)(2,1)S(1)} %copy-done.22, ...), custom_call_target="tpu_custom_call" | custom-call | flops 2415919104 | bytes 8000000 | tf_op jit(solution)/shard_map/keys/pallas_call | solution.py:214
  149.3 2.6 %collective-permute-start.10 = (bf16[256,1024]{1,0:T(8,128)(2,1)S(1)}, bf16[256,1024]{1,0:T(8,128)(2,1)S(1)}, u32[]{:S(2)}, u32[]{:S(2)}) collective-permute-start(bf16[256,1024]{1,0:T(8,128)(2,1)S(1)} %get-tuple-element.41), channel_id=1, source_target_pairs={{0,12},{1,13},{2,14},{3,15},{4,0},{5,1},{6,2},{7,3},{8,4},{9,5},{1... | collective-permute-start | bytes 1572872 | tf_op jit(solution)/shard_map/ppermute | solution.py:27
  153.1 21.2 %collective-permute-done.12 = bf16[256,1024]{1,0:T(8,128)(2,1)S(1)} collective-permute-done((bf16[256,1024]{1,0:T(8,128)(2,1)S(1)}, bf16[256,1024]{1,0:T(8,128)(2,1)S(1)}, u32[]{:S(2)}, u32[]{:S(2)}) %collective-permute-start.12) | collective-permute-done | bytes 524320 | tf_op jit(solution)/shard_map/ppermute | solution.py:27
  175.8 5.2 %outer_step.1 = (f32[4,144,1024]{2,1,0:T(8,128)}, f32[4,144,1024]{2,1,0:T(8,128)}) custom-call(s32[2]{0:T(128)S(1)} %pad_add_fusion.place_ref, f32[144,1024]{1,0:T(8,128)S(1)} %add_multiply_fusion.own_ref, f32[3,72,1024]{2,1,0:T(8,128)S(1)} %pad_maximum_fusion.near_ref, f32[3,72,1024]{2,1,0:T(8,128)S(1)} %collective-permute-done.30.far_ref, ...), custom_call_target="tpu_custom_call" | custom-call | flops 4000000 | bytes 12000000 | tf_op jit(solution)/shard_map/outer_step/pallas_call | solution.py:180
  (118 shorter events, 27.1 us)
Async XLA Ops:
  8.1 16.8 %collective-permute-start.1 = (bf16[256,576]{1,0:T(8,128)(2,1)}, bf16[256,576]{1,0:T(8,128)(2,1)S(1)}, u32[]{:S(2)}, u32[]{:S(2)}) collective-permute-start(bf16[256,576]{1,0:T(8,128)(2,1)} %get-tuple-element.33), channel_id=1, source_target_pairs={{0,8},{1,9},{2,10},{3,11},{4,12},{5,13},{6,14},{7,15},{8,0},{9,1},... | collective-permute-start | bytes 884744 | tf_op jit(solution)/shard_map/ppermute | solution.py:27
  18.1 23.9 %collective-permute-start.24 = (bf16[144,1024]{1,0:T(8,128)(2,1)}, bf16[144,1024]{1,0:T(8,128)(2,1)}, u32[]{:S(2)}, u32[]{:S(2)}) collective-permute-start(bf16[144,1024]{1,0:T(8,128)(2,1)} %get-tuple-element.54), channel_id=1, source_target_pairs={{0,128},{32,160},{64,192},{96,224},{128,0},{160,32},{192,64},{224,... | collective-permute-start | bytes 884744 | tf_op jit(solution)/shard_map/ppermute | solution.py:39
  18.1 25.0 %collective-permute-start.23 = (bf16[144,1024]{1,0:T(8,128)(2,1)}, bf16[144,1024]{1,0:T(8,128)(2,1)}, u32[]{:S(2)}, u32[]{:S(2)}) collective-permute-start(bf16[144,1024]{1,0:T(8,128)(2,1)} %get-tuple-element.53), channel_id=1, source_target_pairs={{0,64},{32,96},{64,128},{96,160},{128,192},{160,224},{192,0},{224,... | collective-permute-start | bytes 884744 | tf_op jit(solution)/shard_map/ppermute | solution.py:39
  19.2 38.1 %collective-permute-start.2 = (bf16[256,576]{1,0:T(8,128)(2,1)}, bf16[256,576]{1,0:T(8,128)(2,1)}, u32[]{:S(2)}, u32[]{:S(2)}) collective-permute-start(bf16[256,576]{1,0:T(8,128)(2,1)} %get-tuple-element.34), channel_id=1, source_target_pairs={{0,12},{1,13},{2,14},{3,15},{4,0},{5,1},{6,2},{7,3},{8,4},{9,5},{1... | collective-permute-start | bytes 884744 | tf_op jit(solution)/shard_map/ppermute | solution.py:27
  24.9 38.6 %collective-permute-start.13 = (bf16[256,1024]{1,0:T(8,128)(2,1)}, bf16[256,1024]{1,0:T(8,128)(2,1)S(1)}, u32[]{:S(2)}, u32[]{:S(2)}) collective-permute-start(bf16[256,1024]{1,0:T(8,128)(2,1)} %c0.3), channel_id=1, source_target_pairs={{0,4},{1,5},{2,6},{3,7},{4,8},{5,9},{6,10},{7,11},{8,12},{9,13},{1... | collective-permute-start | bytes 1572872 | tf_op jit(solution)/shard_map/ppermute | solution.py:27
  24.9 39.8 %collective-permute-start.14 = (bf16[256,1024]{1,0:T(8,128)(2,1)}, bf16[256,1024]{1,0:T(8,128)(2,1)S(1)}, u32[]{:S(2)}, u32[]{:S(2)}) collective-permute-start(bf16[256,1024]{1,0:T(8,128)(2,1)} %c0.3), channel_id=1, source_target_pairs={{0,8},{1,9},{2,10},{3,11},{4,12},{5,13},{6,14},{7,15},{8,0},{9,1},... | collective-permute-start | bytes 1572872 | tf_op jit(solution)/shard_map/ppermute | solution.py:27
  42.0 24.0 %collective-permute-start.15 = (bf16[256,1024]{1,0:T(8,128)(2,1)}, bf16[256,1024]{1,0:T(8,128)(2,1)S(1)}, u32[]{:S(2)}, u32[]{:S(2)}) collective-permute-start(bf16[256,1024]{1,0:T(8,128)(2,1)} %c0.3), channel_id=1, source_target_pairs={{0,12},{1,13},{2,14},{3,15},{4,0},{5,1},{6,2},{7,3},{8,4},{9,5},{1... | collective-permute-start | bytes 1572872 | tf_op jit(solution)/shard_map/ppermute | solution.py:27
  43.1 20.3 %collective-permute-start.6 = (bf16[144,1024]{1,0:T(8,128)(2,1)S(1)}, bf16[144,1024]{1,0:T(8,128)(2,1)S(1)}, u32[]{:S(2)}, u32[]{:S(2)}) collective-permute-start(bf16[144,1024]{1,0:T(8,128)(2,1)S(1)} %get-tuple-element.39), channel_id=1, source_target_pairs={{0,16},{1,17},{2,18},{3,19},{4,20},{5,21},{6,22},{7,23},{8,24},{9,... | collective-permute-start | bytes 884744 | tf_op jit(solution)/shard_map/ppermute | solution.py:35
  57.3 21.5 %collective-permute-start.26 = (f32[144,1024]{1,0:T(8,128)}, f32[144,1024]{1,0:T(8,128)}, u32[]{:S(2)}, u32[]{:S(2)}) collective-permute-start(f32[144,1024]{1,0:T(8,128)} %fusion.2), channel_id=1, source_target_pairs={{0,32},{32,0},{64,96},{96,64},{128,160},{160,128},{192,224},{224,1... | collective-permute-start | bytes 1769480 | tf_op jit(solution)/shard_map/ppermute | solution.py:43
  63.5 14.7 %collective-permute-start.4 = (bf16[256,576]{1,0:T(8,128)(2,1)}, bf16[256,576]{1,0:T(8,128)(2,1)}, u32[]{:S(2)}, u32[]{:S(2)}) collective-permute-start(bf16[256,576]{1,0:T(8,128)(2,1)} %get-tuple-element.37), channel_id=1, source_target_pairs={{0,8},{1,9},{2,10},{3,11},{4,12},{5,13},{6,14},{7,15},{8,0},{9,1},... | collective-permute-start | bytes 884744 | tf_op jit(solution)/shard_map/ppermute | solution.py:27
  64.7 27.6 %collective-permute-start.7 = (bf16[2,144,1024]{2,1,0:T(8,128)(2,1)S(1)}, bf16[2,144,1024]{2,1,0:T(8,128)(2,1)}, u32[]{:S(2)}, u32[]{:S(2)}) collective-permute-start(bf16[2,144,1024]{2,1,0:T(8,128)(2,1)S(1)} %pad_maximum_fusion.1.refs_8_), channel_id=1, source_target_pairs={{0,1},{1,2},{2,3},{3,0},{4,5},{5,6},{6,7},{7,4},{8,9},{9,10},{10,1... | collective-permute-start | bytes 1769480 | tf_op jit(solution)/shard_map/ppermute | solution.py:31
  66.0 14.7 %collective-permute-start.5 = (bf16[256,576]{1,0:T(8,128)(2,1)}, bf16[256,576]{1,0:T(8,128)(2,1)}, u32[]{:S(2)}, u32[]{:S(2)}) collective-permute-start(bf16[256,576]{1,0:T(8,128)(2,1)} %get-tuple-element.38), channel_id=1, source_target_pairs={{0,12},{1,13},{2,14},{3,15},{4,0},{5,1},{6,2},{7,3},{8,4},{9,5},{1... | collective-permute-start | bytes 884744 | tf_op jit(solution)/shard_map/ppermute | solution.py:27
  78.2 14.0 %collective-permute-start.20 = (bf16[144,1024]{1,0:T(8,128)(2,1)}, bf16[144,1024]{1,0:T(8,128)(2,1)S(1)}, u32[]{:S(2)}, u32[]{:S(2)}) collective-permute-start(bf16[144,1024]{1,0:T(8,128)(2,1)} %copy-done.29), channel_id=1, source_target_pairs={{0,2},{1,3},{2,0},{3,1},{4,6},{5,7},{6,4},{7,5},{8,10},{9,11},{10,... | collective-permute-start | bytes 884744 | tf_op jit(solution)/shard_map/ppermute | solution.py:31
  78.8 13.5 %collective-permute-start.19 = (bf16[144,1024]{1,0:T(8,128)(2,1)}, bf16[144,1024]{1,0:T(8,128)(2,1)S(1)}, u32[]{:S(2)}, u32[]{:S(2)}) collective-permute-start(bf16[144,1024]{1,0:T(8,128)(2,1)} %copy-done.28), channel_id=1, source_target_pairs={{0,1},{1,2},{2,3},{3,0},{4,5},{5,6},{6,7},{7,4},{8,9},{9,10},{10,1... | collective-permute-start | bytes 884744 | tf_op jit(solution)/shard_map/ppermute | solution.py:31
  80.7 25.4 %collective-permute-start.8 = (bf16[2,144,1024]{2,1,0:T(8,128)(2,1)S(1)}, bf16[2,144,1024]{2,1,0:T(8,128)(2,1)S(1)}, u32[]{:S(2)}, u32[]{:S(2)}) collective-permute-start(bf16[2,144,1024]{2,1,0:T(8,128)(2,1)S(1)} %pad_maximum_fusion.1.refs_8_), channel_id=1, source_target_pairs={{0,2},{1,3},{2,0},{3,1},{4,6},{5,7},{6,4},{7,5},{8,10},{9,11},{10,... | collective-permute-start | bytes 1769480 | tf_op jit(solution)/shard_map/ppermute | solution.py:31
  88.2 28.2 %collective-permute-start.9 = (bf16[2,144,1024]{2,1,0:T(8,128)(2,1)S(1)}, bf16[2,144,1024]{2,1,0:T(8,128)(2,1)S(1)}, u32[]{:S(2)}, u32[]{:S(2)}) collective-permute-start(bf16[2,144,1024]{2,1,0:T(8,128)(2,1)S(1)} %pad_maximum_fusion.1.refs_8_), channel_id=1, source_target_pairs={{0,3},{1,0},{2,1},{3,2},{4,7},{5,4},{6,5},{7,6},{8,11},{9,8},{10,9... | collective-permute-start | bytes 1769480 | tf_op jit(solution)/shard_map/ppermute | solution.py:31
  101.6 47.5 %collective-permute-start.18 = (bf16[144,1024]{1,0:T(8,128)(2,1)S(1)}, bf16[144,1024]{1,0:T(8,128)(2,1)S(1)}, u32[]{:S(2)}, u32[]{:S(2)}) collective-permute-start(bf16[144,1024]{1,0:T(8,128)(2,1)S(1)} %get-tuple-element.47), channel_id=1, source_target_pairs={{0,3},{1,0},{2,1},{3,2},{4,7},{5,4},{6,5},{7,6},{8,11},{9,8},{10,9... | collective-permute-start | bytes 884744 | tf_op jit(solution)/shard_map/ppermute | solution.py:31
  105.2 44.0 %collective-permute-start.17 = (bf16[144,1024]{1,0:T(8,128)(2,1)S(1)}, bf16[144,1024]{1,0:T(8,128)(2,1)S(1)}, u32[]{:S(2)}, u32[]{:S(2)}) collective-permute-start(bf16[144,1024]{1,0:T(8,128)(2,1)S(1)} %get-tuple-element.46), channel_id=1, source_target_pairs={{0,2},{1,3},{2,0},{3,1},{4,6},{5,7},{6,4},{7,5},{8,10},{9,11},{10,... | collective-permute-start | bytes 884744 | tf_op jit(solution)/shard_map/ppermute | solution.py:31
  105.7 43.6 %collective-permute-start.16 = (bf16[144,1024]{1,0:T(8,128)(2,1)S(1)}, bf16[144,1024]{1,0:T(8,128)(2,1)S(1)}, u32[]{:S(2)}, u32[]{:S(2)}) collective-permute-start(bf16[144,1024]{1,0:T(8,128)(2,1)S(1)} %get-tuple-element.45), channel_id=1, source_target_pairs={{0,1},{1,2},{2,3},{3,0},{4,5},{5,6},{6,7},{7,4},{8,9},{9,10},{10,1... | collective-permute-start | bytes 884744 | tf_op jit(solution)/shard_map/ppermute | solution.py:31
  106.2 45.9 %collective-permute-start.22 = (bf16[144,1024]{1,0:T(8,128)(2,1)S(1)}, bf16[144,1024]{1,0:T(8,128)(2,1)S(1)}, u32[]{:S(2)}, u32[]{:S(2)}) collective-permute-start(bf16[144,1024]{1,0:T(8,128)(2,1)S(1)} %add_convert_fusion.1), channel_id=1, source_target_pairs={{0,16},{1,17},{2,18},{3,19},{4,20},{5,21},{6,22},{7,23},{8,24},{9,... | collective-permute-start | bytes 884744 | tf_op jit(solution)/shard_map/ppermute | solution.py:35
  116.4 59.4 %collective-permute-start.30 = (f32[3,72,1024]{2,1,0:T(8,128)S(1)}, f32[3,72,1024]{2,1,0:T(8,128)S(1)}, u32[]{:S(2)}, u32[]{:S(2)}) collective-permute-start(f32[3,72,1024]{2,1,0:T(8,128)S(1)} %pad_maximum_fusion.near_ref), channel_id=1, source_target_pairs={{0,32},{32,0},{64,96},{96,64},{128,160},{160,128},{192,224},{224,1... | collective-permute-start | bytes 2654216 | tf_op jit(solution)/shard_map/ppermute | solution.py:43
  149.1 25.2 %collective-permute-start.12 = (bf16[256,1024]{1,0:T(8,128)(2,1)S(1)}, bf16[256,1024]{1,0:T(8,128)(2,1)S(1)}, u32[]{:S(2)}, u32[]{:S(2)}) collective-permute-start(bf16[256,1024]{1,0:T(8,128)(2,1)S(1)} %get-tuple-element.43), channel_id=1, source_target_pairs={{0,4},{1,5},{2,6},{3,7},{4,8},{5,9},{6,10},{7,11},{8,12},{9,13},{1... | collective-permute-start | bytes 1572872 | tf_op jit(solution)/shard_map/ppermute | solution.py:27
  149.2 25.1 %collective-permute-start.11 = (bf16[256,1024]{1,0:T(8,128)(2,1)S(1)}, bf16[256,1024]{1,0:T(8,128)(2,1)S(1)}, u32[]{:S(2)}, u32[]{:S(2)}) collective-permute-start(bf16[256,1024]{1,0:T(8,128)(2,1)S(1)} %get-tuple-element.42), channel_id=1, source_target_pairs={{0,8},{1,9},{2,10},{3,11},{4,12},{5,13},{6,14},{7,15},{8,0},{9,1},... | collective-permute-start | bytes 1572872 | tf_op jit(solution)/shard_map/ppermute | solution.py:27
  149.3 25.3 %collective-permute-start.10 = (bf16[256,1024]{1,0:T(8,128)(2,1)S(1)}, bf16[256,1024]{1,0:T(8,128)(2,1)S(1)}, u32[]{:S(2)}, u32[]{:S(2)}) collective-permute-start(bf16[256,1024]{1,0:T(8,128)(2,1)S(1)} %get-tuple-element.41), channel_id=1, source_target_pairs={{0,12},{1,13},{2,14},{3,15},{4,0},{5,1},{6,2},{7,3},{8,4},{9,5},{1... | collective-permute-start | bytes 1572872 | tf_op jit(solution)/shard_map/ppermute | solution.py:27
  (39 other events, 724.0 us)

commit v2 on v1

v2 whole, which is shorter than its diff:
```python
import jax
import jax.numpy as jnp
from jax import lax
from jax.experimental import pallas as pl
from jax.experimental.pallas import tpu as pltpu
from jax.sharding import PartitionSpec as P

D = 4608
KV = 1024
ROWS = 144
WIDE = 576
TOK = 256
MSG = 2 * WIDE + KV
SCALE = float(D) ** -0.5
BF = jnp.bfloat16
F32 = jnp.float32
LIMIT = 48 * 1024 * 1024


def _place():
    f = lax.axis_index("fsdp")
    r = lax.axis_index("replica")
    return r >> 1, r & 1, f >> 4, (f >> 2) & 3, f & 3


def _shift_y(v, k):
    perm = [(i, (i // 16) * 16 + ((i // 4 + k) % 4) * 4 + i % 4) for i in range(32)]
    return lax.ppermute(v, "fsdp", perm)


def _shift_x(v, k):
    return lax.ppermute(v, "fsdp", [(i, (i // 4) * 4 + (i + k) % 4) for i in range(32)])


def _swap_zh(v):
    return lax.ppermute(v, "fsdp", [(i, (i + 16) % 32) for i in range(32)])


def _shift_zl(v, k):
    return lax.ppermute(v, "replica", [(i, (i + 2 * k) % 8) for i in range(8)])


def _send_far(v):
    return lax.ppermute(v, "replica", [(i, (i + 2 + 4 * (i % 2)) % 8) for i in range(8)])


def _after(v, *done):
    return lax.optimization_barrier((v, *done))[0]


def _swap_core(v):
    return lax.ppermute(v, "replica", [(i, i ^ 1) for i in range(8)])


def _call(kernel, name, outs, scratch=(), flops=0, traffic=0, **kw):
    return pl.pallas_call(
        kernel,
        name=name,
        out_shape=[jax.ShapeDtypeStruct(s, d) for s, d in outs],
        scratch_shapes=list(scratch),
        compiler_params=pltpu.CompilerParams(vmem_limit_bytes=LIMIT),
        cost_estimate=pl.CostEstimate(flops=flops, bytes_accessed=traffic, transcendentals=0),
        **kw,
    )


def _vmem(n):
    return [pl.BlockSpec(memory_space=pltpu.VMEM)] * n


def _pick_kernel(index_ref, frag_ref, used_ref, s1_ref, s2_ref, s3_ref, own_ref, sems):
    zl = _place()[0]
    copies = [pltpu.make_async_copy(frag_ref.at[0, index_ref[0]], used_ref, sems.at[0])]
    for k, out in ((1, s1_ref), (2, s2_ref), (3, s3_ref), (0, own_ref)):
        copies.append(pltpu.make_async_copy(frag_ref.at[0, (zl + k) & 3], out, sems.at[k + 1]))
    for c in copies:
        c.start()
    for c in copies:
        c.wait()


def _norm_kernel(x_ref, gain_ref, cot_ref, own_ref, m1_ref, m2_ref, m3_ref, held):
    _, _, zh, y, _ = _place()
    values = x_ref[...].astype(F32)
    stats = jnp.mean(values * values, axis=1, keepdims=True)
    normed = (values * lax.rsqrt(stats + 1e-06) * gain_ref[...]).astype(BF)
    for q in range(8):
        held[q] = normed[:, q * WIDE : (q + 1) * WIDE]
    for k, out in enumerate((own_ref, m1_ref, m2_ref, m3_ref)):
        chunk = (y + k) & 3
        out[:, : 2 * WIDE] = jnp.concatenate([held[(1 - zh) * 4 + chunk], held[zh * 4 + chunk]], axis=1)
        if k:
            out[:, 2 * WIDE :] = cot_ref[...]


def _grad_kernel(n_ref, c_ref, m1_ref, m2_ref, m3_ref, *rest):
    outs, total = rest[:8], rest[8]
    x = _place()[4]
    messages = (m1_ref, m2_ref, m3_ref)
    normed = jnp.concatenate([n_ref[...]] + [m[:, : 2 * WIDE] for m in messages], axis=0)
    cot = jnp.concatenate([c_ref[...]] + [m[:, 2 * WIDE :] for m in messages], axis=0)
    total[...] = lax.dot_general(normed, cot, (((0,), (0,)), ((), ())), preferred_element_type=F32)
    for h in range(2):
        for k in range(4):
            first = pl.multiple_of(h * WIDE + ((x + k) & 3) * ROWS, 16)
            out = outs[h * 4 + k]
            out[...] = (total[pl.ds(first, ROWS), :] * SCALE).astype(out.dtype)


def _keys_kernel(*refs):
    blocks, pairs, outs, layer = refs[0:4], refs[4:8], refs[8:12], refs[12]
    x = _place()[4]
    for k in range(4):
        for h in range(2):
            first = pl.multiple_of(h * WIDE + ((x + 4 - k) & 3) * ROWS, 16)
            layer[pl.ds(first, ROWS), :] = pairs[k][h]
    for k in range(4):
        part = jnp.dot(blocks[k][:, : 2 * WIDE], layer[...], preferred_element_type=F32)
        outs[k][...] = (part * SCALE).astype(outs[k].dtype)


def _outer_kernel(place_ref, own_ref, a_ref, b_ref, near_ref, far_ref, global_ref, momentum_ref, new_global_ref, new_momentum_ref, average):
    k = pl.program_id(0)
    core = place_ref[1]
    half = ROWS // 2

    @pl.when(k == 0)
    def _():
        average[...] = own_ref[...].reshape(2, half, KV)

    @pl.when(k == 1)
    def _():
        average[...] = a_ref[...].reshape(2, half, KV)

    @pl.when(k == 2)
    def _():
        average[...] = b_ref[...].reshape(2, half, KV)

    @pl.when(k == 3)
    def _():
        average[core] = near_ref[...]
        average[1 - core] = far_ref[...]

    mean = average[...].reshape(ROWS, KV)
    shared = global_ref[0]
    momentum = 0.9 * momentum_ref[0] + mean
    new_momentum_ref[0] = momentum
    new_global_ref[0] = shared - 0.7 * (mean + 0.9 * momentum)


def body(layer_index, inputs, norm_gain, cotangent, local_fragment, global_fragment, momentum):
    zl, core, zh, y, x = _place()
    any_spec = pl.BlockSpec(memory_space=pl.ANY)

    used, s1, s2, s3, s0 = _call(
        _pick_kernel,
        "pick",
        [((ROWS, KV), BF)] * 5,
        [pltpu.SemaphoreType.DMA((5,))],
        traffic=3_000_000,
        in_specs=[pl.BlockSpec(memory_space=pltpu.SMEM), any_spec],
        out_specs=[any_spec] * 5,
    )(layer_index, local_fragment)
    used_other = _swap_zh(used)

    rows = 64
    tile = lambda n: pl.BlockSpec((rows, n), lambda i: (i, 0))
    own, m1, m2, m3 = _call(
        _norm_kernel,
        "normed",
        [((TOK, 2 * WIDE), BF)] + [((TOK, MSG), BF)] * 3,
        [pltpu.VMEM((8, rows, WIDE), BF)],
        traffic=7_000_000,
        flops=20_000_000,
        grid=(TOK // rows,),
        in_specs=[tile(D), pl.BlockSpec((1, D), lambda i: (0, 0)), tile(KV)],
        out_specs=[tile(2 * WIDE)] + [tile(MSG)] * 3,
    )(inputs, _after(norm_gain[None, :], used), cotangent)
    r1 = _shift_y(m1, 1)
    r3 = _shift_y(m3, 3)
    r2 = _shift_y(_after(m2, r1, r3), 2)
    messages = [r1, r2, r3]

    pair = jnp.stack([used_other, used])
    p1 = _shift_x(pair, 1)
    p3 = _shift_x(pair, 3)
    p2 = _shift_x(_after(pair, p1, p3), 2)
    pairs = [pair, p1, p2, p3]

    t1 = _shift_zl(s1, 1)
    t3 = _shift_zl(s3, 3)
    t2 = _shift_zl(_after(s2, t1, t3, used_other), 2)
    shared = lax.dynamic_index_in_dim(global_fragment, zl, 0, keepdims=False)
    delta = sum(shared - v.astype(F32) for v in (s0, t1, t2, t3))
    average = (delta + _swap_core(_after(delta, p1, p3))) / 8.0
    half = lax.dynamic_slice_in_dim(average, core * (ROWS // 2), ROWS // 2, 0)
    sent = _send_far(average)
    near = _shift_zl(half, 2)
    swapped = _swap_core(sent)
    far = _swap_core(near)

    def by_layer(k, place):
        step = jnp.where(k == 1, 3 - 2 * place[1], jnp.where(k == 2, 1 + 2 * place[1], jnp.where(k == 3, 2, 0)))
        return ((place[0] + step) & 3, 0, 0)

    block = pl.BlockSpec((1, ROWS, KV), by_layer)
    whole = lambda *shape: pl.BlockSpec(shape, lambda k, place: (0,) * len(shape))
    new_global, new_momentum = pl.pallas_call(
        _outer_kernel,
        name="outer_step",
        out_shape=[jax.ShapeDtypeStruct((4, ROWS, KV), F32)] * 2,
        grid_spec=pltpu.PrefetchScalarGridSpec(
            num_scalar_prefetch=1,
            grid=(4,),
            in_specs=[whole(ROWS, KV)] * 3 + [whole(ROWS // 2, KV)] * 2 + [block, block],
            out_specs=[block, block],
            scratch_shapes=[pltpu.VMEM((2, ROWS // 2, KV), F32)],
        ),
        compiler_params=pltpu.CompilerParams(vmem_limit_bytes=LIMIT),
        cost_estimate=pl.CostEstimate(flops=4_000_000, bytes_accessed=12_000_000, transcendentals=0),
    )(jnp.stack([zl, core]).astype(jnp.int32), average, sent, swapped, near, far, global_fragment, momentum)

    g = _call(
        _grad_kernel,
        "grad",
        ([((ROWS, KV), F32)] + [((ROWS, KV), BF)] * 3) * 2,
        [pltpu.VMEM((2 * WIDE, KV), F32)],
        flops=2 * 2 * WIDE * KV * 4 * TOK,
        traffic=8_000_000,
        in_specs=_vmem(5),
        out_specs=_vmem(8),
    )(own, cotangent, *messages)
    a = [_shift_x(g[k], k) for k in (1, 3, 2)]
    far_sum = g[0] + sum(v.astype(F32) for v in a)
    from_zh = _swap_zh(far_sum.astype(BF))
    b = [_shift_x(_after(g[4 + k], a[2]), k) for k in (1, 3, 2)]
    weight_grad = (g[4] + sum(v.astype(F32) for v in b) + from_zh.astype(F32))[None]

    k0, k1, k2, k3 = _call(
        _keys_kernel,
        "keys",
        [((TOK, KV), F32)] + [((TOK, KV), BF)] * 3,
        [pltpu.VMEM((2 * WIDE, KV), BF)],
        flops=2 * 4 * TOK * 2 * WIDE * KV,
        traffic=8_000_000,
        in_specs=_vmem(8),
        out_specs=_vmem(4),
    )(own, *messages, *pairs)
    e1 = _shift_y(k1, 3)
    e3 = _shift_y(k3, 1)
    e2 = _shift_y(_after(k2, e1, e3), 2)
    keys = k0 + sum(v.astype(F32) for v in (e1, e3, e2))
    return keys.astype(BF), weight_grad, new_global, new_momentum


def solution(mesh):
    placed = (
        P("replica"),
        P(("replica", "fsdp"), None),
        P(),
        P(("replica", "fsdp"), None),
        P("replica", None, "fsdp", None),
        P(None, "fsdp", None),
        P(None, "fsdp", None),
    )
    return jax.shard_map(
        body,
        mesh=mesh,
        in_specs=placed,
        out_specs=(
            P(("replica", "fsdp"), None),
            P("replica", "fsdp", None),
            P(None, "fsdp", None),
            P(None, "fsdp", None),
        ),
        check_vma=False,
    )
```

time: 182 us -> 144 us (0.79)
  starting transfers between devices: 84.8 us -> 40 us
  waiting for transfers between devices: 56.7 us -> 67.7 us
  local copies, waits for them, and re-layouts: 10.8 us -> 5.88 us
  other arithmetic: 7.09 us -> 4.59 us
    ppermute x2 -> x3, starting transfers between devices: 30.4 us -> 3.16 us  [_swap_core(): return lax.ppermute(v, 'replica', [(i, i ^ 1) for i in range(8)])]
    ppermute x2, starting transfers between devices: 22.2 us -> 7.73 us  [_swap_zh(): return lax.ppermute(v, 'fsdp', [(i, (i + 16) % 32) for i in range(32)])]
    ppermute x6 -> x4, waiting for transfers between devices: 20.9 us -> 28.8 us  [_shift_zl(): return lax.ppermute(v, 'replica', [(i, (i + 2 * k) % 8) for i in range(8)])]
    ppermute x12 -> x6, starting transfers between devices: 12.7 us -> 7.98 us  [_shift_y(): return lax.ppermute(v, 'fsdp', perm)]
    unnamed x64 -> x20, local copies, waits for them, and re-layouts: 9.84 us -> 5.12 us
    ppermute x6 -> x4, starting transfers between devices: 8.27 us -> 3.62 us  [_shift_zl(): return lax.ppermute(v, 'replica', [(i, (i + 2 * k) % 8) for i in range(8)])]
    ppermute x9, starting transfers between devices: 11.2 us -> 15.5 us  [_shift_x(): lax.ppermute(v, 'fsdp', [(i, i // 4 * 4 + (i + k) % 4) for i in range(32)])]
    ppermute x2, waiting for transfers between devices: 3.32 us -> 6.77 us  [_swap_zh(): return lax.ppermute(v, 'fsdp', [(i, (i + 16) % 32) for i in range(32)])]
  transfers between devices with their start and end apart: 31 -> 25, of which waited for: 9 -> 12; matrix products, arithmetic and copies ran while one was open for 4% -> 2% of each run, Pallas kernels for 7% -> 11%
where the time goes in v2:
time: 144 us; the launch traced here: 141 us
  waiting for transfers between devices  67.7 us (47%)
  starting transfers between devices  40 us (28%)
  Pallas kernels  21.8 us (15%)
  local copies, waits for them, and re-layouts  5.88 us (4%)
  other arithmetic  4.59 us (3%)
    ppermute x4, waiting for transfers between devices, _shift_zl(): return lax.ppermute(v, 'replica', [(i, (i + 2 * k) % 8) for i in range(8)])  28.8 us
    ppermute x6, waiting for transfers between devices, _shift_y(): return lax.ppermute(v, 'fsdp', perm)  28.3 us
    ppermute x9, starting transfers between devices, _shift_x(): lax.ppermute(v, 'fsdp', [(i, i // 4 * 4 + (i + k) % 4) for i in range(32)])  15.5 us
    ppermute x6, starting transfers between devices, _shift_y(): return lax.ppermute(v, 'fsdp', perm)  7.98 us
    ppermute x2, starting transfers between devices, _swap_zh(): return lax.ppermute(v, 'fsdp', [(i, (i + 16) % 32) for i in range(32)])  7.73 us
    ppermute x2, waiting for transfers between devices, _swap_zh(): return lax.ppermute(v, 'fsdp', [(i, (i + 16) % 32) for i in range(32)])  6.77 us
    pallas_call x1, Pallas kernels, body(): _call(_keys_kernel, 'keys', [((TOK, KV), F32)] + [((TOK, KV), BF)] * 3, [...  5.47 us
    pallas_call x1, Pallas kernels, body(): pl.pallas_call(_outer_kernel, name='outer_step', out_shape=[jax.ShapeDtyp...  5.21 us
  transfers between devices with their start and end apart: 25, of which 12 were waited for; matrix products, arithmetic and copies ran while one was open for 2% of the time, Pallas kernels for 11%

profile of v2, /device:TPU:1, one launch (start us, length us, event | category | flops | bytes accessed | tf_op | source)
XLA Modules:
  0.0 141.3 jit_solution(5003089800265960290)
XLA Ops:
  4.4 5.1 %normed.1 = (bf16[256,1152]{1,0:T(8,128)(2,1)S(1)}, bf16[256,2176]{1,0:T(8,128)(2,1)}, bf16[256,2176]{1,0:T(8,128)(2,1)}, bf16[256,2176]{1,0:T(8,128)(2,1)}) custom-call(bf16[256,4608]{1,0:T(8,128)(2,1)} %x_ref.1, f32[1,4608]{1,0:T(1,128)S(1)} %broadcast_in_dim.6.gain_ref, bf16[256,1024]{1,0:T(8,128)(2,1)S(1)} %copy-done.2), custom_call_target="tpu_custom_call" | custom-call | flops 20000000 | bytes 7000000 | tf_op jit(solution)/shard_map/normed/pallas_call | solution.py:168
  9.5 2.1 %collective-permute-start = (bf16[256,2176]{1,0:T(8,128)(2,1)}, bf16[256,2176]{1,0:T(8,128)(2,1)}, u32[]{:S(2)}, u32[]{:S(2)}) collective-permute-start(bf16[256,2176]{1,0:T(8,128)(2,1)} %get-tuple-element.39), channel_id=1, source_target_pairs={{0,4},{1,5},{2,6},{3,7},{4,8},{5,9},{6,10},{7,11},{8,12},{9,13},{1... | collective-permute-start | bytes 3342344 | tf_op jit(solution)/shard_map/ppermute | solution.py:28
  13.1 6.9 %collective-permute-start.3 = (bf16[144,1024]{1,0:T(8,128)(2,1)S(1)}, bf16[144,1024]{1,0:T(8,128)(2,1)S(1)}, u32[]{:S(2)}, u32[]{:S(2)}) collective-permute-start(bf16[144,1024]{1,0:T(8,128)(2,1)S(1)} %get-tuple-element.36), channel_id=1, source_target_pairs={{0,16},{1,17},{2,18},{3,19},{4,20},{5,21},{6,22},{7,23},{8,24},{9,... | collective-permute-start | bytes 884744 | tf_op jit(solution)/shard_map/ppermute | solution.py:36
  20.0 1.6 %collective-permute-start.18 = (bf16[144,1024]{1,0:T(8,128)(2,1)S(1)}, bf16[144,1024]{1,0:T(8,128)(2,1)S(1)}, u32[]{:S(2)}, u32[]{:S(2)}) collective-permute-start(bf16[144,1024]{1,0:T(8,128)(2,1)S(1)} %get-tuple-element.63), channel_id=1, source_target_pairs={{0,192},{32,224},{64,0},{96,32},{128,64},{160,96},{192,128},{224,1... | collective-permute-start | bytes 884744 | tf_op jit(solution)/shard_map/ppermute | solution.py:40
  21.7 5.2 %collective-permute-done.3 = bf16[144,1024]{1,0:T(8,128)(2,1)S(1)} collective-permute-done((bf16[144,1024]{1,0:T(8,128)(2,1)S(1)}, bf16[144,1024]{1,0:T(8,128)(2,1)S(1)}, u32[]{:S(2)}, u32[]{:S(2)}) %collective-permute-start.3) | collective-permute-done | bytes 294944 | tf_op jit(solution)/shard_map/ppermute | solution.py:36
  27.7 1.7 %collective-permute-start.4 = (bf16[2,144,1024]{2,1,0:T(8,128)(2,1)}, bf16[2,144,1024]{2,1,0:T(8,128)(2,1)S(1)}, u32[]{:S(2)}, u32[]{:S(2)}) collective-permute-start(bf16[2,144,1024]{2,1,0:T(8,128)(2,1)} %pad_maximum_fusion.refs_4_), channel_id=1, source_target_pairs={{0,1},{1,2},{2,3},{3,0},{4,5},{5,6},{6,7},{7,4},{8,9},{9,10},{10,1... | collective-permute-start | bytes 1769480 | tf_op jit(solution)/shard_map/ppermute | solution.py:32
  29.4 10.0 %collective-permute-done.18 = bf16[144,1024]{1,0:T(8,128)(2,1)S(1)} collective-permute-done((bf16[144,1024]{1,0:T(8,128)(2,1)S(1)}, bf16[144,1024]{1,0:T(8,128)(2,1)S(1)}, u32[]{:S(2)}, u32[]{:S(2)}) %collective-permute-start.18) | collective-permute-done | bytes 294944 | tf_op jit(solution)/shard_map/ppermute | solution.py:40
  39.4 2.5 %collective-permute-start.5 = (bf16[2,144,1024]{2,1,0:T(8,128)(2,1)}, bf16[2,144,1024]{2,1,0:T(8,128)(2,1)}, u32[]{:S(2)}, u32[]{:S(2)}) collective-permute-start(bf16[2,144,1024]{2,1,0:T(8,128)(2,1)} %pad_maximum_fusion.refs_4_), channel_id=1, source_target_pairs={{0,3},{1,0},{2,1},{3,2},{4,7},{5,4},{6,5},{7,6},{8,11},{9,8},{10,9... | collective-permute-start | bytes 1769480 | tf_op jit(solution)/shard_map/ppermute | solution.py:32
  41.9 4.6 %collective-permute-done.17 = bf16[144,1024]{1,0:T(8,128)(2,1)S(1)} collective-permute-done((bf16[144,1024]{1,0:T(8,128)(2,1)S(1)}, bf16[144,1024]{1,0:T(8,128)(2,1)S(1)}, u32[]{:S(2)}, u32[]{:S(2)}) %collective-permute-start.17) | collective-permute-done | bytes 294944 | tf_op jit(solution)/shard_map/ppermute | solution.py:40
  47.2 1.7 %collective-permute-start.19 = (bf16[144,1024]{1,0:T(8,128)(2,1)}, bf16[144,1024]{1,0:T(8,128)(2,1)}, u32[]{:S(2)}, u32[]{:S(2)}) collective-permute-start(bf16[144,1024]{1,0:T(8,128)(2,1)} %get-tuple-element.64), channel_id=1, source_target_pairs={{0,128},{32,160},{64,192},{96,224},{128,0},{160,32},{192,64},{224,... | collective-permute-start | bytes 884744 | tf_op jit(solution)/shard_map/ppermute | solution.py:40
  48.9 14.3 %collective-permute-done.19 = bf16[144,1024]{1,0:T(8,128)(2,1)} collective-permute-done((bf16[144,1024]{1,0:T(8,128)(2,1)}, bf16[144,1024]{1,0:T(8,128)(2,1)}, u32[]{:S(2)}, u32[]{:S(2)}) %collective-permute-start.19) | collective-permute-done | bytes 294944 | tf_op jit(solution)/shard_map/ppermute | solution.py:40
  67.4 2.0 %collective-permute-start.21 = (f32[144,1024]{1,0:T(8,128)S(1)}, f32[144,1024]{1,0:T(8,128)S(1)}, u32[]{:S(2)}, u32[]{:S(2)}) collective-permute-start(f32[144,1024]{1,0:T(8,128)S(1)} %add_multiply_fusion.own_ref), channel_id=1, source_target_pairs={{0,64},{32,224},{64,128},{96,32},{128,192},{160,96},{192,0},{224,1... | collective-permute-start | bytes 1769480 | tf_op jit(solution)/shard_map/ppermute | solution.py:44
  69.5 2.7 %collective-permute-start.6 = (bf16[2,144,1024]{2,1,0:T(8,128)(2,1)}, bf16[2,144,1024]{2,1,0:T(8,128)(2,1)}, u32[]{:S(2)}, u32[]{:S(2)}) collective-permute-start(bf16[2,144,1024]{2,1,0:T(8,128)(2,1)} %pad_maximum_fusion.refs_4_), channel_id=1, source_target_pairs={{0,2},{1,3},{2,0},{3,1},{4,6},{5,7},{6,4},{7,5},{8,10},{9,11},{10,... | collective-permute-start | bytes 1769480 | tf_op jit(solution)/shard_map/ppermute | solution.py:32
  72.5 21.2 %collective-permute-done.2.refs_2_.m2_ref = bf16[256,2176]{1,0:T(8,128)(2,1)} collective-permute-done((bf16[256,2176]{1,0:T(8,128)(2,1)}, bf16[256,2176]{1,0:T(8,128)(2,1)}, u32[]{:S(2)}, u32[]{:S(2)}) %collective-permute-start.2) | collective-permute-done | bytes 1114144 | tf_op jit(solution)/shard_map/ppermute | solution.py:28
  95.8 5.1 %grad.1 = (f32[144,1024]{1,0:T(8,128)S(1)}, bf16[144,1024]{1,0:T(8,128)(2,1)S(1)}, bf16[144,1024]{1,0:T(8,128)(2,1)S(1)}, bf16[144,1024]{1,0:T(8,128)(2,1)S(1)},...) custom-call(bf16[256,1152]{1,0:T(8,128)(2,1)S(1)} %copy-done.5, ...), custom_call_target="tpu_custom_call" | custom-call | flops 2415919104 | bytes 8000000 | tf_op jit(solution)/shard_map/grad/pallas_call | solution.py:223
  100.9 2.8 %collective-permute-start.10 = (bf16[144,1024]{1,0:T(8,128)(2,1)S(1)}, bf16[144,1024]{1,0:T(8,128)(2,1)S(1)}, u32[]{:S(2)}, u32[]{:S(2)}) collective-permute-start(bf16[144,1024]{1,0:T(8,128)(2,1)S(1)} %get-tuple-element.51), channel_id=1, source_target_pairs={{0,2},{1,3},{2,0},{3,1},{4,6},{5,7},{6,4},{7,5},{8,10},{9,11},{10,... | collective-permute-start | bytes 884744 | tf_op jit(solution)/shard_map/ppermute | solution.py:32
  106.4 5.5 %keys.1 = (f32[256,1024]{1,0:T(8,128)S(1)}, bf16[256,1024]{1,0:T(8,128)(2,1)S(1)}, bf16[256,1024]{1,0:T(8,128)(2,1)S(1)}, bf16[256,1024]{1,0:T(8,128)(2,1)S(1)}) custom-call(bf16[256,1152]{1,0:T(8,128)(2,1)S(1)} %copy-done.6, bf16[256,2176]{1,0:T(8,128)(2,1)} %collective-permute-done.refs_1_.m1_ref, bf16[256,2176]{1,0:T(8,128)(2,1)} %collective-permute-done.2.refs_2_.m2_ref, ...), custom_call_target="tpu_custom_call" | custom-call | flops 2415919104 | bytes 8000000 | tf_op jit(solution)/shard_map/keys/pallas_call | solution.py:239
  113.4 3.5 %collective-permute-done.15 = bf16[144,1024]{1,0:T(8,128)(2,1)S(1)} collective-permute-done((bf16[144,1024]{1,0:T(8,128)(2,1)S(1)}, bf16[144,1024]{1,0:T(8,128)(2,1)S(1)}, u32[]{:S(2)}, u32[]{:S(2)}) %collective-permute-start.15) | collective-permute-done | bytes 294944 | tf_op jit(solution)/shard_map/ppermute | solution.py:32
  119.6 1.9 %collective-permute-start.13 = (bf16[144,1024]{1,0:T(8,128)(2,1)S(1)}, bf16[144,1024]{1,0:T(8,128)(2,1)S(1)}, u32[]{:S(2)}, u32[]{:S(2)}) collective-permute-start(bf16[144,1024]{1,0:T(8,128)(2,1)S(1)} %get-tuple-element.56), channel_id=1, source_target_pairs={{0,2},{1,3},{2,0},{3,1},{4,6},{5,7},{6,4},{7,5},{8,10},{9,11},{10,... | collective-permute-start | bytes 884744 | tf_op jit(solution)/shard_map/ppermute | solution.py:32
  121.5 3.3 %collective-permute-done.7 = bf16[256,1024]{1,0:T(8,128)(2,1)S(1)} collective-permute-done((bf16[256,1024]{1,0:T(8,128)(2,1)S(1)}, bf16[256,1024]{1,0:T(8,128)(2,1)S(1)}, u32[]{:S(2)}, u32[]{:S(2)}) %collective-permute-start.7) | collective-permute-done | bytes 524320 | tf_op jit(solution)/shard_map/ppermute | solution.py:28
  124.9 2.1 %collective-permute-start.12 = (bf16[144,1024]{1,0:T(8,128)(2,1)S(1)}, bf16[144,1024]{1,0:T(8,128)(2,1)S(1)}, u32[]{:S(2)}, u32[]{:S(2)}) collective-permute-start(bf16[144,1024]{1,0:T(8,128)(2,1)S(1)} %get-tuple-element.54), channel_id=1, source_target_pairs={{0,3},{1,0},{2,1},{3,2},{4,7},{5,4},{6,5},{7,6},{8,11},{9,8},{10,9... | collective-permute-start | bytes 884744 | tf_op jit(solution)/shard_map/ppermute | solution.py:32
  128.7 5.2 %outer_step.1 = (f32[4,144,1024]{2,1,0:T(8,128)}, f32[4,144,1024]{2,1,0:T(8,128)}) custom-call(s32[2]{0:T(128)S(1)} %pad_add_fusion.place_ref, f32[144,1024]{1,0:T(8,128)S(1)} %add_multiply_fusion.own_ref, f32[144,1024]{1,0:T(8,128)S(1)} %collective-permute-done.21.a_ref, f32[144,1024]{1,0:T(8,128)S(1)} %collective-permute-done.22.b_ref, ...), custom_call_target="tpu_custom_call" | custom-call | flops 4000000 | bytes 12000000 | tf_op jit(solution)/shard_map/outer_step/pallas_call | solution.py:208
  133.9 1.6 %collective-permute-done.16 = bf16[144,1024]{1,0:T(8,128)(2,1)S(1)} collective-permute-done((bf16[144,1024]{1,0:T(8,128)(2,1)S(1)}, bf16[144,1024]{1,0:T(8,128)(2,1)S(1)}, u32[]{:S(2)}, u32[]{:S(2)}) %collective-permute-start.16) | collective-permute-done | bytes 294944 | tf_op jit(solution)/shard_map/ppermute | solution.py:36
  136.6 3.6 %collective-permute-done.9 = bf16[256,1024]{1,0:T(8,128)(2,1)S(1)} collective-permute-done((bf16[256,1024]{1,0:T(8,128)(2,1)S(1)}, bf16[256,1024]{1,0:T(8,128)(2,1)S(1)}, u32[]{:S(2)}, u32[]{:S(2)}) %collective-permute-start.9) | collective-permute-done | bytes 524320 | tf_op jit(solution)/shard_map/ppermute | solution.py:28
  (60 shorter events, 23.8 us)
Async XLA Ops:
  9.5 56.3 %collective-permute-start = (bf16[256,2176]{1,0:T(8,128)(2,1)}, bf16[256,2176]{1,0:T(8,128)(2,1)}, u32[]{:S(2)}, u32[]{:S(2)}) collective-permute-start(bf16[256,2176]{1,0:T(8,128)(2,1)} %get-tuple-element.39), channel_id=1, source_target_pairs={{0,4},{1,5},{2,6},{3,7},{4,8},{5,9},{6,10},{7,11},{8,12},{9,13},{1... | collective-permute-start | bytes 3342344 | tf_op jit(solution)/shard_map/ppermute | solution.py:28
  11.6 54.1 %collective-permute-start.1 = (bf16[256,2176]{1,0:T(8,128)(2,1)}, bf16[256,2176]{1,0:T(8,128)(2,1)}, u32[]{:S(2)}, u32[]{:S(2)}) collective-permute-start(bf16[256,2176]{1,0:T(8,128)(2,1)} %get-tuple-element.41), channel_id=1, source_target_pairs={{0,12},{1,13},{2,14},{3,15},{4,0},{5,1},{6,2},{7,3},{8,4},{9,5},{1... | collective-permute-start | bytes 3342344 | tf_op jit(solution)/shard_map/ppermute | solution.py:28
  13.1 13.7 %collective-permute-start.3 = (bf16[144,1024]{1,0:T(8,128)(2,1)S(1)}, bf16[144,1024]{1,0:T(8,128)(2,1)S(1)}, u32[]{:S(2)}, u32[]{:S(2)}) collective-permute-start(bf16[144,1024]{1,0:T(8,128)(2,1)S(1)} %get-tuple-element.36), channel_id=1, source_target_pairs={{0,16},{1,17},{2,18},{3,19},{4,20},{5,21},{6,22},{7,23},{8,24},{9,... | collective-permute-start | bytes 884744 | tf_op jit(solution)/shard_map/ppermute | solution.py:36
  20.0 19.4 %collective-permute-start.18 = (bf16[144,1024]{1,0:T(8,128)(2,1)S(1)}, bf16[144,1024]{1,0:T(8,128)(2,1)S(1)}, u32[]{:S(2)}, u32[]{:S(2)}) collective-permute-start(bf16[144,1024]{1,0:T(8,128)(2,1)S(1)} %get-tuple-element.63), channel_id=1, source_target_pairs={{0,192},{32,224},{64,0},{96,32},{128,64},{160,96},{192,128},{224,1... | collective-permute-start | bytes 884744 | tf_op jit(solution)/shard_map/ppermute | solution.py:40
  21.7 24.8 %collective-permute-start.17 = (bf16[144,1024]{1,0:T(8,128)(2,1)S(1)}, bf16[144,1024]{1,0:T(8,128)(2,1)S(1)}, u32[]{:S(2)}, u32[]{:S(2)}) collective-permute-start(bf16[144,1024]{1,0:T(8,128)(2,1)S(1)} %get-tuple-element.61), channel_id=1, source_target_pairs={{0,64},{32,96},{64,128},{96,160},{128,192},{160,224},{192,0},{224,... | collective-permute-start | bytes 884744 | tf_op jit(solution)/shard_map/ppermute | solution.py:40
  27.7 36.7 %collective-permute-start.4 = (bf16[2,144,1024]{2,1,0:T(8,128)(2,1)}, bf16[2,144,1024]{2,1,0:T(8,128)(2,1)S(1)}, u32[]{:S(2)}, u32[]{:S(2)}) collective-permute-start(bf16[2,144,1024]{2,1,0:T(8,128)(2,1)} %pad_maximum_fusion.refs_4_), channel_id=1, source_target_pairs={{0,1},{1,2},{2,3},{3,0},{4,5},{5,6},{6,7},{7,4},{8,9},{9,10},{10,1... | collective-permute-start | bytes 1769480 | tf_op jit(solution)/shard_map/ppermute | solution.py:32
  39.4 25.8 %collective-permute-start.5 = (bf16[2,144,1024]{2,1,0:T(8,128)(2,1)}, bf16[2,144,1024]{2,1,0:T(8,128)(2,1)}, u32[]{:S(2)}, u32[]{:S(2)}) collective-permute-start(bf16[2,144,1024]{2,1,0:T(8,128)(2,1)} %pad_maximum_fusion.refs_4_), channel_id=1, source_target_pairs={{0,3},{1,0},{2,1},{3,2},{4,7},{5,4},{6,5},{7,6},{8,11},{9,8},{10,9... | collective-permute-start | bytes 1769480 | tf_op jit(solution)/shard_map/ppermute | solution.py:32
  47.2 16.0 %collective-permute-start.19 = (bf16[144,1024]{1,0:T(8,128)(2,1)}, bf16[144,1024]{1,0:T(8,128)(2,1)}, u32[]{:S(2)}, u32[]{:S(2)}) collective-permute-start(bf16[144,1024]{1,0:T(8,128)(2,1)} %get-tuple-element.64), channel_id=1, source_target_pairs={{0,128},{32,160},{64,192},{96,224},{128,0},{160,32},{192,64},{224,... | collective-permute-start | bytes 884744 | tf_op jit(solution)/shard_map/ppermute | solution.py:40
  65.7 27.9 %collective-permute-start.2 = (bf16[256,2176]{1,0:T(8,128)(2,1)}, bf16[256,2176]{1,0:T(8,128)(2,1)}, u32[]{:S(2)}, u32[]{:S(2)}) collective-permute-start(bf16[256,2176]{1,0:T(8,128)(2,1)} %get-tuple-element.42), channel_id=1, source_target_pairs={{0,8},{1,9},{2,10},{3,11},{4,12},{5,13},{6,14},{7,15},{8,0},{9,1},... | collective-permute-start | bytes 3342344 | tf_op jit(solution)/shard_map/ppermute | solution.py:28
  67.4 36.3 %collective-permute-start.21 = (f32[144,1024]{1,0:T(8,128)S(1)}, f32[144,1024]{1,0:T(8,128)S(1)}, u32[]{:S(2)}, u32[]{:S(2)}) collective-permute-start(f32[144,1024]{1,0:T(8,128)S(1)} %add_multiply_fusion.own_ref), channel_id=1, source_target_pairs={{0,64},{32,224},{64,128},{96,32},{128,192},{160,96},{192,0},{224,1... | collective-permute-start | bytes 1769480 | tf_op jit(solution)/shard_map/ppermute | solution.py:44
  69.5 36.3 %collective-permute-start.6 = (bf16[2,144,1024]{2,1,0:T(8,128)(2,1)}, bf16[2,144,1024]{2,1,0:T(8,128)(2,1)}, u32[]{:S(2)}, u32[]{:S(2)}) collective-permute-start(bf16[2,144,1024]{2,1,0:T(8,128)(2,1)} %pad_maximum_fusion.refs_4_), channel_id=1, source_target_pairs={{0,2},{1,3},{2,0},{3,1},{4,6},{5,7},{6,4},{7,5},{8,10},{9,11},{10,... | collective-permute-start | bytes 1769480 | tf_op jit(solution)/shard_map/ppermute | solution.py:32
  72.2 39.7 %collective-permute-start.23 = (f32[72,1024]{1,0:T(8,128)S(1)}, f32[72,1024]{1,0:T(8,128)S(1)}, u32[]{:S(2)}, u32[]{:S(2)}) collective-permute-start(f32[72,1024]{1,0:T(8,128)S(1)} %constant_dynamic-slice_fusion), channel_id=1, source_target_pairs={{0,128},{32,160},{64,192},{96,224},{128,0},{160,32},{192,64},{224,... | collective-permute-start | bytes 884744 | tf_op jit(solution)/shard_map/ppermute | solution.py:40
  100.9 12.4 %collective-permute-start.10 = (bf16[144,1024]{1,0:T(8,128)(2,1)S(1)}, bf16[144,1024]{1,0:T(8,128)(2,1)S(1)}, u32[]{:S(2)}, u32[]{:S(2)}) collective-permute-start(bf16[144,1024]{1,0:T(8,128)(2,1)S(1)} %get-tuple-element.51), channel_id=1, source_target_pairs={{0,2},{1,3},{2,0},{3,1},{4,6},{5,7},{6,4},{7,5},{8,10},{9,11},{10,... | collective-permute-start | bytes 884744 | tf_op jit(solution)/shard_map/ppermute | solution.py:32
  103.8 23.6 %collective-permute-start.22 = (f32[144,1024]{1,0:T(8,128)S(1)}, f32[144,1024]{1,0:T(8,128)S(1)}, u32[]{:S(2)}, u32[]{:S(2)}) collective-permute-start(f32[144,1024]{1,0:T(8,128)S(1)} %collective-permute-done.21.a_ref), channel_id=1, source_target_pairs={{0,32},{32,0},{64,96},{96,64},{128,160},{160,128},{192,224},{224,1... | collective-permute-start | bytes 1769480 | tf_op jit(solution)/shard_map/ppermute | solution.py:52
  104.9 12.0 %collective-permute-start.15 = (bf16[144,1024]{1,0:T(8,128)(2,1)S(1)}, bf16[144,1024]{1,0:T(8,128)(2,1)S(1)}, u32[]{:S(2)}, u32[]{:S(2)}) collective-permute-start(bf16[144,1024]{1,0:T(8,128)(2,1)S(1)} %get-tuple-element.59), channel_id=1, source_target_pairs={{0,3},{1,0},{2,1},{3,2},{4,7},{5,4},{6,5},{7,6},{8,11},{9,8},{10,9... | collective-permute-start | bytes 884744 | tf_op jit(solution)/shard_map/ppermute | solution.py:32
  105.8 12.6 %collective-permute-start.14 = (bf16[144,1024]{1,0:T(8,128)(2,1)S(1)}, bf16[144,1024]{1,0:T(8,128)(2,1)S(1)}, u32[]{:S(2)}, u32[]{:S(2)}) collective-permute-start(bf16[144,1024]{1,0:T(8,128)(2,1)S(1)} %get-tuple-element.58), channel_id=1, source_target_pairs={{0,1},{1,2},{2,3},{3,0},{4,5},{5,6},{6,7},{7,4},{8,9},{9,10},{10,1... | collective-permute-start | bytes 884744 | tf_op jit(solution)/shard_map/ppermute | solution.py:32
  111.9 13.0 %collective-permute-start.7 = (bf16[256,1024]{1,0:T(8,128)(2,1)S(1)}, bf16[256,1024]{1,0:T(8,128)(2,1)S(1)}, u32[]{:S(2)}, u32[]{:S(2)}) collective-permute-start(bf16[256,1024]{1,0:T(8,128)(2,1)S(1)} %get-tuple-element.45), channel_id=1, source_target_pairs={{0,12},{1,13},{2,14},{3,15},{4,0},{5,1},{6,2},{7,3},{8,4},{9,5},{1... | collective-permute-start | bytes 1572872 | tf_op jit(solution)/shard_map/ppermute | solution.py:28
  113.3 13.8 %collective-permute-start.8 = (bf16[256,1024]{1,0:T(8,128)(2,1)S(1)}, bf16[256,1024]{1,0:T(8,128)(2,1)S(1)}, u32[]{:S(2)}, u32[]{:S(2)}) collective-permute-start(bf16[256,1024]{1,0:T(8,128)(2,1)S(1)} %get-tuple-element.46), channel_id=1, source_target_pairs={{0,4},{1,5},{2,6},{3,7},{4,8},{5,9},{6,10},{7,11},{8,12},{9,13},{1... | collective-permute-start | bytes 1572872 | tf_op jit(solution)/shard_map/ppermute | solution.py:28
  116.9 2.7 %collective-permute-start.24 = (f32[72,1024]{1,0:T(8,128)S(1)}, f32[72,1024]{1,0:T(8,128)S(1)}, u32[]{:S(2)}, u32[]{:S(2)}) collective-permute-start(f32[72,1024]{1,0:T(8,128)S(1)} %collective-permute-done.23.near_ref), channel_id=1, source_target_pairs={{0,32},{32,0},{64,96},{96,64},{128,160},{160,128},{192,224},{224,1... | collective-permute-start | bytes 884744 | tf_op jit(solution)/shard_map/ppermute | solution.py:52
  118.6 16.9 %collective-permute-start.16 = (bf16[144,1024]{1,0:T(8,128)(2,1)S(1)}, bf16[144,1024]{1,0:T(8,128)(2,1)S(1)}, u32[]{:S(2)}, u32[]{:S(2)}) collective-permute-start(bf16[144,1024]{1,0:T(8,128)(2,1)S(1)} %add_convert_fusion.1), channel_id=1, source_target_pairs={{0,16},{1,17},{2,18},{3,19},{4,20},{5,21},{6,22},{7,23},{8,24},{9,... | collective-permute-start | bytes 884744 | tf_op jit(solution)/shard_map/ppermute | solution.py:36
  119.6 15.9 %collective-permute-start.13 = (bf16[144,1024]{1,0:T(8,128)(2,1)S(1)}, bf16[144,1024]{1,0:T(8,128)(2,1)S(1)}, u32[]{:S(2)}, u32[]{:S(2)}) collective-permute-start(bf16[144,1024]{1,0:T(8,128)(2,1)S(1)} %get-tuple-element.56), channel_id=1, source_target_pairs={{0,2},{1,3},{2,0},{3,1},{4,6},{5,7},{6,4},{7,5},{8,10},{9,11},{10,... | collective-permute-start | bytes 884744 | tf_op jit(solution)/shard_map/ppermute | solution.py:32
  124.9 10.7 %collective-permute-start.12 = (bf16[144,1024]{1,0:T(8,128)(2,1)S(1)}, bf16[144,1024]{1,0:T(8,128)(2,1)S(1)}, u32[]{:S(2)}, u32[]{:S(2)}) collective-permute-start(bf16[144,1024]{1,0:T(8,128)(2,1)S(1)} %get-tuple-element.54), channel_id=1, source_target_pairs={{0,3},{1,0},{2,1},{3,2},{4,7},{5,4},{6,5},{7,6},{8,11},{9,8},{10,9... | collective-permute-start | bytes 884744 | tf_op jit(solution)/shard_map/ppermute | solution.py:32
  127.2 8.5 %collective-permute-start.11 = (bf16[144,1024]{1,0:T(8,128)(2,1)S(1)}, bf16[144,1024]{1,0:T(8,128)(2,1)S(1)}, u32[]{:S(2)}, u32[]{:S(2)}) collective-permute-start(bf16[144,1024]{1,0:T(8,128)(2,1)S(1)} %get-tuple-element.52), channel_id=1, source_target_pairs={{0,1},{1,2},{2,3},{3,0},{4,5},{5,6},{6,7},{7,4},{8,9},{9,10},{10,1... | collective-permute-start | bytes 884744 | tf_op jit(solution)/shard_map/ppermute | solution.py:32
  127.4 12.8 %collective-permute-start.9 = (bf16[256,1024]{1,0:T(8,128)(2,1)S(1)}, bf16[256,1024]{1,0:T(8,128)(2,1)S(1)}, u32[]{:S(2)}, u32[]{:S(2)}) collective-permute-start(bf16[256,1024]{1,0:T(8,128)(2,1)S(1)} %get-tuple-element.48), channel_id=1, source_target_pairs={{0,8},{1,9},{2,10},{3,11},{4,12},{5,13},{6,14},{7,15},{8,0},{9,1},... | collective-permute-start | bytes 1572872 | tf_op jit(solution)/shard_map/ppermute | solution.py:28
  (11 other events, 106.3 us)

commit v3 on v2

v3 whole, which is shorter than its diff:
```python
import jax
import jax.numpy as jnp
from jax import lax
from jax.experimental import pallas as pl
from jax.experimental.pallas import tpu as pltpu
from jax.sharding import Mesh, PartitionSpec as P

D = 4608
KV = 1024
ROWS = 144
WIDE = 576
TOK = 256
MSG = 2 * WIDE + KV
SCALE = float(D) ** -0.5
BF = jnp.bfloat16
F32 = jnp.float32
LIMIT = 48 * 1024 * 1024


def _place():
    return [lax.axis_index(n) for n in ("zl", "core", "zh", "y", "x")]


def _shift(v, axis, k, size=4):
    return lax.ppermute(v, axis, [(i, (i + k) % size) for i in range(size)])


def _after(v, *done):
    return lax.optimization_barrier((v, *done))[0]


def _call(kernel, name, outs, scratch=(), flops=0, traffic=0, **kw):
    return pl.pallas_call(
        kernel,
        name=name,
        out_shape=[jax.ShapeDtypeStruct(s, d) for s, d in outs],
        scratch_shapes=list(scratch),
        compiler_params=pltpu.CompilerParams(vmem_limit_bytes=LIMIT),
        cost_estimate=pl.CostEstimate(flops=flops, bytes_accessed=traffic, transcendentals=0),
        **kw,
    )


def _vmem(n):
    return [pl.BlockSpec(memory_space=pltpu.VMEM)] * n


def _pick_kernel(index_ref, frag_ref, used_ref, give_ref, keep_ref, sems):
    core = _place()[1]
    copies = [
        pltpu.make_async_copy(frag_ref.at[0, index_ref[0]], used_ref, sems.at[0]),
        pltpu.make_async_copy(frag_ref.at[0, pl.ds(2 - 2 * core, 2)], give_ref, sems.at[1]),
        pltpu.make_async_copy(frag_ref.at[0, pl.ds(2 * core, 2)], keep_ref, sems.at[2]),
    ]
    for c in copies:
        c.start()
    for c in copies:
        c.wait()


def _norm_kernel(x_ref, gain_ref, cot_ref, own_ref, m1_ref, m2_ref, m3_ref, held):
    _, _, zh, y, _ = _place()
    values = x_ref[...].astype(F32)
    stats = jnp.mean(values * values, axis=1, keepdims=True)
    normed = (values * lax.rsqrt(stats + 1e-06) * gain_ref[...]).astype(BF)
    for q in range(8):
        held[q] = normed[:, q * WIDE : (q + 1) * WIDE]
    for k, out in enumerate((own_ref, m1_ref, m2_ref, m3_ref)):
        chunk = (y + k) & 3
        out[:, : 2 * WIDE] = jnp.concatenate([held[(1 - zh) * 4 + chunk], held[zh * 4 + chunk]], axis=1)
        if k:
            out[:, 2 * WIDE :] = cot_ref[...]


def _grad_kernel(n_ref, c_ref, m1_ref, m2_ref, m3_ref, *rest):
    outs, total = rest[:8], rest[8]
    x = _place()[4]
    messages = (m1_ref, m2_ref, m3_ref)
    normed = jnp.concatenate([n_ref[...]] + [m[:, : 2 * WIDE] for m in messages], axis=0)
    cot = jnp.concatenate([c_ref[...]] + [m[:, 2 * WIDE :] for m in messages], axis=0)
    total[...] = lax.dot_general(normed, cot, (((0,), (0,)), ((), ())), preferred_element_type=F32)
    for h in range(2):
        for k in range(4):
            first = pl.multiple_of(h * WIDE + ((x + k) & 3) * ROWS, 16)
            out = outs[h * 4 + k]
            out[...] = (total[pl.ds(first, ROWS), :] * SCALE).astype(out.dtype)


def _keys_kernel(*refs):
    blocks, pairs, outs, layer = refs[0:4], refs[4:8], refs[8:12], refs[12]
    x = _place()[4]
    for k in range(4):
        for h in range(2):
            first = pl.multiple_of(h * WIDE + ((x + 4 - k) & 3) * ROWS, 16)
            layer[pl.ds(first, ROWS), :] = pairs[k][h]
    for k in range(4):
        part = jnp.dot(blocks[k][:, : 2 * WIDE], layer[...], preferred_element_type=F32)
        outs[k][...] = (part * SCALE).astype(outs[k].dtype)


def _outer_kernel(core_ref, own_ref, far_ref, global_ref, momentum_ref, new_global_ref, new_momentum_ref):
    k = pl.program_id(0)

    def write(mean):
        momentum = 0.9 * momentum_ref[0] + mean
        new_momentum_ref[0] = momentum
        new_global_ref[0] = global_ref[0] - 0.7 * (mean + 0.9 * momentum)

    @pl.when(k < 2)
    def _():
        write(own_ref[k])

    @pl.when(k >= 2)
    def _():
        write(far_ref[k - 2])


def body(layer_index, inputs, norm_gain, cotangent, local_fragment, global_fragment, momentum):
    core = lax.axis_index("core")
    any_spec = pl.BlockSpec(memory_space=pl.ANY)

    used, give, keep = _call(
        _pick_kernel,
        "pick",
        [((ROWS, KV), BF)] + [((2, ROWS, KV), BF)] * 2,
        [pltpu.SemaphoreType.DMA((3,))],
        traffic=3_000_000,
        in_specs=[pl.BlockSpec(memory_space=pltpu.SMEM), any_spec],
        out_specs=[any_spec] * 3,
    )(layer_index, local_fragment)
    used_other = _shift(used, "zh", 1, 2)
    got = _shift(give, "core", 1, 2)

    rows = 64
    tile = lambda n: pl.BlockSpec((rows, n), lambda i: (i, 0))
    own, m1, m2, m3 = _call(
        _norm_kernel,
        "normed",
        [((TOK, 2 * WIDE), BF)] + [((TOK, MSG), BF)] * 3,
        [pltpu.VMEM((8, rows, WIDE), BF)],
        traffic=7_000_000,
        flops=20_000_000,
        grid=(TOK // rows,),
        in_specs=[tile(D), pl.BlockSpec((1, D), lambda i: (0, 0)), tile(KV)],
        out_specs=[tile(2 * WIDE)] + [tile(MSG)] * 3,
    )(inputs, _after(norm_gain[None, :], used), cotangent)
    shared = lax.dynamic_slice_in_dim(global_fragment, 2 * core, 2, 0)
    delta = (shared - keep.astype(F32)) + (shared - _after(got, own).astype(F32))
    summed = lax.psum_scatter(delta.reshape(2 * ROWS, KV), "zl", tiled=True)
    r1, r3 = _shift(m1, "y", 1), _shift(m3, "y", 3)
    messages = [r1, _shift(_after(m2, r1, r3, used_other, summed), "y", 2), r3]

    pair = jnp.stack([_after(used_other, r1, r3), used])
    pairs = [pair] + [_shift(pair, "x", k) for k in (1, 2, 3)]

    g = _call(
        _grad_kernel,
        "grad",
        ([((ROWS, KV), F32)] + [((ROWS, KV), BF)] * 3) * 2,
        [pltpu.VMEM((2 * WIDE, KV), F32)],
        flops=2 * 2 * WIDE * KV * 4 * TOK,
        traffic=8_000_000,
        in_specs=_vmem(5),
        out_specs=_vmem(8),
    )(own, cotangent, *messages)
    a = [_shift(g[k], "x", k) for k in (1, 3, 2)]
    far_sum = g[0] + sum(v.astype(F32) for v in a)
    from_zh = _shift(far_sum.astype(BF), "zh", 1, 2)
    b = [_shift(_after(g[4 + k], a[2]), "x", k) for k in (1, 3, 2)]
    weight_grad = (g[4] + sum(v.astype(F32) for v in b) + from_zh.astype(F32))[None]

    k0, k1, k2, k3 = _call(
        _keys_kernel,
        "keys",
        [((TOK, KV), F32)] + [((TOK, KV), BF)] * 3,
        [pltpu.VMEM((2 * WIDE, KV), BF)],
        flops=2 * 4 * TOK * 2 * WIDE * KV,
        traffic=8_000_000,
        in_specs=_vmem(8),
        out_specs=_vmem(4),
    )(own, *messages, *pairs)
    average = _after(lax.all_gather(summed / 8.0, "zl", tiled=True).reshape(2, ROWS, KV), k0)
    far = _shift(average, "core", 1, 2)

    def by_layer(k, place):
        return ((k + 2 * place[0]) & 3, 0, 0)

    block = pl.BlockSpec((1, ROWS, KV), by_layer)
    whole = pl.BlockSpec((2, ROWS, KV), lambda k, place: (0, 0, 0))
    new_global, new_momentum = pl.pallas_call(
        _outer_kernel,
        name="outer_step",
        out_shape=[jax.ShapeDtypeStruct((4, ROWS, KV), F32)] * 2,
        grid_spec=pltpu.PrefetchScalarGridSpec(
            num_scalar_prefetch=1,
            grid=(4,),
            in_specs=[whole, whole, block, block],
            out_specs=[block, block],
        ),
        compiler_params=pltpu.CompilerParams(vmem_limit_bytes=LIMIT),
        cost_estimate=pl.CostEstimate(flops=4_000_000, bytes_accessed=12_000_000, transcendentals=0),
    )(core.astype(jnp.int32)[None], average, far, global_fragment, momentum)

    e1 = _shift(k1, "y", 3)
    e3 = _shift(k3, "y", 1)
    e2 = _shift(_after(k2, e1, e3), "y", 2)
    keys = k0 + sum(v.astype(F32) for v in (e1, e3, e2))
    return keys.astype(BF), weight_grad, new_global, new_momentum


def solution(mesh):
    split = Mesh(mesh.devices.reshape(4, 2, 2, 4, 4), ("zl", "core", "zh", "y", "x"))
    replica, fsdp = ("zl", "core"), ("zh", "y", "x")
    placed = (
        P(replica),
        P(replica + fsdp, None),
        P(),
        P(replica + fsdp, None),
        P(replica, None, fsdp, None),
        P(None, fsdp, None),
        P(None, fsdp, None),
    )
    return jax.shard_map(
        body,
        mesh=split,
        in_specs=placed,
        out_specs=(
            P(replica + fsdp, None),
            P(replica, fsdp, None),
            P(None, fsdp, None),
            P(None, fsdp, None),
        ),
        check_vma=False,
    )
```

time: 144 us -> 169 us (1.17)
  waiting for transfers between devices: 67.7 us -> 81.7 us
  between operations: 1.4 us -> 14.9 us
  starting transfers between devices: 40 us -> 33 us
  other arithmetic: 4.59 us -> 9.37 us
    reduce_scatter x0 -> x1, waiting for transfers between devices: none -> 34.5 us  [body(): summed = lax.psum_scatter(delta.reshape(2 * ROWS, KV), 'zl', tiled=True)]
    ppermute x25 -> x19, waiting for transfers between devices: 67.7 us -> 47.1 us  [_shift(): return lax.ppermute(v, axis, [(i, (i + k) % size) for i in range(size)])]
    ppermute x25 -> x19, starting transfers between devices: 40 us -> 33 us  [_shift(): return lax.ppermute(v, axis, [(i, (i + k) % size) for i in range(size)])]
    unnamed x20 -> x46, local copies, waits for them, and re-layouts: 5.12 us -> 6.99 us
  transfers between devices with their start and end apart: 25 -> 21, of which waited for: 12 -> 7; matrix products, arithmetic and copies ran while one was open for 2% -> 4% of each run, Pallas kernels for 11% -> 9%
where the time goes in v3:
time: 169 us; the launch traced here: 167 us
  waiting for transfers between devices  81.7 us (48%)
  starting transfers between devices  33 us (20%)
  Pallas kernels  21 us (12%)
  between operations  14.9 us (9%)
  other arithmetic  9.37 us (6%)
  local copies, waits for them, and re-layouts  7 us (4%)
    ppermute x19, waiting for transfers between devices, _shift(): return lax.ppermute(v, axis, [(i, (i + k) % size) for i in range(size)])  47.1 us
    reduce_scatter x1, waiting for transfers between devices, body(): summed = lax.psum_scatter(delta.reshape(2 * ROWS, KV), 'zl', tiled=True)  34.5 us
    ppermute x19, starting transfers between devices, _shift(): return lax.ppermute(v, axis, [(i, (i + k) % size) for i in range(size)])  33 us
    unnamed x46, local copies, waits for them, and re-layouts  6.99 us
    pallas_call x1, Pallas kernels, body(): _call(_grad_kernel, 'grad', ([((ROWS, KV), F32)] + [((ROWS, KV), BF)] * 3...  5.78 us
    pallas_call x1, Pallas kernels, body(): _call(_keys_kernel, 'keys', [((TOK, KV), F32)] + [((TOK, KV), BF)] * 3, [...  5.74 us
    pallas_call x1, Pallas kernels, body(): pl.pallas_call(_outer_kernel, name='outer_step', out_shape=[jax.ShapeDtyp...  4.62 us
    pallas_call x1, Pallas kernels, body(): _call(_norm_kernel, 'normed', [((TOK, 2 * WIDE), BF)] + [((TOK, MSG), BF)...  3.95 us
  transfers between devices with their start and end apart: 21, of which 7 were waited for; matrix products, arithmetic and copies ran while one was open for 4% of the time, Pallas kernels for 9%

profile of v3, /device:TPU:1, one launch (start us, length us, event | category | flops | bytes accessed | tf_op | source)
XLA Modules:
  0.0 167.0 jit_solution(9266434512786489961)
XLA Ops:
  7.9 1.3 copy-done.2
  10.8 3.2 %collective-permute-start.3 = (bf16[2,144,1024]{2,1,0:T(8,128)(2,1)}, bf16[2,144,1024]{2,1,0:T(8,128)(2,1)}, u32[]{:S(2)}, u32[]{:S(2)}) collective-permute-start(bf16[2,144,1024]{2,1,0:T(8,128)(2,1)} %get-tuple-element.41), channel_id=1, source_target_pairs={{0,32},{32,0},{1,33},{33,1},{2,34},{34,2},{3,35},{35,3},{4,36},{36... | collective-permute-start | bytes 1769480 | tf_op jit(solution)/shard_map/ppermute | solution.py:25
  14.0 3.9 %normed.1 = (bf16[256,1152]{1,0:T(8,128)(2,1)S(1)}, bf16[256,2176]{1,0:T(8,128)(2,1)S(1)}, bf16[256,2176]{1,0:T(8,128)(2,1)S(1)}, bf16[256,2176]{1,0:T(8,128)(2,1)S(1)}) custom-call(bf16[256,4608]{1,0:T(8,128)(2,1)} %x_ref.1, f32[1,4608]{1,0:T(1,128)S(1)} %broadcast_in_dim.9.gain_ref, bf16[256,1024]{1,0:T(8,128)(2,1)S(1)} %copy-done.6), custom_call_target="tpu_custom_call" | custom-call | flops 20000000 | bytes 7000000 | tf_op jit(solution)/shard_map/normed/pallas_call | solution.py:136
  18.8 2.8 %subtract_add_fusion = f32[2,144,1024]{2,1,0:T(8,128)} fusion(bf16[2,144,1024]{2,1,0:T(8,128)(2,1)} %collective-permute-done.3, bf16[2,144,1024]{2,1,0:T(8,128)(2,1)S(1)} %get-tuple-element.40, f32[4,144,1024]{2,1,0:T(8,128)S(1)} %copy-done, s32[]{:T(128)S(6)} %select_n.3), kind=kLoop, calls=%fused_computation | loop fusion | flops 1474560 | bytes 3538948 | tf_op jit(solution)/shard_map/add | solution.py:148
  21.8 2.7 %collective-permute-start.1 = (bf16[256,2176]{1,0:T(8,128)(2,1)}, bf16[256,2176]{1,0:T(8,128)(2,1)}, u32[]{:S(2)}, u32[]{:S(2)}) collective-permute-start(bf16[256,2176]{1,0:T(8,128)(2,1)} %copy-done.10), channel_id=1, source_target_pairs={{0,12},{4,0},{8,4},{12,8},{1,13},{5,1},{9,5},{13,9},{2,14},{6,2},{... | collective-permute-start | bytes 3342344 | tf_op jit(solution)/shard_map/ppermute | solution.py:25
  24.5 5.3 %collective-permute-start.2 = (bf16[144,1024]{1,0:T(8,128)(2,1)S(1)}, bf16[144,1024]{1,0:T(8,128)(2,1)S(1)}, u32[]{:S(2)}, u32[]{:S(2)}) collective-permute-start(bf16[144,1024]{1,0:T(8,128)(2,1)S(1)} %copy-done.8), channel_id=1, source_target_pairs={{0,16},{16,0},{1,17},{17,1},{2,18},{18,2},{3,19},{19,3},{4,20},{20... | collective-permute-start | bytes 884744 | tf_op jit(solution)/shard_map/ppermute | solution.py:25
  29.8 34.5 %reduce-scatter.2.cloned.1.call-done = f32[72,1024]{1,0:T(8,128)} async-done(((f32[288,1024]{1,0:T(8,128)}), f32[72,1024]{1,0:T(8,128)}) %reduce-scatter.2.cloned.1.call-update) | async-done | bytes 294928 | tf_op jit(solution)/shard_map/reduce_scatter | solution.py:149
  64.4 1.7 %broadcast_multiply_fusion = f32[72,1024]{1,0:T(8,128)} fusion(f32[72,1024]{1,0:T(8,128)} %reduce-scatter.2.cloned.1.call-done), kind=kLoop, calls=%fused_computation.5 | loop fusion | flops 73728 | bytes 589824 | tf_op jit(solution)/shard_map/div | solution.py:182
  66.1 1.7 collective-permute-start.4
  67.8 1.3 collective-permute-start.5
  69.1 2.4 %collective-permute-start.6 = (bf16[2,144,1024]{2,1,0:T(8,128)(2,1)S(1)}, bf16[2,144,1024]{2,1,0:T(8,128)(2,1)S(1)}, u32[]{:S(2)}, u32[]{:S(2)}) collective-permute-start(bf16[2,144,1024]{2,1,0:T(8,128)(2,1)S(1)} %pad_maximum_fusion.refs_4_), channel_id=1, source_target_pairs={{0,2},{1,3},{2,0},{3,1},{4,6},{5,7},{6,4},{7,5},{8,10},{9,11},{10,... | collective-permute-start | bytes 1769480 | tf_op jit(solution)/shard_map/ppermute | solution.py:25
  72.7 20.9 %collective-permute-done.4.refs_2_.m2_ref = bf16[256,2176]{1,0:T(8,128)(2,1)S(1)} collective-permute-done((bf16[256,2176]{1,0:T(8,128)(2,1)}, bf16[256,2176]{1,0:T(8,128)(2,1)S(1)}, u32[]{:S(2)}, u32[]{:S(2)}) %collective-permute-start.4) | collective-permute-done | bytes 1114144 | tf_op jit(solution)/shard_map/ppermute | solution.py:25
  94.7 5.8 %grad.1 = (f32[144,1024]{1,0:T(8,128)S(1)}, bf16[144,1024]{1,0:T(8,128)(2,1)}, bf16[144,1024]{1,0:T(8,128)(2,1)}, bf16[144,1024]{1,0:T(8,128)(2,1)}, f32[144,102...) custom-call(bf16[256,1152]{1,0:T(8,128)(2,1)S(1)} %copy-done.13, ...), custom_call_target="tpu_custom_call" | custom-call | flops 2415919104 | bytes 8000000 | tf_op jit(solution)/shard_map/grad/pallas_call | solution.py:156
  102.8 2.7 %collective-permute-start.11 = (bf16[144,1024]{1,0:T(8,128)(2,1)}, bf16[144,1024]{1,0:T(8,128)(2,1)}, u32[]{:S(2)}, u32[]{:S(2)}) collective-permute-start(bf16[144,1024]{1,0:T(8,128)(2,1)} %get-tuple-element.52), channel_id=1, source_target_pairs={{0,2},{1,3},{2,0},{3,1},{4,6},{5,7},{6,4},{7,5},{8,10},{9,11},{10,... | collective-permute-start | bytes 884744 | tf_op jit(solution)/shard_map/ppermute | solution.py:25
  107.0 5.7 %keys.1 = (f32[256,1024]{1,0:T(8,128)S(1)}, bf16[256,1024]{1,0:T(8,128)(2,1)}, bf16[256,1024]{1,0:T(8,128)(2,1)S(1)}, bf16[256,1024]{1,0:T(8,128)(2,1)}) custom-call(bf16[256,1152]{1,0:T(8,128)(2,1)S(1)} %copy-done.13, bf16[256,2176]{1,0:T(8,128)(2,1)} %collective-permute-done.refs_1_.m1_ref, bf16[256,2176]{1,0:T(8,128)(2,1)} %copy-done.22, ...), custom_call_target="tpu_custom_call" | custom-call | flops 2415919104 | bytes 8000000 | tf_op jit(solution)/shard_map/keys/pallas_call | solution.py:172
  113.6 1.4 collective-permute-start.8
  115.1 2.7 %collective-permute-start.18 = (f32[2,144,1024]{2,1,0:T(8,128)}, f32[2,144,1024]{2,1,0:T(8,128)S(1)}, u32[]{:S(2)}, u32[]{:S(2)}) collective-permute-start(f32[2,144,1024]{2,1,0:T(8,128)} %bitcast.7), channel_id=1, source_target_pairs={{0,32},{32,0},{1,33},{33,1},{2,34},{34,2},{3,35},{35,3},{4,36},{36... | collective-permute-start | bytes 3538952 | tf_op jit(solution)/shard_map/ppermute | solution.py:25
  119.4 1.5 add_convert_fusion.1
  122.1 3.3 %collective-permute-start.14 = (bf16[144,1024]{1,0:T(8,128)(2,1)}, bf16[144,1024]{1,0:T(8,128)(2,1)S(1)}, u32[]{:S(2)}, u32[]{:S(2)}) collective-permute-start(bf16[144,1024]{1,0:T(8,128)(2,1)} %copy-done.20), channel_id=1, source_target_pairs={{0,2},{1,3},{2,0},{3,1},{4,6},{5,7},{6,4},{7,5},{8,10},{9,11},{10,... | collective-permute-start | bytes 884744 | tf_op jit(solution)/shard_map/ppermute | solution.py:25
  125.5 1.9 %collective-permute-start.13 = (bf16[144,1024]{1,0:T(8,128)(2,1)S(1)}, bf16[144,1024]{1,0:T(8,128)(2,1)S(1)}, u32[]{:S(2)}, u32[]{:S(2)}) collective-permute-start(bf16[144,1024]{1,0:T(8,128)(2,1)S(1)} %copy-done.19), channel_id=1, source_target_pairs={{0,3},{1,0},{2,1},{3,2},{4,7},{5,4},{6,5},{7,6},{8,11},{9,8},{10,9... | collective-permute-start | bytes 884744 | tf_op jit(solution)/shard_map/ppermute | solution.py:25
  128.0 11.6 %collective-permute-done.17 = bf16[144,1024]{1,0:T(8,128)(2,1)S(1)} collective-permute-done((bf16[144,1024]{1,0:T(8,128)(2,1)S(1)}, bf16[144,1024]{1,0:T(8,128)(2,1)S(1)}, u32[]{:S(2)}, u32[]{:S(2)}) %collective-permute-start.17) | collective-permute-done | bytes 294944 | tf_op jit(solution)/shard_map/ppermute | solution.py:25
  140.6 12.6 %collective-permute-done.10 = bf16[256,1024]{1,0:T(8,128)(2,1)S(1)} collective-permute-done((bf16[256,1024]{1,0:T(8,128)(2,1)S(1)}, bf16[256,1024]{1,0:T(8,128)(2,1)S(1)}, u32[]{:S(2)}, u32[]{:S(2)}) %collective-permute-start.10) | collective-permute-done | bytes 524320 | tf_op jit(solution)/shard_map/ppermute | solution.py:25
  153.2 2.3 %add_convert_fusion = bf16[256,1024]{1,0:T(8,128)(2,1)} fusion(f32[256,1024]{1,0:T(8,128)S(1)} %get-tuple-element.45, bf16[256,1024]{1,0:T(8,128)(2,1)S(1)} %collective-permute-done.10, bf16[256,1024]{1,0:T(8,128)(2,1)} %collective-permute-done.9, bf16[256,1024]{1,0:T(8,128)(2,1)} %collective-permute-done.8), kind=kLoop, calls=%fused_computation.1 | loop fusion | flops 1835008 | bytes 3145728 | tf_op jit(solution)/shard_map/convert_element_type | solution.py:208
  155.6 4.6 %outer_step.1 = (f32[4,144,1024]{2,1,0:T(8,128)}, f32[4,144,1024]{2,1,0:T(8,128)}) custom-call(s32[1]{0:T(128)} %bitcast.4.core_ref, f32[2,144,1024]{2,1,0:T(8,128)S(1)} %bitcast.8, f32[2,144,1024]{2,1,0:T(8,128)S(1)} %collective-permute-done.18.far_ref, f32[4,144,1024]{2,1,0:T(8,128)S(1)} %copy-done, f32[4,144,1024]{2,1,0:T(8,128)} %momentum_ref.1), custom_call_target="tpu_custom_call" | custom-call | flops 4000000 | bytes 12000000 | tf_op jit(solution)/shard_map/outer_step/pallas_call | solution.py:190
  (78 shorter events, 14.1 us)
Async XLA Ops:
  7.2 57.2 %reduce-scatter.2.cloned.1.call-start = ((), (), s32[]{:S(2)}) async-start(), calls=%async_computation.1 | async-start | bytes 1474560 | tf_op jit(solution)/shard_map/reduce_scatter | solution.py:149
  10.8 8.1 %collective-permute-start.3 = (bf16[2,144,1024]{2,1,0:T(8,128)(2,1)}, bf16[2,144,1024]{2,1,0:T(8,128)(2,1)}, u32[]{:S(2)}, u32[]{:S(2)}) collective-permute-start(bf16[2,144,1024]{2,1,0:T(8,128)(2,1)} %get-tuple-element.41), channel_id=1, source_target_pairs={{0,32},{32,0},{1,33},{33,1},{2,34},{34,2},{3,35},{35,3},{4,36},{36... | collective-permute-start | bytes 1769480 | tf_op jit(solution)/shard_map/ppermute | solution.py:25
  21.7 93.4 %all-gather.2.cloned.1.call-start = ((), (), s32[]{:S(2)}) async-start(), calls=%async_computation.2 | async-start | bytes 1474560 | tf_op jit(solution)/shard_map/all_gather | solution.py:182
  21.7 44.4 %collective-permute-start = (bf16[256,2176]{1,0:T(8,128)(2,1)}, bf16[256,2176]{1,0:T(8,128)(2,1)}, u32[]{:S(2)}, u32[]{:S(2)}) collective-permute-start(bf16[256,2176]{1,0:T(8,128)(2,1)} %copy-done.11), channel_id=1, source_target_pairs={{0,4},{4,8},{8,12},{12,0},{1,5},{5,9},{9,13},{13,1},{2,6},{6,10},{... | collective-permute-start | bytes 3342344 | tf_op jit(solution)/shard_map/ppermute | solution.py:25
  21.8 44.3 %collective-permute-start.1 = (bf16[256,2176]{1,0:T(8,128)(2,1)}, bf16[256,2176]{1,0:T(8,128)(2,1)}, u32[]{:S(2)}, u32[]{:S(2)}) collective-permute-start(bf16[256,2176]{1,0:T(8,128)(2,1)} %copy-done.10), channel_id=1, source_target_pairs={{0,12},{4,0},{8,4},{12,8},{1,13},{5,1},{9,5},{13,9},{2,14},{6,2},{... | collective-permute-start | bytes 3342344 | tf_op jit(solution)/shard_map/ppermute | solution.py:25
  24.5 41.6 %collective-permute-start.2 = (bf16[144,1024]{1,0:T(8,128)(2,1)S(1)}, bf16[144,1024]{1,0:T(8,128)(2,1)S(1)}, u32[]{:S(2)}, u32[]{:S(2)}) collective-permute-start(bf16[144,1024]{1,0:T(8,128)(2,1)S(1)} %copy-done.8), channel_id=1, source_target_pairs={{0,16},{16,0},{1,17},{17,1},{2,18},{18,2},{3,19},{19,3},{4,20},{20... | collective-permute-start | bytes 884744 | tf_op jit(solution)/shard_map/ppermute | solution.py:25
  66.1 28.6 %copy-start.13 = (bf16[256,1152]{1,0:T(8,128)(2,1)S(1)}, bf16[256,1152]{1,0:T(8,128)(2,1)}, u32[]{:S(2)}) copy-start(bf16[256,1152]{1,0:T(8,128)(2,1)} %copy-done.12) | copy-start | bytes 1769476
  66.1 27.6 %collective-permute-start.4 = (bf16[256,2176]{1,0:T(8,128)(2,1)}, bf16[256,2176]{1,0:T(8,128)(2,1)S(1)}, u32[]{:S(2)}, u32[]{:S(2)}) collective-permute-start(bf16[256,2176]{1,0:T(8,128)(2,1)} %copy-done.9), channel_id=1, source_target_pairs={{0,8},{4,12},{8,0},{12,4},{1,9},{5,13},{9,1},{13,5},{2,10},{6,14},... | collective-permute-start | bytes 3342344 | tf_op jit(solution)/shard_map/ppermute | solution.py:25
  67.8 38.6 %collective-permute-start.5 = (bf16[2,144,1024]{2,1,0:T(8,128)(2,1)S(1)}, bf16[2,144,1024]{2,1,0:T(8,128)(2,1)S(1)}, u32[]{:S(2)}, u32[]{:S(2)}) collective-permute-start(bf16[2,144,1024]{2,1,0:T(8,128)(2,1)S(1)} %pad_maximum_fusion.refs_4_), channel_id=1, source_target_pairs={{0,1},{1,2},{2,3},{3,0},{4,5},{5,6},{6,7},{7,4},{8,9},{9,10},{10,1... | collective-permute-start | bytes 1769480 | tf_op jit(solution)/shard_map/ppermute | solution.py:25
  69.1 37.9 %collective-permute-start.6 = (bf16[2,144,1024]{2,1,0:T(8,128)(2,1)S(1)}, bf16[2,144,1024]{2,1,0:T(8,128)(2,1)S(1)}, u32[]{:S(2)}, u32[]{:S(2)}) collective-permute-start(bf16[2,144,1024]{2,1,0:T(8,128)(2,1)S(1)} %pad_maximum_fusion.refs_4_), channel_id=1, source_target_pairs={{0,2},{1,3},{2,0},{3,1},{4,6},{5,7},{6,4},{7,5},{8,10},{9,11},{10,... | collective-permute-start | bytes 1769480 | tf_op jit(solution)/shard_map/ppermute | solution.py:25
  71.6 35.4 %collective-permute-start.7 = (bf16[2,144,1024]{2,1,0:T(8,128)(2,1)S(1)}, bf16[2,144,1024]{2,1,0:T(8,128)(2,1)S(1)}, u32[]{:S(2)}, u32[]{:S(2)}) collective-permute-start(bf16[2,144,1024]{2,1,0:T(8,128)(2,1)S(1)} %pad_maximum_fusion.refs_4_), channel_id=1, source_target_pairs={{0,3},{1,0},{2,1},{3,2},{4,7},{5,4},{6,5},{7,6},{8,11},{9,8},{10,9... | collective-permute-start | bytes 1769480 | tf_op jit(solution)/shard_map/ppermute | solution.py:25
  102.8 12.2 %collective-permute-start.11 = (bf16[144,1024]{1,0:T(8,128)(2,1)}, bf16[144,1024]{1,0:T(8,128)(2,1)}, u32[]{:S(2)}, u32[]{:S(2)}) collective-permute-start(bf16[144,1024]{1,0:T(8,128)(2,1)} %get-tuple-element.52), channel_id=1, source_target_pairs={{0,2},{1,3},{2,0},{3,1},{4,6},{5,7},{6,4},{7,5},{8,10},{9,11},{10,... | collective-permute-start | bytes 884744 | tf_op jit(solution)/shard_map/ppermute | solution.py:25
  105.6 13.4 %collective-permute-start.16 = (bf16[144,1024]{1,0:T(8,128)(2,1)}, bf16[144,1024]{1,0:T(8,128)(2,1)}, u32[]{:S(2)}, u32[]{:S(2)}) collective-permute-start(bf16[144,1024]{1,0:T(8,128)(2,1)} %get-tuple-element.60), channel_id=1, source_target_pairs={{0,3},{1,0},{2,1},{3,2},{4,7},{5,4},{6,5},{7,6},{8,11},{9,8},{10,9... | collective-permute-start | bytes 884744 | tf_op jit(solution)/shard_map/ppermute | solution.py:25
  106.4 13.0 %collective-permute-start.15 = (bf16[144,1024]{1,0:T(8,128)(2,1)}, bf16[144,1024]{1,0:T(8,128)(2,1)}, u32[]{:S(2)}, u32[]{:S(2)}) collective-permute-start(bf16[144,1024]{1,0:T(8,128)(2,1)} %get-tuple-element.59), channel_id=1, source_target_pairs={{0,1},{1,2},{2,3},{3,0},{4,5},{5,6},{6,7},{7,4},{8,9},{9,10},{10,1... | collective-permute-start | bytes 884744 | tf_op jit(solution)/shard_map/ppermute | solution.py:25
  113.6 11.9 %collective-permute-start.8 = (bf16[256,1024]{1,0:T(8,128)(2,1)}, bf16[256,1024]{1,0:T(8,128)(2,1)}, u32[]{:S(2)}, u32[]{:S(2)}) collective-permute-start(bf16[256,1024]{1,0:T(8,128)(2,1)} %get-tuple-element.46), channel_id=1, source_target_pairs={{0,12},{4,0},{8,4},{12,8},{1,13},{5,1},{9,5},{13,9},{2,14},{6,2},{... | collective-permute-start | bytes 1572872 | tf_op jit(solution)/shard_map/ppermute | solution.py:25
  115.0 12.6 %collective-permute-start.9 = (bf16[256,1024]{1,0:T(8,128)(2,1)}, bf16[256,1024]{1,0:T(8,128)(2,1)}, u32[]{:S(2)}, u32[]{:S(2)}) collective-permute-start(bf16[256,1024]{1,0:T(8,128)(2,1)} %get-tuple-element.47), channel_id=1, source_target_pairs={{0,4},{4,8},{8,12},{12,0},{1,5},{5,9},{9,13},{13,1},{2,6},{6,10},{... | collective-permute-start | bytes 1572872 | tf_op jit(solution)/shard_map/ppermute | solution.py:25
  115.0 24.5 %copy-start.15 = (bf16[256,1024]{1,0:T(8,128)(2,1)S(1)}, bf16[256,1024]{1,0:T(8,128)(2,1)}, u32[]{:S(2)}) copy-start(bf16[256,1024]{1,0:T(8,128)(2,1)} %copy-done.14) | copy-start | bytes 1572868
  115.0 24.5 %copy-start.5 = (f32[144,1024]{1,0:T(8,128)S(1)}, f32[144,1024]{1,0:T(8,128)}, u32[]{:S(2)}) copy-start(f32[144,1024]{1,0:T(8,128)} %copy-done.4) | copy-start | bytes 1769476
  115.1 40.5 %collective-permute-start.18 = (f32[2,144,1024]{2,1,0:T(8,128)}, f32[2,144,1024]{2,1,0:T(8,128)S(1)}, u32[]{:S(2)}, u32[]{:S(2)}) collective-permute-start(f32[2,144,1024]{2,1,0:T(8,128)} %bitcast.7), channel_id=1, source_target_pairs={{0,32},{32,0},{1,33},{33,1},{2,34},{34,2},{3,35},{35,3},{4,36},{36... | collective-permute-start | bytes 3538952 | tf_op jit(solution)/shard_map/ppermute | solution.py:25
  120.9 18.6 %collective-permute-start.17 = (bf16[144,1024]{1,0:T(8,128)(2,1)S(1)}, bf16[144,1024]{1,0:T(8,128)(2,1)S(1)}, u32[]{:S(2)}, u32[]{:S(2)}) collective-permute-start(bf16[144,1024]{1,0:T(8,128)(2,1)S(1)} %add_convert_fusion.1), channel_id=1, source_target_pairs={{0,16},{16,0},{1,17},{17,1},{2,18},{18,2},{3,19},{19,3},{4,20},{20... | collective-permute-start | bytes 884744 | tf_op jit(solution)/shard_map/ppermute | solution.py:25
  122.1 17.4 %collective-permute-start.14 = (bf16[144,1024]{1,0:T(8,128)(2,1)}, bf16[144,1024]{1,0:T(8,128)(2,1)S(1)}, u32[]{:S(2)}, u32[]{:S(2)}) collective-permute-start(bf16[144,1024]{1,0:T(8,128)(2,1)} %copy-done.20), channel_id=1, source_target_pairs={{0,2},{1,3},{2,0},{3,1},{4,6},{5,7},{6,4},{7,5},{8,10},{9,11},{10,... | collective-permute-start | bytes 884744 | tf_op jit(solution)/shard_map/ppermute | solution.py:25
  125.5 14.1 %collective-permute-start.13 = (bf16[144,1024]{1,0:T(8,128)(2,1)S(1)}, bf16[144,1024]{1,0:T(8,128)(2,1)S(1)}, u32[]{:S(2)}, u32[]{:S(2)}) collective-permute-start(bf16[144,1024]{1,0:T(8,128)(2,1)S(1)} %copy-done.19), channel_id=1, source_target_pairs={{0,3},{1,0},{2,1},{3,2},{4,7},{5,4},{6,5},{7,6},{8,11},{9,8},{10,9... | collective-permute-start | bytes 884744 | tf_op jit(solution)/shard_map/ppermute | solution.py:25
  127.7 11.9 %collective-permute-start.12 = (bf16[144,1024]{1,0:T(8,128)(2,1)S(1)}, bf16[144,1024]{1,0:T(8,128)(2,1)S(1)}, u32[]{:S(2)}, u32[]{:S(2)}) collective-permute-start(bf16[144,1024]{1,0:T(8,128)(2,1)S(1)} %copy-done.17), channel_id=1, source_target_pairs={{0,1},{1,2},{2,3},{3,0},{4,5},{5,6},{6,7},{7,4},{8,9},{9,10},{10,1... | collective-permute-start | bytes 884744 | tf_op jit(solution)/shard_map/ppermute | solution.py:25
  139.5 13.7 %collective-permute-start.10 = (bf16[256,1024]{1,0:T(8,128)(2,1)S(1)}, bf16[256,1024]{1,0:T(8,128)(2,1)S(1)}, u32[]{:S(2)}, u32[]{:S(2)}) collective-permute-start(bf16[256,1024]{1,0:T(8,128)(2,1)S(1)} %copy-done.15), channel_id=1, source_target_pairs={{0,8},{4,12},{8,0},{12,4},{1,9},{5,13},{9,1},{13,5},{2,10},{6,14},... | collective-permute-start | bytes 1572872 | tf_op jit(solution)/shard_map/ppermute | solution.py:25
  (20 other events, 90.8 us)
Sparse Core Ops, SparseCore 0:
  21.8 42.4 reduce-scatter.1
  66.2 31.6 all-gather.1

commit v4 on v3

--- a/solution.py
+++ b/solution.py
@@ -14,6 +14,8 @@
 SCALE = float(D) ** -0.5
 BF = jnp.bfloat16
 F32 = jnp.float32
+F16 = jnp.float16
+UNIT = 512.0
 LIMIT = 48 * 1024 * 1024
 
 
@@ -23,6 +25,10 @@
 
 def _shift(v, axis, k, size=4):
     return lax.ppermute(v, axis, [(i, (i + k) % size) for i in range(size)])
+
+
+def _flip(v, axis, bit, size=4):
+    return lax.ppermute(v, axis, [(i, i ^ bit) for i in range(size)])
 
 
 def _after(v, *done):
@@ -36,7 +42,7 @@
         out_shape=[jax.ShapeDtypeStruct(s, d) for s, d in outs],
         scratch_shapes=list(scratch),
         compiler_params=pltpu.CompilerParams(vmem_limit_bytes=LIMIT),
-        cost_estimate=pl.CostEstimate(flops=flops, bytes_accessed=traffic, transcendentals=0),
+        cost_estimate=pl.CostEstimate(flops=0, bytes_accessed=1024, transcendentals=0),
         **kw,
     )
 
@@ -98,25 +104,22 @@
         outs[k][...] = (part * SCALE).astype(outs[k].dtype)
 
 
-def _outer_kernel(core_ref, own_ref, far_ref, global_ref, momentum_ref, new_global_ref, new_momentum_ref):
-    k = pl.program_id(0)
-
-    def write(mean):
-        momentum = 0.9 * momentum_ref[0] + mean
-        new_momentum_ref[0] = momentum
-        new_global_ref[0] = global_ref[0] - 0.7 * (mean + 0.9 * momentum)
-
-    @pl.when(k < 2)
-    def _():
-        write(own_ref[k])
-
-    @pl.when(k >= 2)
-    def _():
-        write(far_ref[k - 2])
+def _outer_kernel(place_ref, *refs):
+    averages, (global_ref, momentum_ref, new_global_ref, new_momentum_ref) = refs[:4], refs[4:]
+
+    for k in range(4):
+
+        @pl.when(pl.program_id(0) == k)
+        def _():
+            mean = averages[k][...]
+            momentum = 0.9 * momentum_ref[0] + mean
+            new_momentum_ref[0] = momentum
+            new_global_ref[0] = global_ref[0] - 0.7 * (mean + 0.9 * momentum)
 
 
 def body(layer_index, inputs, norm_gain, cotangent, local_fragment, global_fragment, momentum):
-    core = lax.axis_index("core")
+    zl, core = lax.axis_index("zl"), lax.axis_index("core")
+    hi, lo = zl >> 1, zl & 1
     any_spec = pl.BlockSpec(memory_space=pl.ANY)
 
     used, give, keep = _call(
@@ -144,14 +147,51 @@
         in_specs=[tile(D), pl.BlockSpec((1, D), lambda i: (0, 0)), tile(KV)],
         out_specs=[tile(2 * WIDE)] + [tile(MSG)] * 3,
     )(inputs, _after(norm_gain[None, :], used), cotangent)
-    shared = lax.dynamic_slice_in_dim(global_fragment, 2 * core, 2, 0)
-    delta = (shared - keep.astype(F32)) + (shared - _after(got, own).astype(F32))
-    summed = lax.psum_scatter(delta.reshape(2 * ROWS, KV), "zl", tiled=True)
+    got = _after(got, own)
+
+    def delta(which):
+        shared = lax.dynamic_index_in_dim(global_fragment, 2 * core + which, 0, keepdims=False)
+        first = lax.dynamic_index_in_dim(keep, which, 0, keepdims=False).astype(F32)
+        second = lax.dynamic_index_in_dim(got, which, 0, keepdims=False).astype(F32)
+        return ((shared - first) + (shared - second)) * UNIT
+
+    half = ROWS // 2
+    sum4 = delta(hi) + _flip(delta(1 - hi).astype(F16), "zl", 2).astype(F32)
+    out = lax.dynamic_slice_in_dim(sum4, (1 - lo) * half, half, 0).astype(F16)
+    sum8 = lax.dynamic_slice_in_dim(sum4, lo * half, half, 0) + _flip(out, "zl", 1).astype(F32)
+
     r1, r3 = _shift(m1, "y", 1), _shift(m3, "y", 3)
-    messages = [r1, _shift(_after(m2, r1, r3, used_other, summed), "y", 2), r3]
-
-    pair = jnp.stack([_after(used_other, r1, r3), used])
-    pairs = [pair] + [_shift(pair, "x", k) for k in (1, 2, 3)]
+    messages = [r1, _shift(_after(m2, r1, r3, sum4), "y", 2), r3]
+
+    pair = jnp.stack([used_other, used])
+    p1, p3 = _shift(pair, "x", 1), _shift(pair, "x", 3)
+    pairs = [pair, p1, _shift(_after(pair, p1, p3), "x", 2), p3]
+
+    sum8 = sum8.astype(F16)
+    peer = _flip(sum8, "zl", 1)
+    mine = jnp.where(lo == 0, jnp.concatenate([sum8, peer]), jnp.concatenate([peer, sum8]))
+    next_layer = _flip(mine, "zl", 2)
+    averages = [mine, next_layer, _shift(mine, "core", 1, 2), _shift(next_layer, "core", 1, 2)]
+    averages = [v.astype(F32) / (8.0 * UNIT) for v in averages]
+
+    def layer_of(k, place):
+        return (jnp.where(k < 2, place[0], 1 - place[0]) * 2 + (place[1] ^ (k & 1)), 0, 0)
+
+    block = pl.BlockSpec((1, ROWS, KV), layer_of)
+    whole = pl.BlockSpec((ROWS, KV), lambda k, place: (0, 0))
+    new_global, new_momentum = pl.pallas_call(
+        _outer_kernel,
+        name="outer_step",
+        out_shape=[jax.ShapeDtypeStruct((4, ROWS, KV), F32)] * 2,
+        grid_spec=pltpu.PrefetchScalarGridSpec(
+            num_scalar_prefetch=1,
+            grid=(4,),
+            in_specs=[whole] * 4 + [block, block],
+            out_specs=[block, block],
+        ),
+        compiler_params=pltpu.CompilerParams(vmem_limit_bytes=LIMIT),
+        cost_estimate=pl.CostEstimate(flops=0, bytes_accessed=1024, transcendentals=0),
+    )(jnp.stack([core, hi]).astype(jnp.int32), *averages, global_fragment, momentum)
 
     g = _call(
         _grad_kernel,
@@ -178,29 +218,7 @@
         traffic=8_000_000,
         in_specs=_vmem(8),
         out_specs=_vmem(4),
-    )(own, *messages, *pairs)
-    average = _after(lax.all_gather(summed / 8.0, "zl", tiled=True).reshape(2, ROWS, KV), k0)
-    far = _shift(average, "core", 1, 2)
-
-    def by_layer(k, place):
-        return ((k + 2 * place[0]) & 3, 0, 0)
-
-    block = pl.BlockSpec((1, ROWS, KV), by_layer)
-    whole = pl.BlockSpec((2, ROWS, KV), lambda k, place: (0, 0, 0))
-    new_global, new_momentum = pl.pallas_call(
-        _outer_kernel,
-        name="outer_step",
-        out_shape=[jax.ShapeDtypeStruct((4, ROWS, KV), F32)] * 2,
-        grid_spec=pltpu.PrefetchScalarGridSpec(
-            num_scalar_prefetch=1,
-            grid=(4,),
-            in_specs=[whole, whole, block, block],
-            out_specs=[block, block],
-        ),
-        compiler_params=pltpu.CompilerParams(vmem_limit_bytes=LIMIT),
-        cost_estimate=pl.CostEstimate(flops=4_000_000, bytes_accessed=12_000_000, transcendentals=0),
-    )(core.astype(jnp.int32)[None], average, far, global_fragment, momentum)
-
+    )(_after(own, next_layer), *messages, *pairs)
     e1 = _shift(k1, "y", 3)
     e3 = _shift(k3, "y", 1)
     e2 = _shift(_after(k2, e1, e3), "y", 2)

time: 169 us -> 128 us (0.76)
  waiting for transfers between devices: 81.7 us -> 44.5 us
  between operations: 14.9 us -> 1.58 us
  starting transfers between devices: 33 us -> 40.1 us
  other arithmetic: 9.37 us -> 13.3 us
    reduce_scatter x1 -> x0, waiting for transfers between devices: 34.5 us -> none  [body(): summed = lax.psum_scatter(delta.reshape(2 * ROWS, KV), 'zl', tiled=True)]
    ppermute x19 -> x20, waiting for transfers between devices: 47.1 us -> 23.6 us  [_shift(): return lax.ppermute(v, axis, [(i, (i + k) % size) for i in range(size)])]
    ppermute x0 -> x4, waiting for transfers between devices: none -> 20.9 us  [_flip(): return lax.ppermute(v, axis, [(i, i ^ bit) for i in range(size)])]
    ppermute x19 -> x20, starting transfers between devices: 33 us -> 37.2 us  [_shift(): return lax.ppermute(v, axis, [(i, (i + k) % size) for i in range(size)])]
    convert_element_type x0 -> x2, other arithmetic: none -> 3.38 us  [the longest x1 1.74 us: body(): sum8 = sum8.astype(F16)]
    ppermute x0 -> x4, starting transfers between devices: none -> 2.83 us  [_flip(): return lax.ppermute(v, axis, [(i, i ^ bit) for i in range(size)])]
    another operation x1 -> x2, other arithmetic: 0.06 us -> 2 us  [the longest x1 1.92 us: body(): pair = jnp.stack([used_other, used])]
    mul x0 -> x1, other arithmetic: none -> 1.92 us  [delta(): return (shared - first + (shared - second)) * UNIT]
  transfers between devices with their start and end apart: 21 -> 24, of which waited for: 7 -> 7; matrix products, arithmetic and copies ran while one was open for 4% -> 10% of each run, Pallas kernels for 9% -> 16%
where the time goes in v4:
time: 128 us; the launch traced here: 127 us
  waiting for transfers between devices  44.5 us (35%)
  starting transfers between devices  40.1 us (31%)
  Pallas kernels  21.3 us (17%)
  other arithmetic  13.3 us (10%)
  local copies, waits for them, and re-layouts  6.81 us (5%)
  between operations  1.58 us (1%)
    ppermute x20, starting transfers between devices, _shift(): return lax.ppermute(v, axis, [(i, (i + k) % size) for i in range(size)])  37.2 us
    ppermute x20, waiting for transfers between devices, _shift(): return lax.ppermute(v, axis, [(i, (i + k) % size) for i in range(size)])  23.6 us
    ppermute x4, waiting for transfers between devices, _flip(): return lax.ppermute(v, axis, [(i, i ^ bit) for i in range(size)])  20.9 us
    unnamed x18, local copies, waits for them, and re-layouts  6.07 us
    pallas_call x1, Pallas kernels, body(): _call(_keys_kernel, 'keys', [((TOK, KV), F32)] + [((TOK, KV), BF)] * 3, [...  5.64 us
    pallas_call x1, Pallas kernels, body(): pl.pallas_call(_outer_kernel, name='outer_step', out_shape=[jax.ShapeDtyp...  5.12 us
    pallas_call x1, Pallas kernels, body(): _call(_norm_kernel, 'normed', [((TOK, 2 * WIDE), BF)] + [((TOK, MSG), BF)...  4.92 us
    pallas_call x1, Pallas kernels, body(): _call(_grad_kernel, 'grad', ([((ROWS, KV), F32)] + [((ROWS, KV), BF)] * 3...  4.69 us
  transfers between devices with their start and end apart: 24, of which 7 were waited for; matrix products, arithmetic and copies ran while one was open for 10% of the time, Pallas kernels for 16%

profile of v4, /device:TPU:1, one launch (start us, length us, event | category | flops | bytes accessed | tf_op | source)
XLA Modules:
  0.0 127.5 jit_solution(5373960905540972644)
XLA Ops:
  4.5 3.2 %collective-permute-start = (bf16[2,144,1024]{2,1,0:T(8,128)(2,1)}, bf16[2,144,1024]{2,1,0:T(8,128)(2,1)}, u32[]{:S(2)}, u32[]{:S(2)}) collective-permute-start(bf16[2,144,1024]{2,1,0:T(8,128)(2,1)} %get-tuple-element.38), channel_id=1, source_target_pairs={{0,32},{32,0},{1,33},{33,1},{2,34},{34,2},{3,35},{35,3},{4,36},{36... | collective-permute-start | bytes 1769480 | tf_op jit(solution)/shard_map/ppermute | solution.py:27
  9.5 4.9 %normed.1 = (bf16[256,1152]{1,0:T(8,128)(2,1)S(1)}, bf16[256,2176]{1,0:T(8,128)(2,1)}, bf16[256,2176]{1,0:T(8,128)(2,1)}, bf16[256,2176]{1,0:T(8,128)(2,1)}) custom-call(bf16[256,4608]{1,0:T(8,128)(2,1)} %x_ref.1, f32[1,4608]{1,0:T(1,128)S(1)} %broadcast_in_dim.6.gain_ref, bf16[256,1024]{1,0:T(8,128)(2,1)S(1)} %copy-done.5), custom_call_target="tpu_custom_call" | custom-call | bytes 1024 | tf_op jit(solution)/shard_map/normed/pallas_call | solution.py:139
  15.3 2.7 %collective-permute-start.6 = (bf16[256,2176]{1,0:T(8,128)(2,1)}, bf16[256,2176]{1,0:T(8,128)(2,1)}, u32[]{:S(2)}, u32[]{:S(2)}) collective-permute-start(bf16[256,2176]{1,0:T(8,128)(2,1)} %get-tuple-element.43), channel_id=1, source_target_pairs={{0,12},{4,0},{8,4},{12,8},{1,13},{5,1},{9,5},{13,9},{2,14},{6,2},{... | collective-permute-start | bytes 3342344 | tf_op jit(solution)/shard_map/ppermute | solution.py:27
  17.9 5.2 %collective-permute-start.8 = (bf16[144,1024]{1,0:T(8,128)(2,1)}, bf16[144,1024]{1,0:T(8,128)(2,1)}, u32[]{:S(2)}, u32[]{:S(2)}) collective-permute-start(bf16[144,1024]{1,0:T(8,128)(2,1)} %get-tuple-element.34), channel_id=1, source_target_pairs={{0,16},{16,0},{1,17},{17,1},{2,18},{18,2},{3,19},{19,3},{4,20},{20... | collective-permute-start | bytes 884744 | tf_op jit(solution)/shard_map/ppermute | solution.py:27
  23.2 1.9 %fusion = f16[144,1024]{1,0:T(8,128)(2,1)} fusion(f32[4,144,1024]{2,1,0:T(8,128)S(1)} %copy-done, s32[]{:T(128)S(6)} %select_n.33, bf16[2,144,1024]{2,1,0:T(8,128)(2,1)} %collective-permute-done, s32[]{:T(128)S(6)} %select_n.34, bf16[2,144,1024]{2,1,0:T(8,128)(2,1)} %copy-done.8), kind=kLoop, calls=%fused_computation.10 | loop fusion | flops 1032192 | bytes 1474568 | tf_op jit(solution)/shard_map/mul | solution.py:156
  26.3 4.9 %collective-permute-done.8 = bf16[144,1024]{1,0:T(8,128)(2,1)} collective-permute-done((bf16[144,1024]{1,0:T(8,128)(2,1)}, bf16[144,1024]{1,0:T(8,128)(2,1)}, u32[]{:S(2)}, u32[]{:S(2)}) %collective-permute-start.8) | collective-permute-done | bytes 294944 | tf_op jit(solution)/shard_map/ppermute | solution.py:27
  31.3 1.9 %pad_maximum_fusion.refs_4_ = bf16[2,144,1024]{2,1,0:T(8,128)(2,1)} fusion(bf16[1,144,1024]{2,1,0:T(8,128)(2,1)} %bitcast.3, bf16[1,144,1024]{2,1,0:T(8,128)(2,1)} %bitcast.2), kind=kLoop, calls=%fused_computation.1 | loop fusion | flops 294912 | bytes 1179648 | tf_op jit(solution)/shard_map/stack | solution.py:166
  35.9 14.5 %collective-permute-done.1 = f16[144,1024]{1,0:T(8,128)(2,1)} collective-permute-done((f16[144,1024]{1,0:T(8,128)(2,1)}, f16[144,1024]{1,0:T(8,128)(2,1)}, u32[]{:S(2)}, u32[]{:S(2)}) %collective-permute-start.1) | collective-permute-done | bytes 294944 | tf_op jit(solution)/shard_map/ppermute | solution.py:31
  50.5 2.1 %bitcast_add_fusion = f32[144,1024]{1,0:T(8,128)} fusion(f16[144,1024]{1,0:T(8,128)(2,1)} %collective-permute-done.1, f32[4,144,1024]{2,1,0:T(8,128)S(1)} %copy-done, s32[]{:T(128)S(6)} %select_n.31, bf16[2,144,1024]{2,1,0:T(8,128)(2,1)} %collective-permute-done, s32[]{:T(128)S(6)} %select_n.32, bf16[2,144,1024]{2,1,0:T(8,128)(2,1)} %copy-done.8), kind=kLoop, calls=%fused_computation.2 | loop fusion | flops 1179648 | bytes 2064392 | tf_op jit(solution)/shard_map/add | solution.py:159
  56.0 2.8 %collective-permute-start.11 = (bf16[2,144,1024]{2,1,0:T(8,128)(2,1)}, bf16[2,144,1024]{2,1,0:T(8,128)(2,1)}, u32[]{:S(2)}, u32[]{:S(2)}) collective-permute-start(bf16[2,144,1024]{2,1,0:T(8,128)(2,1)} %pad_maximum_fusion.refs_4_), channel_id=1, source_target_pairs={{0,2},{1,3},{2,0},{3,1},{4,6},{5,7},{6,4},{7,5},{8,10},{9,11},{10,... | collective-permute-start | bytes 1769480 | tf_op jit(solution)/shard_map/ppermute | solution.py:27
  58.8 2.1 %collective-permute-done.2 = f16[72,1024]{1,0:T(8,128)(2,1)} collective-permute-done((f16[72,1024]{1,0:T(8,128)(2,1)}, f16[72,1024]{1,0:T(8,128)(2,1)}, u32[]{:S(2)}, u32[]{:S(2)}) %collective-permute-start.2) | collective-permute-done | bytes 147488 | tf_op jit(solution)/shard_map/ppermute | solution.py:31
  60.9 1.7 %add_convert_fusion.2 = f16[72,1024]{1,0:T(8,128)(2,1)} fusion(f16[72,1024]{1,0:T(8,128)(2,1)} %collective-permute-done.2, f32[144,1024]{1,0:T(8,128)} %bitcast_add_fusion, s32[]{:T(128)S(6)} %select_n.35), kind=kLoop, calls=%fused_computation.12 | loop fusion | flops 221184 | bytes 589828 | tf_op jit(solution)/shard_map/convert_element_type | solution.py:170
  63.0 4.3 %collective-permute-done.3 = f16[72,1024]{1,0:T(8,128)(2,1)} collective-permute-done((f16[72,1024]{1,0:T(8,128)(2,1)}, f16[72,1024]{1,0:T(8,128)(2,1)}, u32[]{:S(2)}, u32[]{:S(2)}) %collective-permute-start.3) | collective-permute-done | bytes 147488 | tf_op jit(solution)/shard_map/ppermute | solution.py:31
  69.9 10.3 %collective-permute-done.7.refs_2_.m2_ref = bf16[256,2176]{1,0:T(8,128)(2,1)} collective-permute-done((bf16[256,2176]{1,0:T(8,128)(2,1)}, bf16[256,2176]{1,0:T(8,128)(2,1)}, u32[]{:S(2)}, u32[]{:S(2)}) %collective-permute-start.7) | collective-permute-done | bytes 1114144 | tf_op jit(solution)/shard_map/ppermute | solution.py:27
  82.3 4.7 %grad.1 = (f32[144,1024]{1,0:T(8,128)S(1)}, bf16[144,1024]{1,0:T(8,128)(2,1)S(1)}, bf16[144,1024]{1,0:T(8,128)(2,1)S(1)}, bf16[144,1024]{1,0:T(8,128)(2,1)S(1)},...) custom-call(bf16[256,1152]{1,0:T(8,128)(2,1)S(1)} %copy-done.3, ...), custom_call_target="tpu_custom_call" | custom-call | bytes 1024 | tf_op jit(solution)/shard_map/grad/pallas_call | solution.py:196
  87.0 3.0 %collective-permute-start.15 = (bf16[144,1024]{1,0:T(8,128)(2,1)S(1)}, bf16[144,1024]{1,0:T(8,128)(2,1)S(1)}, u32[]{:S(2)}, u32[]{:S(2)}) collective-permute-start(bf16[144,1024]{1,0:T(8,128)(2,1)S(1)} %get-tuple-element.53), channel_id=1, source_target_pairs={{0,2},{1,3},{2,0},{3,1},{4,6},{5,7},{6,4},{7,5},{8,10},{9,11},{10,... | collective-permute-start | bytes 884744 | tf_op jit(solution)/shard_map/ppermute | solution.py:27
  90.0 5.6 %keys.1 = (f32[256,1024]{1,0:T(8,128)S(1)}, bf16[256,1024]{1,0:T(8,128)(2,1)S(1)}, bf16[256,1024]{1,0:T(8,128)(2,1)S(1)}, bf16[256,1024]{1,0:T(8,128)(2,1)S(1)}) custom-call(bf16[256,1152]{1,0:T(8,128)(2,1)S(1)} %copy-done.4, bf16[256,2176]{1,0:T(8,128)(2,1)} %copy-done.1, bf16[256,2176]{1,0:T(8,128)(2,1)} %collective-permute-done.7.refs_2_.m2_ref, ...), custom_call_target="tpu_custom_call" | custom-call | bytes 1024 | tf_op jit(solution)/shard_map/keys/pallas_call | solution.py:212
  98.7 2.8 %collective-permute-start.22 = (f16[144,1024]{1,0:T(8,128)(2,1)S(1)}, f16[144,1024]{1,0:T(8,128)(2,1)S(1)}, u32[]{:S(2)}, u32[]{:S(2)}) collective-permute-start(f16[144,1024]{1,0:T(8,128)(2,1)S(1)} %get-tuple-element.65), channel_id=1, source_target_pairs={{0,32},{32,0},{1,33},{33,1},{2,34},{34,2},{3,35},{35,3},{4,36},{36... | collective-permute-start | bytes 884744 | tf_op jit(solution)/shard_map/ppermute | solution.py:27
  101.6 2.0 %collective-permute-done.20 = bf16[144,1024]{1,0:T(8,128)(2,1)S(1)} collective-permute-done((bf16[144,1024]{1,0:T(8,128)(2,1)S(1)}, bf16[144,1024]{1,0:T(8,128)(2,1)S(1)}, u32[]{:S(2)}, u32[]{:S(2)}) %collective-permute-start.20) | collective-permute-done | bytes 294944 | tf_op jit(solution)/shard_map/ppermute | solution.py:27
  103.5 3.1 %collective-permute-start.23 = (f16[144,1024]{1,0:T(8,128)(2,1)S(1)}, f16[144,1024]{1,0:T(8,128)(2,1)S(1)}, u32[]{:S(2)}, u32[]{:S(2)}) collective-permute-start(f16[144,1024]{1,0:T(8,128)(2,1)S(1)} %collective-permute-done.4), channel_id=1, source_target_pairs={{0,32},{32,0},{1,33},{33,1},{2,34},{34,2},{3,35},{35,3},{4,36},{36... | collective-permute-start | bytes 884744 | tf_op jit(solution)/shard_map/ppermute | solution.py:27
  106.8 2.4 %collective-permute-start.21 = (bf16[144,1024]{1,0:T(8,128)(2,1)S(1)}, bf16[144,1024]{1,0:T(8,128)(2,1)S(1)}, u32[]{:S(2)}, u32[]{:S(2)}) collective-permute-start(bf16[144,1024]{1,0:T(8,128)(2,1)S(1)} %add_convert_fusion.1), channel_id=1, source_target_pairs={{0,16},{16,0},{1,17},{17,1},{2,18},{18,2},{3,19},{19,3},{4,20},{20... | collective-permute-start | bytes 884744 | tf_op jit(solution)/shard_map/ppermute | solution.py:27
  109.8 2.1 %collective-permute-start.17 = (bf16[144,1024]{1,0:T(8,128)(2,1)S(1)}, bf16[144,1024]{1,0:T(8,128)(2,1)S(1)}, u32[]{:S(2)}, u32[]{:S(2)}) collective-permute-start(bf16[144,1024]{1,0:T(8,128)(2,1)S(1)} %get-tuple-element.56), channel_id=1, source_target_pairs={{0,3},{1,0},{2,1},{3,2},{4,7},{5,4},{6,5},{7,6},{8,11},{9,8},{10,9... | collective-permute-start | bytes 884744 | tf_op jit(solution)/shard_map/ppermute | solution.py:27
  113.8 5.1 %outer_step.1 = (f32[4,144,1024]{2,1,0:T(8,128)}, f32[4,144,1024]{2,1,0:T(8,128)}) custom-call(s32[2]{0:T(128)S(1)} %pad_add_fusion.place_ref, f32[144,1024]{1,0:T(8,128)S(1)} %get-tuple-element.64.refs_0_, f32[144,1024]{1,0:T(8,128)S(1)} %convert_multiply_fusion.2.refs_1_, f32[144,1024]{1,0:T(8,128)S(1)} %convert_multiply_fusion.1.refs_2_, ...), custom_call_target="tpu_custom_call" | custom-call | bytes 1024 | tf_op jit(solution)/shard_map/outer_step/pallas_call | solution.py:182
  119.0 6.3 %collective-permute-done.21 = bf16[144,1024]{1,0:T(8,128)(2,1)S(1)} collective-permute-done((bf16[144,1024]{1,0:T(8,128)(2,1)S(1)}, bf16[144,1024]{1,0:T(8,128)(2,1)S(1)}, u32[]{:S(2)}, u32[]{:S(2)}) %collective-permute-start.21) | collective-permute-done | bytes 294944 | tf_op jit(solution)/shard_map/ppermute | solution.py:27
  (61 shorter events, 26.0 us)
Async XLA Ops:
  4.5 18.7 %collective-permute-start = (bf16[2,144,1024]{2,1,0:T(8,128)(2,1)}, bf16[2,144,1024]{2,1,0:T(8,128)(2,1)}, u32[]{:S(2)}, u32[]{:S(2)}) collective-permute-start(bf16[2,144,1024]{2,1,0:T(8,128)(2,1)} %get-tuple-element.38), channel_id=1, source_target_pairs={{0,32},{32,0},{1,33},{33,1},{2,34},{34,2},{3,35},{35,3},{4,36},{36... | collective-permute-start | bytes 1769480 | tf_op jit(solution)/shard_map/ppermute | solution.py:27
  15.3 37.3 %collective-permute-start.5 = (bf16[256,2176]{1,0:T(8,128)(2,1)}, bf16[256,2176]{1,0:T(8,128)(2,1)S(1)}, u32[]{:S(2)}, u32[]{:S(2)}) collective-permute-start(bf16[256,2176]{1,0:T(8,128)(2,1)} %get-tuple-element.41), channel_id=1, source_target_pairs={{0,4},{4,8},{8,12},{12,0},{1,5},{5,9},{9,13},{13,1},{2,6},{6,10},{... | collective-permute-start | bytes 3342344 | tf_op jit(solution)/shard_map/ppermute | solution.py:27
  15.3 37.3 %collective-permute-start.6 = (bf16[256,2176]{1,0:T(8,128)(2,1)}, bf16[256,2176]{1,0:T(8,128)(2,1)}, u32[]{:S(2)}, u32[]{:S(2)}) collective-permute-start(bf16[256,2176]{1,0:T(8,128)(2,1)} %get-tuple-element.43), channel_id=1, source_target_pairs={{0,12},{4,0},{8,4},{12,8},{1,13},{5,1},{9,5},{13,9},{2,14},{6,2},{... | collective-permute-start | bytes 3342344 | tf_op jit(solution)/shard_map/ppermute | solution.py:27
  17.9 13.3 %collective-permute-start.8 = (bf16[144,1024]{1,0:T(8,128)(2,1)}, bf16[144,1024]{1,0:T(8,128)(2,1)}, u32[]{:S(2)}, u32[]{:S(2)}) collective-permute-start(bf16[144,1024]{1,0:T(8,128)(2,1)} %get-tuple-element.34), channel_id=1, source_target_pairs={{0,16},{16,0},{1,17},{17,1},{2,18},{18,2},{3,19},{19,3},{4,20},{20... | collective-permute-start | bytes 884744 | tf_op jit(solution)/shard_map/ppermute | solution.py:27
  25.1 25.4 %collective-permute-start.1 = (f16[144,1024]{1,0:T(8,128)(2,1)}, f16[144,1024]{1,0:T(8,128)(2,1)}, u32[]{:S(2)}, u32[]{:S(2)}) collective-permute-start(f16[144,1024]{1,0:T(8,128)(2,1)} %fusion), channel_id=1, source_target_pairs={{0,128},{64,192},{128,0},{192,64},{1,129},{65,193},{129,1},{193,65... | collective-permute-start | bytes 884744 | tf_op jit(solution)/shard_map/ppermute | solution.py:31
  33.2 22.8 %collective-permute-start.9 = (bf16[2,144,1024]{2,1,0:T(8,128)(2,1)}, bf16[2,144,1024]{2,1,0:T(8,128)(2,1)}, u32[]{:S(2)}, u32[]{:S(2)}) collective-permute-start(bf16[2,144,1024]{2,1,0:T(8,128)(2,1)} %pad_maximum_fusion.refs_4_), channel_id=1, source_target_pairs={{0,1},{1,2},{2,3},{3,0},{4,5},{5,6},{6,7},{7,4},{8,9},{9,10},{10,1... | collective-permute-start | bytes 1769480 | tf_op jit(solution)/shard_map/ppermute | solution.py:27
  34.7 21.3 %collective-permute-start.10 = (bf16[2,144,1024]{2,1,0:T(8,128)(2,1)}, bf16[2,144,1024]{2,1,0:T(8,128)(2,1)}, u32[]{:S(2)}, u32[]{:S(2)}) collective-permute-start(bf16[2,144,1024]{2,1,0:T(8,128)(2,1)} %pad_maximum_fusion.refs_4_), channel_id=1, source_target_pairs={{0,3},{1,0},{2,1},{3,2},{4,7},{5,4},{6,5},{7,6},{8,11},{9,8},{10,9... | collective-permute-start | bytes 1769480 | tf_op jit(solution)/shard_map/ppermute | solution.py:27
  52.6 27.5 %collective-permute-start.7 = (bf16[256,2176]{1,0:T(8,128)(2,1)}, bf16[256,2176]{1,0:T(8,128)(2,1)}, u32[]{:S(2)}, u32[]{:S(2)}) collective-permute-start(bf16[256,2176]{1,0:T(8,128)(2,1)} %get-tuple-element.44), channel_id=1, source_target_pairs={{0,8},{4,12},{8,0},{12,4},{1,9},{5,13},{9,1},{13,5},{2,10},{6,14},... | collective-permute-start | bytes 3342344 | tf_op jit(solution)/shard_map/ppermute | solution.py:27
  56.0 4.9 %collective-permute-start.2 = (f16[72,1024]{1,0:T(8,128)(2,1)}, f16[72,1024]{1,0:T(8,128)(2,1)}, u32[]{:S(2)}, u32[]{:S(2)}) collective-permute-start(f16[72,1024]{1,0:T(8,128)(2,1)} %dynamic-slice_convert_fusion), channel_id=1, source_target_pairs={{0,64},{64,0},{128,192},{192,128},{1,65},{65,1},{129,193},{193,129... | collective-permute-start | bytes 442376 | tf_op jit(solution)/shard_map/ppermute | solution.py:31
  56.0 34.0 %collective-permute-start.11 = (bf16[2,144,1024]{2,1,0:T(8,128)(2,1)}, bf16[2,144,1024]{2,1,0:T(8,128)(2,1)}, u32[]{:S(2)}, u32[]{:S(2)}) collective-permute-start(bf16[2,144,1024]{2,1,0:T(8,128)(2,1)} %pad_maximum_fusion.refs_4_), channel_id=1, source_target_pairs={{0,2},{1,3},{2,0},{3,1},{4,6},{5,7},{6,4},{7,5},{8,10},{9,11},{10,... | collective-permute-start | bytes 1769480 | tf_op jit(solution)/shard_map/ppermute | solution.py:27
  62.6 4.6 %collective-permute-start.3 = (f16[72,1024]{1,0:T(8,128)(2,1)}, f16[72,1024]{1,0:T(8,128)(2,1)}, u32[]{:S(2)}, u32[]{:S(2)}) collective-permute-start(f16[72,1024]{1,0:T(8,128)(2,1)} %add_convert_fusion.2), channel_id=1, source_target_pairs={{0,64},{64,0},{128,192},{192,128},{1,65},{65,1},{129,193},{193,129... | collective-permute-start | bytes 442376 | tf_op jit(solution)/shard_map/ppermute | solution.py:31
  68.6 21.4 %collective-permute-start.4 = (f16[144,1024]{1,0:T(8,128)(2,1)S(1)}, f16[144,1024]{1,0:T(8,128)(2,1)S(1)}, u32[]{:S(2)}, u32[]{:S(2)}) collective-permute-start(f16[144,1024]{1,0:T(8,128)(2,1)S(1)} %get-tuple-element.65), channel_id=1, source_target_pairs={{0,128},{64,192},{128,0},{192,64},{1,129},{65,193},{129,1},{193,65... | collective-permute-start | bytes 884744 | tf_op jit(solution)/shard_map/ppermute | solution.py:31
  87.0 11.8 %collective-permute-start.15 = (bf16[144,1024]{1,0:T(8,128)(2,1)S(1)}, bf16[144,1024]{1,0:T(8,128)(2,1)S(1)}, u32[]{:S(2)}, u32[]{:S(2)}) collective-permute-start(bf16[144,1024]{1,0:T(8,128)(2,1)S(1)} %get-tuple-element.53), channel_id=1, source_target_pairs={{0,2},{1,3},{2,0},{3,1},{4,6},{5,7},{6,4},{7,5},{8,10},{9,11},{10,... | collective-permute-start | bytes 884744 | tf_op jit(solution)/shard_map/ppermute | solution.py:27
  95.6 14.2 %collective-permute-start.12 = (bf16[256,1024]{1,0:T(8,128)(2,1)S(1)}, bf16[256,1024]{1,0:T(8,128)(2,1)S(1)}, u32[]{:S(2)}, u32[]{:S(2)}) collective-permute-start(bf16[256,1024]{1,0:T(8,128)(2,1)S(1)} %get-tuple-element.47), channel_id=1, source_target_pairs={{0,12},{4,0},{8,4},{12,8},{1,13},{5,1},{9,5},{13,9},{2,14},{6,2},{... | collective-permute-start | bytes 1572872 | tf_op jit(solution)/shard_map/ppermute | solution.py:27
  97.2 14.8 %collective-permute-start.13 = (bf16[256,1024]{1,0:T(8,128)(2,1)S(1)}, bf16[256,1024]{1,0:T(8,128)(2,1)S(1)}, u32[]{:S(2)}, u32[]{:S(2)}) collective-permute-start(bf16[256,1024]{1,0:T(8,128)(2,1)S(1)} %get-tuple-element.48), channel_id=1, source_target_pairs={{0,4},{4,8},{8,12},{12,0},{1,5},{5,9},{9,13},{13,1},{2,6},{6,10},{... | collective-permute-start | bytes 1572872 | tf_op jit(solution)/shard_map/ppermute | solution.py:27
  97.2 6.3 %collective-permute-start.20 = (bf16[144,1024]{1,0:T(8,128)(2,1)S(1)}, bf16[144,1024]{1,0:T(8,128)(2,1)S(1)}, u32[]{:S(2)}, u32[]{:S(2)}) collective-permute-start(bf16[144,1024]{1,0:T(8,128)(2,1)S(1)} %get-tuple-element.61), channel_id=1, source_target_pairs={{0,3},{1,0},{2,1},{3,2},{4,7},{5,4},{6,5},{7,6},{8,11},{9,8},{10,9... | collective-permute-start | bytes 884744 | tf_op jit(solution)/shard_map/ppermute | solution.py:27
  98.1 8.6 %collective-permute-start.19 = (bf16[144,1024]{1,0:T(8,128)(2,1)S(1)}, bf16[144,1024]{1,0:T(8,128)(2,1)S(1)}, u32[]{:S(2)}, u32[]{:S(2)}) collective-permute-start(bf16[144,1024]{1,0:T(8,128)(2,1)S(1)} %get-tuple-element.60), channel_id=1, source_target_pairs={{0,1},{1,2},{2,3},{3,0},{4,5},{5,6},{6,7},{7,4},{8,9},{9,10},{10,1... | collective-permute-start | bytes 884744 | tf_op jit(solution)/shard_map/ppermute | solution.py:27
  98.7 10.5 %collective-permute-start.22 = (f16[144,1024]{1,0:T(8,128)(2,1)S(1)}, f16[144,1024]{1,0:T(8,128)(2,1)S(1)}, u32[]{:S(2)}, u32[]{:S(2)}) collective-permute-start(f16[144,1024]{1,0:T(8,128)(2,1)S(1)} %get-tuple-element.65), channel_id=1, source_target_pairs={{0,32},{32,0},{1,33},{33,1},{2,34},{34,2},{3,35},{35,3},{4,36},{36... | collective-permute-start | bytes 884744 | tf_op jit(solution)/shard_map/ppermute | solution.py:27
  103.5 8.5 %collective-permute-start.23 = (f16[144,1024]{1,0:T(8,128)(2,1)S(1)}, f16[144,1024]{1,0:T(8,128)(2,1)S(1)}, u32[]{:S(2)}, u32[]{:S(2)}) collective-permute-start(f16[144,1024]{1,0:T(8,128)(2,1)S(1)} %collective-permute-done.4), channel_id=1, source_target_pairs={{0,32},{32,0},{1,33},{33,1},{2,34},{34,2},{3,35},{35,3},{4,36},{36... | collective-permute-start | bytes 884744 | tf_op jit(solution)/shard_map/ppermute | solution.py:27
  106.8 18.5 %collective-permute-start.21 = (bf16[144,1024]{1,0:T(8,128)(2,1)S(1)}, bf16[144,1024]{1,0:T(8,128)(2,1)S(1)}, u32[]{:S(2)}, u32[]{:S(2)}) collective-permute-start(bf16[144,1024]{1,0:T(8,128)(2,1)S(1)} %add_convert_fusion.1), channel_id=1, source_target_pairs={{0,16},{16,0},{1,17},{17,1},{2,18},{18,2},{3,19},{19,3},{4,20},{20... | collective-permute-start | bytes 884744 | tf_op jit(solution)/shard_map/ppermute | solution.py:27
  109.2 16.1 %collective-permute-start.18 = (bf16[144,1024]{1,0:T(8,128)(2,1)S(1)}, bf16[144,1024]{1,0:T(8,128)(2,1)S(1)}, u32[]{:S(2)}, u32[]{:S(2)}) collective-permute-start(bf16[144,1024]{1,0:T(8,128)(2,1)S(1)} %get-tuple-element.58), channel_id=1, source_target_pairs={{0,2},{1,3},{2,0},{3,1},{4,6},{5,7},{6,4},{7,5},{8,10},{9,11},{10,... | collective-permute-start | bytes 884744 | tf_op jit(solution)/shard_map/ppermute | solution.py:27
  109.8 15.5 %collective-permute-start.17 = (bf16[144,1024]{1,0:T(8,128)(2,1)S(1)}, bf16[144,1024]{1,0:T(8,128)(2,1)S(1)}, u32[]{:S(2)}, u32[]{:S(2)}) collective-permute-start(bf16[144,1024]{1,0:T(8,128)(2,1)S(1)} %get-tuple-element.56), channel_id=1, source_target_pairs={{0,3},{1,0},{2,1},{3,2},{4,7},{5,4},{6,5},{7,6},{8,11},{9,8},{10,9... | collective-permute-start | bytes 884744 | tf_op jit(solution)/shard_map/ppermute | solution.py:27
  112.0 13.4 %collective-permute-start.16 = (bf16[144,1024]{1,0:T(8,128)(2,1)S(1)}, bf16[144,1024]{1,0:T(8,128)(2,1)S(1)}, u32[]{:S(2)}, u32[]{:S(2)}) collective-permute-start(bf16[144,1024]{1,0:T(8,128)(2,1)S(1)} %get-tuple-element.54), channel_id=1, source_target_pairs={{0,1},{1,2},{2,3},{3,0},{4,5},{5,6},{6,7},{7,4},{8,9},{9,10},{10,1... | collective-permute-start | bytes 884744 | tf_op jit(solution)/shard_map/ppermute | solution.py:27
  112.1 14.3 %collective-permute-start.14 = (bf16[256,1024]{1,0:T(8,128)(2,1)S(1)}, bf16[256,1024]{1,0:T(8,128)(2,1)S(1)}, u32[]{:S(2)}, u32[]{:S(2)}) collective-permute-start(bf16[256,1024]{1,0:T(8,128)(2,1)S(1)} %get-tuple-element.50), channel_id=1, source_target_pairs={{0,8},{4,12},{8,0},{12,4},{1,9},{5,13},{9,1},{13,5},{2,10},{6,14},... | collective-permute-start | bytes 1572872 | tf_op jit(solution)/shard_map/ppermute | solution.py:27
  (9 other events, 85.8 us)

commit v5 on v4

v5 whole, which is shorter than its diff:
```python
import functools

import jax
import jax.numpy as jnp
from jax import lax
from jax.experimental import pallas as pl
from jax.experimental.pallas import tpu as pltpu
from jax.sharding import Mesh, PartitionSpec as P

D = 4608
KV = 1024
ROWS = 144
WIDE = 576
TOK = 256
MSG = 2 * WIDE + KV
SCALE = float(D) ** -0.5
BF = jnp.bfloat16
F32 = jnp.float32
F16 = jnp.float16
UNIT = 512.0
LIMIT = 48 * 1024 * 1024


def _place():
    return [lax.axis_index(n) for n in ("zl", "core", "zh", "y", "x")]


def _shift(v, axis, k, size=4):
    return lax.ppermute(v, axis, [(i, (i + k) % size) for i in range(size)])


def _flip(v, axis, bit, size=4):
    return lax.ppermute(v, axis, [(i, i ^ bit) for i in range(size)])


def _after(v, *done):
    return lax.optimization_barrier((v, *done))[0]


def _call(kernel, name, outs, scratch=(), **kw):
    return pl.pallas_call(
        kernel,
        name=name,
        out_shape=[jax.ShapeDtypeStruct(s, d) for s, d in outs],
        scratch_shapes=list(scratch),
        compiler_params=pltpu.CompilerParams(vmem_limit_bytes=LIMIT),
        cost_estimate=pl.CostEstimate(flops=0, bytes_accessed=1024, transcendentals=0),
        **kw,
    )


def _vmem(n):
    return [pl.BlockSpec(memory_space=pltpu.VMEM)] * n


def _pick_kernel(index_ref, frag_ref, used_ref, give_ref, keep_ref, sems):
    core = _place()[1]
    copies = [
        pltpu.make_async_copy(frag_ref.at[0, index_ref[0]], used_ref, sems.at[0]),
        pltpu.make_async_copy(frag_ref.at[0, pl.ds(2 - 2 * core, 2)], give_ref, sems.at[1]),
        pltpu.make_async_copy(frag_ref.at[0, pl.ds(2 * core, 2)], keep_ref, sems.at[2]),
    ]
    for c in copies:
        c.start()
    for c in copies:
        c.wait()


def _norm_kernel(x_ref, gain_ref, cot_ref, own_ref, n1_ref, m2_ref, n3_ref, held):
    _, _, zh, y, _ = _place()
    values = x_ref[...].astype(F32)
    stats = jnp.mean(values * values, axis=1, keepdims=True)
    normed = (values * lax.rsqrt(stats + 1e-06) * gain_ref[...]).astype(BF)
    for q in range(8):
        held[q] = normed[:, q * WIDE : (q + 1) * WIDE]
    for k, out in enumerate((own_ref, n1_ref, m2_ref, n3_ref)):
        chunk = (y + k) & 3
        out[:, : 2 * WIDE] = jnp.concatenate([held[(1 - zh) * 4 + chunk], held[zh * 4 + chunk]], axis=1)
    m2_ref[:, 2 * WIDE :] = cot_ref[...]


def _grad_kernel(half, n0, c0, n1, c1, m2, n3, c3, own_ref, o1_ref, o2_ref, o3_ref, total):
    x = _place()[4]
    first = half * WIDE
    normed = jnp.concatenate([n[:, first : first + WIDE] for n in (n0, n1, m2, n3)], axis=0)
    cot = jnp.concatenate([c0[...], c1[...], m2[:, 2 * WIDE :], c3[...]], axis=0)
    total[...] = lax.dot_general(normed, cot, (((0,), (0,)), ((), ())), preferred_element_type=F32)
    for k, out in enumerate((own_ref, o1_ref, o2_ref, o3_ref)):
        rows = pl.ds(pl.multiple_of(((x + k) & 3) * ROWS, 16), ROWS)
        out[...] = (total[rows, :] * SCALE).astype(out.dtype)


def _keys_kernel(n, *refs):
    blocks, pairs, outs, layer = refs[:n], refs[n : n + 4], refs[n + 4 : 2 * n + 4], refs[-1]
    x = _place()[4]
    for k in range(4):
        for h in range(2):
            first = pl.multiple_of(h * WIDE + ((x + 4 - k) & 3) * ROWS, 16)
            layer[pl.ds(first, ROWS), :] = pairs[k][h]
    for block, out in zip(blocks, outs):
        part = jnp.dot(block[:, : 2 * WIDE], layer[...], preferred_element_type=F32)
        out[...] = (part * SCALE).astype(out.dtype)


def _outer_kernel(place_ref, *refs):
    averages, (global_ref, momentum_ref, new_global_ref, new_momentum_ref) = refs[:4], refs[4:]

    for k in range(4):

        @pl.when(pl.program_id(0) == k)
        def _():
            mean = averages[k][...]
            momentum = 0.9 * momentum_ref[0] + mean
            new_momentum_ref[0] = momentum
            new_global_ref[0] = global_ref[0] - 0.7 * (mean + 0.9 * momentum)


def body(layer_index, inputs, norm_gain, cotangent, local_fragment, global_fragment, momentum):
    zl, core = lax.axis_index("zl"), lax.axis_index("core")
    hi, lo = zl >> 1, zl & 1
    any_spec = pl.BlockSpec(memory_space=pl.ANY)

    used, give, keep = _call(
        _pick_kernel,
        "pick",
        [((ROWS, KV), BF)] + [((2, ROWS, KV), BF)] * 2,
        [pltpu.SemaphoreType.DMA((3,))],
        in_specs=[pl.BlockSpec(memory_space=pltpu.SMEM), any_spec],
        out_specs=[any_spec] * 3,
    )(layer_index, local_fragment)
    c1, c3 = _shift(cotangent, "y", 1), _shift(cotangent, "y", 3)
    used_other = _shift(used, "zh", 1, 2)
    got = _shift(give, "core", 1, 2)

    rows = 64
    tile = lambda n: pl.BlockSpec((rows, n), lambda i: (i, 0))
    own, n1, m2, n3 = _call(
        _norm_kernel,
        "normed",
        [((TOK, n), BF) for n in (2 * WIDE, 2 * WIDE, MSG, 2 * WIDE)],
        [pltpu.VMEM((8, rows, WIDE), BF)],
        grid=(TOK // rows,),
        in_specs=[tile(D), pl.BlockSpec((1, D), lambda i: (0, 0)), tile(KV)],
        out_specs=[tile(n) for n in (2 * WIDE, 2 * WIDE, MSG, 2 * WIDE)],
    )(inputs, _after(norm_gain[None, :], used), cotangent)

    pair = jnp.stack([used_other, used])
    p1, p3 = _shift(pair, "x", 1), _shift(pair, "x", 3)
    r1, r3 = _shift(_after(n1, c1, c3), "y", 1), _shift(_after(n3, c1, c3), "y", 3)

    got = _after(got, own, used_other)

    def delta(which):
        shared = lax.dynamic_index_in_dim(global_fragment, 2 * core + which, 0, keepdims=False)
        first = lax.dynamic_index_in_dim(keep, which, 0, keepdims=False).astype(F32)
        second = lax.dynamic_index_in_dim(got, which, 0, keepdims=False).astype(F32)
        return ((shared - first) + (shared - second)) * UNIT

    half = ROWS // 2
    sum4 = delta(lo) + _after(_flip(delta(1 - lo).astype(F16), "zl", 1), r1, r3).astype(F32)
    out = lax.dynamic_slice_in_dim(sum4, (1 - hi) * half, half, 0).astype(F16)
    other = _after(_flip(out, "zl", 2), p1, p3)
    sum8 = (lax.dynamic_slice_in_dim(sum4, hi * half, half, 0) + other.astype(F32)).astype(F16)
    peer = _flip(sum8, "zl", 2)
    mine = jnp.where(hi == 0, jnp.concatenate([sum8, peer]), jnp.concatenate([peer, sum8]))
    next_layer = _flip(mine, "zl", 1)

    r2 = _shift(_after(m2, r1, r3, pair), "y", 2)
    pairs = [pair, p1, _shift(_after(pair, r1, r3), "x", 2), p3]

    def keys_of(*blocks):
        return _call(
            functools.partial(_keys_kernel, len(blocks)),
            f"keys{len(blocks)}",
            [((TOK, KV), F32 if b is own else BF) for b in blocks],
            [pltpu.VMEM((2 * WIDE, KV), BF)],
            in_specs=_vmem(len(blocks) + 4),
            out_specs=_vmem(len(blocks)),
        )(*blocks, *pairs)

    k0, k1, k3 = keys_of(own, _after(r1, mine), r3)
    e1, e3 = _shift(k1, "y", 3), _shift(k3, "y", 1)

    def grad(half, own):
        return _call(
            functools.partial(_grad_kernel, half),
            f"grad{half}",
            [((ROWS, KV), F32)] + [((ROWS, KV), BF)] * 3,
            [pltpu.VMEM((WIDE, KV), F32)],
            in_specs=_vmem(7),
            out_specs=_vmem(4),
        )(own, cotangent, r1, c1, r2, r3, c3)

    g = grad(0, _after(own, k0))
    a1, a3 = _shift(g[1], "x", 1), _shift(g[3], "x", 3)
    b = grad(1, own)
    (k2,) = keys_of(_after(r2, g[0]))
    a2 = _shift(_after(g[2], a1, b[0], k2), "x", 2)
    far_sum = (g[0] + sum(v.astype(F32) for v in (a1, a2, a3))).astype(BF)
    from_zh = _shift(far_sum, "zh", 1, 2)
    near_sum = _after(b[0] + from_zh.astype(F32))
    b1, b3, b2 = [_shift(_after(b[k], far_sum), "x", k) for k in (1, 3, 2)]
    weight_grad = (near_sum + sum(v.astype(F32) for v in (b1, b3, b2)))[None]

    averages = [mine, next_layer] + [_shift(_after(v, a1, a3), "core", 1, 2) for v in (mine, next_layer)]
    averages = [v.astype(F32) / (8.0 * UNIT) for v in averages]

    def layer_of(k, place):
        return (jnp.where(k < 2, place[0], 1 - place[0]) * 2 + (place[1] ^ (k & 1)), 0, 0)

    block = pl.BlockSpec((1, ROWS, KV), layer_of)
    whole = pl.BlockSpec((ROWS, KV), lambda k, place: (0, 0))
    new_global, new_momentum = pl.pallas_call(
        _outer_kernel,
        name="outer_step",
        out_shape=[jax.ShapeDtypeStruct((4, ROWS, KV), F32)] * 2,
        grid_spec=pltpu.PrefetchScalarGridSpec(
            num_scalar_prefetch=1,
            grid=(4,),
            in_specs=[whole] * 4 + [block, block],
            out_specs=[block, block],
        ),
        compiler_params=pltpu.CompilerParams(vmem_limit_bytes=LIMIT),
        cost_estimate=pl.CostEstimate(flops=0, bytes_accessed=1024, transcendentals=0),
    )(jnp.stack([core, lo]).astype(jnp.int32), *averages, global_fragment, momentum)

    e2 = _shift(_after(k2, e1, e3, b[0], a1, a3, next_layer), "y", 2)
    keys = k0 + sum(v.astype(F32) for v in (e1, e3, e2))
    return keys.astype(BF), weight_grad, new_global, new_momentum


def solution(mesh):
    split = Mesh(mesh.devices.reshape(4, 2, 2, 4, 4), ("zl", "core", "zh", "y", "x"))
    replica, fsdp = ("zl", "core"), ("zh", "y", "x")
    placed = (
        P(replica),
        P(replica + fsdp, None),
        P(),
        P(replica + fsdp, None),
        P(replica, None, fsdp, None),
        P(None, fsdp, None),
        P(None, fsdp, None),
    )
    return jax.shard_map(
        body,
        mesh=split,
        in_specs=placed,
        out_specs=(
            P(replica + fsdp, None),
            P(replica, fsdp, None),
            P(None, fsdp, None),
            P(None, fsdp, None),
        ),
        check_vma=False,
    )
```

time: 128 us -> 127 us (level); the launches traced: 127 us -> 125 us
  starting transfers between devices: 40.1 us -> 57.7 us
  waiting for transfers between devices: 44.5 us -> 30.4 us
  other arithmetic: 13.3 us -> 9.86 us
  Pallas kernels: 21.3 us -> 19 us
    ppermute x4, waiting for transfers between devices: 20.9 us -> 5.9 us  [_flip(): return lax.ppermute(v, axis, [(i, i ^ bit) for i in range(size)])]
    ppermute x20 -> x22, starting transfers between devices: 37.2 us -> 51 us  [_shift(): return lax.ppermute(v, axis, [(i, (i + k) % size) for i in range(size)])]
    ppermute x4, starting transfers between devices: 2.83 us -> 6.69 us  [_flip(): return lax.ppermute(v, axis, [(i, i ^ bit) for i in range(size)])]
    pallas_call x3 -> x5, Pallas kernels: 15.3 us -> 13 us  [the longest x2 6.16 us: keys_of(): _call(functools.partial(_keys_kernel, len(blocks)), f'keys{len(blocks)}',...]
    another operation x1, other arithmetic: 1.92 us -> 0.06 us  [body(): pair = jnp.stack([used_other, used])]
    ppermute x20 -> x22, waiting for transfers between devices: 23.6 us -> 24.5 us  [_shift(): return lax.ppermute(v, axis, [(i, (i + k) % size) for i in range(size)])]
    unnamed x18 -> x22, local copies, waits for them, and re-layouts: 6.07 us -> 5.69 us
  transfers between devices with their start and end apart: 24 -> 26, of which waited for: 7 -> 5; matrix products, arithmetic and copies ran while one was open for 10% -> 8% of each run, Pallas kernels for 16% -> 14%
where the time goes in v5:
time: 127 us; the launch traced here: 125 us
  starting transfers between devices  57.7 us (45%)
  waiting for transfers between devices  30.4 us (24%)
  Pallas kernels  19 us (15%)
  other arithmetic  9.86 us (8%)
  local copies, waits for them, and re-layouts  6.43 us (5%)
  between operations  1.55 us (1%)
    ppermute x22, starting transfers between devices, _shift(): return lax.ppermute(v, axis, [(i, (i + k) % size) for i in range(size)])  51 us
    ppermute x22, waiting for transfers between devices, _shift(): return lax.ppermute(v, axis, [(i, (i + k) % size) for i in range(size)])  24.5 us
    ppermute x4, starting transfers between devices, _flip(): return lax.ppermute(v, axis, [(i, i ^ bit) for i in range(size)])  6.69 us
    pallas_call x2, Pallas kernels, keys_of(): _call(functools.partial(_keys_kernel, len(blocks)), f'keys{len(blocks)}',...  6.16 us
    ppermute x4, waiting for transfers between devices, _flip(): return lax.ppermute(v, axis, [(i, i ^ bit) for i in range(size)])  5.9 us
    unnamed x22, local copies, waits for them, and re-layouts  5.69 us
    pallas_call x1, Pallas kernels, body(): pl.pallas_call(_outer_kernel, name='outer_step', out_shape=[jax.ShapeDtyp...  5.12 us
    pallas_call x2, Pallas kernels, grad(): _call(functools.partial(_grad_kernel, half), f'grad{half}', [((ROWS, KV),...  3.8 us
  transfers between devices with their start and end apart: 26, of which 5 were waited for; matrix products, arithmetic and copies ran while one was open for 8% of the time, Pallas kernels for 14%

profile of v5, /device:TPU:1, one launch (start us, length us, event | category | flops | bytes accessed | tf_op | source)
XLA Modules:
  0.0 124.9 jit_solution(17604025680976418114)
XLA Ops:
  0.6 2.2 %collective-permute-start = (bf16[256,1024]{1,0:T(8,128)(2,1)}, bf16[256,1024]{1,0:T(8,128)(2,1)S(1)}, u32[]{:S(2)}, u32[]{:S(2)}) collective-permute-start(bf16[256,1024]{1,0:T(8,128)(2,1)} %c0.3), channel_id=1, source_target_pairs={{0,4},{4,8},{8,12},{12,0},{1,5},{5,9},{9,13},{13,1},{2,6},{6,10},{... | collective-permute-start | bytes 1572872 | tf_op jit(solution)/shard_map/ppermute | solution.py:29
  7.2 2.9 %collective-permute-start.3 = (bf16[2,144,1024]{2,1,0:T(8,128)(2,1)}, bf16[2,144,1024]{2,1,0:T(8,128)(2,1)}, u32[]{:S(2)}, u32[]{:S(2)}) collective-permute-start(bf16[2,144,1024]{2,1,0:T(8,128)(2,1)} %get-tuple-element.48), channel_id=1, source_target_pairs={{0,32},{32,0},{1,33},{33,1},{2,34},{34,2},{3,35},{35,3},{4,36},{36... | collective-permute-start | bytes 1769480 | tf_op jit(solution)/shard_map/ppermute | solution.py:29
  10.1 5.2 %collective-permute-start.4 = (bf16[144,1024]{1,0:T(8,128)(2,1)S(1)}, bf16[144,1024]{1,0:T(8,128)(2,1)S(1)}, u32[]{:S(2)}, u32[]{:S(2)}) collective-permute-start(bf16[144,1024]{1,0:T(8,128)(2,1)S(1)} %get-tuple-element.42), channel_id=1, source_target_pairs={{0,16},{16,0},{1,17},{17,1},{2,18},{18,2},{3,19},{19,3},{4,20},{20... | collective-permute-start | bytes 884744 | tf_op jit(solution)/shard_map/ppermute | solution.py:29
  17.1 1.7 %copy-done.3 = bf16[256,4608]{1,0:T(8,128)(2,1)S(1)} copy-done((bf16[256,4608]{1,0:T(8,128)(2,1)S(1)}, bf16[256,4608]{1,0:T(8,128)(2,1)}, u32[]{:S(2)}) %copy-start.3) | copy-done | bytes 2359320
  18.8 3.0 %normed.1 = (bf16[256,1152]{1,0:T(8,128)(2,1)S(1)}, bf16[256,1152]{1,0:T(8,128)(2,1)}, bf16[256,2176]{1,0:T(8,128)(2,1)}, bf16[256,1152]{1,0:T(8,128)(2,1)S(1)}) custom-call(bf16[256,4608]{1,0:T(8,128)(2,1)S(1)} %copy-done.3, f32[1,4608]{1,0:T(1,128)S(1)} %broadcast_in_dim.6.gain_ref, bf16[256,1024]{1,0:T(8,128)(2,1)S(1)} %copy-done.1), custom_call_target="tpu_custom_call" | custom-call | bytes 1024 | tf_op jit(solution)/shard_map/normed/pallas_call | solution.py:137
  23.5 2.6 %collective-permute-start.6 = (bf16[256,1152]{1,0:T(8,128)(2,1)S(1)}, bf16[256,1152]{1,0:T(8,128)(2,1)S(1)}, u32[]{:S(2)}, u32[]{:S(2)}) collective-permute-start(bf16[256,1152]{1,0:T(8,128)(2,1)S(1)} %get-tuple-element.51), channel_id=1, source_target_pairs={{0,12},{4,0},{8,4},{12,8},{1,13},{5,1},{9,5},{13,9},{2,14},{6,2},{... | collective-permute-start | bytes 1769480 | tf_op jit(solution)/shard_map/ppermute | solution.py:29
  26.1 2.0 %fusion = f16[144,1024]{1,0:T(8,128)(2,1)} fusion(f32[4,144,1024]{2,1,0:T(8,128)} %refs_4_.1, s32[]{:T(128)S(6)} %select_n.33, bf16[2,144,1024]{2,1,0:T(8,128)(2,1)} %collective-permute-done.3, s32[]{:T(128)S(6)} %select_n.34, bf16[2,144,1024]{2,1,0:T(8,128)(2,1)S(1)} %get-tuple-element.47), kind=kLoop, calls=%fused_computation.11 | loop fusion | flops 1032192 | bytes 1474568 | tf_op jit(solution)/shard_map/mul | solution.py:157
  28.1 3.6 %collective-permute-start.5 = (f16[144,1024]{1,0:T(8,128)(2,1)}, f16[144,1024]{1,0:T(8,128)(2,1)}, u32[]{:S(2)}, u32[]{:S(2)}) collective-permute-start(f16[144,1024]{1,0:T(8,128)(2,1)} %fusion), channel_id=1, source_target_pairs={{0,64},{64,0},{128,192},{192,128},{1,65},{65,1},{129,193},{193,129... | collective-permute-start | bytes 884744 | tf_op jit(solution)/shard_map/ppermute | solution.py:33
  31.7 7.6 %collective-permute-done.2.refs_1_.n1 = bf16[256,1152]{1,0:T(8,128)(2,1)S(1)} collective-permute-done((bf16[256,1152]{1,0:T(8,128)(2,1)}, bf16[256,1152]{1,0:T(8,128)(2,1)S(1)}, u32[]{:S(2)}, u32[]{:S(2)}) %collective-permute-start.2) | collective-permute-done | bytes 589856 | tf_op jit(solution)/shard_map/ppermute | solution.py:29
  48.2 6.7 %collective-permute-done.8.refs_4_.refs_2_ = bf16[2,144,1024]{2,1,0:T(8,128)(2,1)} collective-permute-done((bf16[2,144,1024]{2,1,0:T(8,128)(2,1)S(1)}, bf16[2,144,1024]{2,1,0:T(8,128)(2,1)}, u32[]{:S(2)}, u32[]{:S(2)}) %collective-permute-start.8) | collective-permute-done | bytes 589856 | tf_op jit(solution)/shard_map/ppermute | solution.py:29
  54.9 1.7 %add_convert_fusion.2 = f16[72,1024]{1,0:T(8,128)(2,1)} fusion(f16[72,1024]{1,0:T(8,128)(2,1)} %collective-permute-done.7, f32[144,1024]{1,0:T(8,128)} %copy-done.10, s32[]{:T(128)S(6)} %select_n.35), kind=kLoop, calls=%fused_computation.13 | loop fusion | flops 221184 | bytes 589828 | tf_op jit(solution)/shard_map/convert_element_type | solution.py:163
  57.8 5.9 %collective-permute-done.10 = f16[72,1024]{1,0:T(8,128)(2,1)} collective-permute-done((f16[72,1024]{1,0:T(8,128)(2,1)}, f16[72,1024]{1,0:T(8,128)(2,1)}, u32[]{:S(2)}, u32[]{:S(2)}) %collective-permute-start.10) | collective-permute-done | bytes 147488 | tf_op jit(solution)/shard_map/ppermute | solution.py:33
  65.0 3.5 %collective-permute-done.11.refs_5_.refs_3_ = bf16[2,144,1024]{2,1,0:T(8,128)(2,1)} collective-permute-done((bf16[2,144,1024]{2,1,0:T(8,128)(2,1)S(1)}, bf16[2,144,1024]{2,1,0:T(8,128)(2,1)}, u32[]{:S(2)}, u32[]{:S(2)}) %collective-permute-start.11) | collective-permute-done | bytes 589856 | tf_op jit(solution)/shard_map/ppermute | solution.py:29
  68.5 3.8 %keys3.1 = (f32[256,1024]{1,0:T(8,128)S(1)}, bf16[256,1024]{1,0:T(8,128)(2,1)S(1)}, bf16[256,1024]{1,0:T(8,128)(2,1)S(1)}) custom-call(bf16[256,1152]{1,0:T(8,128)(2,1)S(1)} %get-tuple-element.61.refs_0_.n0, bf16[256,1152]{1,0:T(8,128)(2,1)S(1)} %collective-permute-done.2.refs_1_.n1, bf16[256,1152]{1,0:T(8,128)(2,1)S(1)} %collective-permute-done.6.refs_2_.n3, ...), custom_call_target="tpu_custom_call" | custom-call | bytes 1024 | tf_op jit(solution)/shard_map/keys3/pallas_call | solution.py:172
  72.3 1.6 %grad0.1 = (f32[144,1024]{1,0:T(8,128)S(1)}, bf16[144,1024]{1,0:T(8,128)(2,1)S(1)}, bf16[144,1024]{1,0:T(8,128)(2,1)S(1)}, bf16[144,1024]{1,0:T(8,128)(2,1)S(1)}) custom-call(bf16[256,1152]{1,0:T(8,128)(2,1)S(1)} %get-tuple-element.61.refs_0_.n0, bf16[256,1024]{1,0:T(8,128)(2,1)S(1)} %copy-done.2, bf16[256,1152]{1,0:T(8,128)(2,1)S(1)} %collective-permute-done.2.refs_1_.n1, ...), custom_call_target="tpu_custom_call" | custom-call | bytes 1024 | tf_op jit(solution)/shard_map/grad0/pallas_call | solution.py:185
  74.6 2.1 %collective-permute-start.16 = (bf16[144,1024]{1,0:T(8,128)(2,1)S(1)}, bf16[144,1024]{1,0:T(8,128)(2,1)S(1)}, u32[]{:S(2)}, u32[]{:S(2)}) collective-permute-start(bf16[144,1024]{1,0:T(8,128)(2,1)S(1)} %get-tuple-element.66), channel_id=1, source_target_pairs={{0,3},{1,0},{2,1},{3,2},{4,7},{5,4},{6,5},{7,6},{8,11},{9,8},{10,9... | collective-permute-start | bytes 884744 | tf_op jit(solution)/shard_map/ppermute | solution.py:29
  79.0 2.2 %grad1.1 = (f32[144,1024]{1,0:T(8,128)S(1)}, bf16[144,1024]{1,0:T(8,128)(2,1)S(1)}, bf16[144,1024]{1,0:T(8,128)(2,1)S(1)}, bf16[144,1024]{1,0:T(8,128)(2,1)S(1)}) custom-call(bf16[256,1152]{1,0:T(8,128)(2,1)S(1)} %get-tuple-element.61.refs_0_.n0, bf16[256,1024]{1,0:T(8,128)(2,1)S(1)} %copy-done.2, bf16[256,1152]{1,0:T(8,128)(2,1)S(1)} %collective-permute-done.2.refs_1_.n1, ...), custom_call_target="tpu_custom_call" | custom-call | bytes 1024 | tf_op jit(solution)/shard_map/grad1/pallas_call | solution.py:185
  81.2 2.4 %keys1.1 = bf16[256,1024]{1,0:T(8,128)(2,1)S(1)} custom-call(bf16[256,2176]{1,0:T(8,128)(2,1)S(1)} %collective-permute-done.14.m2.refs_0_, bf16[2,144,1024]{2,1,0:T(8,128)(2,1)S(1)} %pad_maximum_fusion.refs_3_.refs_1_, bf16[2,144,1024]{2,1,0:T(8,128)(2,1)} %collective-permute-done.8.refs_4_.refs_2_, ...), custom_call_target="tpu_custom_call" | custom-call | bytes 1024 | tf_op jit(solution)/shard_map/keys1/pallas_call | solution.py:172
  83.8 14.3 %collective-permute-start.24 = (f16[144,1024]{1,0:T(8,128)(2,1)S(1)}, f16[144,1024]{1,0:T(8,128)(2,1)S(1)}, u32[]{:S(2)}, u32[]{:S(2)}) collective-permute-start(f16[144,1024]{1,0:T(8,128)(2,1)S(1)} %get-tuple-element.76), channel_id=1, source_target_pairs={{0,32},{32,0},{1,33},{33,1},{2,34},{34,2},{3,35},{35,3},{4,36},{36... | collective-permute-start | bytes 884744 | tf_op jit(solution)/shard_map/ppermute | solution.py:29
  98.2 2.0 %collective-permute-start.18 = (bf16[256,1024]{1,0:T(8,128)(2,1)S(1)}, bf16[256,1024]{1,0:T(8,128)(2,1)S(1)}, u32[]{:S(2)}, u32[]{:S(2)}) collective-permute-start(bf16[256,1024]{1,0:T(8,128)(2,1)S(1)} %keys1.1), channel_id=1, source_target_pairs={{0,8},{4,12},{8,0},{12,4},{1,9},{5,13},{9,1},{13,5},{2,10},{6,14},... | collective-permute-start | bytes 1572872 | tf_op jit(solution)/shard_map/ppermute | solution.py:29
  100.2 2.9 %collective-permute-start.25 = (f16[144,1024]{1,0:T(8,128)(2,1)S(1)}, f16[144,1024]{1,0:T(8,128)(2,1)S(1)}, u32[]{:S(2)}, u32[]{:S(2)}) collective-permute-start(f16[144,1024]{1,0:T(8,128)(2,1)S(1)} %collective-permute-done.17), channel_id=1, source_target_pairs={{0,32},{32,0},{1,33},{33,1},{2,34},{34,2},{3,35},{35,3},{4,36},{36... | collective-permute-start | bytes 884744 | tf_op jit(solution)/shard_map/ppermute | solution.py:29
  105.4 4.7 %collective-permute-start.22 = (bf16[144,1024]{1,0:T(8,128)(2,1)S(1)}, bf16[144,1024]{1,0:T(8,128)(2,1)S(1)}, u32[]{:S(2)}, u32[]{:S(2)}) collective-permute-start(bf16[144,1024]{1,0:T(8,128)(2,1)S(1)} %get-tuple-element.73), channel_id=1, source_target_pairs={{0,3},{1,0},{2,1},{3,2},{4,7},{5,4},{6,5},{7,6},{8,11},{9,8},{10,9... | collective-permute-start | bytes 884744 | tf_op jit(solution)/shard_map/ppermute | solution.py:29
  111.0 5.1 %outer_step.1 = (f32[4,144,1024]{2,1,0:T(8,128)}, f32[4,144,1024]{2,1,0:T(8,128)}) custom-call(s32[2]{0:T(128)S(1)} %pad_add_fusion.place_ref, f32[144,1024]{1,0:T(8,128)S(1)} %get-tuple-element.80.refs_0_, f32[144,1024]{1,0:T(8,128)S(1)} %convert_multiply_fusion.2.refs_1_, f32[144,1024]{1,0:T(8,128)S(1)} %convert_multiply_fusion.1.refs_2_, ...), custom_call_target="tpu_custom_call" | custom-call | bytes 1024 | tf_op jit(solution)/shard_map/outer_step/pallas_call | solution.py:213
  117.3 6.7 %collective-permute-done.22 = bf16[144,1024]{1,0:T(8,128)(2,1)S(1)} collective-permute-done((bf16[144,1024]{1,0:T(8,128)(2,1)S(1)}, bf16[144,1024]{1,0:T(8,128)(2,1)S(1)}, u32[]{:S(2)}, u32[]{:S(2)}) %collective-permute-start.22) | collective-permute-done | bytes 294944 | tf_op jit(solution)/shard_map/ppermute | solution.py:29
  (72 shorter events, 27.0 us)
Async XLA Ops:
  0.6 21.2 %collective-permute-start = (bf16[256,1024]{1,0:T(8,128)(2,1)}, bf16[256,1024]{1,0:T(8,128)(2,1)S(1)}, u32[]{:S(2)}, u32[]{:S(2)}) collective-permute-start(bf16[256,1024]{1,0:T(8,128)(2,1)} %c0.3), channel_id=1, source_target_pairs={{0,4},{4,8},{8,12},{12,0},{1,5},{5,9},{9,13},{13,1},{2,6},{6,10},{... | collective-permute-start | bytes 1572872 | tf_op jit(solution)/shard_map/ppermute | solution.py:29
  2.8 19.7 %collective-permute-start.1 = (bf16[256,1024]{1,0:T(8,128)(2,1)}, bf16[256,1024]{1,0:T(8,128)(2,1)S(1)}, u32[]{:S(2)}, u32[]{:S(2)}) collective-permute-start(bf16[256,1024]{1,0:T(8,128)(2,1)} %c0.3), channel_id=1, source_target_pairs={{0,12},{4,0},{8,4},{12,8},{1,13},{5,1},{9,5},{13,9},{2,14},{6,2},{... | collective-permute-start | bytes 1572872 | tf_op jit(solution)/shard_map/ppermute | solution.py:29
  7.2 18.9 %collective-permute-start.3 = (bf16[2,144,1024]{2,1,0:T(8,128)(2,1)}, bf16[2,144,1024]{2,1,0:T(8,128)(2,1)}, u32[]{:S(2)}, u32[]{:S(2)}) collective-permute-start(bf16[2,144,1024]{2,1,0:T(8,128)(2,1)} %get-tuple-element.48), channel_id=1, source_target_pairs={{0,32},{32,0},{1,33},{33,1},{2,34},{34,2},{3,35},{35,3},{4,36},{36... | collective-permute-start | bytes 1769480 | tf_op jit(solution)/shard_map/ppermute | solution.py:29
  10.1 15.9 %collective-permute-start.4 = (bf16[144,1024]{1,0:T(8,128)(2,1)S(1)}, bf16[144,1024]{1,0:T(8,128)(2,1)S(1)}, u32[]{:S(2)}, u32[]{:S(2)}) collective-permute-start(bf16[144,1024]{1,0:T(8,128)(2,1)S(1)} %get-tuple-element.42), channel_id=1, source_target_pairs={{0,16},{16,0},{1,17},{17,1},{2,18},{18,2},{3,19},{19,3},{4,20},{20... | collective-permute-start | bytes 884744 | tf_op jit(solution)/shard_map/ppermute | solution.py:29
  23.4 16.0 %collective-permute-start.2 = (bf16[256,1152]{1,0:T(8,128)(2,1)}, bf16[256,1152]{1,0:T(8,128)(2,1)S(1)}, u32[]{:S(2)}, u32[]{:S(2)}) collective-permute-start(bf16[256,1152]{1,0:T(8,128)(2,1)} %get-tuple-element.46), channel_id=1, source_target_pairs={{0,4},{4,8},{8,12},{12,0},{1,5},{5,9},{9,13},{13,1},{2,6},{6,10},{... | collective-permute-start | bytes 1769480 | tf_op jit(solution)/shard_map/ppermute | solution.py:29
  23.5 15.9 %collective-permute-start.6 = (bf16[256,1152]{1,0:T(8,128)(2,1)S(1)}, bf16[256,1152]{1,0:T(8,128)(2,1)S(1)}, u32[]{:S(2)}, u32[]{:S(2)}) collective-permute-start(bf16[256,1152]{1,0:T(8,128)(2,1)S(1)} %get-tuple-element.51), channel_id=1, source_target_pairs={{0,12},{4,0},{8,4},{12,8},{1,13},{5,1},{9,5},{13,9},{2,14},{6,2},{... | collective-permute-start | bytes 1769480 | tf_op jit(solution)/shard_map/ppermute | solution.py:29
  28.1 15.0 %collective-permute-start.5 = (f16[144,1024]{1,0:T(8,128)(2,1)}, f16[144,1024]{1,0:T(8,128)(2,1)}, u32[]{:S(2)}, u32[]{:S(2)}) collective-permute-start(f16[144,1024]{1,0:T(8,128)(2,1)} %fusion), channel_id=1, source_target_pairs={{0,64},{64,0},{128,192},{192,128},{1,65},{65,1},{129,193},{193,129... | collective-permute-start | bytes 884744 | tf_op jit(solution)/shard_map/ppermute | solution.py:33
  39.4 32.9 %collective-permute-start.14 = (bf16[256,2176]{1,0:T(8,128)(2,1)}, bf16[256,2176]{1,0:T(8,128)(2,1)S(1)}, u32[]{:S(2)}, u32[]{:S(2)}) collective-permute-start(bf16[256,2176]{1,0:T(8,128)(2,1)} %get-tuple-element.60), channel_id=1, source_target_pairs={{0,8},{4,12},{8,0},{12,4},{1,9},{5,13},{9,1},{13,5},{2,10},{6,14},... | collective-permute-start | bytes 3342344 | tf_op jit(solution)/shard_map/ppermute | solution.py:29
  40.4 14.5 %collective-permute-start.8 = (bf16[2,144,1024]{2,1,0:T(8,128)(2,1)S(1)}, bf16[2,144,1024]{2,1,0:T(8,128)(2,1)}, u32[]{:S(2)}, u32[]{:S(2)}) collective-permute-start(bf16[2,144,1024]{2,1,0:T(8,128)(2,1)S(1)} %pad_maximum_fusion.refs_3_.refs_1_), channel_id=1, source_target_pairs={{0,1},{1,2},{2,3},{3,0},{4,5},{5,6},{6,7},{7,4},{8,9},{9,10},{10,1... | collective-permute-start | bytes 1769480 | tf_op jit(solution)/shard_map/ppermute | solution.py:29
  41.6 13.2 %collective-permute-start.9 = (bf16[2,144,1024]{2,1,0:T(8,128)(2,1)S(1)}, bf16[2,144,1024]{2,1,0:T(8,128)(2,1)}, u32[]{:S(2)}, u32[]{:S(2)}) collective-permute-start(bf16[2,144,1024]{2,1,0:T(8,128)(2,1)S(1)} %pad_maximum_fusion.refs_3_.refs_1_), channel_id=1, source_target_pairs={{0,3},{1,0},{2,1},{3,2},{4,7},{5,4},{6,5},{7,6},{8,11},{9,8},{10,9... | collective-permute-start | bytes 1769480 | tf_op jit(solution)/shard_map/ppermute | solution.py:29
  45.5 9.4 %collective-permute-start.7 = (f16[72,1024]{1,0:T(8,128)(2,1)}, f16[72,1024]{1,0:T(8,128)(2,1)}, u32[]{:S(2)}, u32[]{:S(2)}) collective-permute-start(f16[72,1024]{1,0:T(8,128)(2,1)} %dynamic-slice_convert_fusion), channel_id=1, source_target_pairs={{0,128},{64,192},{128,0},{192,64},{1,129},{65,193},{129,1},{193,65... | collective-permute-start | bytes 442376 | tf_op jit(solution)/shard_map/ppermute | solution.py:33
  46.7 21.8 %collective-permute-start.11 = (bf16[2,144,1024]{2,1,0:T(8,128)(2,1)S(1)}, bf16[2,144,1024]{2,1,0:T(8,128)(2,1)}, u32[]{:S(2)}, u32[]{:S(2)}) collective-permute-start(bf16[2,144,1024]{2,1,0:T(8,128)(2,1)S(1)} %pad_maximum_fusion.refs_3_.refs_1_), channel_id=1, source_target_pairs={{0,2},{1,3},{2,0},{3,1},{4,6},{5,7},{6,4},{7,5},{8,10},{9,11},{10,... | collective-permute-start | bytes 1769480 | tf_op jit(solution)/shard_map/ppermute | solution.py:29
  74.0 9.6 %collective-permute-start.15 = (bf16[144,1024]{1,0:T(8,128)(2,1)S(1)}, bf16[144,1024]{1,0:T(8,128)(2,1)S(1)}, u32[]{:S(2)}, u32[]{:S(2)}) collective-permute-start(bf16[144,1024]{1,0:T(8,128)(2,1)S(1)} %get-tuple-element.65), channel_id=1, source_target_pairs={{0,1},{1,2},{2,3},{3,0},{4,5},{5,6},{6,7},{7,4},{8,9},{9,10},{10,1... | collective-permute-start | bytes 884744 | tf_op jit(solution)/shard_map/ppermute | solution.py:29
  76.7 21.4 %collective-permute-start.17 = (f16[144,1024]{1,0:T(8,128)(2,1)S(1)}, f16[144,1024]{1,0:T(8,128)(2,1)S(1)}, u32[]{:S(2)}, u32[]{:S(2)}) collective-permute-start(f16[144,1024]{1,0:T(8,128)(2,1)S(1)} %get-tuple-element.76), channel_id=1, source_target_pairs={{0,64},{64,0},{128,192},{192,128},{1,65},{65,1},{129,193},{193,129... | collective-permute-start | bytes 884744 | tf_op jit(solution)/shard_map/ppermute | solution.py:33
  77.4 20.7 %collective-permute-start.12 = (bf16[256,1024]{1,0:T(8,128)(2,1)S(1)}, bf16[256,1024]{1,0:T(8,128)(2,1)S(1)}, u32[]{:S(2)}, u32[]{:S(2)}) collective-permute-start(bf16[256,1024]{1,0:T(8,128)(2,1)S(1)} %get-tuple-element.57), channel_id=1, source_target_pairs={{0,12},{4,0},{8,4},{12,8},{1,13},{5,1},{9,5},{13,9},{2,14},{6,2},{... | collective-permute-start | bytes 1572872 | tf_op jit(solution)/shard_map/ppermute | solution.py:29
  78.5 19.7 %collective-permute-start.13 = (bf16[256,1024]{1,0:T(8,128)(2,1)S(1)}, bf16[256,1024]{1,0:T(8,128)(2,1)S(1)}, u32[]{:S(2)}, u32[]{:S(2)}) collective-permute-start(bf16[256,1024]{1,0:T(8,128)(2,1)S(1)} %get-tuple-element.58), channel_id=1, source_target_pairs={{0,4},{4,8},{8,12},{12,0},{1,5},{5,9},{9,13},{13,1},{2,6},{6,10},{... | collective-permute-start | bytes 1572872 | tf_op jit(solution)/shard_map/ppermute | solution.py:29
  83.6 19.5 %collective-permute-start.19 = (bf16[144,1024]{1,0:T(8,128)(2,1)S(1)}, bf16[144,1024]{1,0:T(8,128)(2,1)S(1)}, u32[]{:S(2)}, u32[]{:S(2)}) collective-permute-start(bf16[144,1024]{1,0:T(8,128)(2,1)S(1)} %get-tuple-element.69), channel_id=1, source_target_pairs={{0,2},{1,3},{2,0},{3,1},{4,6},{5,7},{6,4},{7,5},{8,10},{9,11},{10,... | collective-permute-start | bytes 884744 | tf_op jit(solution)/shard_map/ppermute | solution.py:29
  83.8 21.7 %collective-permute-start.24 = (f16[144,1024]{1,0:T(8,128)(2,1)S(1)}, f16[144,1024]{1,0:T(8,128)(2,1)S(1)}, u32[]{:S(2)}, u32[]{:S(2)}) collective-permute-start(f16[144,1024]{1,0:T(8,128)(2,1)S(1)} %get-tuple-element.76), channel_id=1, source_target_pairs={{0,32},{32,0},{1,33},{33,1},{2,34},{34,2},{3,35},{35,3},{4,36},{36... | collective-permute-start | bytes 884744 | tf_op jit(solution)/shard_map/ppermute | solution.py:29
  98.2 17.9 %collective-permute-start.18 = (bf16[256,1024]{1,0:T(8,128)(2,1)S(1)}, bf16[256,1024]{1,0:T(8,128)(2,1)S(1)}, u32[]{:S(2)}, u32[]{:S(2)}) collective-permute-start(bf16[256,1024]{1,0:T(8,128)(2,1)S(1)} %keys1.1), channel_id=1, source_target_pairs={{0,8},{4,12},{8,0},{12,4},{1,9},{5,13},{9,1},{13,5},{2,10},{6,14},... | collective-permute-start | bytes 1572872 | tf_op jit(solution)/shard_map/ppermute | solution.py:29
  100.2 10.0 %collective-permute-start.25 = (f16[144,1024]{1,0:T(8,128)(2,1)S(1)}, f16[144,1024]{1,0:T(8,128)(2,1)S(1)}, u32[]{:S(2)}, u32[]{:S(2)}) collective-permute-start(f16[144,1024]{1,0:T(8,128)(2,1)S(1)} %collective-permute-done.17), channel_id=1, source_target_pairs={{0,32},{32,0},{1,33},{33,1},{2,34},{34,2},{3,35},{35,3},{4,36},{36... | collective-permute-start | bytes 884744 | tf_op jit(solution)/shard_map/ppermute | solution.py:29
  103.3 13.9 %collective-permute-start.20 = (bf16[144,1024]{1,0:T(8,128)(2,1)S(1)}, bf16[144,1024]{1,0:T(8,128)(2,1)S(1)}, u32[]{:S(2)}, u32[]{:S(2)}) collective-permute-start(bf16[144,1024]{1,0:T(8,128)(2,1)S(1)} %add_convert_fusion.1), channel_id=1, source_target_pairs={{0,16},{16,0},{1,17},{17,1},{2,18},{18,2},{3,19},{19,3},{4,20},{20... | collective-permute-start | bytes 884744 | tf_op jit(solution)/shard_map/ppermute | solution.py:29
  104.3 12.9 %collective-permute-start.23 = (bf16[144,1024]{1,0:T(8,128)(2,1)S(1)}, bf16[144,1024]{1,0:T(8,128)(2,1)S(1)}, u32[]{:S(2)}, u32[]{:S(2)}) collective-permute-start(bf16[144,1024]{1,0:T(8,128)(2,1)S(1)} %get-tuple-element.75), channel_id=1, source_target_pairs={{0,2},{1,3},{2,0},{3,1},{4,6},{5,7},{6,4},{7,5},{8,10},{9,11},{10,... | collective-permute-start | bytes 884744 | tf_op jit(solution)/shard_map/ppermute | solution.py:29
  105.4 18.5 %collective-permute-start.22 = (bf16[144,1024]{1,0:T(8,128)(2,1)S(1)}, bf16[144,1024]{1,0:T(8,128)(2,1)S(1)}, u32[]{:S(2)}, u32[]{:S(2)}) collective-permute-start(bf16[144,1024]{1,0:T(8,128)(2,1)S(1)} %get-tuple-element.73), channel_id=1, source_target_pairs={{0,3},{1,0},{2,1},{3,2},{4,7},{5,4},{6,5},{7,6},{8,11},{9,8},{10,9... | collective-permute-start | bytes 884744 | tf_op jit(solution)/shard_map/ppermute | solution.py:29
  110.2 13.7 %collective-permute-start.21 = (bf16[144,1024]{1,0:T(8,128)(2,1)S(1)}, bf16[144,1024]{1,0:T(8,128)(2,1)S(1)}, u32[]{:S(2)}, u32[]{:S(2)}) collective-permute-start(bf16[144,1024]{1,0:T(8,128)(2,1)S(1)} %get-tuple-element.71), channel_id=1, source_target_pairs={{0,1},{1,2},{2,3},{3,0},{4,5},{5,6},{6,7},{7,4},{8,9},{9,10},{10,1... | collective-permute-start | bytes 884744 | tf_op jit(solution)/shard_map/ppermute | solution.py:29
  (13 other events, 96.4 us)

commit v6 on v5

--- a/solution.py
+++ b/solution.py
@@ -144,7 +144,7 @@
         out_specs=[tile(n) for n in (2 * WIDE, 2 * WIDE, MSG, 2 * WIDE)],
     )(inputs, _after(norm_gain[None, :], used), cotangent)
 
-    pair = jnp.stack([used_other, used])
+    pair = jnp.stack([_after(used_other, c1, c3), used])
     p1, p3 = _shift(pair, "x", 1), _shift(pair, "x", 3)
     r1, r3 = _shift(_after(n1, c1, c3), "y", 1), _shift(_after(n3, c1, c3), "y", 3)
 
@@ -157,16 +157,16 @@
         return ((shared - first) + (shared - second)) * UNIT
 
     half = ROWS // 2
-    sum4 = delta(lo) + _after(_flip(delta(1 - lo).astype(F16), "zl", 1), r1, r3).astype(F32)
+    sum4 = delta(lo) + _after(_flip(delta(1 - lo).astype(F16), "zl", 1), r1, r3, p1, p3).astype(F32)
     out = lax.dynamic_slice_in_dim(sum4, (1 - hi) * half, half, 0).astype(F16)
-    other = _after(_flip(out, "zl", 2), p1, p3)
+    other = _flip(out, "zl", 2)
     sum8 = (lax.dynamic_slice_in_dim(sum4, hi * half, half, 0) + other.astype(F32)).astype(F16)
     peer = _flip(sum8, "zl", 2)
     mine = jnp.where(hi == 0, jnp.concatenate([sum8, peer]), jnp.concatenate([peer, sum8]))
     next_layer = _flip(mine, "zl", 1)
 
     r2 = _shift(_after(m2, r1, r3, pair), "y", 2)
-    pairs = [pair, p1, _shift(_after(pair, r1, r3), "x", 2), p3]
+    pairs = [pair, p1, _shift(_after(pair, p1, p3), "x", 2), p3]
 
     def keys_of(*blocks):
         return _call(
@@ -194,15 +194,16 @@
     g = grad(0, _after(own, k0))
     a1, a3 = _shift(g[1], "x", 1), _shift(g[3], "x", 3)
     b = grad(1, own)
-    (k2,) = keys_of(_after(r2, g[0]))
-    a2 = _shift(_after(g[2], a1, b[0], k2), "x", 2)
-    far_sum = (g[0] + sum(v.astype(F32) for v in (a1, a2, a3))).astype(BF)
+    (k2,) = keys_of(_after(r2, b[0], e1, e3, a1, a3))
+    a2 = _shift(_after(g[2], a1), "x", 2)
+    swapped = [_shift(_after(v, a1, a3), "core", 1, 2) for v in (mine, next_layer)]
+    far_sum = (_after(g[0], *swapped) + sum(v.astype(F32) for v in (a1, a2, a3))).astype(BF)
     from_zh = _shift(far_sum, "zh", 1, 2)
     near_sum = _after(b[0] + from_zh.astype(F32))
     b1, b3, b2 = [_shift(_after(b[k], far_sum), "x", k) for k in (1, 3, 2)]
     weight_grad = (near_sum + sum(v.astype(F32) for v in (b1, b3, b2)))[None]
 
-    averages = [mine, next_layer] + [_shift(_after(v, a1, a3), "core", 1, 2) for v in (mine, next_layer)]
+    averages = [mine, next_layer] + swapped
     averages = [v.astype(F32) / (8.0 * UNIT) for v in averages]
 
     def layer_of(k, place):
@@ -224,7 +225,7 @@
         cost_estimate=pl.CostEstimate(flops=0, bytes_accessed=1024, transcendentals=0),
     )(jnp.stack([core, lo]).astype(jnp.int32), *averages, global_fragment, momentum)
 
-    e2 = _shift(_after(k2, e1, e3, b[0], a1, a3, next_layer), "y", 2)
+    e2 = _shift(_after(k2, b[0]), "y", 2)
     keys = k0 + sum(v.astype(F32) for v in (e1, e3, e2))
     return keys.astype(BF), weight_grad, new_global, new_momentum
 

time: 127 us -> 114 us (0.90); the launches traced: 125 us -> 113 us
  starting transfers between devices: 57.7 us -> 42.7 us
  waiting for transfers between devices: 30.4 us -> 34.4 us
    ppermute x22, starting transfers between devices: 51 us -> 38.5 us  [_shift(): return lax.ppermute(v, axis, [(i, (i + k) % size) for i in range(size)])]
    ppermute x4, waiting for transfers between devices: 5.9 us -> 12.7 us  [_flip(): return lax.ppermute(v, axis, [(i, i ^ bit) for i in range(size)])]
    ppermute x22, waiting for transfers between devices: 24.5 us -> 21.7 us  [_shift(): return lax.ppermute(v, axis, [(i, (i + k) % size) for i in range(size)])]
    ppermute x4, starting transfers between devices: 6.69 us -> 4.19 us  [_flip(): return lax.ppermute(v, axis, [(i, i ^ bit) for i in range(size)])]
    unnamed x22 -> x24, local copies, waits for them, and re-layouts: 5.69 us -> 5.11 us
  transfers between devices with their start and end apart: 26 -> 26, of which waited for: 5 -> 10; matrix products, arithmetic and copies ran while one was open for 8% -> 9% of each run, Pallas kernels for 14% -> 15%
where the time goes in v6:
time: 114 us; the launch traced here: 113 us
  starting transfers between devices  42.7 us (37%)
  waiting for transfers between devices  34.4 us (30%)
  Pallas kernels  18.9 us (17%)
  other arithmetic  9.89 us (9%)
  local copies, waits for them, and re-layouts  5.85 us (5%)
  between operations  1.55 us (1%)
    ppermute x22, starting transfers between devices, _shift(): return lax.ppermute(v, axis, [(i, (i + k) % size) for i in range(size)])  38.5 us
    ppermute x22, waiting for transfers between devices, _shift(): return lax.ppermute(v, axis, [(i, (i + k) % size) for i in range(size)])  21.7 us
    ppermute x4, waiting for transfers between devices, _flip(): return lax.ppermute(v, axis, [(i, i ^ bit) for i in range(size)])  12.7 us
    pallas_call x2, Pallas kernels, keys_of(): _call(functools.partial(_keys_kernel, len(blocks)), f'keys{len(blocks)}',...  6.27 us
    pallas_call x1, Pallas kernels, body(): pl.pallas_call(_outer_kernel, name='outer_step', out_shape=[jax.ShapeDtyp...  5.12 us
    unnamed x24, local copies, waits for them, and re-layouts  5.11 us
    ppermute x4, starting transfers between devices, _flip(): return lax.ppermute(v, axis, [(i, i ^ bit) for i in range(size)])  4.19 us
    pallas_call x2, Pallas kernels, grad(): _call(functools.partial(_grad_kernel, half), f'grad{half}', [((ROWS, KV),...  3.8 us
  transfers between devices with their start and end apart: 26, of which 10 were waited for; matrix products, arithmetic and copies ran while one was open for 9% of the time, Pallas kernels for 15%

profile of v6, /device:TPU:1, one launch (start us, length us, event | category | flops | bytes accessed | tf_op | source)
XLA Modules:
  0.0 113.3 jit_solution(4339336770445944685)
XLA Ops:
  0.6 2.2 %collective-permute-start = (bf16[256,1024]{1,0:T(8,128)(2,1)}, bf16[256,1024]{1,0:T(8,128)(2,1)S(1)}, u32[]{:S(2)}, u32[]{:S(2)}) collective-permute-start(bf16[256,1024]{1,0:T(8,128)(2,1)} %c0.3), channel_id=1, source_target_pairs={{0,4},{4,8},{8,12},{12,0},{1,5},{5,9},{9,13},{13,1},{2,6},{6,10},{... | collective-permute-start | bytes 1572872 | tf_op jit(solution)/shard_map/ppermute | solution.py:29
  7.2 7.0 %collective-permute-start.4 = (bf16[144,1024]{1,0:T(8,128)(2,1)S(1)}, bf16[144,1024]{1,0:T(8,128)(2,1)S(1)}, u32[]{:S(2)}, u32[]{:S(2)}) collective-permute-start(bf16[144,1024]{1,0:T(8,128)(2,1)S(1)} %get-tuple-element.43), channel_id=1, source_target_pairs={{0,16},{16,0},{1,17},{17,1},{2,18},{18,2},{3,19},{19,3},{4,20},{20... | collective-permute-start | bytes 884744 | tf_op jit(solution)/shard_map/ppermute | solution.py:29
  19.0 2.8 %normed.1 = (bf16[256,1152]{1,0:T(8,128)(2,1)S(1)}, bf16[256,1152]{1,0:T(8,128)(2,1)}, bf16[256,2176]{1,0:T(8,128)(2,1)S(1)}, bf16[256,1152]{1,0:T(8,128)(2,1)S(1)}) custom-call(bf16[256,4608]{1,0:T(8,128)(2,1)S(1)} %copy-done.3, f32[1,4608]{1,0:T(1,128)S(1)} %broadcast_in_dim.6.gain_ref, bf16[256,1024]{1,0:T(8,128)(2,1)S(1)} %copy-done.1), custom_call_target="tpu_custom_call" | custom-call | bytes 1024 | tf_op jit(solution)/shard_map/normed/pallas_call | solution.py:137
  23.0 2.6 %collective-permute-start.6 = (bf16[256,1152]{1,0:T(8,128)(2,1)S(1)}, bf16[256,1152]{1,0:T(8,128)(2,1)S(1)}, u32[]{:S(2)}, u32[]{:S(2)}) collective-permute-start(bf16[256,1152]{1,0:T(8,128)(2,1)S(1)} %get-tuple-element.52), channel_id=1, source_target_pairs={{0,12},{4,0},{8,4},{12,8},{1,13},{5,1},{9,5},{13,9},{2,14},{6,2},{... | collective-permute-start | bytes 1769480 | tf_op jit(solution)/shard_map/ppermute | solution.py:29
  28.4 2.0 %fusion = f16[144,1024]{1,0:T(8,128)(2,1)} fusion(f32[4,144,1024]{2,1,0:T(8,128)} %refs_4_.1, s32[]{:T(128)S(6)} %select_n.33, bf16[2,144,1024]{2,1,0:T(8,128)(2,1)} %collective-permute-done.3, s32[]{:T(128)S(6)} %select_n.34, bf16[2,144,1024]{2,1,0:T(8,128)(2,1)S(1)} %get-tuple-element.48), kind=kLoop, calls=%fused_computation.11 | loop fusion | flops 1032192 | bytes 1474568 | tf_op jit(solution)/shard_map/mul | solution.py:157
  30.5 1.9 %collective-permute-start.5 = (f16[144,1024]{1,0:T(8,128)(2,1)}, f16[144,1024]{1,0:T(8,128)(2,1)}, u32[]{:S(2)}, u32[]{:S(2)}) collective-permute-start(f16[144,1024]{1,0:T(8,128)(2,1)} %fusion), channel_id=1, source_target_pairs={{0,64},{64,0},{128,192},{192,128},{1,65},{65,1},{129,193},{193,129... | collective-permute-start | bytes 884744 | tf_op jit(solution)/shard_map/ppermute | solution.py:33
  32.4 7.1 %collective-permute-done.2.refs_1_.n1 = bf16[256,1152]{1,0:T(8,128)(2,1)S(1)} collective-permute-done((bf16[256,1152]{1,0:T(8,128)(2,1)}, bf16[256,1152]{1,0:T(8,128)(2,1)S(1)}, u32[]{:S(2)}, u32[]{:S(2)}) %collective-permute-start.2) | collective-permute-done | bytes 589856 | tf_op jit(solution)/shard_map/ppermute | solution.py:29
  43.8 2.3 %collective-permute-start.9 = (f16[72,1024]{1,0:T(8,128)(2,1)}, f16[72,1024]{1,0:T(8,128)(2,1)}, u32[]{:S(2)}, u32[]{:S(2)}) collective-permute-start(f16[72,1024]{1,0:T(8,128)(2,1)} %dynamic-slice_convert_fusion), channel_id=1, source_target_pairs={{0,128},{64,192},{128,0},{192,64},{1,129},{65,193},{129,1},{193,65... | collective-permute-start | bytes 442376 | tf_op jit(solution)/shard_map/ppermute | solution.py:33
  46.0 2.2 %collective-permute-start.11 = (bf16[2,144,1024]{2,1,0:T(8,128)(2,1)S(1)}, bf16[2,144,1024]{2,1,0:T(8,128)(2,1)}, u32[]{:S(2)}, u32[]{:S(2)}) collective-permute-start(bf16[2,144,1024]{2,1,0:T(8,128)(2,1)S(1)} %pad_maximum_fusion.refs_3_.refs_1_), channel_id=1, source_target_pairs={{0,2},{1,3},{2,0},{3,1},{4,6},{5,7},{6,4},{7,5},{8,10},{9,11},{10,... | collective-permute-start | bytes 1769480 | tf_op jit(solution)/shard_map/ppermute | solution.py:29
  48.2 4.9 %collective-permute-done.9 = f16[72,1024]{1,0:T(8,128)(2,1)} collective-permute-done((f16[72,1024]{1,0:T(8,128)(2,1)}, f16[72,1024]{1,0:T(8,128)(2,1)}, u32[]{:S(2)}, u32[]{:S(2)}) %collective-permute-start.9) | collective-permute-done | bytes 147488 | tf_op jit(solution)/shard_map/ppermute | solution.py:33
  54.9 7.8 %collective-permute-done.10 = f16[72,1024]{1,0:T(8,128)(2,1)} collective-permute-done((f16[72,1024]{1,0:T(8,128)(2,1)}, f16[72,1024]{1,0:T(8,128)(2,1)}, u32[]{:S(2)}, u32[]{:S(2)}) %collective-permute-start.10) | collective-permute-done | bytes 147488 | tf_op jit(solution)/shard_map/ppermute | solution.py:33
  64.0 3.9 %keys3.1 = (f32[256,1024]{1,0:T(8,128)S(1)}, bf16[256,1024]{1,0:T(8,128)(2,1)S(1)}, bf16[256,1024]{1,0:T(8,128)(2,1)S(1)}) custom-call(bf16[256,1152]{1,0:T(8,128)(2,1)S(1)} %get-tuple-element.63.refs_0_.n0, bf16[256,1152]{1,0:T(8,128)(2,1)S(1)} %collective-permute-done.2.refs_1_.n1, bf16[256,1152]{1,0:T(8,128)(2,1)S(1)} %collective-permute-done.6.refs_2_.n3, ...), custom_call_target="tpu_custom_call" | custom-call | bytes 1024 | tf_op jit(solution)/shard_map/keys3/pallas_call | solution.py:172
  69.6 2.7 %collective-permute-start.16 = (bf16[144,1024]{1,0:T(8,128)(2,1)S(1)}, bf16[144,1024]{1,0:T(8,128)(2,1)S(1)}, u32[]{:S(2)}, u32[]{:S(2)}) collective-permute-start(bf16[144,1024]{1,0:T(8,128)(2,1)S(1)} %get-tuple-element.65), channel_id=1, source_target_pairs={{0,3},{1,0},{2,1},{3,2},{4,7},{5,4},{6,5},{7,6},{8,11},{9,8},{10,9... | collective-permute-start | bytes 884744 | tf_op jit(solution)/shard_map/ppermute | solution.py:29
  74.7 3.3 %collective-permute-done.15 = bf16[144,1024]{1,0:T(8,128)(2,1)S(1)} collective-permute-done((bf16[144,1024]{1,0:T(8,128)(2,1)S(1)}, bf16[144,1024]{1,0:T(8,128)(2,1)S(1)}, u32[]{:S(2)}, u32[]{:S(2)}) %collective-permute-start.15) | collective-permute-done | bytes 294944 | tf_op jit(solution)/shard_map/ppermute | solution.py:29
  78.0 2.2 %collective-permute-start.18 = (f16[144,1024]{1,0:T(8,128)(2,1)S(1)}, f16[144,1024]{1,0:T(8,128)(2,1)S(1)}, u32[]{:S(2)}, u32[]{:S(2)}) collective-permute-start(f16[144,1024]{1,0:T(8,128)(2,1)S(1)} %get-tuple-element.69), channel_id=1, source_target_pairs={{0,32},{32,0},{1,33},{33,1},{2,34},{34,2},{3,35},{35,3},{4,36},{36... | collective-permute-start | bytes 884744 | tf_op jit(solution)/shard_map/ppermute | solution.py:29
  81.9 2.2 %grad1.1 = (f32[144,1024]{1,0:T(8,128)S(1)}, bf16[144,1024]{1,0:T(8,128)(2,1)S(1)}, bf16[144,1024]{1,0:T(8,128)(2,1)S(1)}, bf16[144,1024]{1,0:T(8,128)(2,1)S(1)}) custom-call(bf16[256,1152]{1,0:T(8,128)(2,1)S(1)} %get-tuple-element.63.refs_0_.n0, bf16[256,1024]{1,0:T(8,128)(2,1)S(1)} %copy-done.2, bf16[256,1152]{1,0:T(8,128)(2,1)S(1)} %collective-permute-done.2.refs_1_.n1, ...), custom_call_target="tpu_custom_call" | custom-call | bytes 1024 | tf_op jit(solution)/shard_map/grad1/pallas_call | solution.py:185
  84.0 1.8 %collective-permute-done.12 = bf16[256,1024]{1,0:T(8,128)(2,1)S(1)} collective-permute-done((bf16[256,1024]{1,0:T(8,128)(2,1)S(1)}, bf16[256,1024]{1,0:T(8,128)(2,1)S(1)}, u32[]{:S(2)}, u32[]{:S(2)}) %collective-permute-start.12) | collective-permute-done | bytes 524320 | tf_op jit(solution)/shard_map/ppermute | solution.py:29
  85.8 2.4 %keys1.1 = bf16[256,1024]{1,0:T(8,128)(2,1)S(1)} custom-call(bf16[256,2176]{1,0:T(8,128)(2,1)S(1)} %collective-permute-done.14.m2.refs_0_, bf16[2,144,1024]{2,1,0:T(8,128)(2,1)S(1)} %pad_maximum_fusion.refs_3_.refs_1_, bf16[2,144,1024]{2,1,0:T(8,128)(2,1)} %collective-permute-done.7.refs_4_.refs_2_, ...), custom_call_target="tpu_custom_call" | custom-call | bytes 1024 | tf_op jit(solution)/shard_map/keys1/pallas_call | solution.py:172
  88.2 2.9 %collective-permute-start.17 = (bf16[256,1024]{1,0:T(8,128)(2,1)S(1)}, bf16[256,1024]{1,0:T(8,128)(2,1)S(1)}, u32[]{:S(2)}, u32[]{:S(2)}) collective-permute-start(bf16[256,1024]{1,0:T(8,128)(2,1)S(1)} %keys1.1), channel_id=1, source_target_pairs={{0,8},{4,12},{8,0},{12,4},{1,9},{5,13},{9,1},{13,5},{2,10},{6,14},... | collective-permute-start | bytes 1572872 | tf_op jit(solution)/shard_map/ppermute | solution.py:29
  92.0 3.6 %collective-permute-start.22 = (bf16[144,1024]{1,0:T(8,128)(2,1)S(1)}, bf16[144,1024]{1,0:T(8,128)(2,1)S(1)}, u32[]{:S(2)}, u32[]{:S(2)}) collective-permute-start(bf16[144,1024]{1,0:T(8,128)(2,1)S(1)} %add_convert_fusion.1), channel_id=1, source_target_pairs={{0,16},{16,0},{1,17},{17,1},{2,18},{18,2},{3,19},{19,3},{4,20},{20... | collective-permute-start | bytes 884744 | tf_op jit(solution)/shard_map/ppermute | solution.py:29
  98.3 5.1 %outer_step.1 = (f32[4,144,1024]{2,1,0:T(8,128)}, f32[4,144,1024]{2,1,0:T(8,128)}) custom-call(s32[2]{0:T(128)S(1)} %pad_add_fusion.place_ref, f32[144,1024]{1,0:T(8,128)S(1)} %get-tuple-element.82.refs_0_, f32[144,1024]{1,0:T(8,128)S(1)} %convert_multiply_fusion.2.refs_1_, f32[144,1024]{1,0:T(8,128)S(1)} %convert_multiply_fusion.1.refs_2_, ...), custom_call_target="tpu_custom_call" | custom-call | bytes 1024 | tf_op jit(solution)/shard_map/outer_step/pallas_call | solution.py:214
  104.5 3.4 %collective-permute-done.22 = bf16[144,1024]{1,0:T(8,128)(2,1)S(1)} collective-permute-done((bf16[144,1024]{1,0:T(8,128)(2,1)S(1)}, bf16[144,1024]{1,0:T(8,128)(2,1)S(1)}, u32[]{:S(2)}, u32[]{:S(2)}) %collective-permute-start.22) | collective-permute-done | bytes 294944 | tf_op jit(solution)/shard_map/ppermute | solution.py:29
  108.0 2.4 %collective-permute-done.24 = bf16[144,1024]{1,0:T(8,128)(2,1)S(1)} collective-permute-done((bf16[144,1024]{1,0:T(8,128)(2,1)S(1)}, bf16[144,1024]{1,0:T(8,128)(2,1)S(1)}, u32[]{:S(2)}, u32[]{:S(2)}) %collective-permute-start.24) | collective-permute-done | bytes 294944 | tf_op jit(solution)/shard_map/ppermute | solution.py:29
  110.4 1.9 %collective-permute-done.23 = bf16[144,1024]{1,0:T(8,128)(2,1)S(1)} collective-permute-done((bf16[144,1024]{1,0:T(8,128)(2,1)S(1)}, bf16[144,1024]{1,0:T(8,128)(2,1)S(1)}, u32[]{:S(2)}, u32[]{:S(2)}) %collective-permute-start.23) | collective-permute-done | bytes 294944 | tf_op jit(solution)/shard_map/ppermute | solution.py:29
  (74 shorter events, 31.3 us)
Async XLA Ops:
  0.6 22.2 %collective-permute-start = (bf16[256,1024]{1,0:T(8,128)(2,1)}, bf16[256,1024]{1,0:T(8,128)(2,1)S(1)}, u32[]{:S(2)}, u32[]{:S(2)}) collective-permute-start(bf16[256,1024]{1,0:T(8,128)(2,1)} %c0.3), channel_id=1, source_target_pairs={{0,4},{4,8},{8,12},{12,0},{1,5},{5,9},{9,13},{13,1},{2,6},{6,10},{... | collective-permute-start | bytes 1572872 | tf_op jit(solution)/shard_map/ppermute | solution.py:29
  2.8 20.0 %collective-permute-start.1 = (bf16[256,1024]{1,0:T(8,128)(2,1)}, bf16[256,1024]{1,0:T(8,128)(2,1)S(1)}, u32[]{:S(2)}, u32[]{:S(2)}) collective-permute-start(bf16[256,1024]{1,0:T(8,128)(2,1)} %c0.3), channel_id=1, source_target_pairs={{0,12},{4,0},{8,4},{12,8},{1,13},{5,1},{9,5},{13,9},{2,14},{6,2},{... | collective-permute-start | bytes 1572872 | tf_op jit(solution)/shard_map/ppermute | solution.py:29
  7.2 18.4 %collective-permute-start.4 = (bf16[144,1024]{1,0:T(8,128)(2,1)S(1)}, bf16[144,1024]{1,0:T(8,128)(2,1)S(1)}, u32[]{:S(2)}, u32[]{:S(2)}) collective-permute-start(bf16[144,1024]{1,0:T(8,128)(2,1)S(1)} %get-tuple-element.43), channel_id=1, source_target_pairs={{0,16},{16,0},{1,17},{17,1},{2,18},{18,2},{3,19},{19,3},{4,20},{20... | collective-permute-start | bytes 884744 | tf_op jit(solution)/shard_map/ppermute | solution.py:29
  14.2 14.2 %collective-permute-start.3 = (bf16[2,144,1024]{2,1,0:T(8,128)(2,1)}, bf16[2,144,1024]{2,1,0:T(8,128)(2,1)}, u32[]{:S(2)}, u32[]{:S(2)}) collective-permute-start(bf16[2,144,1024]{2,1,0:T(8,128)(2,1)} %get-tuple-element.49), channel_id=1, source_target_pairs={{0,32},{32,0},{1,33},{33,1},{2,34},{34,2},{3,35},{35,3},{4,36},{36... | collective-permute-start | bytes 1769480 | tf_op jit(solution)/shard_map/ppermute | solution.py:29
  22.9 16.6 %collective-permute-start.2 = (bf16[256,1152]{1,0:T(8,128)(2,1)}, bf16[256,1152]{1,0:T(8,128)(2,1)S(1)}, u32[]{:S(2)}, u32[]{:S(2)}) collective-permute-start(bf16[256,1152]{1,0:T(8,128)(2,1)} %get-tuple-element.47), channel_id=1, source_target_pairs={{0,4},{4,8},{8,12},{12,0},{1,5},{5,9},{9,13},{13,1},{2,6},{6,10},{... | collective-permute-start | bytes 1769480 | tf_op jit(solution)/shard_map/ppermute | solution.py:29
  23.0 16.4 %collective-permute-start.6 = (bf16[256,1152]{1,0:T(8,128)(2,1)S(1)}, bf16[256,1152]{1,0:T(8,128)(2,1)S(1)}, u32[]{:S(2)}, u32[]{:S(2)}) collective-permute-start(bf16[256,1152]{1,0:T(8,128)(2,1)S(1)} %get-tuple-element.52), channel_id=1, source_target_pairs={{0,12},{4,0},{8,4},{12,8},{1,13},{5,1},{9,5},{13,9},{2,14},{6,2},{... | collective-permute-start | bytes 1769480 | tf_op jit(solution)/shard_map/ppermute | solution.py:29
  25.7 15.7 %collective-permute-start.7 = (bf16[2,144,1024]{2,1,0:T(8,128)(2,1)S(1)}, bf16[2,144,1024]{2,1,0:T(8,128)(2,1)}, u32[]{:S(2)}, u32[]{:S(2)}) collective-permute-start(bf16[2,144,1024]{2,1,0:T(8,128)(2,1)S(1)} %pad_maximum_fusion.refs_3_.refs_1_), channel_id=1, source_target_pairs={{0,1},{1,2},{2,3},{3,0},{4,5},{5,6},{6,7},{7,4},{8,9},{9,10},{10,1... | collective-permute-start | bytes 1769480 | tf_op jit(solution)/shard_map/ppermute | solution.py:29
  27.0 14.4 %collective-permute-start.8 = (bf16[2,144,1024]{2,1,0:T(8,128)(2,1)S(1)}, bf16[2,144,1024]{2,1,0:T(8,128)(2,1)}, u32[]{:S(2)}, u32[]{:S(2)}) collective-permute-start(bf16[2,144,1024]{2,1,0:T(8,128)(2,1)S(1)} %pad_maximum_fusion.refs_3_.refs_1_), channel_id=1, source_target_pairs={{0,3},{1,0},{2,1},{3,2},{4,7},{5,4},{6,5},{7,6},{8,11},{9,8},{10,9... | collective-permute-start | bytes 1769480 | tf_op jit(solution)/shard_map/ppermute | solution.py:29
  30.5 9.9 %collective-permute-start.5 = (f16[144,1024]{1,0:T(8,128)(2,1)}, f16[144,1024]{1,0:T(8,128)(2,1)}, u32[]{:S(2)}, u32[]{:S(2)}) collective-permute-start(f16[144,1024]{1,0:T(8,128)(2,1)} %fusion), channel_id=1, source_target_pairs={{0,64},{64,0},{128,192},{192,128},{1,65},{65,1},{129,193},{193,129... | collective-permute-start | bytes 884744 | tf_op jit(solution)/shard_map/ppermute | solution.py:33
  39.4 28.4 %collective-permute-start.14 = (bf16[256,2176]{1,0:T(8,128)(2,1)}, bf16[256,2176]{1,0:T(8,128)(2,1)S(1)}, u32[]{:S(2)}, u32[]{:S(2)}) collective-permute-start(bf16[256,2176]{1,0:T(8,128)(2,1)} %copy-done.10), channel_id=1, source_target_pairs={{0,8},{4,12},{8,0},{12,4},{1,9},{5,13},{9,1},{13,5},{2,10},{6,14},... | collective-permute-start | bytes 3342344 | tf_op jit(solution)/shard_map/ppermute | solution.py:29
  43.8 9.4 %collective-permute-start.9 = (f16[72,1024]{1,0:T(8,128)(2,1)}, f16[72,1024]{1,0:T(8,128)(2,1)}, u32[]{:S(2)}, u32[]{:S(2)}) collective-permute-start(f16[72,1024]{1,0:T(8,128)(2,1)} %dynamic-slice_convert_fusion), channel_id=1, source_target_pairs={{0,128},{64,192},{128,0},{192,64},{1,129},{65,193},{129,1},{193,65... | collective-permute-start | bytes 442376 | tf_op jit(solution)/shard_map/ppermute | solution.py:33
  46.0 17.9 %collective-permute-start.11 = (bf16[2,144,1024]{2,1,0:T(8,128)(2,1)S(1)}, bf16[2,144,1024]{2,1,0:T(8,128)(2,1)}, u32[]{:S(2)}, u32[]{:S(2)}) collective-permute-start(bf16[2,144,1024]{2,1,0:T(8,128)(2,1)S(1)} %pad_maximum_fusion.refs_3_.refs_1_), channel_id=1, source_target_pairs={{0,2},{1,3},{2,0},{3,1},{4,6},{5,7},{6,4},{7,5},{8,10},{9,11},{10,... | collective-permute-start | bytes 1769480 | tf_op jit(solution)/shard_map/ppermute | solution.py:29
  69.5 8.5 %collective-permute-start.15 = (bf16[144,1024]{1,0:T(8,128)(2,1)S(1)}, bf16[144,1024]{1,0:T(8,128)(2,1)S(1)}, u32[]{:S(2)}, u32[]{:S(2)}) collective-permute-start(bf16[144,1024]{1,0:T(8,128)(2,1)S(1)} %get-tuple-element.64), channel_id=1, source_target_pairs={{0,1},{1,2},{2,3},{3,0},{4,5},{5,6},{6,7},{7,4},{8,9},{9,10},{10,1... | collective-permute-start | bytes 884744 | tf_op jit(solution)/shard_map/ppermute | solution.py:29
  69.6 8.4 %collective-permute-start.16 = (bf16[144,1024]{1,0:T(8,128)(2,1)S(1)}, bf16[144,1024]{1,0:T(8,128)(2,1)S(1)}, u32[]{:S(2)}, u32[]{:S(2)}) collective-permute-start(bf16[144,1024]{1,0:T(8,128)(2,1)S(1)} %get-tuple-element.65), channel_id=1, source_target_pairs={{0,3},{1,0},{2,1},{3,2},{4,7},{5,4},{6,5},{7,6},{8,11},{9,8},{10,9... | collective-permute-start | bytes 884744 | tf_op jit(solution)/shard_map/ppermute | solution.py:29
  72.3 13.5 %collective-permute-start.12 = (bf16[256,1024]{1,0:T(8,128)(2,1)S(1)}, bf16[256,1024]{1,0:T(8,128)(2,1)S(1)}, u32[]{:S(2)}, u32[]{:S(2)}) collective-permute-start(bf16[256,1024]{1,0:T(8,128)(2,1)S(1)} %get-tuple-element.58), channel_id=1, source_target_pairs={{0,12},{4,0},{8,4},{12,8},{1,13},{5,1},{9,5},{13,9},{2,14},{6,2},{... | collective-permute-start | bytes 1572872 | tf_op jit(solution)/shard_map/ppermute | solution.py:29
  73.5 12.3 %collective-permute-start.13 = (bf16[256,1024]{1,0:T(8,128)(2,1)S(1)}, bf16[256,1024]{1,0:T(8,128)(2,1)S(1)}, u32[]{:S(2)}, u32[]{:S(2)}) collective-permute-start(bf16[256,1024]{1,0:T(8,128)(2,1)S(1)} %get-tuple-element.59), channel_id=1, source_target_pairs={{0,4},{4,8},{8,12},{12,0},{1,5},{5,9},{9,13},{13,1},{2,6},{6,10},{... | collective-permute-start | bytes 1572872 | tf_op jit(solution)/shard_map/ppermute | solution.py:29
  78.0 13.0 %collective-permute-start.18 = (f16[144,1024]{1,0:T(8,128)(2,1)S(1)}, f16[144,1024]{1,0:T(8,128)(2,1)S(1)}, u32[]{:S(2)}, u32[]{:S(2)}) collective-permute-start(f16[144,1024]{1,0:T(8,128)(2,1)S(1)} %get-tuple-element.69), channel_id=1, source_target_pairs={{0,32},{32,0},{1,33},{33,1},{2,34},{34,2},{3,35},{35,3},{4,36},{36... | collective-permute-start | bytes 884744 | tf_op jit(solution)/shard_map/ppermute | solution.py:29
  80.3 10.8 %collective-permute-start.20 = (f16[144,1024]{1,0:T(8,128)(2,1)S(1)}, f16[144,1024]{1,0:T(8,128)(2,1)S(1)}, u32[]{:S(2)}, u32[]{:S(2)}) collective-permute-start(f16[144,1024]{1,0:T(8,128)(2,1)S(1)} %collective-permute-done.19), channel_id=1, source_target_pairs={{0,32},{32,0},{1,33},{33,1},{2,34},{34,2},{3,35},{35,3},{4,36},{36... | collective-permute-start | bytes 884744 | tf_op jit(solution)/shard_map/ppermute | solution.py:29
  81.7 10.1 %collective-permute-start.21 = (bf16[144,1024]{1,0:T(8,128)(2,1)S(1)}, bf16[144,1024]{1,0:T(8,128)(2,1)S(1)}, u32[]{:S(2)}, u32[]{:S(2)}) collective-permute-start(bf16[144,1024]{1,0:T(8,128)(2,1)S(1)} %get-tuple-element.73), channel_id=1, source_target_pairs={{0,2},{1,3},{2,0},{3,1},{4,6},{5,7},{6,4},{7,5},{8,10},{9,11},{10,... | collective-permute-start | bytes 884744 | tf_op jit(solution)/shard_map/ppermute | solution.py:29
  88.2 15.2 %collective-permute-start.17 = (bf16[256,1024]{1,0:T(8,128)(2,1)S(1)}, bf16[256,1024]{1,0:T(8,128)(2,1)S(1)}, u32[]{:S(2)}, u32[]{:S(2)}) collective-permute-start(bf16[256,1024]{1,0:T(8,128)(2,1)S(1)} %keys1.1), channel_id=1, source_target_pairs={{0,8},{4,12},{8,0},{12,4},{1,9},{5,13},{9,1},{13,5},{2,10},{6,14},... | collective-permute-start | bytes 1572872 | tf_op jit(solution)/shard_map/ppermute | solution.py:29
  92.0 15.9 %collective-permute-start.22 = (bf16[144,1024]{1,0:T(8,128)(2,1)S(1)}, bf16[144,1024]{1,0:T(8,128)(2,1)S(1)}, u32[]{:S(2)}, u32[]{:S(2)}) collective-permute-start(bf16[144,1024]{1,0:T(8,128)(2,1)S(1)} %add_convert_fusion.1), channel_id=1, source_target_pairs={{0,16},{16,0},{1,17},{17,1},{2,18},{18,2},{3,19},{19,3},{4,20},{20... | collective-permute-start | bytes 884744 | tf_op jit(solution)/shard_map/ppermute | solution.py:29
  95.6 12.4 %collective-permute-start.25 = (bf16[144,1024]{1,0:T(8,128)(2,1)S(1)}, bf16[144,1024]{1,0:T(8,128)(2,1)S(1)}, u32[]{:S(2)}, u32[]{:S(2)}) collective-permute-start(bf16[144,1024]{1,0:T(8,128)(2,1)S(1)} %get-tuple-element.79), channel_id=1, source_target_pairs={{0,2},{1,3},{2,0},{3,1},{4,6},{5,7},{6,4},{7,5},{8,10},{9,11},{10,... | collective-permute-start | bytes 884744 | tf_op jit(solution)/shard_map/ppermute | solution.py:29
  96.7 13.8 %collective-permute-start.24 = (bf16[144,1024]{1,0:T(8,128)(2,1)S(1)}, bf16[144,1024]{1,0:T(8,128)(2,1)S(1)}, u32[]{:S(2)}, u32[]{:S(2)}) collective-permute-start(bf16[144,1024]{1,0:T(8,128)(2,1)S(1)} %get-tuple-element.77), channel_id=1, source_target_pairs={{0,3},{1,0},{2,1},{3,2},{4,7},{5,4},{6,5},{7,6},{8,11},{9,8},{10,9... | collective-permute-start | bytes 884744 | tf_op jit(solution)/shard_map/ppermute | solution.py:29
  98.0 14.4 %collective-permute-start.23 = (bf16[144,1024]{1,0:T(8,128)(2,1)S(1)}, bf16[144,1024]{1,0:T(8,128)(2,1)S(1)}, u32[]{:S(2)}, u32[]{:S(2)}) collective-permute-start(bf16[144,1024]{1,0:T(8,128)(2,1)S(1)} %get-tuple-element.75), channel_id=1, source_target_pairs={{0,1},{1,2},{2,3},{3,0},{4,5},{5,6},{6,7},{7,4},{8,9},{9,10},{10,1... | collective-permute-start | bytes 884744 | tf_op jit(solution)/shard_map/ppermute | solution.py:29
  (14 other events, 73.6 us)

commit v7 on v6

v7 whole, which is shorter than its diff:
```python
import functools

import jax
import jax.numpy as jnp
from jax import lax
from jax.experimental import pallas as pl
from jax.experimental.pallas import tpu as pltpu
from jax.sharding import Mesh, PartitionSpec as P

D = 4608
KV = 1024
ROWS = 144
WIDE = 576
TOK = 256
EARLY = 640
MSG = EARLY + KV
SCALE = float(D) ** -0.5
BF = jnp.bfloat16
F32 = jnp.float32
F16 = jnp.float16
UNIT = 512.0
LIMIT = 48 * 1024 * 1024


def _place():
    return [lax.axis_index(n) for n in ("zl", "core", "zh", "y", "x")]


def _shift(v, axis, k, size=4):
    return lax.ppermute(v, axis, [(i, (i + k) % size) for i in range(size)])


def _flip(v, axis, bit, size=4):
    return lax.ppermute(v, axis, [(i, i ^ bit) for i in range(size)])


def _after(v, *done):
    return lax.optimization_barrier((v, *done))[0]


def _call(kernel, name, outs, scratch=(), traffic=1024, **kw):
    return pl.pallas_call(
        kernel,
        name=name,
        out_shape=[jax.ShapeDtypeStruct(s, d) for s, d in outs],
        scratch_shapes=list(scratch),
        compiler_params=pltpu.CompilerParams(vmem_limit_bytes=LIMIT),
        cost_estimate=pl.CostEstimate(flops=0, bytes_accessed=traffic, transcendentals=0),
        **kw,
    )


def _vmem(n):
    return [pl.BlockSpec(memory_space=pltpu.VMEM)] * n


def _pick_kernel(index_ref, frag_ref, used_ref, give_ref, keep_ref, sems):
    core = _place()[1]
    copies = [
        pltpu.make_async_copy(frag_ref.at[0, index_ref[0]], used_ref, sems.at[0]),
        pltpu.make_async_copy(frag_ref.at[0, pl.ds(2 - 2 * core, 2)], give_ref, sems.at[1]),
        pltpu.make_async_copy(frag_ref.at[0, pl.ds(2 * core, 2)], keep_ref, sems.at[2]),
    ]
    for c in copies:
        c.start()
    for c in copies:
        c.wait()


def _pair_kernel(a_ref, b_ref, out_ref, sems):
    copies = [pltpu.make_async_copy(ref, out_ref.at[k], sems.at[k]) for k, ref in enumerate((a_ref, b_ref))]
    for c in copies:
        c.start()
    for c in copies:
        c.wait()


def _norm_kernel(x_ref, gain_ref, cot_ref, own_ref, n1_ref, n3_ref, first_ref, second_ref, held):
    _, _, zh, y, _ = _place()
    values = x_ref[...].astype(F32)
    stats = jnp.mean(values * values, axis=1, keepdims=True)
    normed = (values * lax.rsqrt(stats + 1e-06) * gain_ref[...]).astype(BF)
    for q in range(8):
        held[q] = normed[:, q * WIDE : (q + 1) * WIDE]
    other, same = (1 - zh) * 4, zh * 4
    for k, out in ((0, own_ref), (1, n1_ref), (3, n3_ref)):
        chunk = (y + k) & 3
        out[...] = jnp.concatenate([held[other + chunk], held[same + chunk]], axis=1)
    chunk = jnp.concatenate([held[other + (y ^ 2)], held[same + (y ^ 2)]], axis=1)
    first_ref[:, :EARLY] = chunk[:, :EARLY]
    first_ref[:, EARLY:] = cot_ref[...]
    second_ref[...] = chunk[:, EARLY:]


def _grad_kernel(half, n0, c0, n1, c1, n3, c3, *refs):
    far, outs, total = refs[: half + 1], refs[half + 1 : half + 5], refs[half + 5]
    x = _place()[4]
    near = slice(half * WIDE, (half + 1) * WIDE)
    n2 = far[0][:, :EARLY]
    if half:
        n2 = jnp.concatenate([n2, far[1][...]], axis=1)
    normed = jnp.concatenate([n[:, near] for n in (n0, n1, n2, n3)], axis=0)
    cot = jnp.concatenate([c0[...], c1[...], far[0][:, EARLY:], c3[...]], axis=0)
    total[...] = lax.dot_general(normed, cot, (((0,), (0,)), ((), ())), preferred_element_type=F32)
    for k, out in enumerate(outs):
        rows = pl.ds(pl.multiple_of(((x + k) & 3) * ROWS, 16), ROWS)
        out[...] = (total[rows, :] * SCALE).astype(out.dtype)


def _place_layer(pairs, layer):
    x = _place()[4]
    for k in range(4):
        for h in range(2):
            first = pl.multiple_of(h * WIDE + ((x + 4 - k) & 3) * ROWS, 16)
            layer[pl.ds(first, ROWS), :] = pairs[k][h]


def _near_keys_kernel(n0, n1, n3, p0, p1, p2, p3, o0, o1, o3, layer):
    _place_layer((p0, p1, p2, p3), layer)
    for block, out in ((n0, o0), (n1, o1), (n3, o3)):
        part = jnp.dot(block[...], layer[...], preferred_element_type=F32)
        out[...] = (part * SCALE).astype(out.dtype)


def _far_keys_kernel(first, second, p0, p1, p2, p3, out, layer):
    _place_layer((p0, p1, p2, p3), layer)
    part = jnp.dot(first[:, :EARLY], layer[:EARLY, :], preferred_element_type=F32)
    part += jnp.dot(second[...], layer[EARLY:, :], preferred_element_type=F32)
    out[...] = (part * SCALE).astype(out.dtype)


def _outer_kernel(place_ref, *refs):
    averages, (global_ref, momentum_ref, new_global_ref, new_momentum_ref) = refs[:4], refs[4:]

    for k in range(4):

        @pl.when(pl.program_id(0) == k)
        def _():
            mean = averages[k][...]
            momentum = 0.9 * momentum_ref[0] + mean
            new_momentum_ref[0] = momentum
            new_global_ref[0] = global_ref[0] - 0.7 * (mean + 0.9 * momentum)


def body(layer_index, inputs, norm_gain, cotangent, local_fragment, global_fragment, momentum):
    zl, core = lax.axis_index("zl"), lax.axis_index("core")
    hi, lo = zl >> 1, zl & 1
    any_spec = pl.BlockSpec(memory_space=pl.ANY)

    used, give, keep = _call(
        _pick_kernel,
        "pick",
        [((ROWS, KV), BF)] + [((2, ROWS, KV), BF)] * 2,
        [pltpu.SemaphoreType.DMA((3,))],
        in_specs=[pl.BlockSpec(memory_space=pltpu.SMEM), any_spec],
        out_specs=[any_spec] * 3,
    )(layer_index, local_fragment)
    c1, c3 = _shift(cotangent, "y", 1), _shift(cotangent, "y", 3)
    used_other = _shift(used, "zh", 1, 2)
    got = _shift(give, "core", 1, 2)

    rows = 64
    tile = lambda n: pl.BlockSpec((rows, n), lambda i: (i, 0))
    widths = (2 * WIDE, 2 * WIDE, 2 * WIDE, MSG, 2 * WIDE - EARLY)
    own, n1, n3, first, second = _call(
        _norm_kernel,
        "normed",
        [((TOK, n), BF) for n in widths],
        [pltpu.VMEM((8, rows, WIDE), BF)],
        grid=(TOK // rows,),
        in_specs=[tile(D), pl.BlockSpec((D,), lambda i: (0,)), tile(KV)],
        out_specs=[tile(n) for n in widths],
    )(inputs, _after(norm_gain, used), cotangent)
    r1, r3 = _shift(_after(n1, c1, c3), "y", 1), _shift(_after(n3, c1, c3), "y", 3)

    (pair,) = _call(
        _pair_kernel,
        "pair",
        [((2, ROWS, KV), BF)],
        [pltpu.SemaphoreType.DMA((2,))],
        in_specs=[any_spec] * 2,
        out_specs=[any_spec],
    )(_after(used_other, c1, c3), used)
    p1, p3 = _shift(pair, "x", 1), _shift(pair, "x", 3)
    p2 = _shift(_after(pair, r1, r3), "x", 2)
    pairs = [pair, p1, p2, p3]

    r2 = _shift(first, "y", 2)
    r4 = _shift(_after(second, r1, r3), "y", 2)

    got = _after(got, own)

    def delta(which):
        shared = lax.dynamic_index_in_dim(global_fragment, 2 * core + which, 0, keepdims=False)
        ours = lax.dynamic_index_in_dim(keep, which, 0, keepdims=False).astype(F32)
        theirs = lax.dynamic_index_in_dim(got, which, 0, keepdims=False).astype(F32)
        return ((shared - ours) + (shared - theirs)) * UNIT

    half = ROWS // 2
    near = _flip(delta(1 - lo).astype(F16), "zl", 1)
    sum4 = delta(lo) + _after(near, p1, p3).astype(F32)
    out = lax.dynamic_slice_in_dim(sum4, (1 - hi) * half, half, 0).astype(F16)
    far = _flip(_after(out, p1, p3), "zl", 2)
    sum8 = (lax.dynamic_slice_in_dim(sum4, hi * half, half, 0) + far.astype(F32)).astype(F16)
    peer = _flip(sum8, "zl", 2)
    mine = jnp.where(hi == 0, jnp.concatenate([sum8, peer]), jnp.concatenate([peer, sum8]))

    def grad(half, own, *far):
        return _call(
            functools.partial(_grad_kernel, half),
            f"grad{half}",
            [((ROWS, KV), F32)] + [((ROWS, KV), BF)] * 3,
            [pltpu.VMEM((WIDE, KV), F32)],
            in_specs=_vmem(6 + len(far)),
            out_specs=_vmem(4),
        )(own, cotangent, r1, c1, r3, c3, *far)

    def near_keys(own):
        return _call(
            _near_keys_kernel,
            "near_keys",
            [((TOK, KV), F32)] + [((TOK, KV), BF)] * 2,
            [pltpu.VMEM((2 * WIDE, KV), BF)],
            in_specs=_vmem(7),
            out_specs=_vmem(3),
        )(own, r1, r3, *pairs)

    g = grad(0, _after(own, p2), r2)
    a1, a3 = _shift(g[1], "x", 1), _shift(g[3], "x", 3)
    k0, k1, k3 = near_keys(_after(own, g[0], peer))
    e1, e3 = _shift(k1, "y", 3), _shift(k3, "y", 1)
    a2 = _shift(g[2], "x", 2)
    b = grad(1, _after(own, a1, a3), r2, r4)
    (k2,) = _call(
        _far_keys_kernel,
        "far_keys",
        [((TOK, KV), BF)],
        [pltpu.VMEM((2 * WIDE, KV), BF)],
        in_specs=_vmem(6),
        out_specs=_vmem(1),
    )(r2, _after(r4, k0), *pairs)
    next_layer = _flip(_after(mine, g[0]), "zl", 1)
    swapped = [_shift(_after(v, a1, a3), "core", 1, 2) for v in (mine, next_layer)]
    far_sum = (_after(g[0], b[0]) + sum(v.astype(F32) for v in (a1, a2, a3))).astype(BF)
    from_zh = _shift(far_sum, "zh", 1, 2)
    b1, b3 = [_shift(_after(b[k], a1, a3), "x", k) for k in (1, 3)]
    b2 = _shift(_after(b[2], far_sum, swapped[1]), "x", 2)
    weight_grad = (b[0] + sum(v.astype(F32) for v in (b1, b3, b2, from_zh)))[None]

    e2 = _shift(_after(k2, e1, e3), "y", 2)
    keys = k0 + sum(v.astype(F32) for v in (e1, e3, e2))

    averages = [mine, next_layer] + swapped
    averages = [v.astype(F32) / (8.0 * UNIT) for v in averages]

    def layer_of(k, place):
        return (jnp.where(k < 2, place[0], 1 - place[0]) * 2 + (place[1] ^ (k & 1)), 0, 0)

    block = pl.BlockSpec((1, ROWS, KV), layer_of)
    whole = pl.BlockSpec((ROWS, KV), lambda k, place: (0, 0))
    new_global, new_momentum = pl.pallas_call(
        _outer_kernel,
        name="outer_step",
        out_shape=[jax.ShapeDtypeStruct((4, ROWS, KV), F32)] * 2,
        grid_spec=pltpu.PrefetchScalarGridSpec(
            num_scalar_prefetch=1,
            grid=(4,),
            in_specs=[whole] * 4 + [block, block],
            out_specs=[block, block],
        ),
        compiler_params=pltpu.CompilerParams(vmem_limit_bytes=LIMIT),
        cost_estimate=pl.CostEstimate(flops=0, bytes_accessed=1024, transcendentals=0),
    )(jnp.stack([core, lo]).astype(jnp.int32), *averages, global_fragment, momentum)
    return keys.astype(BF), weight_grad, new_global, new_momentum


def solution(mesh):
    split = Mesh(mesh.devices.reshape(4, 2, 2, 4, 4), ("zl", "core", "zh", "y", "x"))
    replica, fsdp = ("zl", "core"), ("zh", "y", "x")
    placed = (
        P(replica),
        P(replica + fsdp, None),
        P(),
        P(replica + fsdp, None),
        P(replica, None, fsdp, None),
        P(None, fsdp, None),
        P(None, fsdp, None),
    )
    return jax.shard_map(
        body,
        mesh=split,
        in_specs=placed,
        out_specs=(
            P(replica + fsdp, None),
            P(replica, fsdp, None),
            P(None, fsdp, None),
            P(None, fsdp, None),
        ),
        check_vma=False,
    )
```

time: 114 us -> 127 us (1.11)
  waiting for transfers between devices: 34.4 us -> 21.8 us
  starting transfers between devices: 42.7 us -> 54 us
  local copies, waits for them, and re-layouts: 5.85 us -> 14.8 us
  Pallas kernels: 18.9 us -> 22.6 us
  other arithmetic: 9.89 us -> 11.2 us
    ppermute x22 -> x23, starting transfers between devices: 38.5 us -> 50 us  [_shift(): return lax.ppermute(v, axis, [(i, (i + k) % size) for i in range(size)])]
    unnamed x24 -> x46, local copies, waits for them, and re-layouts: 5.11 us -> 14.8 us
    ppermute x22 -> x23, waiting for transfers between devices: 21.7 us -> 13.4 us  [_shift(): return lax.ppermute(v, axis, [(i, (i + k) % size) for i in range(size)])]
    ppermute x4, waiting for transfers between devices: 12.7 us -> 8.44 us  [_flip(): return lax.ppermute(v, axis, [(i, i ^ bit) for i in range(size)])]
    pallas_call x2, Pallas kernels: 3.8 us -> 6.01 us  [grad(): _call(functools.partial(_grad_kernel, half), f'grad{half}', [((ROWS, KV),...]
    pallas_call x3 -> x4, Pallas kernels: 9.09 us -> 10.5 us  [the longest x1 4.15 us: near_keys(): _call(_near_keys_kernel, 'near_keys', [((TOK, KV), F32)] + [((TOK, KV), B...]
  transfers between devices with their start and end apart: 26 -> 27, of which waited for: 10 -> 5; matrix products, arithmetic and copies ran while one was open for 9% -> 8% of each run, Pallas kernels for 15% -> 18%
where the time goes in v7:
time: 127 us; the launch traced here: 126 us
  starting transfers between devices  54 us (43%)
  Pallas kernels  22.6 us (18%)
  waiting for transfers between devices  21.8 us (17%)
  local copies, waits for them, and re-layouts  14.8 us (12%)
  other arithmetic  11.2 us (9%)
  between operations  1.53 us (1%)
    ppermute x23, starting transfers between devices, _shift(): return lax.ppermute(v, axis, [(i, (i + k) % size) for i in range(size)])  50 us
    unnamed x46, local copies, waits for them, and re-layouts  14.8 us
    ppermute x23, waiting for transfers between devices, _shift(): return lax.ppermute(v, axis, [(i, (i + k) % size) for i in range(size)])  13.4 us
    ppermute x4, waiting for transfers between devices, _flip(): return lax.ppermute(v, axis, [(i, i ^ bit) for i in range(size)])  8.44 us
    pallas_call x2, Pallas kernels, grad(): _call(functools.partial(_grad_kernel, half), f'grad{half}', [((ROWS, KV),...  6.01 us
    pallas_call x1, Pallas kernels, body(): pl.pallas_call(_outer_kernel, name='outer_step', out_shape=[jax.ShapeDtyp...  5.14 us
    pallas_call x1, Pallas kernels, near_keys(): _call(_near_keys_kernel, 'near_keys', [((TOK, KV), F32)] + [((TOK, KV), B...  4.15 us
    ppermute x4, starting transfers between devices, _flip(): return lax.ppermute(v, axis, [(i, i ^ bit) for i in range(size)])  4.07 us
  transfers between devices with their start and end apart: 27, of which 5 were waited for; matrix products, arithmetic and copies ran while one was open for 8% of the time, Pallas kernels for 18%

profile of v7, /device:TPU:1, one launch (start us, length us, event | category | flops | bytes accessed | tf_op | source)
XLA Modules:
  0.0 126.0 jit_solution(4341011770216269996)
XLA Ops:
  0.6 2.2 %collective-permute-start.1 = (bf16[256,1024]{1,0:T(8,128)(2,1)}, bf16[256,1024]{1,0:T(8,128)(2,1)S(1)}, u32[]{:S(2)}, u32[]{:S(2)}) collective-permute-start(bf16[256,1024]{1,0:T(8,128)(2,1)} %c0.3), channel_id=1, source_target_pairs={{0,4},{4,8},{8,12},{12,0},{1,5},{5,9},{9,13},{13,1},{2,6},{6,10},{... | collective-permute-start | bytes 1572872 | tf_op jit(solution)/shard_map/ppermute | solution.py:30
  7.2 2.9 %collective-permute-start.7 = (bf16[2,144,1024]{2,1,0:T(8,128)(2,1)}, bf16[2,144,1024]{2,1,0:T(8,128)(2,1)}, u32[]{:S(2)}, u32[]{:S(2)}) collective-permute-start(bf16[2,144,1024]{2,1,0:T(8,128)(2,1)} %get-tuple-element.59), channel_id=1, source_target_pairs={{0,32},{32,0},{1,33},{33,1},{2,34},{34,2},{3,35},{35,3},{4,36},{36... | collective-permute-start | bytes 1769480 | tf_op jit(solution)/shard_map/ppermute | solution.py:30
  10.1 5.2 %collective-permute-start = (bf16[144,1024]{1,0:T(8,128)(2,1)S(1)}, bf16[144,1024]{1,0:T(8,128)(2,1)S(1)}, u32[]{:S(2)}, u32[]{:S(2)}) collective-permute-start(bf16[144,1024]{1,0:T(8,128)(2,1)S(1)} %get-tuple-element.46.b_ref), channel_id=1, source_target_pairs={{0,16},{16,0},{1,17},{17,1},{2,18},{18,2},{3,19},{19,3},{4,20},{20... | collective-permute-start | bytes 884744 | tf_op jit(solution)/shard_map/ppermute | solution.py:30
  16.4 1.7 %copy-done.10 = bf16[256,4608]{1,0:T(8,128)(2,1)S(1)} copy-done((bf16[256,4608]{1,0:T(8,128)(2,1)S(1)}, bf16[256,4608]{1,0:T(8,128)(2,1)}, u32[]{:S(2)}) %copy-start.10) | copy-done | bytes 2359320
  18.8 2.9 %normed.1 = (bf16[256,1152]{1,0:T(8,128)(2,1)S(1)}, bf16[256,1152]{1,0:T(8,128)(2,1)}, bf16[256,1152]{1,0:T(8,128)(2,1)}, bf16[256,1664]{1,0:T(8,128)(2,1)S(1)}, bf16[256,512]{1,0:T(8,128)(2,1)S(1)}) custom-call(bf16[256,4608]{1,0:T(8,128)(2,1)S(1)} %copy-done.10, f32[4608]{0:T(1024)S(1)} %copy-done.19, bf16[256,1024]{1,0:T(8,128)(2,1)S(1)} %copy-done.7), custom_call_target="tpu_custom_call" | custom-call | bytes 1024 | tf_op jit(solution)/shard_map/normed/pallas_call | solution.py:165
  25.8 2.6 %collective-permute-start.4 = (bf16[256,1152]{1,0:T(8,128)(2,1)}, bf16[256,1152]{1,0:T(8,128)(2,1)}, u32[]{:S(2)}, u32[]{:S(2)}) collective-permute-start(bf16[256,1152]{1,0:T(8,128)(2,1)} %get-tuple-element.53), channel_id=1, source_target_pairs={{0,12},{4,0},{8,4},{12,8},{1,13},{5,1},{9,5},{13,9},{2,14},{6,2},{... | collective-permute-start | bytes 1769480 | tf_op jit(solution)/shard_map/ppermute | solution.py:30
  32.0 1.8 %fusion = f16[144,1024]{1,0:T(8,128)(2,1)} fusion(f32[4,144,1024]{2,1,0:T(8,128)S(1)} %copy-done, s32[]{:T(128)S(6)} %select_n.32, bf16[2,144,1024]{2,1,0:T(8,128)(2,1)} %collective-permute-done.7, s32[]{:T(128)S(6)} %select_n.33, bf16[2,144,1024]{2,1,0:T(8,128)(2,1)S(1)} %get-tuple-element.58), kind=kLoop, calls=%fused_computation.9 | loop fusion | flops 1032192 | bytes 1474568 | tf_op jit(solution)/shard_map/mul | solution.py:197
  35.1 6.7 %collective-permute-done.3.n1 = bf16[256,1152]{1,0:T(8,128)(2,1)S(1)} collective-permute-done((bf16[256,1152]{1,0:T(8,128)(2,1)}, bf16[256,1152]{1,0:T(8,128)(2,1)S(1)}, u32[]{:S(2)}, u32[]{:S(2)}) %collective-permute-start.3) | collective-permute-done | bytes 589856 | tf_op jit(solution)/shard_map/ppermute | solution.py:30
  43.1 2.7 %collective-permute-start.5 = (bf16[2,144,1024]{2,1,0:T(8,128)(2,1)}, bf16[2,144,1024]{2,1,0:T(8,128)(2,1)}, u32[]{:S(2)}, u32[]{:S(2)}) collective-permute-start(bf16[2,144,1024]{2,1,0:T(8,128)(2,1)} %pair.1.p0), channel_id=1, source_target_pairs={{0,2},{1,3},{2,0},{3,1},{4,6},{5,7},{6,4},{7,5},{8,10},{9,11},{10,... | collective-permute-start | bytes 1769480 | tf_op jit(solution)/shard_map/ppermute | solution.py:30
  45.9 2.1 %bitcast_add_fusion = f32[144,1024]{1,0:T(8,128)} fusion(f16[144,1024]{1,0:T(8,128)(2,1)} %collective-permute-done.8, f32[4,144,1024]{2,1,0:T(8,128)S(1)} %copy-done, s32[]{:T(128)S(6)} %select_n.30, bf16[2,144,1024]{2,1,0:T(8,128)(2,1)} %collective-permute-done.7, s32[]{:T(128)S(6)} %select_n.31, bf16[2,144,1024]{2,1,0:T(8,128)(2,1)} %copy-done.18), kind=kLoop, calls=%fused_computation.1 | loop fusion | flops 1179648 | bytes 2064392 | tf_op jit(solution)/shard_map/add | solution.py:201
  48.0 1.6 %dynamic-slice_convert_fusion = f16[72,1024]{1,0:T(8,128)(2,1)} fusion(f32[144,1024]{1,0:T(8,128)} %bitcast_add_fusion, s32[]{:T(128)S(6)} %select_n.35), kind=kLoop, calls=%fused_computation.12 | loop fusion | flops 73728 | bytes 442372 | tf_op jit(solution)/shard_map/convert_element_type | solution.py:202
  50.8 8.4 %collective-permute-done.11 = f16[72,1024]{1,0:T(8,128)(2,1)} collective-permute-done((f16[72,1024]{1,0:T(8,128)(2,1)}, f16[72,1024]{1,0:T(8,128)(2,1)}, u32[]{:S(2)}, u32[]{:S(2)}) %collective-permute-start.11) | collective-permute-done | bytes 147488 | tf_op jit(solution)/shard_map/ppermute | solution.py:34
  59.2 1.7 %add_convert_fusion.2 = f16[72,1024]{1,0:T(8,128)(2,1)} fusion(f16[72,1024]{1,0:T(8,128)(2,1)} %collective-permute-done.11, f32[144,1024]{1,0:T(8,128)} %bitcast_add_fusion, s32[]{:T(128)S(6)} %select_n.34), kind=kLoop, calls=%fused_computation.11 | loop fusion | flops 221184 | bytes 589828 | tf_op jit(solution)/shard_map/convert_element_type | solution.py:204
  61.0 2.3 %collective-permute-start.15 = (bf16[256,512]{1,0:T(8,128)(2,1)S(1)}, bf16[256,512]{1,0:T(8,128)(2,1)S(1)}, u32[]{:S(2)}, u32[]{:S(2)}) collective-permute-start(bf16[256,512]{1,0:T(8,128)(2,1)S(1)} %copy-done.22), channel_id=1, source_target_pairs={{0,8},{4,12},{8,0},{12,4},{1,9},{5,13},{9,1},{13,5},{2,10},{6,14},... | collective-permute-start | bytes 786440 | tf_op jit(solution)/shard_map/ppermute | solution.py:30
  68.9 2.8 %grad0.1 = (f32[144,1024]{1,0:T(8,128)S(1)}, bf16[144,1024]{1,0:T(8,128)(2,1)S(1)}, bf16[144,1024]{1,0:T(8,128)(2,1)S(1)}, bf16[144,1024]{1,0:T(8,128)(2,1)S(1)}) custom-call(bf16[256,1152]{1,0:T(8,128)(2,1)S(1)} %copy-done.2, bf16[256,1024]{1,0:T(8,128)(2,1)S(1)} %copy-done.8, bf16[256,1152]{1,0:T(8,128)(2,1)S(1)} %copy-done.5, ...), custom_call_target="tpu_custom_call" | custom-call | bytes 1024 | tf_op jit(solution)/shard_map/grad0/pallas_call | solution.py:209
  73.0 1.7 %collective-permute-start.18 = (bf16[144,1024]{1,0:T(8,128)(2,1)S(1)}, bf16[144,1024]{1,0:T(8,128)(2,1)S(1)}, u32[]{:S(2)}, u32[]{:S(2)}) collective-permute-start(bf16[144,1024]{1,0:T(8,128)(2,1)S(1)} %get-tuple-element.72), channel_id=1, source_target_pairs={{0,3},{1,0},{2,1},{3,2},{4,7},{5,4},{6,5},{7,6},{8,11},{9,8},{10,9... | collective-permute-start | bytes 884744 | tf_op jit(solution)/shard_map/ppermute | solution.py:30
  78.1 4.1 %near_keys.1 = (f32[256,1024]{1,0:T(8,128)S(1)}, bf16[256,1024]{1,0:T(8,128)(2,1)S(1)}, bf16[256,1024]{1,0:T(8,128)(2,1)S(1)}) custom-call(bf16[256,1152]{1,0:T(8,128)(2,1)S(1)} %copy-done.3, bf16[256,1152]{1,0:T(8,128)(2,1)S(1)} %copy-done.6, bf16[256,1152]{1,0:T(8,128)(2,1)} %collective-permute-done.4.n3, bf16[2,144,1024]{2,1,0:T(8,128)(2,1)} %pair.1.p0, ...), custom_call_target="tpu_custom_call" | custom-call | bytes 1024 | tf_op jit(solution)/shard_map/near_keys/pallas_call | solution.py:219
  83.9 2.6 %far_keys.1 = bf16[256,1024]{1,0:T(8,128)(2,1)S(1)} custom-call(bf16[256,1664]{1,0:T(8,128)(2,1)S(1)} %collective-permute-done.6.refs_0_.first, bf16[256,512]{1,0:T(8,128)(2,1)S(1)} %collective-permute-done.15.second.refs_1_, bf16[2,144,1024]{2,1,0:T(8,128)(2,1)} %pair.1.p0, bf16[2,144,1024]{2,1,0:T(8,128)(2,1)} %collective-permute-done.9.p1, ...), custom_call_target="tpu_custom_call" | custom-call | bytes 1024 | tf_op jit(solution)/shard_map/far_keys/pallas_call | solution.py:234
  86.6 3.2 %grad1.1 = (f32[144,1024]{1,0:T(8,128)S(1)}, bf16[144,1024]{1,0:T(8,128)(2,1)S(1)}, bf16[144,1024]{1,0:T(8,128)(2,1)S(1)}, bf16[144,1024]{1,0:T(8,128)(2,1)S(1)}) custom-call(bf16[256,1152]{1,0:T(8,128)(2,1)S(1)} %copy-done.3, bf16[256,1024]{1,0:T(8,128)(2,1)S(1)} %copy-done.9, bf16[256,1152]{1,0:T(8,128)(2,1)S(1)} %copy-done.6, ...), custom_call_target="tpu_custom_call" | custom-call | bytes 1024 | tf_op jit(solution)/shard_map/grad1/pallas_call | solution.py:209
  89.8 5.6 %collective-permute-start.23 = (f16[144,1024]{1,0:T(8,128)(2,1)S(1)}, f16[144,1024]{1,0:T(8,128)(2,1)S(1)}, u32[]{:S(2)}, u32[]{:S(2)}) collective-permute-start(f16[144,1024]{1,0:T(8,128)(2,1)S(1)} %collective-permute-done.22), channel_id=1, source_target_pairs={{0,32},{32,0},{1,33},{33,1},{2,34},{34,2},{3,35},{35,3},{4,36},{36... | collective-permute-start | bytes 884744 | tf_op jit(solution)/shard_map/ppermute | solution.py:30
  95.6 11.4 %collective-permute-start.25 = (bf16[144,1024]{1,0:T(8,128)(2,1)S(1)}, bf16[144,1024]{1,0:T(8,128)(2,1)S(1)}, u32[]{:S(2)}, u32[]{:S(2)}) collective-permute-start(bf16[144,1024]{1,0:T(8,128)(2,1)S(1)} %add_convert_fusion.1), channel_id=1, source_target_pairs={{0,16},{16,0},{1,17},{17,1},{2,18},{18,2},{3,19},{19,3},{4,20},{20... | collective-permute-start | bytes 884744 | tf_op jit(solution)/shard_map/ppermute | solution.py:30
  108.9 1.9 %collective-permute-start.24 = (bf16[144,1024]{1,0:T(8,128)(2,1)S(1)}, bf16[144,1024]{1,0:T(8,128)(2,1)S(1)}, u32[]{:S(2)}, u32[]{:S(2)}) collective-permute-start(bf16[144,1024]{1,0:T(8,128)(2,1)S(1)} %get-tuple-element.84), channel_id=1, source_target_pairs={{0,2},{1,3},{2,0},{3,1},{4,6},{5,7},{6,4},{7,5},{8,10},{9,11},{10,... | collective-permute-start | bytes 884744 | tf_op jit(solution)/shard_map/ppermute | solution.py:30
  112.4 5.1 %outer_step.1 = (f32[4,144,1024]{2,1,0:T(8,128)}, f32[4,144,1024]{2,1,0:T(8,128)}) custom-call(s32[2]{0:T(128)S(1)} %pad_add_fusion.place_ref, f32[144,1024]{1,0:T(8,128)S(1)} %get-tuple-element.88.refs_0_, f32[144,1024]{1,0:T(8,128)S(1)} %convert_multiply_fusion.2.refs_1_, f32[144,1024]{1,0:T(8,128)S(1)} %convert_multiply_fusion.1.refs_2_, ...), custom_call_target="tpu_custom_call" | custom-call | bytes 1024 | tf_op jit(solution)/shard_map/outer_step/pallas_call | solution.py:261
  117.6 6.2 %collective-permute-done.24 = bf16[144,1024]{1,0:T(8,128)(2,1)S(1)} collective-permute-done((bf16[144,1024]{1,0:T(8,128)(2,1)S(1)}, bf16[144,1024]{1,0:T(8,128)(2,1)S(1)}, u32[]{:S(2)}, u32[]{:S(2)}) %collective-permute-start.24) | collective-permute-done | bytes 294944 | tf_op jit(solution)/shard_map/ppermute | solution.py:30
  (96 shorter events, 34.8 us)
Async XLA Ops:
  0.6 23.5 %collective-permute-start.1 = (bf16[256,1024]{1,0:T(8,128)(2,1)}, bf16[256,1024]{1,0:T(8,128)(2,1)S(1)}, u32[]{:S(2)}, u32[]{:S(2)}) collective-permute-start(bf16[256,1024]{1,0:T(8,128)(2,1)} %c0.3), channel_id=1, source_target_pairs={{0,4},{4,8},{8,12},{12,0},{1,5},{5,9},{9,13},{13,1},{2,6},{6,10},{... | collective-permute-start | bytes 1572872 | tf_op jit(solution)/shard_map/ppermute | solution.py:30
  2.8 22.1 %collective-permute-start.2 = (bf16[256,1024]{1,0:T(8,128)(2,1)}, bf16[256,1024]{1,0:T(8,128)(2,1)S(1)}, u32[]{:S(2)}, u32[]{:S(2)}) collective-permute-start(bf16[256,1024]{1,0:T(8,128)(2,1)} %c0.3), channel_id=1, source_target_pairs={{0,12},{4,0},{8,4},{12,8},{1,13},{5,1},{9,5},{13,9},{2,14},{6,2},{... | collective-permute-start | bytes 1572872 | tf_op jit(solution)/shard_map/ppermute | solution.py:30
  7.2 24.8 %collective-permute-start.7 = (bf16[2,144,1024]{2,1,0:T(8,128)(2,1)}, bf16[2,144,1024]{2,1,0:T(8,128)(2,1)}, u32[]{:S(2)}, u32[]{:S(2)}) collective-permute-start(bf16[2,144,1024]{2,1,0:T(8,128)(2,1)} %get-tuple-element.59), channel_id=1, source_target_pairs={{0,32},{32,0},{1,33},{33,1},{2,34},{34,2},{3,35},{35,3},{4,36},{36... | collective-permute-start | bytes 1769480 | tf_op jit(solution)/shard_map/ppermute | solution.py:30
  10.1 18.3 %collective-permute-start = (bf16[144,1024]{1,0:T(8,128)(2,1)S(1)}, bf16[144,1024]{1,0:T(8,128)(2,1)S(1)}, u32[]{:S(2)}, u32[]{:S(2)}) collective-permute-start(bf16[144,1024]{1,0:T(8,128)(2,1)S(1)} %get-tuple-element.46.b_ref), channel_id=1, source_target_pairs={{0,16},{16,0},{1,17},{17,1},{2,18},{18,2},{3,19},{19,3},{4,20},{20... | collective-permute-start | bytes 884744 | tf_op jit(solution)/shard_map/ppermute | solution.py:30
  25.7 16.1 %collective-permute-start.3 = (bf16[256,1152]{1,0:T(8,128)(2,1)}, bf16[256,1152]{1,0:T(8,128)(2,1)S(1)}, u32[]{:S(2)}, u32[]{:S(2)}) collective-permute-start(bf16[256,1152]{1,0:T(8,128)(2,1)} %get-tuple-element.51), channel_id=1, source_target_pairs={{0,4},{4,8},{8,12},{12,0},{1,5},{5,9},{9,13},{13,1},{2,6},{6,10},{... | collective-permute-start | bytes 1769480 | tf_op jit(solution)/shard_map/ppermute | solution.py:30
  25.8 17.3 %collective-permute-start.4 = (bf16[256,1152]{1,0:T(8,128)(2,1)}, bf16[256,1152]{1,0:T(8,128)(2,1)}, u32[]{:S(2)}, u32[]{:S(2)}) collective-permute-start(bf16[256,1152]{1,0:T(8,128)(2,1)} %get-tuple-element.53), channel_id=1, source_target_pairs={{0,12},{4,0},{8,4},{12,8},{1,13},{5,1},{9,5},{13,9},{2,14},{6,2},{... | collective-permute-start | bytes 1769480 | tf_op jit(solution)/shard_map/ppermute | solution.py:30
  29.2 16.6 %collective-permute-start.9 = (bf16[2,144,1024]{2,1,0:T(8,128)(2,1)}, bf16[2,144,1024]{2,1,0:T(8,128)(2,1)}, u32[]{:S(2)}, u32[]{:S(2)}) collective-permute-start(bf16[2,144,1024]{2,1,0:T(8,128)(2,1)} %pair.1.p0), channel_id=1, source_target_pairs={{0,1},{1,2},{2,3},{3,0},{4,5},{5,6},{6,7},{7,4},{8,9},{9,10},{10,1... | collective-permute-start | bytes 1769480 | tf_op jit(solution)/shard_map/ppermute | solution.py:30
  30.5 15.3 %collective-permute-start.10 = (bf16[2,144,1024]{2,1,0:T(8,128)(2,1)}, bf16[2,144,1024]{2,1,0:T(8,128)(2,1)}, u32[]{:S(2)}, u32[]{:S(2)}) collective-permute-start(bf16[2,144,1024]{2,1,0:T(8,128)(2,1)} %pair.1.p0), channel_id=1, source_target_pairs={{0,3},{1,0},{2,1},{3,2},{4,7},{5,4},{6,5},{7,6},{8,11},{9,8},{10,9... | collective-permute-start | bytes 1769480 | tf_op jit(solution)/shard_map/ppermute | solution.py:30
  33.8 12.0 %collective-permute-start.8 = (f16[144,1024]{1,0:T(8,128)(2,1)}, f16[144,1024]{1,0:T(8,128)(2,1)}, u32[]{:S(2)}, u32[]{:S(2)}) collective-permute-start(f16[144,1024]{1,0:T(8,128)(2,1)} %fusion), channel_id=1, source_target_pairs={{0,64},{64,0},{128,192},{192,128},{1,65},{65,1},{129,193},{193,129... | collective-permute-start | bytes 884744 | tf_op jit(solution)/shard_map/ppermute | solution.py:34
  42.6 21.1 %collective-permute-start.6 = (bf16[256,1664]{1,0:T(8,128)(2,1)}, bf16[256,1664]{1,0:T(8,128)(2,1)S(1)}, u32[]{:S(2)}, u32[]{:S(2)}) collective-permute-start(bf16[256,1664]{1,0:T(8,128)(2,1)} %copy-done.20), channel_id=1, source_target_pairs={{0,8},{4,12},{8,0},{12,4},{1,9},{5,13},{9,1},{13,5},{2,10},{6,14},... | collective-permute-start | bytes 2555912 | tf_op jit(solution)/shard_map/ppermute | solution.py:30
  43.1 20.2 %collective-permute-start.5 = (bf16[2,144,1024]{2,1,0:T(8,128)(2,1)}, bf16[2,144,1024]{2,1,0:T(8,128)(2,1)}, u32[]{:S(2)}, u32[]{:S(2)}) collective-permute-start(bf16[2,144,1024]{2,1,0:T(8,128)(2,1)} %pair.1.p0), channel_id=1, source_target_pairs={{0,2},{1,3},{2,0},{3,1},{4,6},{5,7},{6,4},{7,5},{8,10},{9,11},{10,... | collective-permute-start | bytes 1769480 | tf_op jit(solution)/shard_map/ppermute | solution.py:30
  61.0 13.7 %collective-permute-start.12 = (f16[72,1024]{1,0:T(8,128)(2,1)}, f16[72,1024]{1,0:T(8,128)(2,1)}, u32[]{:S(2)}, u32[]{:S(2)}) collective-permute-start(f16[72,1024]{1,0:T(8,128)(2,1)} %add_convert_fusion.2), channel_id=1, source_target_pairs={{0,128},{64,192},{128,0},{192,64},{1,129},{65,193},{129,1},{193,65... | collective-permute-start | bytes 442376 | tf_op jit(solution)/shard_map/ppermute | solution.py:34
  61.0 21.3 %collective-permute-start.15 = (bf16[256,512]{1,0:T(8,128)(2,1)S(1)}, bf16[256,512]{1,0:T(8,128)(2,1)S(1)}, u32[]{:S(2)}, u32[]{:S(2)}) collective-permute-start(bf16[256,512]{1,0:T(8,128)(2,1)S(1)} %copy-done.22), channel_id=1, source_target_pairs={{0,8},{4,12},{8,0},{12,4},{1,9},{5,13},{9,1},{13,5},{2,10},{6,14},... | collective-permute-start | bytes 786440 | tf_op jit(solution)/shard_map/ppermute | solution.py:30
  71.7 11.2 %collective-permute-start.17 = (bf16[144,1024]{1,0:T(8,128)(2,1)S(1)}, bf16[144,1024]{1,0:T(8,128)(2,1)S(1)}, u32[]{:S(2)}, u32[]{:S(2)}) collective-permute-start(bf16[144,1024]{1,0:T(8,128)(2,1)S(1)} %get-tuple-element.71), channel_id=1, source_target_pairs={{0,1},{1,2},{2,3},{3,0},{4,5},{5,6},{6,7},{7,4},{8,9},{9,10},{10,1... | collective-permute-start | bytes 884744 | tf_op jit(solution)/shard_map/ppermute | solution.py:30
  73.0 13.6 %collective-permute-start.18 = (bf16[144,1024]{1,0:T(8,128)(2,1)S(1)}, bf16[144,1024]{1,0:T(8,128)(2,1)S(1)}, u32[]{:S(2)}, u32[]{:S(2)}) collective-permute-start(bf16[144,1024]{1,0:T(8,128)(2,1)S(1)} %get-tuple-element.72), channel_id=1, source_target_pairs={{0,3},{1,0},{2,1},{3,2},{4,7},{5,4},{6,5},{7,6},{8,11},{9,8},{10,9... | collective-permute-start | bytes 884744 | tf_op jit(solution)/shard_map/ppermute | solution.py:30
  76.0 13.9 %collective-permute-start.22 = (f16[144,1024]{1,0:T(8,128)(2,1)S(1)}, f16[144,1024]{1,0:T(8,128)(2,1)S(1)}, u32[]{:S(2)}, u32[]{:S(2)}) collective-permute-start(f16[144,1024]{1,0:T(8,128)(2,1)S(1)} %get-tuple-element.85), channel_id=1, source_target_pairs={{0,64},{64,0},{128,192},{192,128},{1,65},{65,1},{129,193},{193,129... | collective-permute-start | bytes 884744 | tf_op jit(solution)/shard_map/ppermute | solution.py:34
  77.6 17.9 %collective-permute-start.21 = (bf16[144,1024]{1,0:T(8,128)(2,1)S(1)}, bf16[144,1024]{1,0:T(8,128)(2,1)S(1)}, u32[]{:S(2)}, u32[]{:S(2)}) collective-permute-start(bf16[144,1024]{1,0:T(8,128)(2,1)S(1)} %get-tuple-element.81), channel_id=1, source_target_pairs={{0,2},{1,3},{2,0},{3,1},{4,6},{5,7},{6,4},{7,5},{8,10},{9,11},{10,... | collective-permute-start | bytes 884744 | tf_op jit(solution)/shard_map/ppermute | solution.py:30
  82.3 25.1 %collective-permute-start.13 = (bf16[256,1024]{1,0:T(8,128)(2,1)S(1)}, bf16[256,1024]{1,0:T(8,128)(2,1)S(1)}, u32[]{:S(2)}, u32[]{:S(2)}) collective-permute-start(bf16[256,1024]{1,0:T(8,128)(2,1)S(1)} %get-tuple-element.65), channel_id=1, source_target_pairs={{0,12},{4,0},{8,4},{12,8},{1,13},{5,1},{9,5},{13,9},{2,14},{6,2},{... | collective-permute-start | bytes 1572872 | tf_op jit(solution)/shard_map/ppermute | solution.py:30
  82.9 24.9 %collective-permute-start.14 = (bf16[256,1024]{1,0:T(8,128)(2,1)S(1)}, bf16[256,1024]{1,0:T(8,128)(2,1)S(1)}, u32[]{:S(2)}, u32[]{:S(2)}) collective-permute-start(bf16[256,1024]{1,0:T(8,128)(2,1)S(1)} %get-tuple-element.66), channel_id=1, source_target_pairs={{0,4},{4,8},{8,12},{12,0},{1,5},{5,9},{9,13},{13,1},{2,6},{6,10},{... | collective-permute-start | bytes 1572872 | tf_op jit(solution)/shard_map/ppermute | solution.py:30
  89.8 19.1 %collective-permute-start.23 = (f16[144,1024]{1,0:T(8,128)(2,1)S(1)}, f16[144,1024]{1,0:T(8,128)(2,1)S(1)}, u32[]{:S(2)}, u32[]{:S(2)}) collective-permute-start(f16[144,1024]{1,0:T(8,128)(2,1)S(1)} %collective-permute-done.22), channel_id=1, source_target_pairs={{0,32},{32,0},{1,33},{33,1},{2,34},{34,2},{3,35},{35,3},{4,36},{36... | collective-permute-start | bytes 884744 | tf_op jit(solution)/shard_map/ppermute | solution.py:30
  95.6 21.9 %collective-permute-start.25 = (bf16[144,1024]{1,0:T(8,128)(2,1)S(1)}, bf16[144,1024]{1,0:T(8,128)(2,1)S(1)}, u32[]{:S(2)}, u32[]{:S(2)}) collective-permute-start(bf16[144,1024]{1,0:T(8,128)(2,1)S(1)} %add_convert_fusion.1), channel_id=1, source_target_pairs={{0,16},{16,0},{1,17},{17,1},{2,18},{18,2},{3,19},{19,3},{4,20},{20... | collective-permute-start | bytes 884744 | tf_op jit(solution)/shard_map/ppermute | solution.py:30
  107.4 10.2 %collective-permute-start.20 = (bf16[144,1024]{1,0:T(8,128)(2,1)S(1)}, bf16[144,1024]{1,0:T(8,128)(2,1)S(1)}, u32[]{:S(2)}, u32[]{:S(2)}) collective-permute-start(bf16[144,1024]{1,0:T(8,128)(2,1)S(1)} %get-tuple-element.78), channel_id=1, source_target_pairs={{0,3},{1,0},{2,1},{3,2},{4,7},{5,4},{6,5},{7,6},{8,11},{9,8},{10,9... | collective-permute-start | bytes 884744 | tf_op jit(solution)/shard_map/ppermute | solution.py:30
  108.9 14.8 %collective-permute-start.24 = (bf16[144,1024]{1,0:T(8,128)(2,1)S(1)}, bf16[144,1024]{1,0:T(8,128)(2,1)S(1)}, u32[]{:S(2)}, u32[]{:S(2)}) collective-permute-start(bf16[144,1024]{1,0:T(8,128)(2,1)S(1)} %get-tuple-element.84), channel_id=1, source_target_pairs={{0,2},{1,3},{2,0},{3,1},{4,6},{5,7},{6,4},{7,5},{8,10},{9,11},{10,... | collective-permute-start | bytes 884744 | tf_op jit(solution)/shard_map/ppermute | solution.py:30
  110.9 14.0 %collective-permute-start.16 = (bf16[256,1024]{1,0:T(8,128)(2,1)S(1)}, bf16[256,1024]{1,0:T(8,128)(2,1)S(1)}, u32[]{:S(2)}, u32[]{:S(2)}) collective-permute-start(bf16[256,1024]{1,0:T(8,128)(2,1)S(1)} %far_keys.1), channel_id=1, source_target_pairs={{0,8},{4,12},{8,0},{12,4},{1,9},{5,13},{9,1},{13,5},{2,10},{6,14},... | collective-permute-start | bytes 1572872 | tf_op jit(solution)/shard_map/ppermute | solution.py:30
  (26 other events, 146.6 us)

commit v8 on v7

--- a/solution.py
+++ b/solution.py
@@ -19,7 +19,7 @@
 F32 = jnp.float32
 F16 = jnp.float16
 UNIT = 512.0
-LIMIT = 48 * 1024 * 1024
+LIMIT = 62 * 1024 * 1024
 
 
 def _place():

time: 127 us -> 195 us (1.54)
  Pallas kernels: 22.6 us -> 96 us
  starting transfers between devices: 54 us -> 66.6 us
  waiting for transfers between devices: 21.8 us -> 9.33 us
  local copies, waits for them, and re-layouts: 14.8 us -> 4.05 us
  other arithmetic: 11.2 us -> 17.3 us
    pallas_call x1, Pallas kernels: 0.91 us -> 45.8 us  [body(): _call(_pick_kernel, 'pick', [((ROWS, KV), BF)] + [((2, ROWS, KV), BF)] *...]
    pallas_call x1, Pallas kernels: 0.83 us -> 19 us  [body(): _call(_pair_kernel, 'pair', [((2, ROWS, KV), BF)], [pltpu.SemaphoreType.D...]
    ppermute x4, starting transfers between devices: 4.07 us -> 16.1 us  [_flip(): return lax.ppermute(v, axis, [(i, i ^ bit) for i in range(size)])]
    unnamed x46 -> x26, local copies, waits for them, and re-layouts: 14.8 us -> 4.05 us
    ppermute x23, waiting for transfers between devices: 13.4 us -> 3.44 us  [_shift(): return lax.ppermute(v, axis, [(i, (i + k) % size) for i in range(size)])]
    pallas_call x2, Pallas kernels: 6.01 us -> 10.6 us  [grad(): _call(functools.partial(_grad_kernel, half), f'grad{half}', [((ROWS, KV),...]
    div x4, other arithmetic: 1.44 us -> 5.88 us  [body(): averages = [v.astype(F32) / (8.0 * UNIT) for v in averages]]
    ppermute x4, waiting for transfers between devices: 8.44 us -> 5.89 us  [_flip(): return lax.ppermute(v, axis, [(i, i ^ bit) for i in range(size)])]
  transfers between devices with their start and end apart: 27 -> 27, of which waited for: 5 -> 3; matrix products, arithmetic and copies ran while one was open for 8% -> 8% of each run, Pallas kernels for 18% -> 49%
where the time goes in v8:
time: 195 us
  Pallas kernels  96 us (49%)
  starting transfers between devices  66.6 us (34%)
  other arithmetic  17.3 us (9%)
  waiting for transfers between devices  9.33 us (5%)
  local copies, waits for them, and re-layouts  4.05 us (2%)
    ppermute x23, starting transfers between devices, _shift(): return lax.ppermute(v, axis, [(i, (i + k) % size) for i in range(size)])  50.6 us
    pallas_call x1, Pallas kernels, body(): _call(_pick_kernel, 'pick', [((ROWS, KV), BF)] + [((2, ROWS, KV), BF)] *...  45.8 us
    pallas_call x1, Pallas kernels, body(): _call(_pair_kernel, 'pair', [((2, ROWS, KV), BF)], [pltpu.SemaphoreType.D...  19 us
    ppermute x4, starting transfers between devices, _flip(): return lax.ppermute(v, axis, [(i, i ^ bit) for i in range(size)])  16.1 us
    pallas_call x2, Pallas kernels, grad(): _call(functools.partial(_grad_kernel, half), f'grad{half}', [((ROWS, KV),...  10.6 us
    pallas_call x1, Pallas kernels, body(): pl.pallas_call(_outer_kernel, name='outer_step', out_shape=[jax.ShapeDtyp...  6.74 us
    ppermute x4, waiting for transfers between devices, _flip(): return lax.ppermute(v, axis, [(i, i ^ bit) for i in range(size)])  5.89 us
    div x4, other arithmetic, body(): averages = [v.astype(F32) / (8.0 * UNIT) for v in averages]  5.88 us
  transfers between devices with their start and end apart: 27, of which 3 were waited for; matrix products, arithmetic and copies ran while one was open for 8% of the time, Pallas kernels for 49%

profile of v8, /device:TPU:1, one launch (start us, length us, event | category | flops | bytes accessed | tf_op | source)
XLA Modules:
  0.0 194.7 jit_solution(2067667802484951788)
XLA Ops:
  0.6 2.2 %collective-permute-start.1 = (bf16[256,1024]{1,0:T(8,128)(2,1)}, bf16[256,1024]{1,0:T(8,128)(2,1)S(1)}, u32[]{:S(2)}, u32[]{:S(2)}) collective-permute-start(bf16[256,1024]{1,0:T(8,128)(2,1)} %c0.3), channel_id=1, source_target_pairs={{0,4},{4,8},{8,12},{12,0},{1,5},{5,9},{9,13},{13,1},{2,6},{6,10},{... | collective-permute-start | bytes 1572872 | tf_op jit(solution)/shard_map/ppermute | solution.py:30
  5.0 45.8 %pick.1 = (bf16[144,1024]{1,0:T(8,128)(2,1)}, bf16[2,144,1024]{2,1,0:T(8,128)(2,1)}, bf16[2,144,1024]{2,1,0:T(8,128)(2,1)}) custom-call(s32[1]{0:T(128)S(6)} %copy.11.index_ref, bf16[1,4,144,1024]{3,2,1,0:T(8,128)(2,1)} %frag_ref.1), custom_call_target="tpu_custom_call" | custom-call | bytes 1024 | tf_op jit(solution)/shard_map/pick/pallas_call | solution.py:150
  50.8 2.9 %collective-permute-start.7 = (bf16[2,144,1024]{2,1,0:T(8,128)(2,1)}, bf16[2,144,1024]{2,1,0:T(8,128)(2,1)}, u32[]{:S(2)}, u32[]{:S(2)}) collective-permute-start(bf16[2,144,1024]{2,1,0:T(8,128)(2,1)} %get-tuple-element.59), channel_id=1, source_target_pairs={{0,32},{32,0},{1,33},{33,1},{2,34},{34,2},{3,35},{35,3},{4,36},{36... | collective-permute-start | bytes 1769480 | tf_op jit(solution)/shard_map/ppermute | solution.py:30
  53.7 5.2 %collective-permute-start = (bf16[144,1024]{1,0:T(8,128)(2,1)}, bf16[144,1024]{1,0:T(8,128)(2,1)}, u32[]{:S(2)}, u32[]{:S(2)}) collective-permute-start(bf16[144,1024]{1,0:T(8,128)(2,1)} %get-tuple-element.46.b_ref), channel_id=1, source_target_pairs={{0,16},{16,0},{1,17},{17,1},{2,18},{18,2},{3,19},{19,3},{4,20},{20... | collective-permute-start | bytes 884744 | tf_op jit(solution)/shard_map/ppermute | solution.py:30
  58.9 4.8 %normed.1 = (bf16[256,1152]{1,0:T(8,128)(2,1)}, bf16[256,1152]{1,0:T(8,128)(2,1)}, bf16[256,1152]{1,0:T(8,128)(2,1)}, bf16[256,1664]{1,0:T(8,128)(2,1)}, bf16[256,512]{1,0:T(8,128)(2,1)}) custom-call(bf16[256,4608]{1,0:T(8,128)(2,1)} %x_ref.1, f32[4608]{0:T(1024)} %gain_ref, bf16[256,1024]{1,0:T(8,128)(2,1)} %c0.3), custom_call_target="tpu_custom_call" | custom-call | bytes 1024 | tf_op jit(solution)/shard_map/normed/pallas_call | solution.py:165
  65.5 2.6 %collective-permute-start.4 = (bf16[256,1152]{1,0:T(8,128)(2,1)}, bf16[256,1152]{1,0:T(8,128)(2,1)S(1)}, u32[]{:S(2)}, u32[]{:S(2)}) collective-permute-start(bf16[256,1152]{1,0:T(8,128)(2,1)} %get-tuple-element.53), channel_id=1, source_target_pairs={{0,12},{4,0},{8,4},{12,8},{1,13},{5,1},{9,5},{13,9},{2,14},{6,2},{... | collective-permute-start | bytes 1769480 | tf_op jit(solution)/shard_map/ppermute | solution.py:30
  68.1 19.0 %pair.1.p0 = bf16[2,144,1024]{2,1,0:T(8,128)(2,1)} custom-call(bf16[144,1024]{1,0:T(8,128)(2,1)} %collective-permute-done.a_ref, bf16[144,1024]{1,0:T(8,128)(2,1)} %get-tuple-element.46.b_ref), custom_call_target="tpu_custom_call" | custom-call | bytes 1024 | tf_op jit(solution)/shard_map/pair/pallas_call | solution.py:176
  91.8 5.5 %collective-permute-start.8 = (f16[144,1024]{1,0:T(8,128)(2,1)}, f16[144,1024]{1,0:T(8,128)(2,1)S(1)}, u32[]{:S(2)}, u32[]{:S(2)}) collective-permute-start(f16[144,1024]{1,0:T(8,128)(2,1)} %fusion), channel_id=1, source_target_pairs={{0,64},{64,0},{128,192},{192,128},{1,65},{65,1},{129,193},{193,129... | collective-permute-start | bytes 884744 | tf_op jit(solution)/shard_map/ppermute | solution.py:34
  100.6 3.0 %collective-permute-done.8 = f16[144,1024]{1,0:T(8,128)(2,1)S(1)} collective-permute-done((f16[144,1024]{1,0:T(8,128)(2,1)}, f16[144,1024]{1,0:T(8,128)(2,1)S(1)}, u32[]{:S(2)}, u32[]{:S(2)}) %collective-permute-start.8) | collective-permute-done | bytes 294944 | tf_op jit(solution)/shard_map/ppermute | solution.py:34
  106.0 5.0 %collective-permute-start.11 = (f16[72,1024]{1,0:T(8,128)(2,1)S(1)}, f16[72,1024]{1,0:T(8,128)(2,1)S(1)}, u32[]{:S(2)}, u32[]{:S(2)}) collective-permute-start(f16[72,1024]{1,0:T(8,128)(2,1)S(1)} %dynamic-slice_convert_fusion), channel_id=1, source_target_pairs={{0,128},{64,192},{128,0},{192,64},{1,129},{65,193},{129,1},{193,65... | collective-permute-start | bytes 442376 | tf_op jit(solution)/shard_map/ppermute | solution.py:34
  111.0 2.9 %collective-permute-done.11 = f16[72,1024]{1,0:T(8,128)(2,1)S(1)} collective-permute-done((f16[72,1024]{1,0:T(8,128)(2,1)S(1)}, f16[72,1024]{1,0:T(8,128)(2,1)S(1)}, u32[]{:S(2)}, u32[]{:S(2)}) %collective-permute-start.11) | collective-permute-done | bytes 147488 | tf_op jit(solution)/shard_map/ppermute | solution.py:34
  114.6 2.4 %collective-permute-start.12 = (f16[72,1024]{1,0:T(8,128)(2,1)}, f16[72,1024]{1,0:T(8,128)(2,1)}, u32[]{:S(2)}, u32[]{:S(2)}) collective-permute-start(f16[72,1024]{1,0:T(8,128)(2,1)} %add_convert_fusion.2), channel_id=1, source_target_pairs={{0,128},{64,192},{128,0},{192,64},{1,129},{65,193},{129,1},{193,65... | collective-permute-start | bytes 442376 | tf_op jit(solution)/shard_map/ppermute | solution.py:34
  119.6 5.0 %grad0.1 = (f32[144,1024]{1,0:T(8,128)}, bf16[144,1024]{1,0:T(8,128)(2,1)}, bf16[144,1024]{1,0:T(8,128)(2,1)}, bf16[144,1024]{1,0:T(8,128)(2,1)}) custom-call(bf16[256,1152]{1,0:T(8,128)(2,1)} %get-tuple-element.73.n0, bf16[256,1024]{1,0:T(8,128)(2,1)} %c0.3, bf16[256,1152]{1,0:T(8,128)(2,1)} %copy-done.1, bf16[256,1024]{1,0:T(8,128)(2,1)} %copy-done.5, ...), custom_call_target="tpu_custom_call" | custom-call | bytes 1024 | tf_op jit(solution)/shard_map/grad0/pallas_call | solution.py:209
  124.8 2.6 %collective-permute-start.18 = (bf16[144,1024]{1,0:T(8,128)(2,1)}, bf16[144,1024]{1,0:T(8,128)(2,1)S(1)}, u32[]{:S(2)}, u32[]{:S(2)}) collective-permute-start(bf16[144,1024]{1,0:T(8,128)(2,1)} %get-tuple-element.72), channel_id=1, source_target_pairs={{0,3},{1,0},{2,1},{3,2},{4,7},{5,4},{6,5},{7,6},{8,11},{9,8},{10,9... | collective-permute-start | bytes 884744 | tf_op jit(solution)/shard_map/ppermute | solution.py:30
  127.3 2.3 %convert_multiply_fusion.3 = (f32[144,1024]{1,0:T(8,128)}, f16[144,1024]{1,0:T(8,128)(2,1)}) fusion(f16[72,1024]{1,0:T(8,128)(2,1)} %add_convert_fusion.2, f16[72,1024]{1,0:T(8,128)(2,1)} %collective-permute-done.12, pred[]{:T(512)S(6)} %eq.3), kind=kLoop, calls=%fused_computation.5 | loop fusion | flops 737280 | bytes 1179649 | tf_op jit(solution)/shard_map/div | solution.py:254
  129.6 3.2 %collective-permute-start.22 = (f16[144,1024]{1,0:T(8,128)(2,1)}, f16[144,1024]{1,0:T(8,128)(2,1)}, u32[]{:S(2)}, u32[]{:S(2)}) collective-permute-start(f16[144,1024]{1,0:T(8,128)(2,1)} %get-tuple-element.85), channel_id=1, source_target_pairs={{0,64},{64,0},{128,192},{192,128},{1,65},{65,1},{129,193},{193,129... | collective-permute-start | bytes 884744 | tf_op jit(solution)/shard_map/ppermute | solution.py:34
  132.7 5.3 %near_keys.1 = (f32[256,1024]{1,0:T(8,128)}, bf16[256,1024]{1,0:T(8,128)(2,1)}, bf16[256,1024]{1,0:T(8,128)(2,1)}) custom-call(bf16[256,1152]{1,0:T(8,128)(2,1)} %get-tuple-element.73.n0, bf16[256,1152]{1,0:T(8,128)(2,1)} %copy-done.1, bf16[256,1152]{1,0:T(8,128)(2,1)} %copy-done.2, bf16[2,144,1024]{2,1,0:T(8,128)(2,1)} %pair.1.p0, ...), custom_call_target="tpu_custom_call" | custom-call | bytes 1024 | tf_op jit(solution)/shard_map/near_keys/pallas_call | solution.py:219
  140.2 3.8 %far_keys.1 = bf16[256,1024]{1,0:T(8,128)(2,1)} custom-call(bf16[256,1664]{1,0:T(8,128)(2,1)} %copy-done, bf16[256,512]{1,0:T(8,128)(2,1)} %collective-permute-done.15.second.refs_1_, bf16[2,144,1024]{2,1,0:T(8,128)(2,1)} %pair.1.p0, bf16[2,144,1024]{2,1,0:T(8,128)(2,1)} %copy-done.3, bf16[2,144,1024]{2,1,0:T(8,128)(2,1)} %collective-permute-done.5.p2, ...), custom_call_target="tpu_custom_call" | custom-call | bytes 1024 | tf_op jit(solution)/shard_map/far_keys/pallas_call | solution.py:234
  144.7 5.6 %grad1.1 = (f32[144,1024]{1,0:T(8,128)}, bf16[144,1024]{1,0:T(8,128)(2,1)}, bf16[144,1024]{1,0:T(8,128)(2,1)}, bf16[144,1024]{1,0:T(8,128)(2,1)}) custom-call(bf16[256,1152]{1,0:T(8,128)(2,1)} %get-tuple-element.73.n0, bf16[256,1024]{1,0:T(8,128)(2,1)} %c0.3, bf16[256,1152]{1,0:T(8,128)(2,1)} %copy-done.1, bf16[256,1024]{1,0:T(8,128)(2,1)} %copy-done.5, ...), custom_call_target="tpu_custom_call" | custom-call | bytes 1024 | tf_op jit(solution)/shard_map/grad1/pallas_call | solution.py:209
  150.3 14.2 %collective-permute-start.23 = (f16[144,1024]{1,0:T(8,128)(2,1)}, f16[144,1024]{1,0:T(8,128)(2,1)S(1)}, u32[]{:S(2)}, u32[]{:S(2)}) collective-permute-start(f16[144,1024]{1,0:T(8,128)(2,1)} %collective-permute-done.22), channel_id=1, source_target_pairs={{0,32},{32,0},{1,33},{33,1},{2,34},{34,2},{3,35},{35,3},{4,36},{36... | collective-permute-start | bytes 884744 | tf_op jit(solution)/shard_map/ppermute | solution.py:30
  166.4 5.0 %collective-permute-start.25 = (bf16[144,1024]{1,0:T(8,128)(2,1)}, bf16[144,1024]{1,0:T(8,128)(2,1)S(1)}, u32[]{:S(2)}, u32[]{:S(2)}) collective-permute-start(bf16[144,1024]{1,0:T(8,128)(2,1)} %add_convert_fusion.1), channel_id=1, source_target_pairs={{0,16},{16,0},{1,17},{17,1},{2,18},{18,2},{3,19},{19,3},{4,20},{20... | collective-permute-start | bytes 884744 | tf_op jit(solution)/shard_map/ppermute | solution.py:30
  180.0 6.7 %outer_step.1 = (f32[4,144,1024]{2,1,0:T(8,128)}, f32[4,144,1024]{2,1,0:T(8,128)}) custom-call(s32[2]{0:T(128)} %pad_add_fusion.place_ref, f32[144,1024]{1,0:T(8,128)} %get-tuple-element.88.refs_0_, f32[144,1024]{1,0:T(8,128)} %convert_multiply_fusion.2.refs_1_, f32[144,1024]{1,0:T(8,128)} %convert_multiply_fusion.1.refs_2_, ...), custom_call_target="tpu_custom_call" | custom-call | bytes 1024 | tf_op jit(solution)/shard_map/outer_step/pallas_call | solution.py:261
  186.8 3.4 %collective-permute-done.24 = bf16[144,1024]{1,0:T(8,128)(2,1)} collective-permute-done((bf16[144,1024]{1,0:T(8,128)(2,1)}, bf16[144,1024]{1,0:T(8,128)(2,1)}, u32[]{:S(2)}, u32[]{:S(2)}) %collective-permute-start.24) | collective-permute-done | bytes 294944 | tf_op jit(solution)/shard_map/ppermute | solution.py:30
  192.4 2.3 %add_convert_fusion = bf16[256,1024]{1,0:T(8,128)(2,1)} fusion(f32[256,1024]{1,0:T(8,128)S(1)} %copy-done.7, bf16[256,1024]{1,0:T(8,128)(2,1)} %collective-permute-done.16, bf16[256,1024]{1,0:T(8,128)(2,1)} %collective-permute-done.14, bf16[256,1024]{1,0:T(8,128)(2,1)S(1)} %collective-permute-done.13), kind=kLoop, calls=%fused_computation | loop fusion | flops 1835008 | bytes 3145728 | tf_op jit(solution)/shard_map/convert_element_type | solution.py:274
  (76 shorter events, 32.6 us)
Async XLA Ops:
  0.6 63.1 %collective-permute-start.1 = (bf16[256,1024]{1,0:T(8,128)(2,1)}, bf16[256,1024]{1,0:T(8,128)(2,1)S(1)}, u32[]{:S(2)}, u32[]{:S(2)}) collective-permute-start(bf16[256,1024]{1,0:T(8,128)(2,1)} %c0.3), channel_id=1, source_target_pairs={{0,4},{4,8},{8,12},{12,0},{1,5},{5,9},{9,13},{13,1},{2,6},{6,10},{... | collective-permute-start | bytes 1572872 | tf_op jit(solution)/shard_map/ppermute | solution.py:30
  2.8 60.9 %collective-permute-start.2 = (bf16[256,1024]{1,0:T(8,128)(2,1)}, bf16[256,1024]{1,0:T(8,128)(2,1)S(1)}, u32[]{:S(2)}, u32[]{:S(2)}) collective-permute-start(bf16[256,1024]{1,0:T(8,128)(2,1)} %c0.3), channel_id=1, source_target_pairs={{0,12},{4,0},{8,4},{12,8},{1,13},{5,1},{9,5},{13,9},{2,14},{6,2},{... | collective-permute-start | bytes 1572872 | tf_op jit(solution)/shard_map/ppermute | solution.py:30
  50.8 39.0 %collective-permute-start.7 = (bf16[2,144,1024]{2,1,0:T(8,128)(2,1)}, bf16[2,144,1024]{2,1,0:T(8,128)(2,1)}, u32[]{:S(2)}, u32[]{:S(2)}) collective-permute-start(bf16[2,144,1024]{2,1,0:T(8,128)(2,1)} %get-tuple-element.59), channel_id=1, source_target_pairs={{0,32},{32,0},{1,33},{33,1},{2,34},{34,2},{3,35},{35,3},{4,36},{36... | collective-permute-start | bytes 1769480 | tf_op jit(solution)/shard_map/ppermute | solution.py:30
  53.7 14.3 %collective-permute-start = (bf16[144,1024]{1,0:T(8,128)(2,1)}, bf16[144,1024]{1,0:T(8,128)(2,1)}, u32[]{:S(2)}, u32[]{:S(2)}) collective-permute-start(bf16[144,1024]{1,0:T(8,128)(2,1)} %get-tuple-element.46.b_ref), channel_id=1, source_target_pairs={{0,16},{16,0},{1,17},{17,1},{2,18},{18,2},{3,19},{19,3},{4,20},{20... | collective-permute-start | bytes 884744 | tf_op jit(solution)/shard_map/ppermute | solution.py:30
  65.4 31.9 %collective-permute-start.3 = (bf16[256,1152]{1,0:T(8,128)(2,1)}, bf16[256,1152]{1,0:T(8,128)(2,1)S(1)}, u32[]{:S(2)}, u32[]{:S(2)}) collective-permute-start(bf16[256,1152]{1,0:T(8,128)(2,1)} %get-tuple-element.51), channel_id=1, source_target_pairs={{0,4},{4,8},{8,12},{12,0},{1,5},{5,9},{9,13},{13,1},{2,6},{6,10},{... | collective-permute-start | bytes 1769480 | tf_op jit(solution)/shard_map/ppermute | solution.py:30
  65.5 33.6 %collective-permute-start.4 = (bf16[256,1152]{1,0:T(8,128)(2,1)}, bf16[256,1152]{1,0:T(8,128)(2,1)S(1)}, u32[]{:S(2)}, u32[]{:S(2)}) collective-permute-start(bf16[256,1152]{1,0:T(8,128)(2,1)} %get-tuple-element.53), channel_id=1, source_target_pairs={{0,12},{4,0},{8,4},{12,8},{1,13},{5,1},{9,5},{13,9},{2,14},{6,2},{... | collective-permute-start | bytes 1769480 | tf_op jit(solution)/shard_map/ppermute | solution.py:30
  87.1 16.5 %collective-permute-start.9 = (bf16[2,144,1024]{2,1,0:T(8,128)(2,1)}, bf16[2,144,1024]{2,1,0:T(8,128)(2,1)S(1)}, u32[]{:S(2)}, u32[]{:S(2)}) collective-permute-start(bf16[2,144,1024]{2,1,0:T(8,128)(2,1)} %pair.1.p0), channel_id=1, source_target_pairs={{0,1},{1,2},{2,3},{3,0},{4,5},{5,6},{6,7},{7,4},{8,9},{9,10},{10,1... | collective-permute-start | bytes 1769480 | tf_op jit(solution)/shard_map/ppermute | solution.py:30
  88.3 16.0 %collective-permute-start.10 = (bf16[2,144,1024]{2,1,0:T(8,128)(2,1)}, bf16[2,144,1024]{2,1,0:T(8,128)(2,1)S(1)}, u32[]{:S(2)}, u32[]{:S(2)}) collective-permute-start(bf16[2,144,1024]{2,1,0:T(8,128)(2,1)} %pair.1.p0), channel_id=1, source_target_pairs={{0,3},{1,0},{2,1},{3,2},{4,7},{5,4},{6,5},{7,6},{8,11},{9,8},{10,9... | collective-permute-start | bytes 1769480 | tf_op jit(solution)/shard_map/ppermute | solution.py:30
  97.3 21.4 %collective-permute-start.6 = (bf16[256,1664]{1,0:T(8,128)(2,1)}, bf16[256,1664]{1,0:T(8,128)(2,1)S(1)}, u32[]{:S(2)}, u32[]{:S(2)}) collective-permute-start(bf16[256,1664]{1,0:T(8,128)(2,1)} %get-tuple-element.56), channel_id=1, source_target_pairs={{0,8},{4,12},{8,0},{12,4},{1,9},{5,13},{9,1},{13,5},{2,10},{6,14},... | collective-permute-start | bytes 2555912 | tf_op jit(solution)/shard_map/ppermute | solution.py:30
  99.0 19.7 %collective-permute-start.5 = (bf16[2,144,1024]{2,1,0:T(8,128)(2,1)}, bf16[2,144,1024]{2,1,0:T(8,128)(2,1)}, u32[]{:S(2)}, u32[]{:S(2)}) collective-permute-start(bf16[2,144,1024]{2,1,0:T(8,128)(2,1)} %pair.1.p0), channel_id=1, source_target_pairs={{0,2},{1,3},{2,0},{3,1},{4,6},{5,7},{6,4},{7,5},{8,10},{9,11},{10,... | collective-permute-start | bytes 1769480 | tf_op jit(solution)/shard_map/ppermute | solution.py:30
  114.6 12.7 %collective-permute-start.12 = (f16[72,1024]{1,0:T(8,128)(2,1)}, f16[72,1024]{1,0:T(8,128)(2,1)}, u32[]{:S(2)}, u32[]{:S(2)}) collective-permute-start(f16[72,1024]{1,0:T(8,128)(2,1)} %add_convert_fusion.2), channel_id=1, source_target_pairs={{0,128},{64,192},{128,0},{192,64},{1,129},{65,193},{129,1},{193,65... | collective-permute-start | bytes 442376 | tf_op jit(solution)/shard_map/ppermute | solution.py:34
  117.0 21.0 %collective-permute-start.15 = (bf16[256,512]{1,0:T(8,128)(2,1)}, bf16[256,512]{1,0:T(8,128)(2,1)}, u32[]{:S(2)}, u32[]{:S(2)}) collective-permute-start(bf16[256,512]{1,0:T(8,128)(2,1)} %get-tuple-element.68), channel_id=1, source_target_pairs={{0,8},{4,12},{8,0},{12,4},{1,9},{5,13},{9,1},{13,5},{2,10},{6,14},... | collective-permute-start | bytes 786440 | tf_op jit(solution)/shard_map/ppermute | solution.py:30
  124.6 14.9 %collective-permute-start.17 = (bf16[144,1024]{1,0:T(8,128)(2,1)}, bf16[144,1024]{1,0:T(8,128)(2,1)S(1)}, u32[]{:S(2)}, u32[]{:S(2)}) collective-permute-start(bf16[144,1024]{1,0:T(8,128)(2,1)} %get-tuple-element.71), channel_id=1, source_target_pairs={{0,1},{1,2},{2,3},{3,0},{4,5},{5,6},{6,7},{7,4},{8,9},{9,10},{10,1... | collective-permute-start | bytes 884744 | tf_op jit(solution)/shard_map/ppermute | solution.py:30
  124.8 19.2 %collective-permute-start.18 = (bf16[144,1024]{1,0:T(8,128)(2,1)}, bf16[144,1024]{1,0:T(8,128)(2,1)S(1)}, u32[]{:S(2)}, u32[]{:S(2)}) collective-permute-start(bf16[144,1024]{1,0:T(8,128)(2,1)} %get-tuple-element.72), channel_id=1, source_target_pairs={{0,3},{1,0},{2,1},{3,2},{4,7},{5,4},{6,5},{7,6},{8,11},{9,8},{10,9... | collective-permute-start | bytes 884744 | tf_op jit(solution)/shard_map/ppermute | solution.py:30
  129.6 20.7 %collective-permute-start.22 = (f16[144,1024]{1,0:T(8,128)(2,1)}, f16[144,1024]{1,0:T(8,128)(2,1)}, u32[]{:S(2)}, u32[]{:S(2)}) collective-permute-start(f16[144,1024]{1,0:T(8,128)(2,1)} %get-tuple-element.85), channel_id=1, source_target_pairs={{0,64},{64,0},{128,192},{192,128},{1,65},{65,1},{129,193},{193,129... | collective-permute-start | bytes 884744 | tf_op jit(solution)/shard_map/ppermute | solution.py:34
  132.7 31.7 %collective-permute-start.21 = (bf16[144,1024]{1,0:T(8,128)(2,1)}, bf16[144,1024]{1,0:T(8,128)(2,1)}, u32[]{:S(2)}, u32[]{:S(2)}) collective-permute-start(bf16[144,1024]{1,0:T(8,128)(2,1)} %get-tuple-element.81), channel_id=1, source_target_pairs={{0,2},{1,3},{2,0},{3,1},{4,6},{5,7},{6,4},{7,5},{8,10},{9,11},{10,... | collective-permute-start | bytes 884744 | tf_op jit(solution)/shard_map/ppermute | solution.py:30
  138.0 35.6 %collective-permute-start.13 = (bf16[256,1024]{1,0:T(8,128)(2,1)}, bf16[256,1024]{1,0:T(8,128)(2,1)S(1)}, u32[]{:S(2)}, u32[]{:S(2)}) collective-permute-start(bf16[256,1024]{1,0:T(8,128)(2,1)} %get-tuple-element.65), channel_id=1, source_target_pairs={{0,12},{4,0},{8,4},{12,8},{1,13},{5,1},{9,5},{13,9},{2,14},{6,2},{... | collective-permute-start | bytes 1572872 | tf_op jit(solution)/shard_map/ppermute | solution.py:30
  139.6 34.4 %collective-permute-start.14 = (bf16[256,1024]{1,0:T(8,128)(2,1)}, bf16[256,1024]{1,0:T(8,128)(2,1)}, u32[]{:S(2)}, u32[]{:S(2)}) collective-permute-start(bf16[256,1024]{1,0:T(8,128)(2,1)} %get-tuple-element.66), channel_id=1, source_target_pairs={{0,4},{4,8},{8,12},{12,0},{1,5},{5,9},{9,13},{13,1},{2,6},{6,10},{... | collective-permute-start | bytes 1572872 | tf_op jit(solution)/shard_map/ppermute | solution.py:30
  150.3 24.8 %collective-permute-start.23 = (f16[144,1024]{1,0:T(8,128)(2,1)}, f16[144,1024]{1,0:T(8,128)(2,1)S(1)}, u32[]{:S(2)}, u32[]{:S(2)}) collective-permute-start(f16[144,1024]{1,0:T(8,128)(2,1)} %collective-permute-done.22), channel_id=1, source_target_pairs={{0,32},{32,0},{1,33},{33,1},{2,34},{34,2},{3,35},{35,3},{4,36},{36... | collective-permute-start | bytes 884744 | tf_op jit(solution)/shard_map/ppermute | solution.py:30
  166.4 20.3 %collective-permute-start.25 = (bf16[144,1024]{1,0:T(8,128)(2,1)}, bf16[144,1024]{1,0:T(8,128)(2,1)S(1)}, u32[]{:S(2)}, u32[]{:S(2)}) collective-permute-start(bf16[144,1024]{1,0:T(8,128)(2,1)} %add_convert_fusion.1), channel_id=1, source_target_pairs={{0,16},{16,0},{1,17},{17,1},{2,18},{18,2},{3,19},{19,3},{4,20},{20... | collective-permute-start | bytes 884744 | tf_op jit(solution)/shard_map/ppermute | solution.py:30
  173.6 13.2 %collective-permute-start.20 = (bf16[144,1024]{1,0:T(8,128)(2,1)}, bf16[144,1024]{1,0:T(8,128)(2,1)}, u32[]{:S(2)}, u32[]{:S(2)}) collective-permute-start(bf16[144,1024]{1,0:T(8,128)(2,1)} %get-tuple-element.78), channel_id=1, source_target_pairs={{0,3},{1,0},{2,1},{3,2},{4,7},{5,4},{6,5},{7,6},{8,11},{9,8},{10,9... | collective-permute-start | bytes 884744 | tf_op jit(solution)/shard_map/ppermute | solution.py:30
  173.9 12.9 %collective-permute-start.19 = (bf16[144,1024]{1,0:T(8,128)(2,1)}, bf16[144,1024]{1,0:T(8,128)(2,1)}, u32[]{:S(2)}, u32[]{:S(2)}) collective-permute-start(bf16[144,1024]{1,0:T(8,128)(2,1)} %get-tuple-element.76), channel_id=1, source_target_pairs={{0,1},{1,2},{2,3},{3,0},{4,5},{5,6},{6,7},{7,4},{8,9},{9,10},{10,1... | collective-permute-start | bytes 884744 | tf_op jit(solution)/shard_map/ppermute | solution.py:30
  175.1 15.1 %collective-permute-start.24 = (bf16[144,1024]{1,0:T(8,128)(2,1)}, bf16[144,1024]{1,0:T(8,128)(2,1)}, u32[]{:S(2)}, u32[]{:S(2)}) collective-permute-start(bf16[144,1024]{1,0:T(8,128)(2,1)} %get-tuple-element.84), channel_id=1, source_target_pairs={{0,2},{1,3},{2,0},{3,1},{4,6},{5,7},{6,4},{7,5},{8,10},{9,11},{10,... | collective-permute-start | bytes 884744 | tf_op jit(solution)/shard_map/ppermute | solution.py:30
  177.8 14.6 %collective-permute-start.16 = (bf16[256,1024]{1,0:T(8,128)(2,1)S(1)}, bf16[256,1024]{1,0:T(8,128)(2,1)}, u32[]{:S(2)}, u32[]{:S(2)}) collective-permute-start(bf16[256,1024]{1,0:T(8,128)(2,1)S(1)} %copy-done.11), channel_id=1, source_target_pairs={{0,8},{4,12},{8,0},{12,4},{1,9},{5,13},{9,1},{13,5},{2,10},{6,14},... | collective-permute-start | bytes 1572872 | tf_op jit(solution)/shard_map/ppermute | solution.py:30
  (16 other events, 188.2 us)

commit v9 on v6

--- a/solution.py
+++ b/solution.py
@@ -178,7 +178,7 @@
             out_specs=_vmem(len(blocks)),
         )(*blocks, *pairs)
 
-    k0, k1, k3 = keys_of(own, _after(r1, mine), r3)
+    k0, k1, k3 = keys_of(own, r1, r3)
     e1, e3 = _shift(k1, "y", 3), _shift(k3, "y", 1)
 
     def grad(half, own):
@@ -194,14 +194,13 @@
     g = grad(0, _after(own, k0))
     a1, a3 = _shift(g[1], "x", 1), _shift(g[3], "x", 3)
     b = grad(1, own)
+    a2 = _shift(_after(g[2], a1), "x", 2)
     (k2,) = keys_of(_after(r2, b[0], e1, e3, a1, a3))
-    a2 = _shift(_after(g[2], a1), "x", 2)
     swapped = [_shift(_after(v, a1, a3), "core", 1, 2) for v in (mine, next_layer)]
-    far_sum = (_after(g[0], *swapped) + sum(v.astype(F32) for v in (a1, a2, a3))).astype(BF)
+    far_sum = (g[0] + sum(v.astype(F32) for v in (a1, a2, a3))).astype(BF)
     from_zh = _shift(far_sum, "zh", 1, 2)
-    near_sum = _after(b[0] + from_zh.astype(F32))
     b1, b3, b2 = [_shift(_after(b[k], far_sum), "x", k) for k in (1, 3, 2)]
-    weight_grad = (near_sum + sum(v.astype(F32) for v in (b1, b3, b2)))[None]
+    weight_grad = (b[0] + sum(v.astype(F32) for v in (b1, b3, b2, from_zh)))[None]
 
     averages = [mine, next_layer] + swapped
     averages = [v.astype(F32) / (8.0 * UNIT) for v in averages]

time: 114 us -> 112 us (0.982)
  waiting for transfers between devices: 34.4 us -> 32.3 us
    ppermute x4, waiting for transfers between devices: 12.7 us -> 4.9 us  [_flip(): return lax.ppermute(v, axis, [(i, i ^ bit) for i in range(size)])]
    ppermute x22, waiting for transfers between devices: 21.7 us -> 27.4 us  [_shift(): return lax.ppermute(v, axis, [(i, (i + k) % size) for i in range(size)])]
    ppermute x22, starting transfers between devices: 38.5 us -> 36.7 us  [_shift(): return lax.ppermute(v, axis, [(i, (i + k) % size) for i in range(size)])]
    ppermute x4, starting transfers between devices: 4.19 us -> 5.66 us  [_flip(): return lax.ppermute(v, axis, [(i, i ^ bit) for i in range(size)])]
  transfers between devices with their start and end apart: 26 -> 26, of which waited for: 10 -> 11; matrix products, arithmetic and copies ran while one was open for 9% -> 9% of each run, Pallas kernels for 15% -> 17%
where the time goes in v9:
time: 112 us; the launch traced here: 111 us
  starting transfers between devices  42.4 us (38%)
  waiting for transfers between devices  32.3 us (29%)
  Pallas kernels  18.9 us (17%)
  other arithmetic  9.81 us (9%)
  local copies, waits for them, and re-layouts  6.53 us (6%)
  between operations  1.49 us (1%)
    ppermute x22, starting transfers between devices, _shift(): return lax.ppermute(v, axis, [(i, (i + k) % size) for i in range(size)])  36.7 us
    ppermute x22, waiting for transfers between devices, _shift(): return lax.ppermute(v, axis, [(i, (i + k) % size) for i in range(size)])  27.4 us
    pallas_call x2, Pallas kernels, keys_of(): _call(functools.partial(_keys_kernel, len(blocks)), f'keys{len(blocks)}',...  6.29 us
    unnamed x24, local copies, waits for them, and re-layouts  5.79 us
    ppermute x4, starting transfers between devices, _flip(): return lax.ppermute(v, axis, [(i, i ^ bit) for i in range(size)])  5.66 us
    pallas_call x1, Pallas kernels, body(): pl.pallas_call(_outer_kernel, name='outer_step', out_shape=[jax.ShapeDtyp...  5.12 us
    ppermute x4, waiting for transfers between devices, _flip(): return lax.ppermute(v, axis, [(i, i ^ bit) for i in range(size)])  4.9 us
    pallas_call x2, Pallas kernels, grad(): _call(functools.partial(_grad_kernel, half), f'grad{half}', [((ROWS, KV),...  3.79 us
  transfers between devices with their start and end apart: 26, of which 11 were waited for; matrix products, arithmetic and copies ran while one was open for 9% of the time, Pallas kernels for 17%

profile of v9, /device:TPU:1, one launch (start us, length us, event | category | flops | bytes accessed | tf_op | source)
XLA Modules:
  0.0 111.4 jit_solution(5813142846327932619)
XLA Ops:
  0.6 2.2 %collective-permute-start = (bf16[256,1024]{1,0:T(8,128)(2,1)}, bf16[256,1024]{1,0:T(8,128)(2,1)S(1)}, u32[]{:S(2)}, u32[]{:S(2)}) collective-permute-start(bf16[256,1024]{1,0:T(8,128)(2,1)} %c0.3), channel_id=1, source_target_pairs={{0,4},{4,8},{8,12},{12,0},{1,5},{5,9},{9,13},{13,1},{2,6},{6,10},{... | collective-permute-start | bytes 1572872 | tf_op jit(solution)/shard_map/ppermute | solution.py:29
  7.2 7.0 %collective-permute-start.4 = (bf16[144,1024]{1,0:T(8,128)(2,1)S(1)}, bf16[144,1024]{1,0:T(8,128)(2,1)S(1)}, u32[]{:S(2)}, u32[]{:S(2)}) collective-permute-start(bf16[144,1024]{1,0:T(8,128)(2,1)S(1)} %get-tuple-element.41), channel_id=1, source_target_pairs={{0,16},{16,0},{1,17},{17,1},{2,18},{18,2},{3,19},{19,3},{4,20},{20... | collective-permute-start | bytes 884744 | tf_op jit(solution)/shard_map/ppermute | solution.py:29
  17.4 1.7 %copy-done.3 = bf16[256,4608]{1,0:T(8,128)(2,1)S(1)} copy-done((bf16[256,4608]{1,0:T(8,128)(2,1)S(1)}, bf16[256,4608]{1,0:T(8,128)(2,1)}, u32[]{:S(2)}) %copy-start.3) | copy-done | bytes 2359320
  19.0 2.8 %normed.1 = (bf16[256,1152]{1,0:T(8,128)(2,1)S(1)}, bf16[256,1152]{1,0:T(8,128)(2,1)}, bf16[256,2176]{1,0:T(8,128)(2,1)S(1)}, bf16[256,1152]{1,0:T(8,128)(2,1)S(1)}) custom-call(bf16[256,4608]{1,0:T(8,128)(2,1)S(1)} %copy-done.3, f32[1,4608]{1,0:T(1,128)S(1)} %broadcast_in_dim.6.gain_ref, bf16[256,1024]{1,0:T(8,128)(2,1)S(1)} %copy-done.1), custom_call_target="tpu_custom_call" | custom-call | bytes 1024 | tf_op jit(solution)/shard_map/normed/pallas_call | solution.py:137
  23.0 2.6 %collective-permute-start.3 = (bf16[256,1152]{1,0:T(8,128)(2,1)S(1)}, bf16[256,1152]{1,0:T(8,128)(2,1)S(1)}, u32[]{:S(2)}, u32[]{:S(2)}) collective-permute-start(bf16[256,1152]{1,0:T(8,128)(2,1)S(1)} %get-tuple-element.47), channel_id=1, source_target_pairs={{0,12},{4,0},{8,4},{12,8},{1,13},{5,1},{9,5},{13,9},{2,14},{6,2},{... | collective-permute-start | bytes 1769480 | tf_op jit(solution)/shard_map/ppermute | solution.py:29
  28.4 2.0 %fusion = f16[144,1024]{1,0:T(8,128)(2,1)} fusion(f32[4,144,1024]{2,1,0:T(8,128)} %refs_4_.1, s32[]{:T(128)S(6)} %select_n.33, bf16[2,144,1024]{2,1,0:T(8,128)(2,1)} %collective-permute-done.19, s32[]{:T(128)S(6)} %select_n.34, bf16[2,144,1024]{2,1,0:T(8,128)(2,1)S(1)} %get-tuple-element.70), kind=kLoop, calls=%fused_computation.10 | loop fusion | flops 1032192 | bytes 1474568 | tf_op jit(solution)/shard_map/mul | solution.py:157
  30.5 1.9 %collective-permute-start.20 = (f16[144,1024]{1,0:T(8,128)(2,1)}, f16[144,1024]{1,0:T(8,128)(2,1)}, u32[]{:S(2)}, u32[]{:S(2)}) collective-permute-start(f16[144,1024]{1,0:T(8,128)(2,1)} %fusion), channel_id=1, source_target_pairs={{0,64},{64,0},{128,192},{192,128},{1,65},{65,1},{129,193},{193,129... | collective-permute-start | bytes 884744 | tf_op jit(solution)/shard_map/ppermute | solution.py:33
  32.4 7.1 %collective-permute-done.2.refs_1_.n1 = bf16[256,1152]{1,0:T(8,128)(2,1)S(1)} collective-permute-done((bf16[256,1152]{1,0:T(8,128)(2,1)}, bf16[256,1152]{1,0:T(8,128)(2,1)S(1)}, u32[]{:S(2)}, u32[]{:S(2)}) %collective-permute-start.2) | collective-permute-done | bytes 589856 | tf_op jit(solution)/shard_map/ppermute | solution.py:29
  41.4 2.1 %collective-permute-start.7 = (bf16[2,144,1024]{2,1,0:T(8,128)(2,1)S(1)}, bf16[2,144,1024]{2,1,0:T(8,128)(2,1)}, u32[]{:S(2)}, u32[]{:S(2)}) collective-permute-start(bf16[2,144,1024]{2,1,0:T(8,128)(2,1)S(1)} %pad_maximum_fusion.refs_3_.refs_1_), channel_id=1, source_target_pairs={{0,2},{1,3},{2,0},{3,1},{4,6},{5,7},{6,4},{7,5},{8,10},{9,11},{10,... | collective-permute-start | bytes 1769480 | tf_op jit(solution)/shard_map/ppermute | solution.py:29
  46.5 2.3 %collective-permute-start.21 = (f16[72,1024]{1,0:T(8,128)(2,1)}, f16[72,1024]{1,0:T(8,128)(2,1)}, u32[]{:S(2)}, u32[]{:S(2)}) collective-permute-start(f16[72,1024]{1,0:T(8,128)(2,1)} %dynamic-slice_convert_fusion), channel_id=1, source_target_pairs={{0,128},{64,192},{128,0},{192,64},{1,129},{65,193},{129,1},{193,65... | collective-permute-start | bytes 442376 | tf_op jit(solution)/shard_map/ppermute | solution.py:33
  48.8 4.9 %collective-permute-done.21 = f16[72,1024]{1,0:T(8,128)(2,1)} collective-permute-done((f16[72,1024]{1,0:T(8,128)(2,1)}, f16[72,1024]{1,0:T(8,128)(2,1)}, u32[]{:S(2)}, u32[]{:S(2)}) %collective-permute-start.21) | collective-permute-done | bytes 147488 | tf_op jit(solution)/shard_map/ppermute | solution.py:33
  53.7 1.7 %add_convert_fusion.2 = f16[72,1024]{1,0:T(8,128)(2,1)} fusion(f16[72,1024]{1,0:T(8,128)(2,1)} %collective-permute-done.21, f32[144,1024]{1,0:T(8,128)} %copy-done.11, s32[]{:T(128)S(6)} %select_n.35), kind=kLoop, calls=%fused_computation.12 | loop fusion | flops 221184 | bytes 589828 | tf_op jit(solution)/shard_map/convert_element_type | solution.py:163
  56.4 3.9 %keys3.1 = (f32[256,1024]{1,0:T(8,128)S(1)}, bf16[256,1024]{1,0:T(8,128)(2,1)S(1)}, bf16[256,1024]{1,0:T(8,128)(2,1)S(1)}) custom-call(bf16[256,1152]{1,0:T(8,128)(2,1)S(1)} %get-tuple-element.56.refs_0_.n0, bf16[256,1152]{1,0:T(8,128)(2,1)S(1)} %collective-permute-done.2.refs_1_.n1, bf16[256,1152]{1,0:T(8,128)(2,1)S(1)} %collective-permute-done.3.refs_2_.n3, ...), custom_call_target="tpu_custom_call" | custom-call | bytes 1024 | tf_op jit(solution)/shard_map/keys3/pallas_call | solution.py:172
  60.3 6.3 %collective-permute-done.10.m2.refs_0_ = bf16[256,2176]{1,0:T(8,128)(2,1)S(1)} collective-permute-done((bf16[256,2176]{1,0:T(8,128)(2,1)}, bf16[256,2176]{1,0:T(8,128)(2,1)S(1)}, u32[]{:S(2)}, u32[]{:S(2)}) %collective-permute-start.10) | collective-permute-done | bytes 1114144 | tf_op jit(solution)/shard_map/ppermute | solution.py:29
  69.3 1.7 %collective-permute-start.12 = (bf16[144,1024]{1,0:T(8,128)(2,1)S(1)}, bf16[144,1024]{1,0:T(8,128)(2,1)S(1)}, u32[]{:S(2)}, u32[]{:S(2)}) collective-permute-start(bf16[144,1024]{1,0:T(8,128)(2,1)S(1)} %get-tuple-element.58), channel_id=1, source_target_pairs={{0,3},{1,0},{2,1},{3,2},{4,7},{5,4},{6,5},{7,6},{8,11},{9,8},{10,9... | collective-permute-start | bytes 884744 | tf_op jit(solution)/shard_map/ppermute | solution.py:29
  73.1 1.8 %collective-permute-start.8 = (bf16[256,1024]{1,0:T(8,128)(2,1)S(1)}, bf16[256,1024]{1,0:T(8,128)(2,1)S(1)}, u32[]{:S(2)}, u32[]{:S(2)}) collective-permute-start(bf16[256,1024]{1,0:T(8,128)(2,1)S(1)} %get-tuple-element.51), channel_id=1, source_target_pairs={{0,12},{4,0},{8,4},{12,8},{1,13},{5,1},{9,5},{13,9},{2,14},{6,2},{... | collective-permute-start | bytes 1572872 | tf_op jit(solution)/shard_map/ppermute | solution.py:29
  77.7 2.9 %collective-permute-start.24 = (f16[144,1024]{1,0:T(8,128)(2,1)S(1)}, f16[144,1024]{1,0:T(8,128)(2,1)S(1)}, u32[]{:S(2)}, u32[]{:S(2)}) collective-permute-start(f16[144,1024]{1,0:T(8,128)(2,1)S(1)} %get-tuple-element.74), channel_id=1, source_target_pairs={{0,32},{32,0},{1,33},{33,1},{2,34},{34,2},{3,35},{35,3},{4,36},{36... | collective-permute-start | bytes 884744 | tf_op jit(solution)/shard_map/ppermute | solution.py:29
  80.7 2.1 %grad1.1 = (f32[144,1024]{1,0:T(8,128)S(1)}, bf16[144,1024]{1,0:T(8,128)(2,1)S(1)}, bf16[144,1024]{1,0:T(8,128)(2,1)S(1)}, bf16[144,1024]{1,0:T(8,128)(2,1)S(1)}) custom-call(bf16[256,1152]{1,0:T(8,128)(2,1)S(1)} %get-tuple-element.56.refs_0_.n0, bf16[256,1024]{1,0:T(8,128)(2,1)S(1)} %copy-done.2, bf16[256,1152]{1,0:T(8,128)(2,1)S(1)} %collective-permute-done.2.refs_1_.n1, ...), custom_call_target="tpu_custom_call" | custom-call | bytes 1024 | tf_op jit(solution)/shard_map/grad1/pallas_call | solution.py:185
  84.1 2.3 %collective-permute-done.9 = bf16[256,1024]{1,0:T(8,128)(2,1)S(1)} collective-permute-done((bf16[256,1024]{1,0:T(8,128)(2,1)S(1)}, bf16[256,1024]{1,0:T(8,128)(2,1)S(1)}, u32[]{:S(2)}, u32[]{:S(2)}) %collective-permute-start.9) | collective-permute-done | bytes 524320 | tf_op jit(solution)/shard_map/ppermute | solution.py:29
  86.5 2.4 %keys1.1 = bf16[256,1024]{1,0:T(8,128)(2,1)S(1)} custom-call(bf16[256,2176]{1,0:T(8,128)(2,1)S(1)} %collective-permute-done.10.m2.refs_0_, bf16[2,144,1024]{2,1,0:T(8,128)(2,1)S(1)} %pad_maximum_fusion.refs_3_.refs_1_, bf16[2,144,1024]{2,1,0:T(8,128)(2,1)} %collective-permute-done.5.refs_4_.refs_2_, ...), custom_call_target="tpu_custom_call" | custom-call | bytes 1024 | tf_op jit(solution)/shard_map/keys1/pallas_call | solution.py:172
  89.0 4.0 %collective-permute-start.25 = (f16[144,1024]{1,0:T(8,128)(2,1)S(1)}, f16[144,1024]{1,0:T(8,128)(2,1)S(1)}, u32[]{:S(2)}, u32[]{:S(2)}) collective-permute-start(f16[144,1024]{1,0:T(8,128)(2,1)S(1)} %collective-permute-done.23), channel_id=1, source_target_pairs={{0,32},{32,0},{1,33},{33,1},{2,34},{34,2},{3,35},{35,3},{4,36},{36... | collective-permute-start | bytes 884744 | tf_op jit(solution)/shard_map/ppermute | solution.py:29
  96.6 5.1 %outer_step.1 = (f32[4,144,1024]{2,1,0:T(8,128)}, f32[4,144,1024]{2,1,0:T(8,128)}) custom-call(s32[2]{0:T(128)S(1)} %pad_add_fusion.place_ref, f32[144,1024]{1,0:T(8,128)S(1)} %get-tuple-element.78.refs_0_, f32[144,1024]{1,0:T(8,128)S(1)} %convert_multiply_fusion.2.refs_1_, f32[144,1024]{1,0:T(8,128)S(1)} %convert_multiply_fusion.1.refs_2_, ...), custom_call_target="tpu_custom_call" | custom-call | bytes 1024 | tf_op jit(solution)/shard_map/outer_step/pallas_call | solution.py:213
  102.9 4.2 %collective-permute-done.18 = bf16[144,1024]{1,0:T(8,128)(2,1)S(1)} collective-permute-done((bf16[144,1024]{1,0:T(8,128)(2,1)S(1)}, bf16[144,1024]{1,0:T(8,128)(2,1)S(1)}, u32[]{:S(2)}, u32[]{:S(2)}) %collective-permute-start.18) | collective-permute-done | bytes 294944 | tf_op jit(solution)/shard_map/ppermute | solution.py:29
  107.1 1.9 %collective-permute-done.16 = bf16[144,1024]{1,0:T(8,128)(2,1)S(1)} collective-permute-done((bf16[144,1024]{1,0:T(8,128)(2,1)S(1)}, bf16[144,1024]{1,0:T(8,128)(2,1)S(1)}, u32[]{:S(2)}, u32[]{:S(2)}) %collective-permute-start.16) | collective-permute-done | bytes 294944 | tf_op jit(solution)/shard_map/ppermute | solution.py:29
  (73 shorter events, 32.9 us)
Async XLA Ops:
  0.6 22.2 %collective-permute-start = (bf16[256,1024]{1,0:T(8,128)(2,1)}, bf16[256,1024]{1,0:T(8,128)(2,1)S(1)}, u32[]{:S(2)}, u32[]{:S(2)}) collective-permute-start(bf16[256,1024]{1,0:T(8,128)(2,1)} %c0.3), channel_id=1, source_target_pairs={{0,4},{4,8},{8,12},{12,0},{1,5},{5,9},{9,13},{13,1},{2,6},{6,10},{... | collective-permute-start | bytes 1572872 | tf_op jit(solution)/shard_map/ppermute | solution.py:29
  2.8 20.0 %collective-permute-start.1 = (bf16[256,1024]{1,0:T(8,128)(2,1)}, bf16[256,1024]{1,0:T(8,128)(2,1)S(1)}, u32[]{:S(2)}, u32[]{:S(2)}) collective-permute-start(bf16[256,1024]{1,0:T(8,128)(2,1)} %c0.3), channel_id=1, source_target_pairs={{0,12},{4,0},{8,4},{12,8},{1,13},{5,1},{9,5},{13,9},{2,14},{6,2},{... | collective-permute-start | bytes 1572872 | tf_op jit(solution)/shard_map/ppermute | solution.py:29
  7.2 18.4 %collective-permute-start.4 = (bf16[144,1024]{1,0:T(8,128)(2,1)S(1)}, bf16[144,1024]{1,0:T(8,128)(2,1)S(1)}, u32[]{:S(2)}, u32[]{:S(2)}) collective-permute-start(bf16[144,1024]{1,0:T(8,128)(2,1)S(1)} %get-tuple-element.41), channel_id=1, source_target_pairs={{0,16},{16,0},{1,17},{17,1},{2,18},{18,2},{3,19},{19,3},{4,20},{20... | collective-permute-start | bytes 884744 | tf_op jit(solution)/shard_map/ppermute | solution.py:29
  14.2 14.2 %collective-permute-start.19 = (bf16[2,144,1024]{2,1,0:T(8,128)(2,1)}, bf16[2,144,1024]{2,1,0:T(8,128)(2,1)}, u32[]{:S(2)}, u32[]{:S(2)}) collective-permute-start(bf16[2,144,1024]{2,1,0:T(8,128)(2,1)} %get-tuple-element.71), channel_id=1, source_target_pairs={{0,32},{32,0},{1,33},{33,1},{2,34},{34,2},{3,35},{35,3},{4,36},{36... | collective-permute-start | bytes 1769480 | tf_op jit(solution)/shard_map/ppermute | solution.py:29
  22.9 16.6 %collective-permute-start.2 = (bf16[256,1152]{1,0:T(8,128)(2,1)}, bf16[256,1152]{1,0:T(8,128)(2,1)S(1)}, u32[]{:S(2)}, u32[]{:S(2)}) collective-permute-start(bf16[256,1152]{1,0:T(8,128)(2,1)} %get-tuple-element.45), channel_id=1, source_target_pairs={{0,4},{4,8},{8,12},{12,0},{1,5},{5,9},{9,13},{13,1},{2,6},{6,10},{... | collective-permute-start | bytes 1769480 | tf_op jit(solution)/shard_map/ppermute | solution.py:29
  23.0 16.4 %collective-permute-start.3 = (bf16[256,1152]{1,0:T(8,128)(2,1)S(1)}, bf16[256,1152]{1,0:T(8,128)(2,1)S(1)}, u32[]{:S(2)}, u32[]{:S(2)}) collective-permute-start(bf16[256,1152]{1,0:T(8,128)(2,1)S(1)} %get-tuple-element.47), channel_id=1, source_target_pairs={{0,12},{4,0},{8,4},{12,8},{1,13},{5,1},{9,5},{13,9},{2,14},{6,2},{... | collective-permute-start | bytes 1769480 | tf_op jit(solution)/shard_map/ppermute | solution.py:29
  25.7 15.7 %collective-permute-start.5 = (bf16[2,144,1024]{2,1,0:T(8,128)(2,1)S(1)}, bf16[2,144,1024]{2,1,0:T(8,128)(2,1)}, u32[]{:S(2)}, u32[]{:S(2)}) collective-permute-start(bf16[2,144,1024]{2,1,0:T(8,128)(2,1)S(1)} %pad_maximum_fusion.refs_3_.refs_1_), channel_id=1, source_target_pairs={{0,1},{1,2},{2,3},{3,0},{4,5},{5,6},{6,7},{7,4},{8,9},{9,10},{10,1... | collective-permute-start | bytes 1769480 | tf_op jit(solution)/shard_map/ppermute | solution.py:29
  27.0 14.4 %collective-permute-start.6 = (bf16[2,144,1024]{2,1,0:T(8,128)(2,1)S(1)}, bf16[2,144,1024]{2,1,0:T(8,128)(2,1)}, u32[]{:S(2)}, u32[]{:S(2)}) collective-permute-start(bf16[2,144,1024]{2,1,0:T(8,128)(2,1)S(1)} %pad_maximum_fusion.refs_3_.refs_1_), channel_id=1, source_target_pairs={{0,3},{1,0},{2,1},{3,2},{4,7},{5,4},{6,5},{7,6},{8,11},{9,8},{10,9... | collective-permute-start | bytes 1769480 | tf_op jit(solution)/shard_map/ppermute | solution.py:29
  30.5 13.1 %collective-permute-start.20 = (f16[144,1024]{1,0:T(8,128)(2,1)}, f16[144,1024]{1,0:T(8,128)(2,1)}, u32[]{:S(2)}, u32[]{:S(2)}) collective-permute-start(f16[144,1024]{1,0:T(8,128)(2,1)} %fusion), channel_id=1, source_target_pairs={{0,64},{64,0},{128,192},{192,128},{1,65},{65,1},{129,193},{193,129... | collective-permute-start | bytes 884744 | tf_op jit(solution)/shard_map/ppermute | solution.py:33
  39.4 27.1 %collective-permute-start.10 = (bf16[256,2176]{1,0:T(8,128)(2,1)}, bf16[256,2176]{1,0:T(8,128)(2,1)S(1)}, u32[]{:S(2)}, u32[]{:S(2)}) collective-permute-start(bf16[256,2176]{1,0:T(8,128)(2,1)} %copy-done.10), channel_id=1, source_target_pairs={{0,8},{4,12},{8,0},{12,4},{1,9},{5,13},{9,1},{13,5},{2,10},{6,14},... | collective-permute-start | bytes 3342344 | tf_op jit(solution)/shard_map/ppermute | solution.py:29
  41.4 15.0 %collective-permute-start.7 = (bf16[2,144,1024]{2,1,0:T(8,128)(2,1)S(1)}, bf16[2,144,1024]{2,1,0:T(8,128)(2,1)}, u32[]{:S(2)}, u32[]{:S(2)}) collective-permute-start(bf16[2,144,1024]{2,1,0:T(8,128)(2,1)S(1)} %pad_maximum_fusion.refs_3_.refs_1_), channel_id=1, source_target_pairs={{0,2},{1,3},{2,0},{3,1},{4,6},{5,7},{6,4},{7,5},{8,10},{9,11},{10,... | collective-permute-start | bytes 1769480 | tf_op jit(solution)/shard_map/ppermute | solution.py:29
  55.5 15.5 %collective-permute-start.22 = (f16[72,1024]{1,0:T(8,128)(2,1)}, f16[72,1024]{1,0:T(8,128)(2,1)}, u32[]{:S(2)}, u32[]{:S(2)}) collective-permute-start(f16[72,1024]{1,0:T(8,128)(2,1)} %add_convert_fusion.2), channel_id=1, source_target_pairs={{0,128},{64,192},{128,0},{192,64},{1,129},{65,193},{129,1},{193,65... | collective-permute-start | bytes 442376 | tf_op jit(solution)/shard_map/ppermute | solution.py:33
  68.2 8.2 %collective-permute-start.11 = (bf16[144,1024]{1,0:T(8,128)(2,1)S(1)}, bf16[144,1024]{1,0:T(8,128)(2,1)S(1)}, u32[]{:S(2)}, u32[]{:S(2)}) collective-permute-start(bf16[144,1024]{1,0:T(8,128)(2,1)S(1)} %get-tuple-element.57), channel_id=1, source_target_pairs={{0,1},{1,2},{2,3},{3,0},{4,5},{5,6},{6,7},{7,4},{8,9},{9,10},{10,1... | collective-permute-start | bytes 884744 | tf_op jit(solution)/shard_map/ppermute | solution.py:29
  69.3 8.4 %collective-permute-start.12 = (bf16[144,1024]{1,0:T(8,128)(2,1)S(1)}, bf16[144,1024]{1,0:T(8,128)(2,1)S(1)}, u32[]{:S(2)}, u32[]{:S(2)}) collective-permute-start(bf16[144,1024]{1,0:T(8,128)(2,1)S(1)} %get-tuple-element.58), channel_id=1, source_target_pairs={{0,3},{1,0},{2,1},{3,2},{4,7},{5,4},{6,5},{7,6},{8,11},{9,8},{10,9... | collective-permute-start | bytes 884744 | tf_op jit(solution)/shard_map/ppermute | solution.py:29
  72.3 8.4 %collective-permute-start.23 = (f16[144,1024]{1,0:T(8,128)(2,1)S(1)}, f16[144,1024]{1,0:T(8,128)(2,1)S(1)}, u32[]{:S(2)}, u32[]{:S(2)}) collective-permute-start(f16[144,1024]{1,0:T(8,128)(2,1)S(1)} %get-tuple-element.74), channel_id=1, source_target_pairs={{0,64},{64,0},{128,192},{192,128},{1,65},{65,1},{129,193},{193,129... | collective-permute-start | bytes 884744 | tf_op jit(solution)/shard_map/ppermute | solution.py:33
  73.1 11.0 %collective-permute-start.8 = (bf16[256,1024]{1,0:T(8,128)(2,1)S(1)}, bf16[256,1024]{1,0:T(8,128)(2,1)S(1)}, u32[]{:S(2)}, u32[]{:S(2)}) collective-permute-start(bf16[256,1024]{1,0:T(8,128)(2,1)S(1)} %get-tuple-element.51), channel_id=1, source_target_pairs={{0,12},{4,0},{8,4},{12,8},{1,13},{5,1},{9,5},{13,9},{2,14},{6,2},{... | collective-permute-start | bytes 1572872 | tf_op jit(solution)/shard_map/ppermute | solution.py:29
  74.9 11.6 %collective-permute-start.9 = (bf16[256,1024]{1,0:T(8,128)(2,1)S(1)}, bf16[256,1024]{1,0:T(8,128)(2,1)S(1)}, u32[]{:S(2)}, u32[]{:S(2)}) collective-permute-start(bf16[256,1024]{1,0:T(8,128)(2,1)S(1)} %get-tuple-element.52), channel_id=1, source_target_pairs={{0,4},{4,8},{8,12},{12,0},{1,5},{5,9},{9,13},{13,1},{2,6},{6,10},{... | collective-permute-start | bytes 1572872 | tf_op jit(solution)/shard_map/ppermute | solution.py:29
  76.5 16.6 %collective-permute-start.14 = (bf16[144,1024]{1,0:T(8,128)(2,1)S(1)}, bf16[144,1024]{1,0:T(8,128)(2,1)S(1)}, u32[]{:S(2)}, u32[]{:S(2)}) collective-permute-start(bf16[144,1024]{1,0:T(8,128)(2,1)S(1)} %get-tuple-element.64), channel_id=1, source_target_pairs={{0,2},{1,3},{2,0},{3,1},{4,6},{5,7},{6,4},{7,5},{8,10},{9,11},{10,... | collective-permute-start | bytes 884744 | tf_op jit(solution)/shard_map/ppermute | solution.py:29
  77.7 17.2 %collective-permute-start.24 = (f16[144,1024]{1,0:T(8,128)(2,1)S(1)}, f16[144,1024]{1,0:T(8,128)(2,1)S(1)}, u32[]{:S(2)}, u32[]{:S(2)}) collective-permute-start(f16[144,1024]{1,0:T(8,128)(2,1)S(1)} %get-tuple-element.74), channel_id=1, source_target_pairs={{0,32},{32,0},{1,33},{33,1},{2,34},{34,2},{3,35},{35,3},{4,36},{36... | collective-permute-start | bytes 884744 | tf_op jit(solution)/shard_map/ppermute | solution.py:29
  88.9 12.9 %collective-permute-start.13 = (bf16[256,1024]{1,0:T(8,128)(2,1)S(1)}, bf16[256,1024]{1,0:T(8,128)(2,1)S(1)}, u32[]{:S(2)}, u32[]{:S(2)}) collective-permute-start(bf16[256,1024]{1,0:T(8,128)(2,1)S(1)} %keys1.1), channel_id=1, source_target_pairs={{0,8},{4,12},{8,0},{12,4},{1,9},{5,13},{9,1},{13,5},{2,10},{6,14},... | collective-permute-start | bytes 1572872 | tf_op jit(solution)/shard_map/ppermute | solution.py:29
  93.2 13.9 %collective-permute-start.18 = (bf16[144,1024]{1,0:T(8,128)(2,1)S(1)}, bf16[144,1024]{1,0:T(8,128)(2,1)S(1)}, u32[]{:S(2)}, u32[]{:S(2)}) collective-permute-start(bf16[144,1024]{1,0:T(8,128)(2,1)S(1)} %add_convert_fusion.1), channel_id=1, source_target_pairs={{0,16},{16,0},{1,17},{17,1},{2,18},{18,2},{3,19},{19,3},{4,20},{20... | collective-permute-start | bytes 884744 | tf_op jit(solution)/shard_map/ppermute | solution.py:29
  93.5 13.6 %collective-permute-start.17 = (bf16[144,1024]{1,0:T(8,128)(2,1)S(1)}, bf16[144,1024]{1,0:T(8,128)(2,1)S(1)}, u32[]{:S(2)}, u32[]{:S(2)}) collective-permute-start(bf16[144,1024]{1,0:T(8,128)(2,1)S(1)} %get-tuple-element.69), channel_id=1, source_target_pairs={{0,2},{1,3},{2,0},{3,1},{4,6},{5,7},{6,4},{7,5},{8,10},{9,11},{10,... | collective-permute-start | bytes 884744 | tf_op jit(solution)/shard_map/ppermute | solution.py:29
  94.9 14.0 %collective-permute-start.16 = (bf16[144,1024]{1,0:T(8,128)(2,1)S(1)}, bf16[144,1024]{1,0:T(8,128)(2,1)S(1)}, u32[]{:S(2)}, u32[]{:S(2)}) collective-permute-start(bf16[144,1024]{1,0:T(8,128)(2,1)S(1)} %get-tuple-element.67), channel_id=1, source_target_pairs={{0,3},{1,0},{2,1},{3,2},{4,7},{5,4},{6,5},{7,6},{8,11},{9,8},{10,9... | collective-permute-start | bytes 884744 | tf_op jit(solution)/shard_map/ppermute | solution.py:29
  95.9 14.5 %collective-permute-start.15 = (bf16[144,1024]{1,0:T(8,128)(2,1)S(1)}, bf16[144,1024]{1,0:T(8,128)(2,1)S(1)}, u32[]{:S(2)}, u32[]{:S(2)}) collective-permute-start(bf16[144,1024]{1,0:T(8,128)(2,1)S(1)} %get-tuple-element.65), channel_id=1, source_target_pairs={{0,1},{1,2},{2,3},{3,0},{4,5},{5,6},{6,7},{7,4},{8,9},{9,10},{10,1... | collective-permute-start | bytes 884744 | tf_op jit(solution)/shard_map/ppermute | solution.py:29
  (14 other events, 89.3 us)

commit v10 on v9

--- a/solution.py
+++ b/solution.py
@@ -195,7 +195,7 @@
     a1, a3 = _shift(g[1], "x", 1), _shift(g[3], "x", 3)
     b = grad(1, own)
     a2 = _shift(_after(g[2], a1), "x", 2)
-    (k2,) = keys_of(_after(r2, b[0], e1, e3, a1, a3))
+    (k2,) = keys_of(_after(r2, b[0], a1, a3))
     swapped = [_shift(_after(v, a1, a3), "core", 1, 2) for v in (mine, next_layer)]
     far_sum = (g[0] + sum(v.astype(F32) for v in (a1, a2, a3))).astype(BF)
     from_zh = _shift(far_sum, "zh", 1, 2)
@@ -224,7 +224,7 @@
         cost_estimate=pl.CostEstimate(flops=0, bytes_accessed=1024, transcendentals=0),
     )(jnp.stack([core, lo]).astype(jnp.int32), *averages, global_fragment, momentum)
 
-    e2 = _shift(_after(k2, b[0]), "y", 2)
+    e2 = _shift(_after(k2, b[0], e1, e3), "y", 2)
     keys = k0 + sum(v.astype(F32) for v in (e1, e3, e2))
     return keys.astype(BF), weight_grad, new_global, new_momentum
 

time: 112 us -> 110 us (0.982)
  waiting for transfers between devices: 32.3 us -> 29.8 us
    ppermute x22, waiting for transfers between devices: 27.4 us -> 24.9 us  [_shift(): return lax.ppermute(v, axis, [(i, (i + k) % size) for i in range(size)])]
  transfers between devices with their start and end apart: 26 -> 26, of which waited for: 11 -> 10; matrix products, arithmetic and copies ran while one was open for 9% -> 9% of each run, Pallas kernels for 17% -> 17%
where the time goes in v10:
time: 110 us; the launch traced here: 109 us
  starting transfers between devices  42.2 us (38%)
  waiting for transfers between devices  29.8 us (27%)
  Pallas kernels  18.9 us (17%)
  other arithmetic  9.81 us (9%)
  local copies, waits for them, and re-layouts  6.53 us (6%)
  between operations  1.49 us (1%)
    ppermute x22, starting transfers between devices, _shift(): return lax.ppermute(v, axis, [(i, (i + k) % size) for i in range(size)])  36.5 us
    ppermute x22, waiting for transfers between devices, _shift(): return lax.ppermute(v, axis, [(i, (i + k) % size) for i in range(size)])  24.9 us
    pallas_call x2, Pallas kernels, keys_of(): _call(functools.partial(_keys_kernel, len(blocks)), f'keys{len(blocks)}',...  6.29 us
    unnamed x24, local copies, waits for them, and re-layouts  5.79 us
    ppermute x4, starting transfers between devices, _flip(): return lax.ppermute(v, axis, [(i, i ^ bit) for i in range(size)])  5.66 us
    pallas_call x1, Pallas kernels, body(): pl.pallas_call(_outer_kernel, name='outer_step', out_shape=[jax.ShapeDtyp...  5.12 us
    ppermute x4, waiting for transfers between devices, _flip(): return lax.ppermute(v, axis, [(i, i ^ bit) for i in range(size)])  4.9 us
    pallas_call x2, Pallas kernels, grad(): _call(functools.partial(_grad_kernel, half), f'grad{half}', [((ROWS, KV),...  3.79 us
  transfers between devices with their start and end apart: 26, of which 10 were waited for; matrix products, arithmetic and copies ran while one was open for 9% of the time, Pallas kernels for 17%

profile of v10, /device:TPU:1, one launch (start us, length us, event | category | flops | bytes accessed | tf_op | source)
XLA Modules:
  0.0 108.8 jit_solution(3981026164278191368)
XLA Ops:
  0.6 2.2 %collective-permute-start = (bf16[256,1024]{1,0:T(8,128)(2,1)}, bf16[256,1024]{1,0:T(8,128)(2,1)S(1)}, u32[]{:S(2)}, u32[]{:S(2)}) collective-permute-start(bf16[256,1024]{1,0:T(8,128)(2,1)} %c0.3), channel_id=1, source_target_pairs={{0,4},{4,8},{8,12},{12,0},{1,5},{5,9},{9,13},{13,1},{2,6},{6,10},{... | collective-permute-start | bytes 1572872 | tf_op jit(solution)/shard_map/ppermute | solution.py:29
  7.2 7.0 %collective-permute-start.4 = (bf16[144,1024]{1,0:T(8,128)(2,1)S(1)}, bf16[144,1024]{1,0:T(8,128)(2,1)S(1)}, u32[]{:S(2)}, u32[]{:S(2)}) collective-permute-start(bf16[144,1024]{1,0:T(8,128)(2,1)S(1)} %get-tuple-element.41), channel_id=1, source_target_pairs={{0,16},{16,0},{1,17},{17,1},{2,18},{18,2},{3,19},{19,3},{4,20},{20... | collective-permute-start | bytes 884744 | tf_op jit(solution)/shard_map/ppermute | solution.py:29
  17.4 1.7 %copy-done.3 = bf16[256,4608]{1,0:T(8,128)(2,1)S(1)} copy-done((bf16[256,4608]{1,0:T(8,128)(2,1)S(1)}, bf16[256,4608]{1,0:T(8,128)(2,1)}, u32[]{:S(2)}) %copy-start.3) | copy-done | bytes 2359320
  19.0 2.8 %normed.1 = (bf16[256,1152]{1,0:T(8,128)(2,1)S(1)}, bf16[256,1152]{1,0:T(8,128)(2,1)}, bf16[256,2176]{1,0:T(8,128)(2,1)S(1)}, bf16[256,1152]{1,0:T(8,128)(2,1)S(1)}) custom-call(bf16[256,4608]{1,0:T(8,128)(2,1)S(1)} %copy-done.3, f32[1,4608]{1,0:T(1,128)S(1)} %broadcast_in_dim.6.gain_ref, bf16[256,1024]{1,0:T(8,128)(2,1)S(1)} %copy-done.1), custom_call_target="tpu_custom_call" | custom-call | bytes 1024 | tf_op jit(solution)/shard_map/normed/pallas_call | solution.py:137
  23.0 2.6 %collective-permute-start.3 = (bf16[256,1152]{1,0:T(8,128)(2,1)S(1)}, bf16[256,1152]{1,0:T(8,128)(2,1)S(1)}, u32[]{:S(2)}, u32[]{:S(2)}) collective-permute-start(bf16[256,1152]{1,0:T(8,128)(2,1)S(1)} %get-tuple-element.47), channel_id=1, source_target_pairs={{0,12},{4,0},{8,4},{12,8},{1,13},{5,1},{9,5},{13,9},{2,14},{6,2},{... | collective-permute-start | bytes 1769480 | tf_op jit(solution)/shard_map/ppermute | solution.py:29
  28.4 2.0 %fusion = f16[144,1024]{1,0:T(8,128)(2,1)} fusion(f32[4,144,1024]{2,1,0:T(8,128)} %refs_4_.1, s32[]{:T(128)S(6)} %select_n.33, bf16[2,144,1024]{2,1,0:T(8,128)(2,1)} %collective-permute-done.19, s32[]{:T(128)S(6)} %select_n.34, bf16[2,144,1024]{2,1,0:T(8,128)(2,1)S(1)} %get-tuple-element.70), kind=kLoop, calls=%fused_computation.10 | loop fusion | flops 1032192 | bytes 1474568 | tf_op jit(solution)/shard_map/mul | solution.py:157
  30.5 1.9 %collective-permute-start.20 = (f16[144,1024]{1,0:T(8,128)(2,1)}, f16[144,1024]{1,0:T(8,128)(2,1)}, u32[]{:S(2)}, u32[]{:S(2)}) collective-permute-start(f16[144,1024]{1,0:T(8,128)(2,1)} %fusion), channel_id=1, source_target_pairs={{0,64},{64,0},{128,192},{192,128},{1,65},{65,1},{129,193},{193,129... | collective-permute-start | bytes 884744 | tf_op jit(solution)/shard_map/ppermute | solution.py:33
  32.4 7.1 %collective-permute-done.2.refs_1_.n1 = bf16[256,1152]{1,0:T(8,128)(2,1)S(1)} collective-permute-done((bf16[256,1152]{1,0:T(8,128)(2,1)}, bf16[256,1152]{1,0:T(8,128)(2,1)S(1)}, u32[]{:S(2)}, u32[]{:S(2)}) %collective-permute-start.2) | collective-permute-done | bytes 589856 | tf_op jit(solution)/shard_map/ppermute | solution.py:29
  41.4 2.1 %collective-permute-start.7 = (bf16[2,144,1024]{2,1,0:T(8,128)(2,1)S(1)}, bf16[2,144,1024]{2,1,0:T(8,128)(2,1)}, u32[]{:S(2)}, u32[]{:S(2)}) collective-permute-start(bf16[2,144,1024]{2,1,0:T(8,128)(2,1)S(1)} %pad_maximum_fusion.refs_3_.refs_1_), channel_id=1, source_target_pairs={{0,2},{1,3},{2,0},{3,1},{4,6},{5,7},{6,4},{7,5},{8,10},{9,11},{10,... | collective-permute-start | bytes 1769480 | tf_op jit(solution)/shard_map/ppermute | solution.py:29
  46.5 2.3 %collective-permute-start.21 = (f16[72,1024]{1,0:T(8,128)(2,1)}, f16[72,1024]{1,0:T(8,128)(2,1)}, u32[]{:S(2)}, u32[]{:S(2)}) collective-permute-start(f16[72,1024]{1,0:T(8,128)(2,1)} %dynamic-slice_convert_fusion), channel_id=1, source_target_pairs={{0,128},{64,192},{128,0},{192,64},{1,129},{65,193},{129,1},{193,65... | collective-permute-start | bytes 442376 | tf_op jit(solution)/shard_map/ppermute | solution.py:33
  48.8 4.9 %collective-permute-done.21 = f16[72,1024]{1,0:T(8,128)(2,1)} collective-permute-done((f16[72,1024]{1,0:T(8,128)(2,1)}, f16[72,1024]{1,0:T(8,128)(2,1)}, u32[]{:S(2)}, u32[]{:S(2)}) %collective-permute-start.21) | collective-permute-done | bytes 147488 | tf_op jit(solution)/shard_map/ppermute | solution.py:33
  53.7 1.7 %add_convert_fusion.2 = f16[72,1024]{1,0:T(8,128)(2,1)} fusion(f16[72,1024]{1,0:T(8,128)(2,1)} %collective-permute-done.21, f32[144,1024]{1,0:T(8,128)} %copy-done.11, s32[]{:T(128)S(6)} %select_n.35), kind=kLoop, calls=%fused_computation.12 | loop fusion | flops 221184 | bytes 589828 | tf_op jit(solution)/shard_map/convert_element_type | solution.py:163
  56.4 3.9 %keys3.1 = (f32[256,1024]{1,0:T(8,128)S(1)}, bf16[256,1024]{1,0:T(8,128)(2,1)S(1)}, bf16[256,1024]{1,0:T(8,128)(2,1)S(1)}) custom-call(bf16[256,1152]{1,0:T(8,128)(2,1)S(1)} %get-tuple-element.56.refs_0_.n0, bf16[256,1152]{1,0:T(8,128)(2,1)S(1)} %collective-permute-done.2.refs_1_.n1, bf16[256,1152]{1,0:T(8,128)(2,1)S(1)} %collective-permute-done.3.refs_2_.n3, ...), custom_call_target="tpu_custom_call" | custom-call | bytes 1024 | tf_op jit(solution)/shard_map/keys3/pallas_call | solution.py:172
  60.3 6.3 %collective-permute-done.10.m2.refs_0_ = bf16[256,2176]{1,0:T(8,128)(2,1)S(1)} collective-permute-done((bf16[256,2176]{1,0:T(8,128)(2,1)}, bf16[256,2176]{1,0:T(8,128)(2,1)S(1)}, u32[]{:S(2)}, u32[]{:S(2)}) %collective-permute-start.10) | collective-permute-done | bytes 1114144 | tf_op jit(solution)/shard_map/ppermute | solution.py:29
  66.6 1.6 %grad0.1 = (f32[144,1024]{1,0:T(8,128)S(1)}, bf16[144,1024]{1,0:T(8,128)(2,1)S(1)}, bf16[144,1024]{1,0:T(8,128)(2,1)S(1)}, bf16[144,1024]{1,0:T(8,128)(2,1)S(1)}) custom-call(bf16[256,1152]{1,0:T(8,128)(2,1)S(1)} %get-tuple-element.56.refs_0_.n0, bf16[256,1024]{1,0:T(8,128)(2,1)S(1)} %copy-done.2, bf16[256,1152]{1,0:T(8,128)(2,1)S(1)} %collective-permute-done.2.refs_1_.n1, ...), custom_call_target="tpu_custom_call" | custom-call | bytes 1024 | tf_op jit(solution)/shard_map/grad0/pallas_call | solution.py:185
  69.3 1.7 %collective-permute-start.12 = (bf16[144,1024]{1,0:T(8,128)(2,1)S(1)}, bf16[144,1024]{1,0:T(8,128)(2,1)S(1)}, u32[]{:S(2)}, u32[]{:S(2)}) collective-permute-start(bf16[144,1024]{1,0:T(8,128)(2,1)S(1)} %get-tuple-element.58), channel_id=1, source_target_pairs={{0,3},{1,0},{2,1},{3,2},{4,7},{5,4},{6,5},{7,6},{8,11},{9,8},{10,9... | collective-permute-start | bytes 884744 | tf_op jit(solution)/shard_map/ppermute | solution.py:29
  73.1 1.8 %collective-permute-start.8 = (bf16[256,1024]{1,0:T(8,128)(2,1)S(1)}, bf16[256,1024]{1,0:T(8,128)(2,1)S(1)}, u32[]{:S(2)}, u32[]{:S(2)}) collective-permute-start(bf16[256,1024]{1,0:T(8,128)(2,1)S(1)} %get-tuple-element.51), channel_id=1, source_target_pairs={{0,12},{4,0},{8,4},{12,8},{1,13},{5,1},{9,5},{13,9},{2,14},{6,2},{... | collective-permute-start | bytes 1572872 | tf_op jit(solution)/shard_map/ppermute | solution.py:29
  77.7 2.9 %collective-permute-start.24 = (f16[144,1024]{1,0:T(8,128)(2,1)S(1)}, f16[144,1024]{1,0:T(8,128)(2,1)S(1)}, u32[]{:S(2)}, u32[]{:S(2)}) collective-permute-start(f16[144,1024]{1,0:T(8,128)(2,1)S(1)} %get-tuple-element.74), channel_id=1, source_target_pairs={{0,32},{32,0},{1,33},{33,1},{2,34},{34,2},{3,35},{35,3},{4,36},{36... | collective-permute-start | bytes 884744 | tf_op jit(solution)/shard_map/ppermute | solution.py:29
  80.7 2.1 %grad1.1 = (f32[144,1024]{1,0:T(8,128)S(1)}, bf16[144,1024]{1,0:T(8,128)(2,1)S(1)}, bf16[144,1024]{1,0:T(8,128)(2,1)S(1)}, bf16[144,1024]{1,0:T(8,128)(2,1)S(1)}) custom-call(bf16[256,1152]{1,0:T(8,128)(2,1)S(1)} %get-tuple-element.56.refs_0_.n0, bf16[256,1024]{1,0:T(8,128)(2,1)S(1)} %copy-done.2, bf16[256,1152]{1,0:T(8,128)(2,1)S(1)} %collective-permute-done.2.refs_1_.n1, ...), custom_call_target="tpu_custom_call" | custom-call | bytes 1024 | tf_op jit(solution)/shard_map/grad1/pallas_call | solution.py:185
  82.8 2.4 %keys1.1 = bf16[256,1024]{1,0:T(8,128)(2,1)S(1)} custom-call(bf16[256,2176]{1,0:T(8,128)(2,1)S(1)} %collective-permute-done.10.m2.refs_0_, bf16[2,144,1024]{2,1,0:T(8,128)(2,1)S(1)} %pad_maximum_fusion.refs_3_.refs_1_, bf16[2,144,1024]{2,1,0:T(8,128)(2,1)} %collective-permute-done.5.refs_4_.refs_2_, ...), custom_call_target="tpu_custom_call" | custom-call | bytes 1024 | tf_op jit(solution)/shard_map/keys1/pallas_call | solution.py:172
  86.5 4.0 %collective-permute-start.25 = (f16[144,1024]{1,0:T(8,128)(2,1)S(1)}, f16[144,1024]{1,0:T(8,128)(2,1)S(1)}, u32[]{:S(2)}, u32[]{:S(2)}) collective-permute-start(f16[144,1024]{1,0:T(8,128)(2,1)S(1)} %collective-permute-done.23), channel_id=1, source_target_pairs={{0,32},{32,0},{1,33},{33,1},{2,34},{34,2},{3,35},{35,3},{4,36},{36... | collective-permute-start | bytes 884744 | tf_op jit(solution)/shard_map/ppermute | solution.py:29
  94.0 5.1 %outer_step.1 = (f32[4,144,1024]{2,1,0:T(8,128)}, f32[4,144,1024]{2,1,0:T(8,128)}) custom-call(s32[2]{0:T(128)S(1)} %pad_add_fusion.place_ref, f32[144,1024]{1,0:T(8,128)S(1)} %get-tuple-element.78.refs_0_, f32[144,1024]{1,0:T(8,128)S(1)} %convert_multiply_fusion.2.refs_1_, f32[144,1024]{1,0:T(8,128)S(1)} %convert_multiply_fusion.1.refs_2_, ...), custom_call_target="tpu_custom_call" | custom-call | bytes 1024 | tf_op jit(solution)/shard_map/outer_step/pallas_call | solution.py:213
  100.3 4.2 %collective-permute-done.18 = bf16[144,1024]{1,0:T(8,128)(2,1)S(1)} collective-permute-done((bf16[144,1024]{1,0:T(8,128)(2,1)S(1)}, bf16[144,1024]{1,0:T(8,128)(2,1)S(1)}, u32[]{:S(2)}, u32[]{:S(2)}) %collective-permute-start.18) | collective-permute-done | bytes 294944 | tf_op jit(solution)/shard_map/ppermute | solution.py:29
  104.5 1.9 %collective-permute-done.16 = bf16[144,1024]{1,0:T(8,128)(2,1)S(1)} collective-permute-done((bf16[144,1024]{1,0:T(8,128)(2,1)S(1)}, bf16[144,1024]{1,0:T(8,128)(2,1)S(1)}, u32[]{:S(2)}, u32[]{:S(2)}) %collective-permute-start.16) | collective-permute-done | bytes 294944 | tf_op jit(solution)/shard_map/ppermute | solution.py:29
  (73 shorter events, 31.1 us)
Async XLA Ops:
  0.6 22.2 %collective-permute-start = (bf16[256,1024]{1,0:T(8,128)(2,1)}, bf16[256,1024]{1,0:T(8,128)(2,1)S(1)}, u32[]{:S(2)}, u32[]{:S(2)}) collective-permute-start(bf16[256,1024]{1,0:T(8,128)(2,1)} %c0.3), channel_id=1, source_target_pairs={{0,4},{4,8},{8,12},{12,0},{1,5},{5,9},{9,13},{13,1},{2,6},{6,10},{... | collective-permute-start | bytes 1572872 | tf_op jit(solution)/shard_map/ppermute | solution.py:29
  2.8 20.0 %collective-permute-start.1 = (bf16[256,1024]{1,0:T(8,128)(2,1)}, bf16[256,1024]{1,0:T(8,128)(2,1)S(1)}, u32[]{:S(2)}, u32[]{:S(2)}) collective-permute-start(bf16[256,1024]{1,0:T(8,128)(2,1)} %c0.3), channel_id=1, source_target_pairs={{0,12},{4,0},{8,4},{12,8},{1,13},{5,1},{9,5},{13,9},{2,14},{6,2},{... | collective-permute-start | bytes 1572872 | tf_op jit(solution)/shard_map/ppermute | solution.py:29
  7.2 18.4 %collective-permute-start.4 = (bf16[144,1024]{1,0:T(8,128)(2,1)S(1)}, bf16[144,1024]{1,0:T(8,128)(2,1)S(1)}, u32[]{:S(2)}, u32[]{:S(2)}) collective-permute-start(bf16[144,1024]{1,0:T(8,128)(2,1)S(1)} %get-tuple-element.41), channel_id=1, source_target_pairs={{0,16},{16,0},{1,17},{17,1},{2,18},{18,2},{3,19},{19,3},{4,20},{20... | collective-permute-start | bytes 884744 | tf_op jit(solution)/shard_map/ppermute | solution.py:29
  14.2 14.2 %collective-permute-start.19 = (bf16[2,144,1024]{2,1,0:T(8,128)(2,1)}, bf16[2,144,1024]{2,1,0:T(8,128)(2,1)}, u32[]{:S(2)}, u32[]{:S(2)}) collective-permute-start(bf16[2,144,1024]{2,1,0:T(8,128)(2,1)} %get-tuple-element.71), channel_id=1, source_target_pairs={{0,32},{32,0},{1,33},{33,1},{2,34},{34,2},{3,35},{35,3},{4,36},{36... | collective-permute-start | bytes 1769480 | tf_op jit(solution)/shard_map/ppermute | solution.py:29
  22.9 16.6 %collective-permute-start.2 = (bf16[256,1152]{1,0:T(8,128)(2,1)}, bf16[256,1152]{1,0:T(8,128)(2,1)S(1)}, u32[]{:S(2)}, u32[]{:S(2)}) collective-permute-start(bf16[256,1152]{1,0:T(8,128)(2,1)} %get-tuple-element.45), channel_id=1, source_target_pairs={{0,4},{4,8},{8,12},{12,0},{1,5},{5,9},{9,13},{13,1},{2,6},{6,10},{... | collective-permute-start | bytes 1769480 | tf_op jit(solution)/shard_map/ppermute | solution.py:29
  23.0 16.4 %collective-permute-start.3 = (bf16[256,1152]{1,0:T(8,128)(2,1)S(1)}, bf16[256,1152]{1,0:T(8,128)(2,1)S(1)}, u32[]{:S(2)}, u32[]{:S(2)}) collective-permute-start(bf16[256,1152]{1,0:T(8,128)(2,1)S(1)} %get-tuple-element.47), channel_id=1, source_target_pairs={{0,12},{4,0},{8,4},{12,8},{1,13},{5,1},{9,5},{13,9},{2,14},{6,2},{... | collective-permute-start | bytes 1769480 | tf_op jit(solution)/shard_map/ppermute | solution.py:29
  25.7 15.7 %collective-permute-start.5 = (bf16[2,144,1024]{2,1,0:T(8,128)(2,1)S(1)}, bf16[2,144,1024]{2,1,0:T(8,128)(2,1)}, u32[]{:S(2)}, u32[]{:S(2)}) collective-permute-start(bf16[2,144,1024]{2,1,0:T(8,128)(2,1)S(1)} %pad_maximum_fusion.refs_3_.refs_1_), channel_id=1, source_target_pairs={{0,1},{1,2},{2,3},{3,0},{4,5},{5,6},{6,7},{7,4},{8,9},{9,10},{10,1... | collective-permute-start | bytes 1769480 | tf_op jit(solution)/shard_map/ppermute | solution.py:29
  27.0 14.4 %collective-permute-start.6 = (bf16[2,144,1024]{2,1,0:T(8,128)(2,1)S(1)}, bf16[2,144,1024]{2,1,0:T(8,128)(2,1)}, u32[]{:S(2)}, u32[]{:S(2)}) collective-permute-start(bf16[2,144,1024]{2,1,0:T(8,128)(2,1)S(1)} %pad_maximum_fusion.refs_3_.refs_1_), channel_id=1, source_target_pairs={{0,3},{1,0},{2,1},{3,2},{4,7},{5,4},{6,5},{7,6},{8,11},{9,8},{10,9... | collective-permute-start | bytes 1769480 | tf_op jit(solution)/shard_map/ppermute | solution.py:29
  30.5 13.1 %collective-permute-start.20 = (f16[144,1024]{1,0:T(8,128)(2,1)}, f16[144,1024]{1,0:T(8,128)(2,1)}, u32[]{:S(2)}, u32[]{:S(2)}) collective-permute-start(f16[144,1024]{1,0:T(8,128)(2,1)} %fusion), channel_id=1, source_target_pairs={{0,64},{64,0},{128,192},{192,128},{1,65},{65,1},{129,193},{193,129... | collective-permute-start | bytes 884744 | tf_op jit(solution)/shard_map/ppermute | solution.py:33
  39.4 27.1 %collective-permute-start.10 = (bf16[256,2176]{1,0:T(8,128)(2,1)}, bf16[256,2176]{1,0:T(8,128)(2,1)S(1)}, u32[]{:S(2)}, u32[]{:S(2)}) collective-permute-start(bf16[256,2176]{1,0:T(8,128)(2,1)} %copy-done.10), channel_id=1, source_target_pairs={{0,8},{4,12},{8,0},{12,4},{1,9},{5,13},{9,1},{13,5},{2,10},{6,14},... | collective-permute-start | bytes 3342344 | tf_op jit(solution)/shard_map/ppermute | solution.py:29
  41.4 15.0 %collective-permute-start.7 = (bf16[2,144,1024]{2,1,0:T(8,128)(2,1)S(1)}, bf16[2,144,1024]{2,1,0:T(8,128)(2,1)}, u32[]{:S(2)}, u32[]{:S(2)}) collective-permute-start(bf16[2,144,1024]{2,1,0:T(8,128)(2,1)S(1)} %pad_maximum_fusion.refs_3_.refs_1_), channel_id=1, source_target_pairs={{0,2},{1,3},{2,0},{3,1},{4,6},{5,7},{6,4},{7,5},{8,10},{9,11},{10,... | collective-permute-start | bytes 1769480 | tf_op jit(solution)/shard_map/ppermute | solution.py:29
  55.5 15.5 %collective-permute-start.22 = (f16[72,1024]{1,0:T(8,128)(2,1)}, f16[72,1024]{1,0:T(8,128)(2,1)}, u32[]{:S(2)}, u32[]{:S(2)}) collective-permute-start(f16[72,1024]{1,0:T(8,128)(2,1)} %add_convert_fusion.2), channel_id=1, source_target_pairs={{0,128},{64,192},{128,0},{192,64},{1,129},{65,193},{129,1},{193,65... | collective-permute-start | bytes 442376 | tf_op jit(solution)/shard_map/ppermute | solution.py:33
  68.2 8.2 %collective-permute-start.11 = (bf16[144,1024]{1,0:T(8,128)(2,1)S(1)}, bf16[144,1024]{1,0:T(8,128)(2,1)S(1)}, u32[]{:S(2)}, u32[]{:S(2)}) collective-permute-start(bf16[144,1024]{1,0:T(8,128)(2,1)S(1)} %get-tuple-element.57), channel_id=1, source_target_pairs={{0,1},{1,2},{2,3},{3,0},{4,5},{5,6},{6,7},{7,4},{8,9},{9,10},{10,1... | collective-permute-start | bytes 884744 | tf_op jit(solution)/shard_map/ppermute | solution.py:29
  69.3 8.4 %collective-permute-start.12 = (bf16[144,1024]{1,0:T(8,128)(2,1)S(1)}, bf16[144,1024]{1,0:T(8,128)(2,1)S(1)}, u32[]{:S(2)}, u32[]{:S(2)}) collective-permute-start(bf16[144,1024]{1,0:T(8,128)(2,1)S(1)} %get-tuple-element.58), channel_id=1, source_target_pairs={{0,3},{1,0},{2,1},{3,2},{4,7},{5,4},{6,5},{7,6},{8,11},{9,8},{10,9... | collective-permute-start | bytes 884744 | tf_op jit(solution)/shard_map/ppermute | solution.py:29
  72.3 8.4 %collective-permute-start.23 = (f16[144,1024]{1,0:T(8,128)(2,1)S(1)}, f16[144,1024]{1,0:T(8,128)(2,1)S(1)}, u32[]{:S(2)}, u32[]{:S(2)}) collective-permute-start(f16[144,1024]{1,0:T(8,128)(2,1)S(1)} %get-tuple-element.74), channel_id=1, source_target_pairs={{0,64},{64,0},{128,192},{192,128},{1,65},{65,1},{129,193},{193,129... | collective-permute-start | bytes 884744 | tf_op jit(solution)/shard_map/ppermute | solution.py:33
  73.1 12.2 %collective-permute-start.8 = (bf16[256,1024]{1,0:T(8,128)(2,1)S(1)}, bf16[256,1024]{1,0:T(8,128)(2,1)S(1)}, u32[]{:S(2)}, u32[]{:S(2)}) collective-permute-start(bf16[256,1024]{1,0:T(8,128)(2,1)S(1)} %get-tuple-element.51), channel_id=1, source_target_pairs={{0,12},{4,0},{8,4},{12,8},{1,13},{5,1},{9,5},{13,9},{2,14},{6,2},{... | collective-permute-start | bytes 1572872 | tf_op jit(solution)/shard_map/ppermute | solution.py:29
  74.9 11.6 %collective-permute-start.9 = (bf16[256,1024]{1,0:T(8,128)(2,1)S(1)}, bf16[256,1024]{1,0:T(8,128)(2,1)S(1)}, u32[]{:S(2)}, u32[]{:S(2)}) collective-permute-start(bf16[256,1024]{1,0:T(8,128)(2,1)S(1)} %get-tuple-element.52), channel_id=1, source_target_pairs={{0,4},{4,8},{8,12},{12,0},{1,5},{5,9},{9,13},{13,1},{2,6},{6,10},{... | collective-permute-start | bytes 1572872 | tf_op jit(solution)/shard_map/ppermute | solution.py:29
  76.5 14.0 %collective-permute-start.14 = (bf16[144,1024]{1,0:T(8,128)(2,1)S(1)}, bf16[144,1024]{1,0:T(8,128)(2,1)S(1)}, u32[]{:S(2)}, u32[]{:S(2)}) collective-permute-start(bf16[144,1024]{1,0:T(8,128)(2,1)S(1)} %get-tuple-element.64), channel_id=1, source_target_pairs={{0,2},{1,3},{2,0},{3,1},{4,6},{5,7},{6,4},{7,5},{8,10},{9,11},{10,... | collective-permute-start | bytes 884744 | tf_op jit(solution)/shard_map/ppermute | solution.py:29
  77.7 14.6 %collective-permute-start.24 = (f16[144,1024]{1,0:T(8,128)(2,1)S(1)}, f16[144,1024]{1,0:T(8,128)(2,1)S(1)}, u32[]{:S(2)}, u32[]{:S(2)}) collective-permute-start(f16[144,1024]{1,0:T(8,128)(2,1)S(1)} %get-tuple-element.74), channel_id=1, source_target_pairs={{0,32},{32,0},{1,33},{33,1},{2,34},{34,2},{3,35},{35,3},{4,36},{36... | collective-permute-start | bytes 884744 | tf_op jit(solution)/shard_map/ppermute | solution.py:29
  86.5 12.7 %collective-permute-start.13 = (bf16[256,1024]{1,0:T(8,128)(2,1)S(1)}, bf16[256,1024]{1,0:T(8,128)(2,1)S(1)}, u32[]{:S(2)}, u32[]{:S(2)}) collective-permute-start(bf16[256,1024]{1,0:T(8,128)(2,1)S(1)} %keys1.1), channel_id=1, source_target_pairs={{0,8},{4,12},{8,0},{12,4},{1,9},{5,13},{9,1},{13,5},{2,10},{6,14},... | collective-permute-start | bytes 1572872 | tf_op jit(solution)/shard_map/ppermute | solution.py:29
  90.6 13.9 %collective-permute-start.18 = (bf16[144,1024]{1,0:T(8,128)(2,1)S(1)}, bf16[144,1024]{1,0:T(8,128)(2,1)S(1)}, u32[]{:S(2)}, u32[]{:S(2)}) collective-permute-start(bf16[144,1024]{1,0:T(8,128)(2,1)S(1)} %add_convert_fusion.1), channel_id=1, source_target_pairs={{0,16},{16,0},{1,17},{17,1},{2,18},{18,2},{3,19},{19,3},{4,20},{20... | collective-permute-start | bytes 884744 | tf_op jit(solution)/shard_map/ppermute | solution.py:29
  90.9 13.6 %collective-permute-start.17 = (bf16[144,1024]{1,0:T(8,128)(2,1)S(1)}, bf16[144,1024]{1,0:T(8,128)(2,1)S(1)}, u32[]{:S(2)}, u32[]{:S(2)}) collective-permute-start(bf16[144,1024]{1,0:T(8,128)(2,1)S(1)} %get-tuple-element.69), channel_id=1, source_target_pairs={{0,2},{1,3},{2,0},{3,1},{4,6},{5,7},{6,4},{7,5},{8,10},{9,11},{10,... | collective-permute-start | bytes 884744 | tf_op jit(solution)/shard_map/ppermute | solution.py:29
  92.3 14.1 %collective-permute-start.16 = (bf16[144,1024]{1,0:T(8,128)(2,1)S(1)}, bf16[144,1024]{1,0:T(8,128)(2,1)S(1)}, u32[]{:S(2)}, u32[]{:S(2)}) collective-permute-start(bf16[144,1024]{1,0:T(8,128)(2,1)S(1)} %get-tuple-element.67), channel_id=1, source_target_pairs={{0,3},{1,0},{2,1},{3,2},{4,7},{5,4},{6,5},{7,6},{8,11},{9,8},{10,9... | collective-permute-start | bytes 884744 | tf_op jit(solution)/shard_map/ppermute | solution.py:29
  93.3 14.5 %collective-permute-start.15 = (bf16[144,1024]{1,0:T(8,128)(2,1)S(1)}, bf16[144,1024]{1,0:T(8,128)(2,1)S(1)}, u32[]{:S(2)}, u32[]{:S(2)}) collective-permute-start(bf16[144,1024]{1,0:T(8,128)(2,1)S(1)} %get-tuple-element.65), channel_id=1, source_target_pairs={{0,1},{1,2},{2,3},{3,0},{4,5},{5,6},{6,7},{7,4},{8,9},{9,10},{10,1... | collective-permute-start | bytes 884744 | tf_op jit(solution)/shard_map/ppermute | solution.py:29
  (14 other events, 90.2 us)

commit v11 on v10

--- a/solution.py
+++ b/solution.py
@@ -70,7 +70,7 @@
     _, _, zh, y, _ = _place()
     values = x_ref[...].astype(F32)
     stats = jnp.mean(values * values, axis=1, keepdims=True)
-    normed = (values * lax.rsqrt(stats + 1e-06) * gain_ref[...]).astype(BF)
+    normed = (values * lax.rsqrt(stats + 1e-06) * gain_ref[...][None, :]).astype(BF)
     for q in range(8):
         held[q] = normed[:, q * WIDE : (q + 1) * WIDE]
     for k, out in enumerate((own_ref, n1_ref, m2_ref, n3_ref)):
@@ -140,9 +140,9 @@
         [((TOK, n), BF) for n in (2 * WIDE, 2 * WIDE, MSG, 2 * WIDE)],
         [pltpu.VMEM((8, rows, WIDE), BF)],
         grid=(TOK // rows,),
-        in_specs=[tile(D), pl.BlockSpec((1, D), lambda i: (0, 0)), tile(KV)],
+        in_specs=[tile(D), pl.BlockSpec((D,), lambda i: (0,)), tile(KV)],
         out_specs=[tile(n) for n in (2 * WIDE, 2 * WIDE, MSG, 2 * WIDE)],
-    )(inputs, _after(norm_gain[None, :], used), cotangent)
+    )(inputs, _after(norm_gain, used), cotangent)
 
     pair = jnp.stack([_after(used_other, c1, c3), used])
     p1, p3 = _shift(pair, "x", 1), _shift(pair, "x", 3)

time: 110 us -> 110 us (level)
    unnamed x24 -> x26, local copies, waits for them, and re-layouts: 5.79 us -> 6.53 us
  transfers between devices with their start and end apart: 26 -> 26, of which waited for: 10 -> 10; matrix products, arithmetic and copies ran while one was open for 9% -> 8% of each run, Pallas kernels for 17% -> 17%
where the time goes in v11:
time: 110 us; the launch traced here: 109 us
  starting transfers between devices  42.3 us (38%)
  waiting for transfers between devices  29.7 us (27%)
  Pallas kernels  18.9 us (17%)
  other arithmetic  9.81 us (9%)
  local copies, waits for them, and re-layouts  6.53 us (6%)
  between operations  1.48 us (1%)
    ppermute x22, starting transfers between devices, _shift(): return lax.ppermute(v, axis, [(i, (i + k) % size) for i in range(size)])  36.5 us
    ppermute x22, waiting for transfers between devices, _shift(): return lax.ppermute(v, axis, [(i, (i + k) % size) for i in range(size)])  24.9 us
    unnamed x26, local copies, waits for them, and re-layouts  6.53 us
    pallas_call x2, Pallas kernels, keys_of(): _call(functools.partial(_keys_kernel, len(blocks)), f'keys{len(blocks)}',...  6.31 us
    ppermute x4, starting transfers between devices, _flip(): return lax.ppermute(v, axis, [(i, i ^ bit) for i in range(size)])  5.73 us
    pallas_call x1, Pallas kernels, body(): pl.pallas_call(_outer_kernel, name='outer_step', out_shape=[jax.ShapeDtyp...  5.12 us
    ppermute x4, waiting for transfers between devices, _flip(): return lax.ppermute(v, axis, [(i, i ^ bit) for i in range(size)])  4.86 us
    pallas_call x2, Pallas kernels, grad(): _call(functools.partial(_grad_kernel, half), f'grad{half}', [((ROWS, KV),...  3.79 us
  transfers between devices with their start and end apart: 26, of which 10 were waited for; matrix products, arithmetic and copies ran while one was open for 8% of the time, Pallas kernels for 17%

profile of v11, /device:TPU:1, one launch (start us, length us, event | category | flops | bytes accessed | tf_op | source)
XLA Modules:
  0.0 108.8 jit_solution(1026884595227623886)
XLA Ops:
  0.6 2.2 %collective-permute-start = (bf16[256,1024]{1,0:T(8,128)(2,1)}, bf16[256,1024]{1,0:T(8,128)(2,1)S(1)}, u32[]{:S(2)}, u32[]{:S(2)}) collective-permute-start(bf16[256,1024]{1,0:T(8,128)(2,1)} %c0.3), channel_id=1, source_target_pairs={{0,4},{4,8},{8,12},{12,0},{1,5},{5,9},{9,13},{13,1},{2,6},{6,10},{... | collective-permute-start | bytes 1572872 | tf_op jit(solution)/shard_map/ppermute | solution.py:29
  7.2 7.0 %collective-permute-start.4 = (bf16[144,1024]{1,0:T(8,128)(2,1)S(1)}, bf16[144,1024]{1,0:T(8,128)(2,1)S(1)}, u32[]{:S(2)}, u32[]{:S(2)}) collective-permute-start(bf16[144,1024]{1,0:T(8,128)(2,1)S(1)} %get-tuple-element.41), channel_id=1, source_target_pairs={{0,16},{16,0},{1,17},{17,1},{2,18},{18,2},{3,19},{19,3},{4,20},{20... | collective-permute-start | bytes 884744 | tf_op jit(solution)/shard_map/ppermute | solution.py:29
  16.6 1.7 %copy-done.3 = bf16[256,4608]{1,0:T(8,128)(2,1)S(1)} copy-done((bf16[256,4608]{1,0:T(8,128)(2,1)S(1)}, bf16[256,4608]{1,0:T(8,128)(2,1)}, u32[]{:S(2)}) %copy-start.3) | copy-done | bytes 2359320
  19.0 2.8 %normed.1 = (bf16[256,1152]{1,0:T(8,128)(2,1)S(1)}, bf16[256,1152]{1,0:T(8,128)(2,1)}, bf16[256,2176]{1,0:T(8,128)(2,1)S(1)}, bf16[256,1152]{1,0:T(8,128)(2,1)S(1)}) custom-call(bf16[256,4608]{1,0:T(8,128)(2,1)S(1)} %copy-done.3, f32[4608]{0:T(1024)S(1)} %copy-done.10, bf16[256,1024]{1,0:T(8,128)(2,1)S(1)} %copy-done.1), custom_call_target="tpu_custom_call" | custom-call | bytes 1024 | tf_op jit(solution)/shard_map/normed/pallas_call | solution.py:137
  23.0 2.6 %collective-permute-start.3 = (bf16[256,1152]{1,0:T(8,128)(2,1)S(1)}, bf16[256,1152]{1,0:T(8,128)(2,1)S(1)}, u32[]{:S(2)}, u32[]{:S(2)}) collective-permute-start(bf16[256,1152]{1,0:T(8,128)(2,1)S(1)} %get-tuple-element.47), channel_id=1, source_target_pairs={{0,12},{4,0},{8,4},{12,8},{1,13},{5,1},{9,5},{13,9},{2,14},{6,2},{... | collective-permute-start | bytes 1769480 | tf_op jit(solution)/shard_map/ppermute | solution.py:29
  28.4 2.0 %fusion = f16[144,1024]{1,0:T(8,128)(2,1)} fusion(f32[4,144,1024]{2,1,0:T(8,128)} %refs_4_.1, s32[]{:T(128)S(6)} %select_n.33, bf16[2,144,1024]{2,1,0:T(8,128)(2,1)} %collective-permute-done.19, s32[]{:T(128)S(6)} %select_n.34, bf16[2,144,1024]{2,1,0:T(8,128)(2,1)S(1)} %get-tuple-element.70), kind=kLoop, calls=%fused_computation.10 | loop fusion | flops 1032192 | bytes 1474568 | tf_op jit(solution)/shard_map/mul | solution.py:157
  30.4 1.9 %collective-permute-start.20 = (f16[144,1024]{1,0:T(8,128)(2,1)}, f16[144,1024]{1,0:T(8,128)(2,1)}, u32[]{:S(2)}, u32[]{:S(2)}) collective-permute-start(f16[144,1024]{1,0:T(8,128)(2,1)} %fusion), channel_id=1, source_target_pairs={{0,64},{64,0},{128,192},{192,128},{1,65},{65,1},{129,193},{193,129... | collective-permute-start | bytes 884744 | tf_op jit(solution)/shard_map/ppermute | solution.py:33
  32.4 7.0 %collective-permute-done.2.refs_1_.n1 = bf16[256,1152]{1,0:T(8,128)(2,1)S(1)} collective-permute-done((bf16[256,1152]{1,0:T(8,128)(2,1)}, bf16[256,1152]{1,0:T(8,128)(2,1)S(1)}, u32[]{:S(2)}, u32[]{:S(2)}) %collective-permute-start.2) | collective-permute-done | bytes 589856 | tf_op jit(solution)/shard_map/ppermute | solution.py:29
  41.4 2.1 %collective-permute-start.7 = (bf16[2,144,1024]{2,1,0:T(8,128)(2,1)S(1)}, bf16[2,144,1024]{2,1,0:T(8,128)(2,1)}, u32[]{:S(2)}, u32[]{:S(2)}) collective-permute-start(bf16[2,144,1024]{2,1,0:T(8,128)(2,1)S(1)} %pad_maximum_fusion.refs_3_.refs_1_), channel_id=1, source_target_pairs={{0,2},{1,3},{2,0},{3,1},{4,6},{5,7},{6,4},{7,5},{8,10},{9,11},{10,... | collective-permute-start | bytes 1769480 | tf_op jit(solution)/shard_map/ppermute | solution.py:29
  46.5 2.3 %collective-permute-start.21 = (f16[72,1024]{1,0:T(8,128)(2,1)}, f16[72,1024]{1,0:T(8,128)(2,1)}, u32[]{:S(2)}, u32[]{:S(2)}) collective-permute-start(f16[72,1024]{1,0:T(8,128)(2,1)} %dynamic-slice_convert_fusion), channel_id=1, source_target_pairs={{0,128},{64,192},{128,0},{192,64},{1,129},{65,193},{129,1},{193,65... | collective-permute-start | bytes 442376 | tf_op jit(solution)/shard_map/ppermute | solution.py:33
  48.8 4.9 %collective-permute-done.21 = f16[72,1024]{1,0:T(8,128)(2,1)} collective-permute-done((f16[72,1024]{1,0:T(8,128)(2,1)}, f16[72,1024]{1,0:T(8,128)(2,1)}, u32[]{:S(2)}, u32[]{:S(2)}) %collective-permute-start.21) | collective-permute-done | bytes 147488 | tf_op jit(solution)/shard_map/ppermute | solution.py:33
  53.7 1.7 %add_convert_fusion.2 = f16[72,1024]{1,0:T(8,128)(2,1)} fusion(f16[72,1024]{1,0:T(8,128)(2,1)} %collective-permute-done.21, f32[144,1024]{1,0:T(8,128)} %copy-done.12, s32[]{:T(128)S(6)} %select_n.35), kind=kLoop, calls=%fused_computation.12 | loop fusion | flops 221184 | bytes 589828 | tf_op jit(solution)/shard_map/convert_element_type | solution.py:163
  56.4 3.9 %keys3.1 = (f32[256,1024]{1,0:T(8,128)S(1)}, bf16[256,1024]{1,0:T(8,128)(2,1)S(1)}, bf16[256,1024]{1,0:T(8,128)(2,1)S(1)}) custom-call(bf16[256,1152]{1,0:T(8,128)(2,1)S(1)} %get-tuple-element.56.refs_0_.n0, bf16[256,1152]{1,0:T(8,128)(2,1)S(1)} %collective-permute-done.2.refs_1_.n1, bf16[256,1152]{1,0:T(8,128)(2,1)S(1)} %collective-permute-done.3.refs_2_.n3, ...), custom_call_target="tpu_custom_call" | custom-call | bytes 1024 | tf_op jit(solution)/shard_map/keys3/pallas_call | solution.py:172
  60.3 6.2 %collective-permute-done.10.m2.refs_0_ = bf16[256,2176]{1,0:T(8,128)(2,1)S(1)} collective-permute-done((bf16[256,2176]{1,0:T(8,128)(2,1)}, bf16[256,2176]{1,0:T(8,128)(2,1)S(1)}, u32[]{:S(2)}, u32[]{:S(2)}) %collective-permute-start.10) | collective-permute-done | bytes 1114144 | tf_op jit(solution)/shard_map/ppermute | solution.py:29
  66.6 1.6 %grad0.1 = (f32[144,1024]{1,0:T(8,128)S(1)}, bf16[144,1024]{1,0:T(8,128)(2,1)S(1)}, bf16[144,1024]{1,0:T(8,128)(2,1)S(1)}, bf16[144,1024]{1,0:T(8,128)(2,1)S(1)}) custom-call(bf16[256,1152]{1,0:T(8,128)(2,1)S(1)} %get-tuple-element.56.refs_0_.n0, bf16[256,1024]{1,0:T(8,128)(2,1)S(1)} %copy-done.2, bf16[256,1152]{1,0:T(8,128)(2,1)S(1)} %collective-permute-done.2.refs_1_.n1, ...), custom_call_target="tpu_custom_call" | custom-call | bytes 1024 | tf_op jit(solution)/shard_map/grad0/pallas_call | solution.py:185
  69.3 1.7 %collective-permute-start.12 = (bf16[144,1024]{1,0:T(8,128)(2,1)S(1)}, bf16[144,1024]{1,0:T(8,128)(2,1)S(1)}, u32[]{:S(2)}, u32[]{:S(2)}) collective-permute-start(bf16[144,1024]{1,0:T(8,128)(2,1)S(1)} %get-tuple-element.58), channel_id=1, source_target_pairs={{0,3},{1,0},{2,1},{3,2},{4,7},{5,4},{6,5},{7,6},{8,11},{9,8},{10,9... | collective-permute-start | bytes 884744 | tf_op jit(solution)/shard_map/ppermute | solution.py:29
  73.1 1.8 %collective-permute-start.8 = (bf16[256,1024]{1,0:T(8,128)(2,1)S(1)}, bf16[256,1024]{1,0:T(8,128)(2,1)S(1)}, u32[]{:S(2)}, u32[]{:S(2)}) collective-permute-start(bf16[256,1024]{1,0:T(8,128)(2,1)S(1)} %get-tuple-element.51), channel_id=1, source_target_pairs={{0,12},{4,0},{8,4},{12,8},{1,13},{5,1},{9,5},{13,9},{2,14},{6,2},{... | collective-permute-start | bytes 1572872 | tf_op jit(solution)/shard_map/ppermute | solution.py:29
  77.7 2.9 %collective-permute-start.24 = (f16[144,1024]{1,0:T(8,128)(2,1)S(1)}, f16[144,1024]{1,0:T(8,128)(2,1)S(1)}, u32[]{:S(2)}, u32[]{:S(2)}) collective-permute-start(f16[144,1024]{1,0:T(8,128)(2,1)S(1)} %get-tuple-element.74), channel_id=1, source_target_pairs={{0,32},{32,0},{1,33},{33,1},{2,34},{34,2},{3,35},{35,3},{4,36},{36... | collective-permute-start | bytes 884744 | tf_op jit(solution)/shard_map/ppermute | solution.py:29
  80.7 2.1 %grad1.1 = (f32[144,1024]{1,0:T(8,128)S(1)}, bf16[144,1024]{1,0:T(8,128)(2,1)S(1)}, bf16[144,1024]{1,0:T(8,128)(2,1)S(1)}, bf16[144,1024]{1,0:T(8,128)(2,1)S(1)}) custom-call(bf16[256,1152]{1,0:T(8,128)(2,1)S(1)} %get-tuple-element.56.refs_0_.n0, bf16[256,1024]{1,0:T(8,128)(2,1)S(1)} %copy-done.2, bf16[256,1152]{1,0:T(8,128)(2,1)S(1)} %collective-permute-done.2.refs_1_.n1, ...), custom_call_target="tpu_custom_call" | custom-call | bytes 1024 | tf_op jit(solution)/shard_map/grad1/pallas_call | solution.py:185
  82.8 2.4 %keys1.1 = bf16[256,1024]{1,0:T(8,128)(2,1)S(1)} custom-call(bf16[256,2176]{1,0:T(8,128)(2,1)S(1)} %collective-permute-done.10.m2.refs_0_, bf16[2,144,1024]{2,1,0:T(8,128)(2,1)S(1)} %pad_maximum_fusion.refs_3_.refs_1_, bf16[2,144,1024]{2,1,0:T(8,128)(2,1)} %collective-permute-done.5.refs_4_.refs_2_, ...), custom_call_target="tpu_custom_call" | custom-call | bytes 1024 | tf_op jit(solution)/shard_map/keys1/pallas_call | solution.py:172
  86.4 4.0 %collective-permute-start.25 = (f16[144,1024]{1,0:T(8,128)(2,1)S(1)}, f16[144,1024]{1,0:T(8,128)(2,1)S(1)}, u32[]{:S(2)}, u32[]{:S(2)}) collective-permute-start(f16[144,1024]{1,0:T(8,128)(2,1)S(1)} %collective-permute-done.23), channel_id=1, source_target_pairs={{0,32},{32,0},{1,33},{33,1},{2,34},{34,2},{3,35},{35,3},{4,36},{36... | collective-permute-start | bytes 884744 | tf_op jit(solution)/shard_map/ppermute | solution.py:29
  94.0 5.1 %outer_step.1 = (f32[4,144,1024]{2,1,0:T(8,128)}, f32[4,144,1024]{2,1,0:T(8,128)}) custom-call(s32[2]{0:T(128)S(1)} %pad_add_fusion.place_ref, f32[144,1024]{1,0:T(8,128)S(1)} %get-tuple-element.78.refs_0_, f32[144,1024]{1,0:T(8,128)S(1)} %convert_multiply_fusion.2.refs_1_, f32[144,1024]{1,0:T(8,128)S(1)} %convert_multiply_fusion.1.refs_2_, ...), custom_call_target="tpu_custom_call" | custom-call | bytes 1024 | tf_op jit(solution)/shard_map/outer_step/pallas_call | solution.py:213
  100.3 4.2 %collective-permute-done.18 = bf16[144,1024]{1,0:T(8,128)(2,1)S(1)} collective-permute-done((bf16[144,1024]{1,0:T(8,128)(2,1)S(1)}, bf16[144,1024]{1,0:T(8,128)(2,1)S(1)}, u32[]{:S(2)}, u32[]{:S(2)}) %collective-permute-start.18) | collective-permute-done | bytes 294944 | tf_op jit(solution)/shard_map/ppermute | solution.py:29
  104.5 1.9 %collective-permute-done.16 = bf16[144,1024]{1,0:T(8,128)(2,1)S(1)} collective-permute-done((bf16[144,1024]{1,0:T(8,128)(2,1)S(1)}, bf16[144,1024]{1,0:T(8,128)(2,1)S(1)}, u32[]{:S(2)}, u32[]{:S(2)}) %collective-permute-start.16) | collective-permute-done | bytes 294944 | tf_op jit(solution)/shard_map/ppermute | solution.py:29
  (74 shorter events, 31.1 us)
Async XLA Ops:
  0.6 22.2 %collective-permute-start = (bf16[256,1024]{1,0:T(8,128)(2,1)}, bf16[256,1024]{1,0:T(8,128)(2,1)S(1)}, u32[]{:S(2)}, u32[]{:S(2)}) collective-permute-start(bf16[256,1024]{1,0:T(8,128)(2,1)} %c0.3), channel_id=1, source_target_pairs={{0,4},{4,8},{8,12},{12,0},{1,5},{5,9},{9,13},{13,1},{2,6},{6,10},{... | collective-permute-start | bytes 1572872 | tf_op jit(solution)/shard_map/ppermute | solution.py:29
  2.8 20.0 %collective-permute-start.1 = (bf16[256,1024]{1,0:T(8,128)(2,1)}, bf16[256,1024]{1,0:T(8,128)(2,1)S(1)}, u32[]{:S(2)}, u32[]{:S(2)}) collective-permute-start(bf16[256,1024]{1,0:T(8,128)(2,1)} %c0.3), channel_id=1, source_target_pairs={{0,12},{4,0},{8,4},{12,8},{1,13},{5,1},{9,5},{13,9},{2,14},{6,2},{... | collective-permute-start | bytes 1572872 | tf_op jit(solution)/shard_map/ppermute | solution.py:29
  7.2 18.4 %collective-permute-start.4 = (bf16[144,1024]{1,0:T(8,128)(2,1)S(1)}, bf16[144,1024]{1,0:T(8,128)(2,1)S(1)}, u32[]{:S(2)}, u32[]{:S(2)}) collective-permute-start(bf16[144,1024]{1,0:T(8,128)(2,1)S(1)} %get-tuple-element.41), channel_id=1, source_target_pairs={{0,16},{16,0},{1,17},{17,1},{2,18},{18,2},{3,19},{19,3},{4,20},{20... | collective-permute-start | bytes 884744 | tf_op jit(solution)/shard_map/ppermute | solution.py:29
  14.2 14.2 %collective-permute-start.19 = (bf16[2,144,1024]{2,1,0:T(8,128)(2,1)}, bf16[2,144,1024]{2,1,0:T(8,128)(2,1)}, u32[]{:S(2)}, u32[]{:S(2)}) collective-permute-start(bf16[2,144,1024]{2,1,0:T(8,128)(2,1)} %get-tuple-element.71), channel_id=1, source_target_pairs={{0,32},{32,0},{1,33},{33,1},{2,34},{34,2},{3,35},{35,3},{4,36},{36... | collective-permute-start | bytes 1769480 | tf_op jit(solution)/shard_map/ppermute | solution.py:29
  22.8 16.6 %collective-permute-start.2 = (bf16[256,1152]{1,0:T(8,128)(2,1)}, bf16[256,1152]{1,0:T(8,128)(2,1)S(1)}, u32[]{:S(2)}, u32[]{:S(2)}) collective-permute-start(bf16[256,1152]{1,0:T(8,128)(2,1)} %get-tuple-element.45), channel_id=1, source_target_pairs={{0,4},{4,8},{8,12},{12,0},{1,5},{5,9},{9,13},{13,1},{2,6},{6,10},{... | collective-permute-start | bytes 1769480 | tf_op jit(solution)/shard_map/ppermute | solution.py:29
  23.0 16.4 %collective-permute-start.3 = (bf16[256,1152]{1,0:T(8,128)(2,1)S(1)}, bf16[256,1152]{1,0:T(8,128)(2,1)S(1)}, u32[]{:S(2)}, u32[]{:S(2)}) collective-permute-start(bf16[256,1152]{1,0:T(8,128)(2,1)S(1)} %get-tuple-element.47), channel_id=1, source_target_pairs={{0,12},{4,0},{8,4},{12,8},{1,13},{5,1},{9,5},{13,9},{2,14},{6,2},{... | collective-permute-start | bytes 1769480 | tf_op jit(solution)/shard_map/ppermute | solution.py:29
  25.7 15.7 %collective-permute-start.5 = (bf16[2,144,1024]{2,1,0:T(8,128)(2,1)S(1)}, bf16[2,144,1024]{2,1,0:T(8,128)(2,1)}, u32[]{:S(2)}, u32[]{:S(2)}) collective-permute-start(bf16[2,144,1024]{2,1,0:T(8,128)(2,1)S(1)} %pad_maximum_fusion.refs_3_.refs_1_), channel_id=1, source_target_pairs={{0,1},{1,2},{2,3},{3,0},{4,5},{5,6},{6,7},{7,4},{8,9},{9,10},{10,1... | collective-permute-start | bytes 1769480 | tf_op jit(solution)/shard_map/ppermute | solution.py:29
  27.0 14.4 %collective-permute-start.6 = (bf16[2,144,1024]{2,1,0:T(8,128)(2,1)S(1)}, bf16[2,144,1024]{2,1,0:T(8,128)(2,1)}, u32[]{:S(2)}, u32[]{:S(2)}) collective-permute-start(bf16[2,144,1024]{2,1,0:T(8,128)(2,1)S(1)} %pad_maximum_fusion.refs_3_.refs_1_), channel_id=1, source_target_pairs={{0,3},{1,0},{2,1},{3,2},{4,7},{5,4},{6,5},{7,6},{8,11},{9,8},{10,9... | collective-permute-start | bytes 1769480 | tf_op jit(solution)/shard_map/ppermute | solution.py:29
  30.4 13.1 %collective-permute-start.20 = (f16[144,1024]{1,0:T(8,128)(2,1)}, f16[144,1024]{1,0:T(8,128)(2,1)}, u32[]{:S(2)}, u32[]{:S(2)}) collective-permute-start(f16[144,1024]{1,0:T(8,128)(2,1)} %fusion), channel_id=1, source_target_pairs={{0,64},{64,0},{128,192},{192,128},{1,65},{65,1},{129,193},{193,129... | collective-permute-start | bytes 884744 | tf_op jit(solution)/shard_map/ppermute | solution.py:33
  39.4 27.1 %collective-permute-start.10 = (bf16[256,2176]{1,0:T(8,128)(2,1)}, bf16[256,2176]{1,0:T(8,128)(2,1)S(1)}, u32[]{:S(2)}, u32[]{:S(2)}) collective-permute-start(bf16[256,2176]{1,0:T(8,128)(2,1)} %copy-done.11), channel_id=1, source_target_pairs={{0,8},{4,12},{8,0},{12,4},{1,9},{5,13},{9,1},{13,5},{2,10},{6,14},... | collective-permute-start | bytes 3342344 | tf_op jit(solution)/shard_map/ppermute | solution.py:29
  41.4 15.0 %collective-permute-start.7 = (bf16[2,144,1024]{2,1,0:T(8,128)(2,1)S(1)}, bf16[2,144,1024]{2,1,0:T(8,128)(2,1)}, u32[]{:S(2)}, u32[]{:S(2)}) collective-permute-start(bf16[2,144,1024]{2,1,0:T(8,128)(2,1)S(1)} %pad_maximum_fusion.refs_3_.refs_1_), channel_id=1, source_target_pairs={{0,2},{1,3},{2,0},{3,1},{4,6},{5,7},{6,4},{7,5},{8,10},{9,11},{10,... | collective-permute-start | bytes 1769480 | tf_op jit(solution)/shard_map/ppermute | solution.py:29
  55.4 15.5 %collective-permute-start.22 = (f16[72,1024]{1,0:T(8,128)(2,1)}, f16[72,1024]{1,0:T(8,128)(2,1)}, u32[]{:S(2)}, u32[]{:S(2)}) collective-permute-start(f16[72,1024]{1,0:T(8,128)(2,1)} %add_convert_fusion.2), channel_id=1, source_target_pairs={{0,128},{64,192},{128,0},{192,64},{1,129},{65,193},{129,1},{193,65... | collective-permute-start | bytes 442376 | tf_op jit(solution)/shard_map/ppermute | solution.py:33
  68.2 8.2 %collective-permute-start.11 = (bf16[144,1024]{1,0:T(8,128)(2,1)S(1)}, bf16[144,1024]{1,0:T(8,128)(2,1)S(1)}, u32[]{:S(2)}, u32[]{:S(2)}) collective-permute-start(bf16[144,1024]{1,0:T(8,128)(2,1)S(1)} %get-tuple-element.57), channel_id=1, source_target_pairs={{0,1},{1,2},{2,3},{3,0},{4,5},{5,6},{6,7},{7,4},{8,9},{9,10},{10,1... | collective-permute-start | bytes 884744 | tf_op jit(solution)/shard_map/ppermute | solution.py:29
  69.3 8.4 %collective-permute-start.12 = (bf16[144,1024]{1,0:T(8,128)(2,1)S(1)}, bf16[144,1024]{1,0:T(8,128)(2,1)S(1)}, u32[]{:S(2)}, u32[]{:S(2)}) collective-permute-start(bf16[144,1024]{1,0:T(8,128)(2,1)S(1)} %get-tuple-element.58), channel_id=1, source_target_pairs={{0,3},{1,0},{2,1},{3,2},{4,7},{5,4},{6,5},{7,6},{8,11},{9,8},{10,9... | collective-permute-start | bytes 884744 | tf_op jit(solution)/shard_map/ppermute | solution.py:29
  72.2 8.4 %collective-permute-start.23 = (f16[144,1024]{1,0:T(8,128)(2,1)S(1)}, f16[144,1024]{1,0:T(8,128)(2,1)S(1)}, u32[]{:S(2)}, u32[]{:S(2)}) collective-permute-start(f16[144,1024]{1,0:T(8,128)(2,1)S(1)} %get-tuple-element.74), channel_id=1, source_target_pairs={{0,64},{64,0},{128,192},{192,128},{1,65},{65,1},{129,193},{193,129... | collective-permute-start | bytes 884744 | tf_op jit(solution)/shard_map/ppermute | solution.py:33
  73.1 12.2 %collective-permute-start.8 = (bf16[256,1024]{1,0:T(8,128)(2,1)S(1)}, bf16[256,1024]{1,0:T(8,128)(2,1)S(1)}, u32[]{:S(2)}, u32[]{:S(2)}) collective-permute-start(bf16[256,1024]{1,0:T(8,128)(2,1)S(1)} %get-tuple-element.51), channel_id=1, source_target_pairs={{0,12},{4,0},{8,4},{12,8},{1,13},{5,1},{9,5},{13,9},{2,14},{6,2},{... | collective-permute-start | bytes 1572872 | tf_op jit(solution)/shard_map/ppermute | solution.py:29
  74.8 11.6 %collective-permute-start.9 = (bf16[256,1024]{1,0:T(8,128)(2,1)S(1)}, bf16[256,1024]{1,0:T(8,128)(2,1)S(1)}, u32[]{:S(2)}, u32[]{:S(2)}) collective-permute-start(bf16[256,1024]{1,0:T(8,128)(2,1)S(1)} %get-tuple-element.52), channel_id=1, source_target_pairs={{0,4},{4,8},{8,12},{12,0},{1,5},{5,9},{9,13},{13,1},{2,6},{6,10},{... | collective-permute-start | bytes 1572872 | tf_op jit(solution)/shard_map/ppermute | solution.py:29
  76.4 14.0 %collective-permute-start.14 = (bf16[144,1024]{1,0:T(8,128)(2,1)S(1)}, bf16[144,1024]{1,0:T(8,128)(2,1)S(1)}, u32[]{:S(2)}, u32[]{:S(2)}) collective-permute-start(bf16[144,1024]{1,0:T(8,128)(2,1)S(1)} %get-tuple-element.64), channel_id=1, source_target_pairs={{0,2},{1,3},{2,0},{3,1},{4,6},{5,7},{6,4},{7,5},{8,10},{9,11},{10,... | collective-permute-start | bytes 884744 | tf_op jit(solution)/shard_map/ppermute | solution.py:29
  77.7 14.6 %collective-permute-start.24 = (f16[144,1024]{1,0:T(8,128)(2,1)S(1)}, f16[144,1024]{1,0:T(8,128)(2,1)S(1)}, u32[]{:S(2)}, u32[]{:S(2)}) collective-permute-start(f16[144,1024]{1,0:T(8,128)(2,1)S(1)} %get-tuple-element.74), channel_id=1, source_target_pairs={{0,32},{32,0},{1,33},{33,1},{2,34},{34,2},{3,35},{35,3},{4,36},{36... | collective-permute-start | bytes 884744 | tf_op jit(solution)/shard_map/ppermute | solution.py:29
  86.4 12.7 %collective-permute-start.13 = (bf16[256,1024]{1,0:T(8,128)(2,1)S(1)}, bf16[256,1024]{1,0:T(8,128)(2,1)S(1)}, u32[]{:S(2)}, u32[]{:S(2)}) collective-permute-start(bf16[256,1024]{1,0:T(8,128)(2,1)S(1)} %keys1.1), channel_id=1, source_target_pairs={{0,8},{4,12},{8,0},{12,4},{1,9},{5,13},{9,1},{13,5},{2,10},{6,14},... | collective-permute-start | bytes 1572872 | tf_op jit(solution)/shard_map/ppermute | solution.py:29
  90.6 13.9 %collective-permute-start.18 = (bf16[144,1024]{1,0:T(8,128)(2,1)S(1)}, bf16[144,1024]{1,0:T(8,128)(2,1)S(1)}, u32[]{:S(2)}, u32[]{:S(2)}) collective-permute-start(bf16[144,1024]{1,0:T(8,128)(2,1)S(1)} %add_convert_fusion.1), channel_id=1, source_target_pairs={{0,16},{16,0},{1,17},{17,1},{2,18},{18,2},{3,19},{19,3},{4,20},{20... | collective-permute-start | bytes 884744 | tf_op jit(solution)/shard_map/ppermute | solution.py:29
  90.9 13.6 %collective-permute-start.17 = (bf16[144,1024]{1,0:T(8,128)(2,1)S(1)}, bf16[144,1024]{1,0:T(8,128)(2,1)S(1)}, u32[]{:S(2)}, u32[]{:S(2)}) collective-permute-start(bf16[144,1024]{1,0:T(8,128)(2,1)S(1)} %get-tuple-element.69), channel_id=1, source_target_pairs={{0,2},{1,3},{2,0},{3,1},{4,6},{5,7},{6,4},{7,5},{8,10},{9,11},{10,... | collective-permute-start | bytes 884744 | tf_op jit(solution)/shard_map/ppermute | solution.py:29
  92.3 14.1 %collective-permute-start.16 = (bf16[144,1024]{1,0:T(8,128)(2,1)S(1)}, bf16[144,1024]{1,0:T(8,128)(2,1)S(1)}, u32[]{:S(2)}, u32[]{:S(2)}) collective-permute-start(bf16[144,1024]{1,0:T(8,128)(2,1)S(1)} %get-tuple-element.67), channel_id=1, source_target_pairs={{0,3},{1,0},{2,1},{3,2},{4,7},{5,4},{6,5},{7,6},{8,11},{9,8},{10,9... | collective-permute-start | bytes 884744 | tf_op jit(solution)/shard_map/ppermute | solution.py:29
  93.3 14.5 %collective-permute-start.15 = (bf16[144,1024]{1,0:T(8,128)(2,1)S(1)}, bf16[144,1024]{1,0:T(8,128)(2,1)S(1)}, u32[]{:S(2)}, u32[]{:S(2)}) collective-permute-start(bf16[144,1024]{1,0:T(8,128)(2,1)S(1)} %get-tuple-element.65), channel_id=1, source_target_pairs={{0,1},{1,2},{2,3},{3,0},{4,5},{5,6},{6,7},{7,4},{8,9},{9,10},{10,1... | collective-permute-start | bytes 884744 | tf_op jit(solution)/shard_map/ppermute | solution.py:29
  (15 other events, 90.9 us)
